TPU v7x, 32 devices: a whole 2x2x4 slice. The times are simulated.
32 devices in a mesh: dp: 8 (over z, core), expert: 4 (over y, x).
Axes of the slice: x: 2, y: 2, z: 4, core: 2. Of those that a mesh axis runs over, the one named last changes fastest.
Arguments:
- tokens: bfloat16 [75264, 512], P(('dp', 'expert')), may hold values from -6 to 6
- gain_one: float32 [512], replicated, may hold values from 0.5 to 1.5
- w_qkv: bfloat16 [512, 1536], replicated, may hold values from -0.25 to 0.25
- w_proj: bfloat16 [512, 512], replicated, may hold values from -1 to 1
- gain_two: float32 [512], replicated, may hold values from 0.5 to 1.5
- w_router: float32 [512, 8], replicated, may hold values from -0.1875 to 0.1875
- w_in: bfloat16 [8, 512, 2048], P('expert'), may hold values from -0.25 to 0.25
- w_eout: bfloat16 [8, 2048, 512], P('expert'), may hold values from -3 to 3
- picks: int32 [75264, 2], P(('dp', 'expert')), may hold values from 0 to 7, all different within a row; in each aligned block of 2352 rows (0 to 2351, 2352 to 4703, ...) at most 624 rows name the same one
- keep: int32 [75264, 2], P(('dp', 'expert')), may hold values 0 or 1
- grad_out: bfloat16 [75264, 512], P(('dp', 'expert')), may hold values from -6 to 6
Outputs:
- block_out: bfloat16 [75264, 512], P(('dp', 'expert'))
- grad_tokens: float32 [75264, 512], P(('dp', 'expert'))
- grad_gain_one: float32 [512], replicated
- grad_qkv: float32 [512, 1536], replicated
- grad_proj: float32 [512, 512], replicated
- grad_gain_two: float32 [512], replicated
- grad_router: float32 [512, 8], replicated
- grad_in: float32 [8, 512, 2048], P('expert', 'dp')
- grad_eout: float32 [8, 2048, 512], P('expert', 'dp')
Inputs may be any that keep to these rules, and one draw needn't show every extreme that they name: `picks`: each row names two different experts; among the 2352 rows of one device no expert is named by more than 624 rows, a bound that some block reaches. `keep`: 1 keeps the pick, 0 drops it.
All inputs are finite; a program needn't handle non-finite values. No bound on the sum of `keep` on one device may be relied on, other than what follows from the above.
Results may differ from a plain program's by a relative error of at most 0.015.
Values may be sent and summed in bfloat16 or wider, within the bound.
No kernel may reach another device: no remote copies, remote signals or barrier semaphores. Data moves between devices by JAX's collectives and lax.ppermute only.
A program may use at most 320 MiB of HBM per device.

v0:
```python
import jax
import jax.numpy as jnp
from jax import lax
from jax.sharding import PartitionSpec as P

HEADS = 8
PATCHES = 49


def norm_parts(values):
    mean = jnp.mean(values, axis=-1, keepdims=True)
    cent = values - mean
    factor = lax.rsqrt(jnp.mean(cent * cent, axis=-1, keepdims=True) + 1e-06)
    return (cent * factor, factor)


def norm_back(grad_normed, normed_hat, factor, gain):
    grad_hat = grad_normed * gain
    inner = grad_hat - jnp.mean(grad_hat, axis=-1, keepdims=True)
    inner = inner - normed_hat * jnp.mean(grad_hat * normed_hat, axis=-1, keepdims=True)
    return (factor * inner, jnp.sum(grad_normed * normed_hat, axis=0))


def expert_up(rows_here, w_in):
    return jnp.einsum("sjcd,jdf->sjcf", rows_here, w_in, preferred_element_type=jnp.float32)


def exact_gelu(values):
    return jax.nn.gelu(values, approximate=False)


def per_device(
    tokens, gain_one, w_qkv, w_proj, gain_two, w_router, w_in, w_eout, picks, keep, grad_out
):
    tok_rows, width = tokens.shape
    images = tok_rows // PATCHES
    head_dim = width // HEADS
    local_exp = w_in.shape[0]
    owners = lax.axis_size("expert")
    experts_all = local_exp * owners
    capacity = 8 * ((21 * tok_rows + 80 * experts_all - 1) // (80 * experts_all))
    factor_qk = head_dim ** (-0.5)
    bf = jnp.bfloat16
    f32 = jnp.float32
    inputs = tokens.astype(f32)
    hat_one, scale_one = norm_parts(inputs)
    act_one = (hat_one * gain_one).astype(bf)
    qkv = jnp.dot(act_one, w_qkv, preferred_element_type=f32).astype(bf)
    qkv_five = qkv.reshape(images, PATCHES, 3, HEADS, head_dim)
    query, keys, values = (qkv_five[:, :, 0], qkv_five[:, :, 1], qkv_five[:, :, 2])
    scores = jnp.einsum("bqhd,bkhd->bhqk", query, keys, preferred_element_type=f32) * factor_qk
    highest = jnp.max(scores, axis=-1, keepdims=True)
    expo = jnp.exp(scores - highest)
    total = jnp.sum(expo, axis=-1, keepdims=True)
    probs = expo / total
    log_total = highest + jnp.log(total)
    mixed = jnp.einsum("bhqk,bkhd->bqhd", probs.astype(bf), values, preferred_element_type=f32)
    mixed = mixed.astype(bf).reshape(tok_rows, width)
    hidden = inputs + jnp.dot(mixed, w_proj, preferred_element_type=f32)
    hat_two, scale_two = norm_parts(hidden)
    normed_two = hat_two * gain_two
    logits = jnp.dot(normed_two, w_router, precision=lax.Precision.HIGHEST)
    gates = jax.nn.softmax(logits, axis=-1)
    expert_ids = jnp.arange(experts_all, dtype=jnp.int32)
    onehot_int = (picks[:, :, None] == expert_ids).astype(jnp.int32)
    onehot = onehot_int.astype(f32)
    keep_f = keep.astype(f32)
    chosen = jnp.sum(onehot * gates[:, None, :], axis=2) * keep_f
    counts = jnp.sum(onehot_int, axis=1)
    before = jnp.cumsum(counts, axis=0) - counts
    slot = jnp.sum(before[:, None, :] * onehot_int, axis=2)
    index = (picks * capacity + slot).reshape(-1)
    rows_b = normed_two.astype(bf)
    pair_rows = rows_b[:, None, :] * keep.astype(bf)[:, :, None]
    buffer = (
        jnp.zeros((experts_all * capacity, width), bf).at[index].add(pair_rows.reshape(-1, width))
    )
    outgoing = buffer.reshape(owners, local_exp * capacity, width)
    received = lax.all_to_all(outgoing, "expert", split_axis=0, concat_axis=0, tiled=True)
    received = received.reshape(owners, local_exp, capacity, width)
    pre = expert_up(received, w_in)
    act = exact_gelu(pre).astype(bf)
    expert_out = jnp.einsum("sjcf,jfd->sjcd", act, w_eout, preferred_element_type=f32).astype(bf)
    returned = lax.all_to_all(
        expert_out.reshape(owners, local_exp * capacity, width),
        "expert",
        split_axis=0,
        concat_axis=0,
        tiled=True,
    )
    pair_out = returned.reshape(experts_all * capacity, width)[index].reshape(tok_rows, 2, width)
    moe = jnp.sum(chosen[:, :, None] * pair_out.astype(f32), axis=1)
    block_out = (hidden + moe).astype(bf)
    grad_top = grad_out.astype(f32)
    pair_grad = jnp.sum(pair_out.astype(f32) * grad_top[:, None, :], axis=2) * keep_f
    grad_gates = jnp.sum(onehot * pair_grad[:, :, None], axis=1)
    grad_logits = gates * (grad_gates - jnp.sum(gates * grad_gates, axis=-1, keepdims=True))
    grad_router = jnp.dot(normed_two.T, grad_logits, precision=lax.Precision.HIGHEST)
    grad_normed = jnp.dot(grad_logits, w_router.T, precision=lax.Precision.HIGHEST)
    grad_pairs = (chosen[:, :, None] * grad_top[:, None, :]).astype(bf)
    grad_buffer = (
        jnp.zeros((experts_all * capacity, width), bf).at[index].add(grad_pairs.reshape(-1, width))
    )
    grad_send = grad_buffer.reshape(owners, local_exp * capacity, width)
    grad_recv, again = (
        lax.all_to_all(grad_send, "expert", split_axis=0, concat_axis=0, tiled=True),
        lax.all_to_all(outgoing, "expert", split_axis=0, concat_axis=0, tiled=True),
    )
    rows_here = again.reshape(owners, local_exp, capacity, width)
    grad_recv = grad_recv.reshape(owners, local_exp, capacity, width)
    pre_again = expert_up(rows_here, w_in)
    gelu_val, gelu_pull = jax.vjp(exact_gelu, pre_again)
    act_again = gelu_val.astype(bf)
    grad_act = jnp.einsum("sjcd,jfd->sjcf", grad_recv, w_eout, preferred_element_type=f32)
    grad_pre = gelu_pull(grad_act)[0].astype(bf)
    grad_eout_local = jnp.einsum("sjcf,sjcd->jfd", act_again, grad_recv, preferred_element_type=f32)
    grad_in_local = jnp.einsum("sjcd,sjcf->jdf", rows_here, grad_pre, preferred_element_type=f32)
    grad_rows = jnp.einsum("sjcf,jdf->sjcd", grad_pre, w_in, preferred_element_type=f32).astype(bf)
    came_back = lax.all_to_all(
        grad_rows.reshape(owners, local_exp * capacity, width),
        "expert",
        split_axis=0,
        concat_axis=0,
        tiled=True,
    )
    grad_pair_rows = came_back.reshape(experts_all * capacity, width)[index].reshape(
        tok_rows, 2, width
    )
    grad_normed = grad_normed + jnp.sum(grad_pair_rows.astype(f32) * keep_f[:, :, None], axis=1)
    grad_hidden_norm, grad_gain_two = norm_back(grad_normed, hat_two, scale_two, gain_two)
    grad_hidden = grad_top + grad_hidden_norm
    grad_attn = grad_hidden.astype(bf)
    grad_proj = jnp.dot(mixed.T, grad_attn, preferred_element_type=f32)
    grad_mixed = jnp.dot(grad_attn, w_proj.T, preferred_element_type=f32).astype(bf)
    grad_mixed = grad_mixed.reshape(images, PATCHES, HEADS, head_dim)
    scores_again = (
        jnp.einsum("bqhd,bkhd->bhqk", query, keys, preferred_element_type=f32) * factor_qk
    )
    probs_again = jnp.exp(scores_again - log_total)
    grad_probs = jnp.einsum("bqhd,bkhd->bhqk", grad_mixed, values, preferred_element_type=f32)
    grad_values = jnp.einsum(
        "bhqk,bqhd->bkhd", probs_again.astype(bf), grad_mixed, preferred_element_type=f32
    )
    grad_scores = probs_again * (
        grad_probs - jnp.sum(probs_again * grad_probs, axis=-1, keepdims=True)
    )
    grad_scores = grad_scores.astype(bf)
    grad_query = (
        jnp.einsum("bhqk,bkhd->bqhd", grad_scores, keys, preferred_element_type=f32) * factor_qk
    )
    grad_keys = (
        jnp.einsum("bhqk,bqhd->bkhd", grad_scores, query, preferred_element_type=f32) * factor_qk
    )
    grad_qkv_rows = (
        jnp.stack([grad_query, grad_keys, grad_values], axis=2)
        .astype(bf)
        .reshape(tok_rows, 3 * width)
    )
    grad_qkv_local = jnp.dot(act_one.T, grad_qkv_rows, preferred_element_type=f32)
    grad_act_one = jnp.dot(grad_qkv_rows, w_qkv.T, preferred_element_type=f32)
    grad_input_norm, grad_gain_one = norm_back(grad_act_one, hat_one, scale_one, gain_one)
    grad_tokens = grad_hidden + grad_input_norm
    summed = lax.psum(
        (grad_gain_one, grad_qkv_local, grad_proj, grad_gain_two, grad_router), ("dp", "expert")
    )
    expert_summed = (
        lax.psum_scatter(
            grad_in_local.astype(jnp.bfloat16), "dp", scatter_dimension=1, tiled=True
        ).astype(jnp.float32),
        lax.psum_scatter(
            grad_eout_local.astype(jnp.bfloat16), "dp", scatter_dimension=1, tiled=True
        ).astype(jnp.float32),
    )
    return (
        block_out,
        grad_tokens,
        summed[0],
        summed[1],
        summed[2],
        summed[3],
        summed[4],
        expert_summed[0],
        expert_summed[1],
    )


def solution(mesh):
    placed = (
        P(("dp", "expert"), None),
        P(),
        P(),
        P(),
        P(),
        P(),
        P("expert", None, None),
        P("expert", None, None),
        P(("dp", "expert"), None),
        P(("dp", "expert"), None),
        P(("dp", "expert"), None),
    )
    return jax.shard_map(
        per_device,
        mesh=mesh,
        in_specs=placed,
        out_specs=(
            P(("dp", "expert"), None),
            P(("dp", "expert"), None),
            P(),
            P(),
            P(),
            P(),
            P(),
            P("expert", "dp", None),
            P("expert", "dp", None),
        ),
        check_vma=False,
    )
```

profile of v0, /device:TPU:0, one launch (start us, length us, event | category | flops | bytes accessed | tf_op | source)
XLA Modules:
  0.0 927.5 jit_solution(8975562006478498640)
XLA Ops:
  22.2 18.3 %reshape.184 = bf16[48,49,3,8,64]{4,3,2,1,0:T(8,128)(2,1)} reshape(bf16[2352,1536]{1,0:T(8,128)(2,1)} %convolution_convert_fusion) | data formatting | bytes 14450688 | tf_op jit(solution)/shard_map/reshape | solution.py:49
  50.5 11.5 %multiply_reduce_fusion.4 = (f32[48,8,49]{2,1,0:T(8,128)S(1)}, f32[48,8,49,49]{2,3,1,0:T(8,128)}) fusion(bf16[48,49,1,8,64]{4,3,2,1,0:T(8,128)(2,1)} %get-tuple-element.26, bf16[48,49,1,8,64]{4,3,2,1,0:T(8,128)(2,1)S(1)} %get-tuple-element.25), kind=kOutput, calls=%fused_computation.51 | convolution fusion | flops 119839104 | bytes 8580096 | tf_op jit(solution)/shard_map/bqhd,bkhd->bhqk/dot_general | solution.py:51
  69.4 11.6 %convert_bitcast_fusion.1 = bf16[48,49,8,64]{3,1,2,0:T(8,128)(2,1)} fusion(f32[48,8,49,49]{2,3,1,0:T(8,128)} %get-tuple-element.32, f32[48,8,49]{2,1,0:T(8,128)S(1)} %fusion.24, f32[48,8,49]{2,1,0:T(8,128)S(1)} %get-tuple-element.31, bf16[48,49,1,8,64]{4,3,2,1,0:T(8,128)(2,1)} %get-tuple-element.24), kind=kOutput, calls=%fused_computation.72 | convolution fusion | flops 122906112 | bytes 8655360 | tf_op jit(solution)/shard_map/bhqk,bkhd->bqhd/dot_general | solution.py:57
  108.8 13.3 %mul.274 = bf16[2352,2,512]{2,1,0:T(2,128)(2,1)} broadcast(bf16[2352,512]{1,0:T(8,128)(2,1)S(1)} %multiply_convert_fusion.5), dimensions={0,2} | broadcast | bytes 7225344 | tf_op jit(solution)/shard_map/mul | solution.py:74
  134.1 42.2 %scatter_custom_fusion = bf16[4992,512]{1,0:T(8,128)(2,1)} fusion(s32[4704]{0:T(1024)S(1)} %fusion.100, bf16[4704,512]{1,0:T(8,128)(2,1)} %mul.275, bf16[]{:T(256)} %constant.11.clone.1, bf16[4704]{0:T(1024)(128)(2,1)S(1)} %mul.276), kind=kCustom, calls=%fused_computation.99 | custom fusion | flops 4816896 | bytes 9938946 | tf_op jit(solution)/shard_map/scatter-add | solution.py:76
  195.4 12.4 %mul.285 = f32[2352,2,512]{2,1,0:T(2,128)} broadcast(bf16[2352,512]{1,0:T(8,128)(2,1)S(1)} %copy-done.5), dimensions={0,2} | broadcast | bytes 12042240 | tf_op jit(solution)/shard_map/mul | solution.py:95
  207.8 12.6 %mul.294 = f32[4704,512]{1,0:T(8,128)} reshape(f32[2352,2,512]{2,1,0:T(2,128)} %mul.285) | data formatting | bytes 19267584 | tf_op jit(solution)/shard_map/mul | solution.py:95
  221.8 43.6 %scatter_custom_fusion.1 = bf16[4992,512]{1,0:T(8,128)(2,1)} fusion(s32[4704]{0:T(1024)S(1)} %fusion.100, f32[4704,512]{1,0:T(8,128)} %mul.294, f32[4704]{0:T(1024)S(1)} %mul.292, bf16[]{:T(256)} %constant.11.clone.1), kind=kCustom, calls=%fused_computation.93 | custom fusion | flops 7225344 | bytes 14766082 | tf_op jit(solution)/shard_map/scatter-add | solution.py:102
  271.8 98.9 %fusion.9 = (bf16[4,2,624,2048]{3,2,0,1:T(8,128)(2,1)}, f32[4,2,624,2048]{3,2,0,1:T(8,128)}, f32[2,4,624,2048]{3,2,1,0:T(8,128)}) fusion(bf16[2,512,2048]{2,1,0:T(8,128)(2,1)} %param.17, bf16[4,2,624,512]{3,2,1,0:T(8,128)(2,1)} %bitcast.8), kind=kOutput, calls=%fused_computation.21 | convolution fusion | flops 11133517824 | bytes 111542272 | tf_op jit(solution)/shard_map/sjcd,jdf->sjcf/dot_general | solution.py:25
  370.7 17.9 %bitcast_convert_fusion = bf16[2,2048,512]{2,1,0:T(8,128)(2,1)} fusion(bf16[4,2,624,2048]{3,2,0,1:T(8,128)(2,1)} %get-tuple-element.22, bf16[4,2,624,512]{3,2,1,0:T(8,128)(2,1)} %bitcast.19), kind=kOutput, calls=%fused_computation.52 | convolution fusion | flops 10471079936 | bytes 29753344 | tf_op jit(solution)/shard_map/sjcf,sjcd->jfd/dot_general | solution.py:116
  388.7 16.2 %convert_bitcast_fusion.3 = bf16[4,2,624,512]{3,2,0,1:T(8,128)(2,1)S(1)} fusion(bf16[4,2,624,2048]{3,2,0,1:T(8,128)(2,1)} %get-tuple-element.22, bf16[2,2048,512]{2,1,0:T(8,128)(2,1)} %param.18), kind=kOutput, calls=%fused_computation.84 | convolution fusion | flops 10471538688 | bytes 29753344 | tf_op jit(solution)/shard_map/sjcf,jfd->sjcd/dot_general | solution.py:83
  412.6 38.3 %fusion.6 = bf16[4,2,624,2048]{3,2,0,1:T(8,128)(2,1)} fusion(f32[4,2,624,2048]{3,2,0,1:T(8,128)} %get-tuple-element.23, f32[2,4,624,2048]{3,2,1,0:T(8,128)} %get-tuple-element.35, bf16[4,2,624,512]{3,2,1,0:T(8,128)(2,1)} %bitcast.19, bf16[2,2048,512]{2,1,0:T(8,128)(2,1)} %param.18), kind=kOutput, calls=%fused_computation.13 | convolution fusion | flops 10612113408 | bytes 111542272 | tf_op jit(solution)/shard_map/sjcd,jfd->sjcf/dot_general | solution.py:114
  450.9 16.1 %convert_bitcast_fusion.2 = bf16[4,2,624,512]{3,2,0,1:T(8,128)(2,1)S(1)} fusion(bf16[4,2,624,2048]{3,2,0,1:T(8,128)(2,1)} %fusion.6, bf16[2,512,2048]{2,1,0:T(8,128)(2,1)} %param.17), kind=kOutput, calls=%fused_computation.83 | convolution fusion | flops 10471538688 | bytes 29753344 | tf_op jit(solution)/shard_map/sjcf,jdf->sjcd/dot_general | solution.py:118
  476.4 18.3 %bitcast_convert_fusion.1 = bf16[2,512,2048]{2,1,0:T(8,128)(2,1)} fusion(bf16[4,2,624,512]{3,2,1,0:T(8,128)(2,1)} %bitcast.8, bf16[4,2,624,2048]{3,2,0,1:T(8,128)(2,1)} %fusion.6), kind=kOutput, calls=%fused_computation.53 | convolution fusion | flops 10471079936 | bytes 29753344 | tf_op jit(solution)/shard_map/sjcd,sjcf->jdf/dot_general | solution.py:117
  494.8 18.2 %gather_fusion = bf16[4704,512]{1,0:T(8,128)(2,1)} fusion(bf16[4992,512]{1,0:T(8,128)(2,1)} %bitcast.17, s32[5120]{0:T(1024)S(1)} %copy-done.28), kind=kCustom, calls=%fused_computation | custom fusion | bytes 9652608 | tf_op jit(solution)/shard_map/gather | solution.py:91
  512.9 11.6 %reshape.198 = f32[2352,2,512]{2,1,0:T(2,128)} reshape(bf16[4704,512]{1,0:T(8,128)(2,1)} %gather_fusion) | data formatting | bytes 14450688 | tf_op jit(solution)/shard_map/convert_element_type | solution.py:92
  524.6 31.2 %multiply_reduce_fusion.2 = (f32[2352,2]{1,0:T(8,128)}, f32[2352,512]{1,0:T(8,128)}) fusion(f32[2352,2,512]{2,1,0:T(2,128)} %reshape.198, f32[2352,512]{1,0:T(8,128)} %convert_element_type.125, f32[2352,2]{1,0:T(8,128)S(1)} %copy-done.8), kind=kLoop, calls=%fused_computation.49 | loop fusion | flops 8424864 | bytes 19305216 | tf_op jit(solution)/shard_map/reduce_sum | solution.py:95
  558.3 17.8 %gather_fusion.1 = bf16[4704,512]{1,0:T(8,128)(2,1)} fusion(bf16[4992,512]{1,0:T(8,128)(2,1)} %bitcast.25, s32[5120]{0:T(1024)S(1)} %copy-done.28), kind=kCustom, calls=%fused_computation.1 | custom fusion | bytes 9652608 | tf_op jit(solution)/shard_map/gather | solution.py:126
  576.0 11.6 %reshape.199 = f32[2352,2,512]{2,1,0:T(2,128)} reshape(bf16[4704,512]{1,0:T(8,128)(2,1)} %gather_fusion.1) | data formatting | bytes 14450688 | tf_op jit(solution)/shard_map/convert_element_type | solution.py:129
  587.8 52.1 %multiply_reduce_fusion.1 = f32[2352,512]{1,0:T(8,128)S(1)} fusion(f32[2352,2,512]{2,1,0:T(2,128)} %reshape.199, f32[2352,2]{1,0:T(8,128)S(1)} %copy-done.9), kind=kLoop, calls=%fused_computation.47 | loop fusion | flops 3612672 | bytes 14469504 | tf_op jit(solution)/shard_map/reduce_sum | solution.py:129
  663.5 15.7 %multiply_reduce_fusion = (f32[48,8,49]{2,1,0:T(8,128)S(1)}, f32[48,8,49,49]{2,3,1,0:T(8,128)}) fusion(f32[48,8,49,49]{2,3,1,0:T(8,128)} %get-tuple-element.32, f32[48,8,49]{2,1,0:T(8,128)S(1)} %copy-done.10, bf16[48,49,1,8,64]{4,3,2,1,0:T(8,128)(2,1)} %get-tuple-element.24, bf16[48,49,8,64]{3,2,1,0:T(8,128)(2,1)} %reshape.197), kind=kOutput, calls=%fused_computation.42 | convolution fusion | flops 121683072 | bytes 12343296 | tf_op jit(solution)/shard_map/bqhd,bkhd->bhqk/dot_general | solution.py:140
  736.8 19.2 %convert_element_type.136 = bf16[2352,1536]{1,0:T(8,128)(2,1)} reshape(bf16[48,49,3,8,64]{4,3,2,1,0:T(8,128)(2,1)} %copy.101) | data formatting | bytes 14450688 | tf_op jit(solution)/shard_map/convert_element_type | solution.py:156
  785.5 41.4 %all-reduce.1 = (f32[512]{0:T(512)}, f32[512]{0:T(512)}, f32[512,8]{0,1:T(8,128)}) all-reduce(f32[512]{0:T(512)S(1)} %get-tuple-element.13, f32[512]{0:T(512)S(1)} %get-tuple-element.9, f32[512,8]{0,1:T(8,128)S(1)} %fusion.66), channel_id=1, replica_groups=mesh['dp'=8,'expert'=4] {'dp','expert'}, use_global_device_ids=true, to_apply=%region_26.27 | all-reduce | flops 5120 | bytes 40960 | tf_op jit(solution)/shard_map/psum | solution.py:163
  838.2 76.8 %all-reduce.5.cloned.1.call-done = (f32[512,1536]{1,0:T(8,128)}, f32[512,512]{1,0:T(8,128)}) async-done(((f32[512,1536]{1,0:T(8,128)}, f32[512,512]{1,0:T(8,128)}), (f32[512,1536]{1,0:T(8,128)}, f32[512,512]{1,0:T(8,128)})) %all-reduce.5.cloned.1.call-update) | async-done | bytes 4194320 | tf_op jit(solution)/shard_map/psum | solution.py:163
  (187 shorter events, 243.9 us)
Async XLA Ops:
  98.3 83.5 %copy-start.18 = (f32[2352]{0:T(1024)}, f32[2352]{0:T(1024)S(1)}, u32[]{:S(2)}) copy-start(f32[2352]{0:T(1024)S(1)} %broadcast_multiply_fusion.4) | copy-start | bytes 28228
  101.3 80.5 %copy-start.23 = (f32[2352]{0:T(1024)}, f32[2352]{0:T(1024)S(1)}, u32[]{:S(2)}) copy-start(f32[2352]{0:T(1024)S(1)} %add_rsqrt_fusion) | copy-start | bytes 28228
  176.3 90.5 %all-to-all-start = ((bf16[4,1248,512]{2,1,0:T(8,128)(2,1)}), bf16[4,1248,512]{2,1,0:T(8,128)(2,1)}, u32[]{:S(2)}, u32[]{:S(2)}) async-start(bf16[4,1248,512]{2,1,0:T(8,128)(2,1)} %bitcast.192), calls=%async_computation | async-start | bytes 10223616 | tf_op jit(solution)/shard_map/all_to_all | solution.py:79
  189.0 18.8 %copy-start.26 = (f32[2352]{0:T(1024)}, f32[2352]{0:T(1024)S(1)}, u32[]{:S(2)}) copy-start(f32[2352]{0:T(1024)S(1)} %get-tuple-element.36) | copy-start | bytes 28228
  266.8 104.0 %all-to-all-start.2 = ((bf16[4,1248,512]{2,1,0:T(8,128)(2,1)}), bf16[4,1248,512]{2,1,0:T(8,128)(2,1)}, u32[]{:S(2)}, u32[]{:S(2)}) async-start(bf16[4,1248,512]{2,1,0:T(8,128)(2,1)} %bitcast.194), calls=%async_computation.2 | async-start | bytes 10223616 | tf_op jit(solution)/shard_map/all_to_all | solution.py:106
  271.8 562.1 %reduce-scatter.5.cloned.1.call-start = ((), (), s32[]{:S(2)}) async-start(), calls=%async_computation.7 | async-start | bytes 4718592 | tf_op jit(solution)/shard_map/reduce_scatter | solution.py:170
  407.6 63.7 %all-to-all-start.1 = ((bf16[4,1248,512]{2,1,0:T(8,128)(2,1)}), bf16[4,1248,512]{2,1,0:T(8,128)(2,1)}, u32[]{:S(2)}, u32[]{:S(2)}) async-start(bf16[4,1248,512]{2,1,0:T(8,128)(2,1)} %bitcast.193), calls=%async_computation.1 | async-start | bytes 10223616 | tf_op jit(solution)/shard_map/all_to_all | solution.py:84
  471.3 87.0 %all-to-all-start.3 = ((bf16[4,1248,512]{2,1,0:T(8,128)(2,1)}), bf16[4,1248,512]{2,1,0:T(8,128)(2,1)}, u32[]{:S(2)}, u32[]{:S(2)}) async-start(bf16[4,1248,512]{2,1,0:T(8,128)(2,1)} %bitcast.191), calls=%async_computation.3 | async-start | bytes 10223616 | tf_op jit(solution)/shard_map/all_to_all | solution.py:119
  476.3 359.7 %reduce-scatter.3.cloned.1.call-start = ((), (), s32[]{:S(2)}) async-start(), calls=%async_computation.6 | async-start | bytes 4718592 | tf_op jit(solution)/shard_map/reduce_scatter | solution.py:167
  494.7 420.3 %all-reduce.5.cloned.1.call-start = ((), (), s32[]{:S(2)}) async-start(), calls=%async_computation.8 | async-start | bytes 8388608 | tf_op jit(solution)/shard_map/psum | solution.py:163
  524.6 32.9 %copy-start.30 = (s32[2352,2]{0,1:T(2,128)S(1)}, s32[2352,2]{0,1:T(2,128)}, u32[]{:S(2)}) copy-start(s32[2352,2]{0,1:T(2,128)} %param.20) | copy-start | bytes 56452
  524.6 33.0 %copy-start.22 = (s32[2352,2]{0,1:T(2,128)S(1)}, s32[2352,2]{0,1:T(2,128)}, u32[]{:S(2)}) copy-start(s32[2352,2]{0,1:T(2,128)} %param.19) | copy-start | bytes 56452
  524.6 33.0 %copy-start.16 = (f32[2352,8]{0,1:T(8,128)S(1)}, f32[2352,8]{0,1:T(8,128)}, u32[]{:S(2)}) copy-start(f32[2352,8]{0,1:T(8,128)} %copy-done.15) | copy-start | bytes 225796
  524.6 33.0 %copy-start.27 = (f32[2352]{0:T(1024)S(1)}, f32[2352]{0:T(1024)}, u32[]{:S(2)}) copy-start(f32[2352]{0:T(1024)} %copy-done.26) | copy-start | bytes 28228
  524.6 33.0 %copy-start.34 = (f32[2352]{0:T(1024)S(1)}, f32[2352]{0:T(1024)}, u32[]{:S(2)}) copy-start(f32[2352]{0:T(1024)} %copy-done.33) | copy-start | bytes 28228
  576.0 63.8 %slice-start = ((s8[4816896]{0:T(1024)(128)(4,1)}), s8[622592]{0:T(1024)(128)(4,1)S(1)}, s32[]{:S(2)}) async-start(s8[4816896]{0:T(1024)(128)(4,1)} %bitcast.187), calls=%async_computation.9 | async-start | bytes 1245184
  587.7 52.2 %slice-start.1 = ((s8[4816896]{0:T(1024)(128)(4,1)}), s8[4194304]{0:T(1024)(128)(4,1)S(1)}, s32[]{:S(2)}) async-start(s8[4816896]{0:T(1024)(128)(4,1)} %bitcast.187), calls=%async_computation.10 | async-start | bytes 8388608
  587.7 52.2 %copy-start.14 = (f32[2352,8]{0,1:T(8,128)S(1)}, f32[2352,8]{0,1:T(8,128)}, u32[]{:S(2)}) copy-start(f32[2352,8]{0,1:T(8,128)} %copy-done.13) | copy-start | bytes 225796
  587.7 52.2 %copy-start.19 = (f32[2352]{0:T(1024)S(1)}, f32[2352]{0:T(1024)}, u32[]{:S(2)}) copy-start(f32[2352]{0:T(1024)} %copy-done.18) | copy-start | bytes 28228
  587.7 52.2 %copy-start.24 = (f32[2352]{0:T(1024)S(1)}, f32[2352]{0:T(1024)}, u32[]{:S(2)}) copy-start(f32[2352]{0:T(1024)} %copy-done.23) | copy-start | bytes 28228
  587.7 52.2 %copy-start.35 = (f32[2352]{0:T(1024)S(1)}, f32[2352]{0:T(1024)}, u32[]{:S(2)}) copy-start(f32[2352]{0:T(1024)} %multiply_reduce_fusion.10) | copy-start | bytes 28228
  587.7 52.2 %copy-start.38 = (f32[512,8]{0,1:T(8,128)S(1)}, f32[512,8]{0,1:T(8,128)}, u32[]{:S(2)}) copy-start(f32[512,8]{0,1:T(8,128)} %param.16) | copy-start | bytes 49156
  587.7 52.2 %copy-start.40 = (f32[512]{0:T(512)S(1)}, f32[512]{0:T(512)}, u32[]{:S(2)}) copy-start(f32[512]{0:T(512)} %param.15) | copy-start | bytes 6148
  761.8 20.4 %slice-start.2 = ((s8[4816896]{0:T(1024)(128)(4,1)}), s8[622592]{0:T(1024)(128)(4,1)S(1)}, s32[]{:S(2)}) async-start(s8[4816896]{0:T(1024)(128)(4,1)} %bitcast.189), calls=%async_computation.11 | async-start | bytes 1245184
  (32 other events, 250.5 us)
Sparse Core Ops, SparseCore 0:
  388.8 52.9 reduce-scatter.4
  494.8 51.7 reduce-scatter.2
Sparse Core Ops, SparseCore 1:
  771.2 143.7 all-reduce.4
where the time goes:
time: 936 us; the launch traced here: 927 us
  matrix products  332 us (35%)
  other arithmetic  232 us (25%)
  local copies, waits for them, and re-layouts  207 us (22%)
  waiting for transfers between devices  78.5 us (8%)
  blocking collectives  41.4 us (4%)
  starting transfers between devices  20.6 us (2%)
  between operations  16.5 us (2%)
    dot_general x1, matrix products, expert_up(): jnp.einsum('sjcd,jdf->sjcf', rows_here, w_in, preferred_element_type=jnp....  98.9 us
    scatter-add x2, other arithmetic, per_device(): jnp.zeros((experts_all * capacity, width), bf).at[index]  85.8 us
    psum x1, waiting for transfers between devices, per_device(): lax.psum((grad_gain_one, grad_qkv_local, grad_proj, grad_gain_two, grad_r...  76.8 us
    reduce_sum x1, other arithmetic, per_device(): jnp.sum(grad_pair_rows.astype(f32) * keep_f[:, :, None], axis=1)  52.1 us
    psum x1, blocking collectives, per_device(): lax.psum((grad_gain_one, grad_qkv_local, grad_proj, grad_gain_two, grad_r...  41.4 us
    dot_general x1, matrix products, per_device(): jnp.einsum('sjcd,jfd->sjcf', grad_recv, w_eout, preferred_element_type=f32)  38.3 us
    reduce_sum x1, other arithmetic, per_device(): jnp.sum(pair_out.astype(f32) * grad_top[:, None, :], axis=2) * keep_f  31.2 us
    mul x2, local copies, waits for them, and re-layouts, per_device(): pair_out.astype(f32) * grad_top[:, None, :]  24.9 us
  transfers between devices with their start and end apart: 7, of which 2 were waited for; matrix products, arithmetic and copies ran while one was open for 62% of the time, Pallas kernels for 0%

commit v1 on v0

v1 whole, which is shorter than its diff:
```python
import functools

import jax
import jax.numpy as jnp
from jax import lax
from jax.experimental import pallas as pl
from jax.experimental.pallas import tpu as pltpu
from jax.sharding import PartitionSpec as P

HEADS = 8
PATCHES = 49
LANES = 128
PAIR = 2 * PATCHES
PAIR_PAD = 112
BLOCK_PAIRS = 4
BLOCK = BLOCK_PAIRS * PAIR
BLOCK_PAD = BLOCK_PAIRS * PAIR_PAD
BF = jnp.bfloat16
F32 = jnp.float32
VMEM_BYTES = 56 * 1024 * 1024


def params():
    return pltpu.CompilerParams(
        dimension_semantics=("arbitrary",), vmem_limit_bytes=VMEM_BYTES
    )


def cost(flops, moved, special=0):
    return pl.CostEstimate(
        flops=int(flops), bytes_accessed=int(moved), transcendentals=int(special)
    )


def whole(shape):
    return pl.BlockSpec(shape, lambda *_: (0,) * len(shape))


def dot(left, right):
    return jnp.dot(left, right, preferred_element_type=F32)


def dot_rt(left, right):
    return lax.dot_general(left, right, (((1,), (1,)), ((), ())), preferred_element_type=F32)


def dot_lt(left, right):
    return lax.dot_general(left, right, (((0,), (0,)), ((), ())), preferred_element_type=F32)


def norm_parts(values):
    mean = jnp.mean(values, axis=-1, keepdims=True)
    cent = values - mean
    factor = lax.rsqrt(jnp.mean(cent * cent, axis=-1, keepdims=True) + 1e-06)
    return cent * factor, factor


def norm_back(grad_normed, normed_hat, factor, gain):
    grad_hat = grad_normed * gain
    inner = grad_hat - jnp.mean(grad_hat, axis=-1, keepdims=True)
    inner = inner - normed_hat * jnp.mean(grad_hat * normed_hat, axis=-1, keepdims=True)
    return factor * inner


def spread_rows(compact, padded):
    for pair in range(BLOCK_PAIRS):
        padded[PAIR_PAD * pair : PAIR_PAD * pair + PAIR] = compact[PAIR * pair : PAIR * pair + PAIR]


def gather_rows(padded, compact):
    for pair in range(BLOCK_PAIRS):
        compact[PAIR * pair : PAIR * pair + PAIR] = padded[PAIR_PAD * pair : PAIR_PAD * pair + PAIR]


def clear_gaps(padded):
    for pair in range(BLOCK_PAIRS):
        low = PAIR_PAD * pair + PAIR
        padded[low : low + PAIR_PAD - PAIR] = jnp.zeros((PAIR_PAD - PAIR, padded.shape[1]), F32)


def image_of(position):
    return (position >= PATCHES).astype(jnp.int32) + (position >= PAIR).astype(jnp.int32)


def same_image():
    rows = lax.broadcasted_iota(jnp.int32, (2 * PAIR_PAD, PAIR_PAD), 0)
    rows = jnp.where(rows >= PAIR_PAD, rows - PAIR_PAD, rows)
    cols = lax.broadcasted_iota(jnp.int32, (2 * PAIR_PAD, PAIR_PAD), 1)
    return image_of(rows) == image_of(cols)


def low_half():
    return lax.broadcasted_iota(jnp.int32, (PAIR_PAD, LANES), 1) < LANES // 2


def two_heads(values, low):
    zero = jnp.zeros_like(values)
    return jnp.concatenate([jnp.where(low, values, zero), jnp.where(low, zero, values)], axis=0)


def one_row(values, low):
    return jnp.where(low, values[:PAIR_PAD], values[PAIR_PAD:])


def attend_kernel(
    tok_ref, gain_one_ref, qkv_w_ref, proj_w_ref, gain_two_ref,
    hidden_ref, rows_ref, qkv_ref, probs_ref, mixed_ref,
    compact, padded,
):
    width = tok_ref.shape[1]
    factor_qk = (width // HEADS) ** (-0.5)
    clear_gaps(padded)
    inputs = tok_ref[...].astype(F32)
    compact[...] = norm_parts(inputs)[0] * gain_one_ref[...]
    spread_rows(compact, padded)
    qkv_ref[...] = dot(padded[...].astype(BF), qkv_w_ref[...]).astype(BF)
    valid = same_image()
    low = low_half()
    for pair in range(BLOCK_PAIRS):
        rows = slice(PAIR_PAD * pair, PAIR_PAD * (pair + 1))
        for two in range(width // LANES):
            cols = slice(LANES * two, LANES * (two + 1))
            query = qkv_ref[rows, cols]
            keys = qkv_ref[rows, width + LANES * two : width + LANES * (two + 1)]
            values = qkv_ref[rows, 2 * width + LANES * two : 2 * width + LANES * (two + 1)]
            scores = jnp.where(valid, dot_rt(two_heads(query, low), keys), -1e30)
            highest = jnp.max(scores, axis=-1, keepdims=True)
            expo = jnp.exp((scores - highest) * factor_qk)
            probs = (expo / jnp.sum(expo, axis=-1, keepdims=True)).astype(BF)
            step = (pair * (width // LANES) + two) * 2 * PAIR_PAD
            probs_ref[step : step + 2 * PAIR_PAD, :] = probs
            mixed_ref[rows, cols] = one_row(dot(probs, values), low).astype(BF)
    padded[...] = dot(mixed_ref[...], proj_w_ref[...])
    gather_rows(padded, compact)
    hidden = inputs + compact[...]
    hidden_ref[...] = hidden
    rows_ref[...] = (norm_parts(hidden)[0] * gain_two_ref[...]).astype(BF)


def attend(tokens, gain_one, w_qkv, w_proj, gain_two):
    count, width = tokens.shape
    blocks = count // BLOCK
    prob_rows = BLOCK_PAIRS * (width // LANES) * 2 * PAIR_PAD
    row = lambda shape: pl.BlockSpec(shape, lambda step: (step, 0))
    flops = 2 * blocks * BLOCK_PAD * width * (4 * width + 4 * PAIR_PAD)
    return pl.pallas_call(
        attend_kernel,
        grid=(blocks,),
        in_specs=[
            row((BLOCK, width)), whole((1, width)), whole(w_qkv.shape), whole(w_proj.shape),
            whole((1, width)),
        ],
        out_specs=[
            row((BLOCK, width)), row((BLOCK, width)), row((BLOCK_PAD, 3 * width)),
            row((prob_rows, PAIR_PAD)), row((BLOCK_PAD, width)),
        ],
        out_shape=[
            jax.ShapeDtypeStruct((count, width), F32),
            jax.ShapeDtypeStruct((count, width), BF),
            jax.ShapeDtypeStruct((blocks * BLOCK_PAD, 3 * width), BF),
            jax.ShapeDtypeStruct((blocks * prob_rows, PAIR_PAD), BF),
            jax.ShapeDtypeStruct((blocks * BLOCK_PAD, width), BF),
        ],
        scratch_shapes=[pltpu.VMEM((BLOCK, width), F32), pltpu.VMEM((BLOCK_PAD, width), F32)],
        compiler_params=params(),
        cost_estimate=cost(flops, 30e6, blocks * prob_rows * LANES),
        name="attend",
    )(tokens, gain_one[None, :], w_qkv, w_proj, gain_two[None, :])


def dispatch_kernel(window, starts_ref, src_ref, index_ref, *refs):
    outs, total = refs, refs[0].shape[0]
    step = pl.program_id(0)
    experts = starts_ref.shape[1]
    owners = experts // len(outs)
    capacity = total // owners
    block = src_ref.shape[0]

    @pl.when(step == 0)
    def _():
        for out in outs:
            out[...] = jnp.zeros(out.shape, out.dtype)

    place = lax.broadcasted_iota(jnp.int32, (window, block), 0)
    for local, out in enumerate(outs):
        first, second = index_ref[0, 0:1, :], index_ref[0, 1:2, :]
        shift = local * total
        first = jnp.where((first >= shift) & (first < shift + total), first - shift, -1)
        second = jnp.where((second >= shift) & (second < shift + total), second - shift, -1)

        def one_expert(owner, carry):
            expert = local * owners + owner
            low = owner * capacity + starts_ref[step, expert]
            high = owner * capacity + starts_ref[step + 1, expert]
            base = (low // 16) * 16

            def one_window(chunk, inner):
                begin = base + chunk * window
                at = pl.multiple_of(jnp.minimum(begin, total - window), 16)
                near = (first >= begin) & (first >= low) & (first < high)
                far = (second >= begin) & (second >= low) & (second < high)
                hit = jnp.where(near, first - at, jnp.where(far, second - at, -1))
                spot = (place == hit).astype(F32).astype(BF)
                held = out[pl.ds(at, window), :].astype(F32)
                out[pl.ds(at, window), :] = (held + dot(spot, src_ref[...])).astype(BF)
                return inner

            return lax.fori_loop(0, (high - base + window - 1) // window, one_window, carry)

        lax.fori_loop(0, owners, one_expert, 0)


def dispatch(src, starts, index_rows, local, capacity):
    count, width = src.shape
    blocks = count // BLOCK
    experts = starts.shape[1]
    total = (experts // local) * capacity
    window = LANES
    return pl.pallas_call(
        functools.partial(dispatch_kernel, window),
        grid_spec=pltpu.PrefetchScalarGridSpec(
            num_scalar_prefetch=1,
            grid=(blocks,),
            in_specs=[
                pl.BlockSpec((BLOCK, width), lambda step, *_: (step, 0)),
                pl.BlockSpec((1, 2, BLOCK), lambda step, *_: (step, 0, 0)),
            ],
            out_specs=[whole((total, width))] * local,
        ),
        out_shape=[jax.ShapeDtypeStruct((total, width), BF)] * local,
        compiler_params=params(),
        cost_estimate=cost(12e9, 8e6),
        name="dispatch",
    )(starts, src, index_rows)


def combine_block(window, step, starts_ref, index_ref, bufs, acc):
    total = bufs[0].shape[0]
    experts = starts_ref.shape[1]
    owners = experts // len(bufs)
    capacity = total // owners
    block = index_ref.shape[0]
    first = jnp.broadcast_to(index_ref[:, 0:1], (block, window))
    second = jnp.broadcast_to(index_ref[:, 1:2], (block, window))
    place = lax.broadcasted_iota(jnp.int32, (block, window), 1)
    acc[...] = jnp.zeros(acc.shape, F32)
    for local, buf in enumerate(bufs):
        shift = local * total

        def one_expert(owner, carry):
            expert = local * owners + owner
            low = owner * capacity + starts_ref[step, expert]
            high = owner * capacity + starts_ref[step + 1, expert]
            base = (low // 16) * 16

            def one_window(chunk, inner):
                begin = base + chunk * window
                at = pl.multiple_of(jnp.minimum(begin, total - window), 16)
                seen = place + (at + shift)
                fresh = (seen >= begin + shift) & (seen < high + shift)
                hit = ((seen == first) | (seen == second)) & fresh
                acc[...] += dot(hit.astype(F32).astype(BF), buf[pl.ds(at, window), :])
                return inner

            return lax.fori_loop(0, (high - base + window - 1) // window, one_window, carry)

        lax.fori_loop(0, owners, one_expert, 0)


def combine_window(capacity):
    return 2 * LANES if capacity > 2 * LANES else LANES


def top_kernel(window, local, starts_ref, index_ref, hidden_ref, *refs):
    bufs, out_ref, acc = refs[:local], refs[local], refs[local + 1]
    combine_block(window, pl.program_id(0), starts_ref, index_ref, bufs, acc)
    out_ref[...] = (hidden_ref[...] + acc[...]).astype(BF)


def top(starts, index, hidden, bufs, capacity):
    count, width = hidden.shape
    blocks = count // BLOCK
    local = len(bufs)
    row = lambda shape: pl.BlockSpec(shape, lambda step, *_: (step, 0))
    return pl.pallas_call(
        functools.partial(top_kernel, combine_window(capacity), local),
        grid_spec=pltpu.PrefetchScalarGridSpec(
            num_scalar_prefetch=1,
            grid=(blocks,),
            in_specs=[row((BLOCK, 2)), row((BLOCK, width))] + [whole(bufs[0].shape)] * local,
            out_specs=row((BLOCK, width)),
            scratch_shapes=[pltpu.VMEM((BLOCK, width), F32)],
        ),
        out_shape=jax.ShapeDtypeStruct((count, width), BF),
        compiler_params=params(),
        cost_estimate=cost(12e9, 12e6),
        name="top",
    )(starts, index, hidden, *bufs)


def gelu_parts(values):
    size = jnp.abs(values)
    near = 1.0 / (1.0 + (0.3275911 * 0.7071067811865476) * size)
    expo = jnp.exp(-0.5 * (values * values))
    poly = 0.5 * 1.061405429
    for term in (-1.453152027, 1.421413741, -0.284496736, 0.254829592):
        poly = poly * near + 0.5 * term
    tail = poly * near * expo
    share = jnp.where(values >= 0, 1.0 - tail, tail)
    return values * share, share + values * (0.3989422804014327 * expo)


def expert_kernel(
    experts, fcut, mine_ref, x_ref, dy_ref, up_ref, down_ref, router_ref, back_ref,
    out_ref, dx_ref, gup_ref, gdown_ref, grouter_ref,
    acc_up, acc_down, acc_router, acc_out, acc_dx,
):
    step = pl.program_id(0)
    hidden_units = up_ref.shape[1]

    @pl.when(step == 0)
    def _():
        acc_up[...] = jnp.zeros(acc_up.shape, F32)
        acc_down[...] = jnp.zeros(acc_down.shape, F32)
        acc_router[...] = jnp.zeros(acc_router.shape, F32)

    rows = x_ref[...]
    count = rows.shape[0]
    logits = dot(rows, router_ref[...])
    logits = logits[:, :LANES] + logits[:, LANES:]
    lane = lax.broadcasted_iota(jnp.int32, (count, LANES), 1)
    logits = jnp.where(lane < experts, logits, -1e30)
    expo = jnp.exp(logits - jnp.max(logits, axis=-1, keepdims=True))
    gates = expo / jnp.sum(expo, axis=-1, keepdims=True)
    own = (lane == mine_ref[0]).astype(F32)
    chosen = jnp.sum(gates * own, axis=-1, keepdims=True)
    pair = (chosen * dy_ref[...].astype(F32)).astype(BF)
    rows_t = rows.T
    pair_t = pair.T
    inner = jnp.zeros((count, LANES), F32)
    for low in range(0, hidden_units, fcut):
        cols = slice(low, low + fcut)
        pre = dot(rows, up_ref[:, cols])
        grad_act = dot_rt(pair, down_ref[cols, :])
        act, slope = gelu_parts(pre)
        both = act * grad_act
        for part in range(0, fcut, LANES):
            inner = inner + both[:, part : part + LANES]
        act = act.astype(BF)
        grad_pre = (grad_act * slope).astype(BF)
        acc_up[:, cols] += dot(rows_t, grad_pre)
        acc_down[:, cols] += dot(pair_t, act)
        if low == 0:
            acc_out[...] = dot(act, down_ref[cols, :])
            acc_dx[...] = dot_rt(grad_pre, up_ref[:, cols])
        else:
            acc_out[...] += dot(act, down_ref[cols, :])
            acc_dx[...] += dot_rt(grad_pre, up_ref[:, cols])
    grad_logits = jnp.sum(inner, axis=-1, keepdims=True) * (own - gates)
    head = grad_logits.astype(BF)
    rest = (grad_logits - head.astype(F32)).astype(BF)
    acc_router[...] += dot(rows_t, jnp.concatenate([head, rest], axis=1))
    out_ref[...] = (chosen * acc_out[...]).astype(BF)
    dx_ref[...] = (acc_dx[...] + dot(jnp.concatenate([head, head], axis=1), back_ref[...])).astype(BF)

    @pl.when(step == pl.num_programs(0) - 1)
    def _():
        gup_ref[...] = acc_up[...].astype(BF)
        for low in range(0, hidden_units, 512):
            gdown_ref[low : low + 512, :] = acc_down[:, low : low + 512].T.astype(BF)
        grouter_ref[...] = acc_router[:, :LANES] + acc_router[:, LANES:]


def expert_pass(mine, rows, grads, w_up, w_down, router, router_back, experts, capacity):
    count, width = rows.shape
    units = w_up.shape[1]
    parts = count // capacity
    times = max(n for n in range(1, parts + 1) if parts % n == 0 and n * capacity <= max(640, capacity))
    tile = times * capacity
    fcut = min(512, units)
    row = lambda shape: pl.BlockSpec(shape, lambda step, *_: (step, 0))
    return pl.pallas_call(
        functools.partial(expert_kernel, experts, fcut),
        grid_spec=pltpu.PrefetchScalarGridSpec(
            num_scalar_prefetch=1,
            grid=(count // tile,),
            in_specs=[
                row((tile, width)), row((tile, width)), whole(w_up.shape), whole(w_down.shape),
                whole(router.shape), whole(router_back.shape),
            ],
            out_specs=[
                row((tile, width)), row((tile, width)), whole(w_up.shape), whole(w_down.shape),
                whole((width, LANES)),
            ],
            scratch_shapes=[
                pltpu.VMEM((width, units), F32),
                pltpu.VMEM((width, units), F32),
                pltpu.VMEM((width, 2 * LANES), F32),
                pltpu.VMEM((tile, width), F32),
                pltpu.VMEM((tile, width), F32),
            ],
        ),
        out_shape=[
            jax.ShapeDtypeStruct((count, width), BF),
            jax.ShapeDtypeStruct((count, width), BF),
            jax.ShapeDtypeStruct(w_up.shape, BF),
            jax.ShapeDtypeStruct(w_down.shape, BF),
            jax.ShapeDtypeStruct((width, LANES), F32),
        ],
        compiler_params=params(),
        cost_estimate=cost(12 * count * width * units, 30e6, 2 * count * units),
        name="expert_pass",
    )(mine, rows, grads, w_up, w_down, router, router_back)


def back_kernel(
    window, local, starts_ref, index_ref, hidden_ref, tok_ref, dy_ref, qkv_ref, probs_ref,
    mixed_ref, gain_one_ref, qkv_w_ref, proj_w_ref, gain_two_ref, *refs,
):
    bufs = refs[:local]
    gtok_ref, gqkv_ref, gproj_ref, ggain_one_ref, ggain_two_ref = refs[local : local + 5]
    acc, compact, padded, dqkv = refs[local + 5 :]
    step = pl.program_id(0)
    width = tok_ref.shape[1]
    factor_qk = (width // HEADS) ** (-0.5)

    @pl.when(step == 0)
    def _():
        for ref in (gqkv_ref, gproj_ref, ggain_one_ref, ggain_two_ref):
            ref[...] = jnp.zeros(ref.shape, F32)

    combine_block(window, step, starts_ref, index_ref, bufs, acc)
    clear_gaps(padded)
    hat_two, scale_two = norm_parts(hidden_ref[...])
    grad_normed = acc[...]
    ggain_two_ref[...] += jnp.sum(grad_normed * hat_two, axis=0, keepdims=True)
    grad_hidden = dy_ref[...].astype(F32) + norm_back(
        grad_normed, hat_two, scale_two, gain_two_ref[...]
    )
    gtok_ref[...] = grad_hidden
    compact[...] = grad_hidden
    spread_rows(compact, padded)
    grad_attn = padded[...].astype(BF)
    gproj_ref[...] += dot_lt(mixed_ref[...], grad_attn)
    grad_mixed = dot_rt(grad_attn, proj_w_ref[...]).astype(BF)
    low = low_half()
    for pair in range(BLOCK_PAIRS):
        rows = slice(PAIR_PAD * pair, PAIR_PAD * (pair + 1))
        for two in range(width // LANES):
            cols = slice(LANES * two, LANES * (two + 1))
            key_cols = slice(width + LANES * two, width + LANES * (two + 1))
            value_cols = slice(2 * width + LANES * two, 2 * width + LANES * (two + 1))
            at = (pair * (width // LANES) + two) * 2 * PAIR_PAD
            probs = probs_ref[at : at + 2 * PAIR_PAD, :]
            wide = probs.astype(F32)
            grad_out = two_heads(grad_mixed[rows, cols], low)
            grad_probs = dot_rt(grad_out, qkv_ref[rows, value_cols])
            meet = jnp.sum(wide * grad_probs, axis=-1, keepdims=True)
            grad_scores = (wide * (grad_probs - meet) * factor_qk).astype(BF)
            grad_query = one_row(dot(grad_scores, qkv_ref[rows, key_cols]), low)
            dqkv[rows, cols] = grad_query.astype(BF)
            dqkv[rows, key_cols] = dot_lt(grad_scores, two_heads(qkv_ref[rows, cols], low)).astype(BF)
            dqkv[rows, value_cols] = dot_lt(probs, grad_out).astype(BF)
    hat_one, scale_one = norm_parts(tok_ref[...].astype(F32))
    compact[...] = hat_one * gain_one_ref[...]
    spread_rows(compact, padded)
    act_one = padded[...].astype(BF)
    gqkv_ref[...] += dot_lt(act_one, dqkv[...])
    padded[...] = dot_rt(dqkv[...], qkv_w_ref[...])
    gather_rows(padded, compact)
    grad_act_one = compact[...]
    ggain_one_ref[...] += jnp.sum(grad_act_one * hat_one, axis=0, keepdims=True)
    gtok_ref[...] += norm_back(grad_act_one, hat_one, scale_one, gain_one_ref[...])


def back(starts, index, hidden, tokens, dy, qkv, probs, mixed, gain_one, w_qkv, w_proj, gain_two, bufs, capacity):
    count, width = tokens.shape
    blocks = count // BLOCK
    local = len(bufs)
    row = lambda shape: pl.BlockSpec(shape, lambda step, *_: (step, 0))
    flops = 2 * blocks * BLOCK_PAD * width * (8 * width + 10 * PAIR_PAD)
    return pl.pallas_call(
        functools.partial(back_kernel, combine_window(capacity), local),
        grid_spec=pltpu.PrefetchScalarGridSpec(
            num_scalar_prefetch=1,
            grid=(blocks,),
            in_specs=[
                row((BLOCK, 2)), row((BLOCK, width)), row((BLOCK, width)), row((BLOCK, width)),
                row((BLOCK_PAD, 3 * width)), row((probs.shape[0] // blocks, PAIR_PAD)),
                row((BLOCK_PAD, width)),
                whole((1, width)), whole(w_qkv.shape), whole(w_proj.shape), whole((1, width)),
            ] + [whole(bufs[0].shape)] * local,
            out_specs=[
                row((BLOCK, width)), whole(w_qkv.shape), whole(w_proj.shape),
                whole((1, width)), whole((1, width)),
            ],
            scratch_shapes=[
                pltpu.VMEM((BLOCK, width), F32),
                pltpu.VMEM((BLOCK, width), F32),
                pltpu.VMEM((BLOCK_PAD, width), F32),
                pltpu.VMEM((BLOCK_PAD, 3 * width), BF),
            ],
        ),
        out_shape=[
            jax.ShapeDtypeStruct((count, width), F32),
            jax.ShapeDtypeStruct(w_qkv.shape, F32),
            jax.ShapeDtypeStruct(w_proj.shape, F32),
            jax.ShapeDtypeStruct((1, width), F32),
            jax.ShapeDtypeStruct((1, width), F32),
        ],
        compiler_params=params(),
        cost_estimate=cost(flops + 12e9, 40e6),
        name="back",
    )(
        starts, index, hidden, tokens, dy, qkv, probs, mixed, gain_one[None, :], w_qkv, w_proj,
        gain_two[None, :], *bufs,
    )


def places(picks, keep, experts, local, capacity):
    count = picks.shape[0]
    owners = experts // local
    picks_t, keep_t = picks.T, keep.T
    ids = jnp.arange(experts, dtype=jnp.int32)[:, None]
    named = ((picks_t[0][None, :] == ids) | (picks_t[1][None, :] == ids)).astype(jnp.int32)
    before = jnp.cumsum(named, axis=1) - named
    slot = jnp.stack([jnp.sum(jnp.where(picks_t[c][None, :] == ids, before, 0), axis=0) for c in (0, 1)])
    home = (picks_t % local) * owners + picks_t // local
    index = jnp.where(keep_t > 0, home * capacity + slot, -1)
    starts = jnp.concatenate([before[:, ::BLOCK], before[:, -1:] + named[:, -1:]], axis=1)
    order = jnp.arange(experts, dtype=jnp.int32).reshape(owners, local).T.reshape(-1)
    starts = starts[order].T
    index_rows = index.reshape(2, count // BLOCK, BLOCK).transpose(1, 0, 2)
    return index.T, index_rows, starts


def per_device(
    tokens, gain_one, w_qkv, w_proj, gain_two, w_router, w_in, w_eout, picks, keep, grad_out
):
    count, width = tokens.shape
    local = w_in.shape[0]
    owners = lax.axis_size("expert")
    experts = local * owners
    capacity = 8 * ((21 * count + 80 * experts - 1) // (80 * experts))

    def swap(part):
        sent = part.reshape(owners, capacity, width)
        got = lax.all_to_all(sent, "expert", split_axis=0, concat_axis=0, tiled=True)
        return got.reshape(owners * capacity, width)

    index, index_rows, starts = places(picks, keep, experts, local, capacity)
    grad_parts = [swap(part) for part in dispatch(grad_out, starts, index_rows, local, capacity)]
    hidden, rows, qkv, probs, mixed = attend(tokens, gain_one, w_qkv, w_proj, gain_two)
    row_parts = [swap(part) for part in dispatch(rows, starts, index_rows, local, capacity)]
    head = w_router.astype(BF)
    rest = (w_router - head.astype(F32)).astype(BF)
    gap = ((0, 0), (0, LANES - experts))
    router = jnp.concatenate([jnp.pad(head, gap), jnp.pad(rest, gap)], axis=1)
    router_back = jnp.concatenate([jnp.pad(head, gap).T, jnp.pad(rest, gap).T], axis=0)
    outs, downs, grad_ups, grad_downs, grad_router = [], [], [], [], 0
    for part in range(local):
        mine = (lax.axis_index("expert") * local + part).astype(jnp.int32)[None]
        out, grad_rows, grad_up, grad_down, router_part = expert_pass(
            mine, row_parts[part], grad_parts[part], w_in[part], w_eout[part], router,
            router_back, experts, capacity,
        )
        downs.append(swap(grad_rows))
        outs.append(swap(out))
        grad_ups.append(lax.psum_scatter(grad_up, "dp", scatter_dimension=0, tiled=True))
        grad_downs.append(lax.psum_scatter(grad_down, "dp", scatter_dimension=0, tiled=True))
        grad_router = grad_router + router_part[:, :experts]
    grad_tokens, grad_qkv, grad_proj, grad_gain_one, grad_gain_two = back(
        starts, index, hidden, tokens, grad_out, qkv, probs, mixed, gain_one, w_qkv, w_proj,
        gain_two, downs, capacity,
    )
    block_out = top(starts, index, hidden, outs, capacity)
    both = ("dp", "expert")
    big = lax.psum((grad_qkv.astype(BF), grad_proj.astype(BF)), both)
    small = lax.psum((grad_gain_one[0], grad_gain_two[0], grad_router), both)
    return (
        block_out,
        grad_tokens,
        small[0],
        big[0].astype(F32),
        big[1].astype(F32),
        small[1],
        small[2],
        jnp.stack(grad_ups).astype(F32),
        jnp.stack(grad_downs).astype(F32),
    )


def solution(mesh):
    rows = P(("dp", "expert"), None)
    experts = P("expert", None, None)
    return jax.shard_map(
        per_device,
        mesh=mesh,
        in_specs=(rows, P(), P(), P(), P(), P(), experts, experts, rows, rows, rows),
        out_specs=(
            rows, rows, P(), P(), P(), P(), P(), P("expert", "dp", None), P("expert", "dp", None),
        ),
        check_vma=False,
    )
```

time: 936 us -> 575 us (0.61)
  matrix products: 332 us -> 0 us
  Pallas kernels: 0 us -> 254 us
  other arithmetic: 232 us -> 18.8 us
  local copies, waits for them, and re-layouts: 207 us -> 19.8 us
  blocking collectives: 41.4 us -> 139 us
  waiting for transfers between devices: 78.5 us -> 92.7 us
    dot_general x21 -> x0, matrix products: 332 us -> none  [the longest x1 98.9 us: expert_up(): jnp.einsum('sjcd,jdf->sjcf', rows_here, w_in, preferred_element_type=jnp....]
    pallas_call x0 -> x7, Pallas kernels: none -> 254 us  [the longest x2 108 us: expert_pass(): pl.pallas_call(functools.partial(expert_kernel, experts, fcut), grid_spec...]
    reduce_sum x12 -> x1, other arithmetic: 97.4 us -> 0.06 us  [places(): jnp.sum(jnp.where(picks_t[c][None, :] == ids, before, 0), axis=0)]
    scatter-add x2 -> x0, other arithmetic: 85.8 us -> none  [per_device(): jnp.zeros((experts_all * capacity, width), bf).at[index]]
    all_to_all x0 -> x2, blocking collectives: none -> 68.9 us  [swap(): lax.all_to_all(sent, 'expert', split_axis=0, concat_axis=0, tiled=True)]
    all_to_all x4 -> x6, waiting for transfers between devices: 1.65 us -> 63.6 us  [swap(): lax.all_to_all(sent, 'expert', split_axis=0, concat_axis=0, tiled=True)]
    convert_element_type x8 -> x0, local copies, waits for them, and re-layouts: 54.9 us -> none  [the longest x1 19.2 us: per_device(): grad_qkv_rows = jnp.stack([grad_query, grad_keys, grad_values], axis=2).a...]
    mul x7 -> x0, local copies, waits for them, and re-layouts: 50.8 us -> none  [the longest x2 24.9 us: per_device(): pair_out.astype(f32) * grad_top[:, None, :]]
  transfers between devices with their start and end apart: 7 -> 11, of which waited for: 2 -> 4; matrix products, arithmetic and copies ran while one was open for 62% -> 3% of each run, Pallas kernels for 0% -> 26%
where the time goes in v1:
time: 575 us; the launch traced here: 567 us
  Pallas kernels  254 us (44%)
  blocking collectives  139 us (24%)
  waiting for transfers between devices  92.7 us (16%)
  starting transfers between devices  26.4 us (5%)
  local copies, waits for them, and re-layouts  19.8 us (3%)
  other arithmetic  18.8 us (3%)
  between operations  16.5 us (3%)
    pallas_call x2, Pallas kernels, expert_pass(): pl.pallas_call(functools.partial(expert_kernel, experts, fcut), grid_spec...  108 us
    pallas_call x1, Pallas kernels, back(): pl.pallas_call(functools.partial(back_kernel, combine_window(capacity), l...  71.4 us
    psum x1, blocking collectives, per_device(): small = lax.psum((grad_gain_one[0], grad_gain_two[0], grad_router), both)  70 us
    all_to_all x2, blocking collectives, swap(): lax.all_to_all(sent, 'expert', split_axis=0, concat_axis=0, tiled=True)  68.9 us
    all_to_all x6, waiting for transfers between devices, swap(): lax.all_to_all(sent, 'expert', split_axis=0, concat_axis=0, tiled=True)  63.6 us
    pallas_call x2, Pallas kernels, dispatch(): pl.pallas_call(functools.partial(dispatch_kernel, window), grid_spec=pltp...  33.3 us
    psum x1, waiting for transfers between devices, per_device(): big = lax.psum((grad_qkv.astype(BF), grad_proj.astype(BF)), both)  26.7 us
    all_to_all x6, starting transfers between devices, swap(): lax.all_to_all(sent, 'expert', split_axis=0, concat_axis=0, tiled=True)  26.3 us
  transfers between devices with their start and end apart: 11, of which 4 were waited for; matrix products, arithmetic and copies ran while one was open for 3% of the time, Pallas kernels for 26%

profile of v1, /device:TPU:0, one launch (start us, length us, event | category | flops | bytes accessed | tf_op | source)
XLA Modules:
  0.0 566.7 jit_solution(6101355329544157525)
XLA Ops:
  21.1 20.8 %attend.1 = (f32[2352,512]{1,0:T(8,128)}, bf16[2352,512]{1,0:T(8,128)(2,1)}, bf16[2688,1536]{1,0:T(8,128)(2,1)}, bf16[21504,112]{1,0:T(8,128)(2,1)}, bf16[2688,512]{1,0:T(8,128)(2,1)}) custom-call(bf16[2352,512]{1,0:T(8,128)(2,1)} %tok_ref.3, f32[1,512]{1,0:T(1,128)} %bitcast.87, bf16[512,1536]{1,0:T(8,128)(2,1)} %qkv_w_ref.3, bf16[512,512]{1,0:T(8,128)(2,1)} %proj_w_ref.3, ...), custom_call_target="tpu_custom_call" | custom-call | flops 6870269952 | bytes 30000000 | tf_op jit(solution)/shard_map/attend/pallas_call | solution.py:146
  41.9 16.7 %dispatch.2 = (bf16[2496,512]{1,0:T(8,128)(2,1)}, bf16[2496,512]{1,0:T(8,128)(2,1)}) custom-call(s32[7,8]{1,0:T(8,128)} %bitcast.81, bf16[2352,512]{1,0:T(8,128)(2,1)} %get-tuple-element.34.src_ref, s32[6,2,392]{2,1,0:T(2,128)} %bitcast.78), custom_call_target="tpu_custom_call" | custom-call | flops 12000000000 | bytes 8000000 | tf_op jit(solution)/shard_map/dispatch/pallas_call | solution.py:219
  58.6 5.6 all-to-all-start.3
  64.2 16.7 %dispatch.3 = (bf16[2496,512]{1,0:T(8,128)(2,1)}, bf16[2496,512]{1,0:T(8,128)(2,1)}) custom-call(s32[7,8]{1,0:T(8,128)} %bitcast.82, bf16[2352,512]{1,0:T(8,128)(2,1)} %dy_ref.1, s32[6,2,392]{2,1,0:T(2,128)} %bitcast.79), custom_call_target="tpu_custom_call" | custom-call | flops 12000000000 | bytes 8000000 | tf_op jit(solution)/shard_map/dispatch/pallas_call | solution.py:219
  80.9 13.0 %all-to-all-done.3 = bf16[4,624,512]{2,1,0:T(8,128)(2,1)S(1)} async-done(((bf16[4,624,512]{2,1,0:T(8,128)(2,1)}), bf16[4,624,512]{2,1,0:T(8,128)(2,1)S(1)}, u32[]{:S(2)}, u32[]{:S(2)}) %all-to-all-start.3) | async-done | bytes 2555936 | tf_op jit(solution)/shard_map/all_to_all | solution.py:548
  94.0 34.9 %all_to_all.40 = bf16[4,624,512]{2,1,0:T(8,128)(2,1)} all-to-all(bf16[4,624,512]{2,1,0:T(8,128)(2,1)} %bitcast.72), channel_id=1, replica_groups=mesh['dp'=8,'expert'=4] {'expert'}, dimensions={0} | all-to-all | bytes 5111808 | tf_op jit(solution)/shard_map/all_to_all | solution.py:548
  128.9 3.8 all-to-all-start
  134.3 4.7 slice_bitcast_fusion
  139.0 2.6 slice_bitcast_fusion.1
  141.6 19.7 %all-to-all-done = bf16[4,624,512]{2,1,0:T(8,128)(2,1)S(1)} async-done(((bf16[4,624,512]{2,1,0:T(8,128)(2,1)}), bf16[4,624,512]{2,1,0:T(8,128)(2,1)S(1)}, u32[]{:S(2)}, u32[]{:S(2)}) %all-to-all-start) | async-done | bytes 2555936 | tf_op jit(solution)/shard_map/all_to_all | solution.py:548
  162.7 4.5 all-to-all-start.1
  167.3 53.7 %expert_pass.3 = (bf16[2496,512]{1,0:T(8,128)(2,1)}, bf16[2496,512]{1,0:T(8,128)(2,1)}, bf16[512,2048]{1,0:T(8,128)(2,1)}, bf16[2048,512]{1,0:T(8,128)(2,1)}, f32[512,128]{1,0:T(8,128)}) custom-call(s32[1]{0:T(128)} %bitcast.21.mine_ref, bf16[2496,512]{1,0:T(8,128)(2,1)} %bitcast.62, bf16[2496,512]{1,0:T(8,128)(2,1)} %bitcast.64, ...), custom_call_target="tpu_custom_call" | custom-call | flops 31406948352 | bytes 30000000 | tf_op jit(solution)/shard_map/expert_pass/pallas_call | solution.py:382
  221.0 4.1 all-to-all-start.7
  225.2 53.9 %expert_pass.2 = (bf16[2496,512]{1,0:T(8,128)(2,1)}, bf16[2496,512]{1,0:T(8,128)(2,1)}, bf16[512,2048]{1,0:T(8,128)(2,1)}, bf16[2048,512]{1,0:T(8,128)(2,1)}, f32[512,128]{1,0:T(8,128)}) custom-call(s32[1]{0:T(128)} %bitcast.8.mine_ref, bf16[2496,512]{1,0:T(8,128)(2,1)} %bitcast.61, bf16[2496,512]{1,0:T(8,128)(2,1)} %bitcast.14.dy_ref, ...), custom_call_target="tpu_custom_call" | custom-call | flops 31406948352 | bytes 30000000 | tf_op jit(solution)/shard_map/expert_pass/pallas_call | solution.py:382
  279.1 34.0 %all_to_all.41 = bf16[4,624,512]{2,1,0:T(8,128)(2,1)} all-to-all(bf16[4,624,512]{2,1,0:T(8,128)(2,1)} %bitcast.69), channel_id=1, replica_groups=mesh['dp'=8,'expert'=4] {'expert'}, dimensions={0} | all-to-all | bytes 5111808 | tf_op jit(solution)/shard_map/all_to_all | solution.py:548
  313.1 71.4 %back.1 = (f32[2352,512]{1,0:T(8,128)}, f32[512,1536]{1,0:T(8,128)}, f32[512,512]{1,0:T(8,128)}, f32[1,512]{1,0:T(1,128)}, f32[1,512]{1,0:T(1,128)}) custom-call(s32[7,8]{1,0:T(8,128)} %bitcast.83, s32[2352,2]{1,0:T(8,128)} %bitcast.59, f32[2352,512]{1,0:T(8,128)} %get-tuple-element.33.hidden_ref, bf16[2352,512]{1,0:T(8,128)(2,1)} %tok_ref.3, ...), custom_call_target="tpu_custom_call" | custom-call | flops 26357102592 | bytes 40000000 | tf_op jit(solution)/shard_map/back/pallas_call | solution.py:482
  384.5 3.4 convert_element_type.39
  390.5 3.7 all-to-all-start.5
  394.9 30.9 %all-to-all-done.5 = bf16[4,624,512]{2,1,0:T(8,128)(2,1)S(1)} async-done(((bf16[4,624,512]{2,1,0:T(8,128)(2,1)}), bf16[4,624,512]{2,1,0:T(8,128)(2,1)S(1)}, u32[]{:S(2)}, u32[]{:S(2)}) %all-to-all-start.5) | async-done | bytes 2555936 | tf_op jit(solution)/shard_map/all_to_all | solution.py:548
  427.2 4.5 all-to-all-start.2
  431.9 70.0 %all-reduce.3 = (f32[512]{0:T(512)}, f32[512]{0:T(512)}, f32[512,8]{1,0:T(8,128)S(1)}) all-reduce(f32[512]{0:T(512)S(1)} %bitcast.85, f32[512]{0:T(512)S(1)} %bitcast.86, f32[512,8]{1,0:T(8,128)S(1)} %slice_add_fusion), channel_id=1, replica_groups=mesh['dp'=8,'expert'=4] {'dp','expert'}, use_global_device_ids=true, to_apply=%region_4.5 | all-reduce | flops 5120 | bytes 40960 | tf_op jit(solution)/shard_map/psum | solution.py:579
  502.5 20.6 %top.1 = bf16[2352,512]{1,0:T(8,128)(2,1)} custom-call(s32[7,8]{1,0:T(8,128)} %bitcast.84, s32[2352,2]{1,0:T(8,128)} %bitcast.60, f32[2352,512]{1,0:T(8,128)} %get-tuple-element.33.hidden_ref, bf16[2496,512]{1,0:T(8,128)(2,1)} %bitcast.20.refs_0_, bf16[2496,512]{1,0:T(8,128)(2,1)} %bitcast.66), custom_call_target="tpu_custom_call" | custom-call | flops 12000000000 | bytes 12000000 | tf_op jit(solution)/shard_map/top/pallas_call | solution.py:285
  523.1 26.7 %all-reduce.7.cloned.1.call-done = (bf16[512,1536]{1,0:T(8,128)(2,1)}, bf16[512,512]{1,0:T(8,128)(2,1)}) async-done(((bf16[512,1536]{1,0:T(8,128)(2,1)}, bf16[512,512]{1,0:T(8,128)(2,1)}), (bf16[512,1536]{1,0:T(8,128)(2,1)}, bf16[512,512]{1,0:T(8,128)(2,1)})) %all-reduce.7.cloned.1.call-update) | async-done | bytes 2097168 | tf_op jit(solution)/shard_map/psum | solution.py:578
  549.9 3.5 convert_element_type.40
  (87 shorter events, 26.9 us)
Async XLA Ops:
  15.4 3.9 copy-start.10
  20.1 21.9 %copy-start = (s32[2,2352]{0,1:T(8,128)}, s32[2,2352]{0,1:T(8,128)S(1)}, u32[]{:S(2)}) copy-start(s32[2,2352]{0,1:T(8,128)S(1)} %bitcast_select_fusion) | copy-start | bytes 56452
  58.6 35.3 %all-to-all-start.3 = ((bf16[4,624,512]{2,1,0:T(8,128)(2,1)}), bf16[4,624,512]{2,1,0:T(8,128)(2,1)S(1)}, u32[]{:S(2)}, u32[]{:S(2)}) async-start(bf16[4,624,512]{2,1,0:T(8,128)(2,1)} %bitcast.70), calls=%async_computation.3 | async-start | bytes 5111808 | tf_op jit(solution)/shard_map/all_to_all | solution.py:548
  94.0 34.9 %copy-start.3 = (bf16[4,624,512]{2,1,0:T(8,128)(2,1)}, bf16[4,624,512]{2,1,0:T(8,128)(2,1)S(1)}, u32[]{:S(2)}) copy-start(bf16[4,624,512]{2,1,0:T(8,128)(2,1)S(1)} %all-to-all-done.3) | copy-start | bytes 7667716
  128.9 3.8 copy-start.11
  128.9 32.4 %all-to-all-start = ((bf16[4,624,512]{2,1,0:T(8,128)(2,1)}), bf16[4,624,512]{2,1,0:T(8,128)(2,1)S(1)}, u32[]{:S(2)}, u32[]{:S(2)}) async-start(bf16[4,624,512]{2,1,0:T(8,128)(2,1)} %bitcast.65), calls=%async_computation | async-start | bytes 5111808 | tf_op jit(solution)/shard_map/all_to_all | solution.py:548
  134.3 4.7 copy-start.1
  161.3 1.5 copy-start.2
  162.7 58.3 %all-to-all-start.1 = ((bf16[4,624,512]{2,1,0:T(8,128)(2,1)}), bf16[4,624,512]{2,1,0:T(8,128)(2,1)}, u32[]{:S(2)}, u32[]{:S(2)}) async-start(bf16[4,624,512]{2,1,0:T(8,128)(2,1)} %bitcast.63), calls=%async_computation.1 | async-start | bytes 5111808 | tf_op jit(solution)/shard_map/all_to_all | solution.py:548
  221.0 58.1 %all-to-all-start.7 = ((bf16[4,624,512]{2,1,0:T(8,128)(2,1)}), bf16[4,624,512]{2,1,0:T(8,128)(2,1)S(1)}, u32[]{:S(2)}, u32[]{:S(2)}) async-start(bf16[4,624,512]{2,1,0:T(8,128)(2,1)} %bitcast.68), calls=%async_computation.7 | async-start | bytes 5111808 | tf_op jit(solution)/shard_map/all_to_all | solution.py:548
  225.2 324.7 %all-reduce.7.cloned.1.call-start = ((), (), s32[]{:S(2)}) async-start(), calls=%async_computation.16 | async-start | bytes 4194304 | tf_op jit(solution)/shard_map/psum | solution.py:578
  279.1 34.0 %copy-start.5 = (bf16[4,624,512]{2,1,0:T(8,128)(2,1)}, bf16[4,624,512]{2,1,0:T(8,128)(2,1)S(1)}, u32[]{:S(2)}) copy-start(bf16[4,624,512]{2,1,0:T(8,128)(2,1)S(1)} %all-to-all-done.7) | copy-start | bytes 7667716
  384.5 3.4 copy-start.6
  388.7 165.8 %reduce-scatter.11.cloned.1.call-start = ((), (), s32[]{:S(2)}) async-start(), calls=%async_computation.15 | async-start | bytes 2359296 | tf_op jit(solution)/shard_map/reduce_scatter | solution.py:570
  389.3 165.2 %reduce-scatter.9.cloned.1.call-start = ((), (), s32[]{:S(2)}) async-start(), calls=%async_computation.14 | async-start | bytes 2359296 | tf_op jit(solution)/shard_map/reduce_scatter | solution.py:570
  389.9 166.7 %reduce-scatter.7.cloned.1.call-start = ((), (), s32[]{:S(2)}) async-start(), calls=%async_computation.13 | async-start | bytes 2359296 | tf_op jit(solution)/shard_map/reduce_scatter | solution.py:569
  390.5 35.3 %all-to-all-start.5 = ((bf16[4,624,512]{2,1,0:T(8,128)(2,1)}), bf16[4,624,512]{2,1,0:T(8,128)(2,1)S(1)}, u32[]{:S(2)}, u32[]{:S(2)}) async-start(bf16[4,624,512]{2,1,0:T(8,128)(2,1)} %bitcast.28), calls=%async_computation.5 | async-start | bytes 5111808 | tf_op jit(solution)/shard_map/all_to_all | solution.py:548
  394.1 162.5 %reduce-scatter.5.cloned.1.call-start = ((), (), s32[]{:S(2)}) async-start(), calls=%async_computation.12 | async-start | bytes 2359296 | tf_op jit(solution)/shard_map/reduce_scatter | solution.py:569
  425.8 6.0 %copy-start.8 = (f32[512,128]{1,0:T(8,128)S(1)}, f32[512,128]{1,0:T(8,128)}, u32[]{:S(2)}) copy-start(f32[512,128]{1,0:T(8,128)} %get-tuple-element.52) | copy-start | bytes 786436
  425.8 6.0 %copy-start.9 = (f32[512,128]{1,0:T(8,128)S(1)}, f32[512,128]{1,0:T(8,128)}, u32[]{:S(2)}) copy-start(f32[512,128]{1,0:T(8,128)} %get-tuple-element.51) | copy-start | bytes 786436
  425.8 6.1 %copy-start.12 = (f32[1,512]{1,0:T(1,128)S(1)}, f32[1,512]{1,0:T(1,128)}, u32[]{:S(2)}) copy-start(f32[1,512]{1,0:T(1,128)} %get-tuple-element.47) | copy-start | bytes 6148
  425.8 6.1 %copy-start.13 = (f32[1,512]{1,0:T(1,128)S(1)}, f32[1,512]{1,0:T(1,128)}, u32[]{:S(2)}) copy-start(f32[1,512]{1,0:T(1,128)} %get-tuple-element.50) | copy-start | bytes 6148
  427.2 75.3 %all-to-all-start.2 = ((bf16[4,624,512]{2,1,0:T(8,128)(2,1)}), bf16[4,624,512]{2,1,0:T(8,128)(2,1)}, u32[]{:S(2)}, u32[]{:S(2)}) async-start(bf16[4,624,512]{2,1,0:T(8,128)(2,1)} %bitcast.19), calls=%async_computation.2 | async-start | bytes 5111808 | tf_op jit(solution)/shard_map/all_to_all | solution.py:548
  549.9 3.5 copy-start.7
  (1 other events, 1.5 us)
Sparse Core Ops, SparseCore 0:
  388.8 160.9 all-reduce.6
Sparse Core Ops, SparseCore 1:
  391.6 36.7 reduce-scatter.10
  430.6 36.3 reduce-scatter.8
  469.2 35.3 reduce-scatter.6
  507.0 38.0 reduce-scatter.4

commit v2 on v1

v2 whole, which is shorter than its diff:
```python
import functools

import jax
import jax.numpy as jnp
from jax import lax
from jax.experimental import pallas as pl
from jax.experimental.pallas import tpu as pltpu
from jax.sharding import PartitionSpec as P

HEADS = 8
PATCHES = 49
LANES = 128
PAIR = 2 * PATCHES
PAIR_PAD = 112
BLOCK_PAIRS = 4
BLOCK = BLOCK_PAIRS * PAIR
BLOCK_PAD = BLOCK_PAIRS * PAIR_PAD
BF = jnp.bfloat16
F32 = jnp.float32
VMEM_BYTES = 56 * 1024 * 1024
TILE_ROWS = 640
FCUT = 1024


def params():
    return pltpu.CompilerParams(
        dimension_semantics=("arbitrary",), vmem_limit_bytes=VMEM_BYTES
    )


def cost(flops, moved, special=0):
    return pl.CostEstimate(
        flops=int(flops), bytes_accessed=int(moved), transcendentals=int(special)
    )


def whole(shape):
    return pl.BlockSpec(shape, lambda *_: (0,) * len(shape))


def dot(left, right):
    return jnp.dot(left, right, preferred_element_type=F32)


def dot_rt(left, right):
    return lax.dot_general(left, right, (((1,), (1,)), ((), ())), preferred_element_type=F32)


def dot_lt(left, right):
    return lax.dot_general(left, right, (((0,), (0,)), ((), ())), preferred_element_type=F32)


def norm_parts(values):
    mean = jnp.mean(values, axis=-1, keepdims=True)
    cent = values - mean
    factor = lax.rsqrt(jnp.mean(cent * cent, axis=-1, keepdims=True) + 1e-06)
    return cent * factor, factor


def norm_back(grad_normed, normed_hat, factor, gain):
    grad_hat = grad_normed * gain
    inner = grad_hat - jnp.mean(grad_hat, axis=-1, keepdims=True)
    inner = inner - normed_hat * jnp.mean(grad_hat * normed_hat, axis=-1, keepdims=True)
    return factor * inner


def spread_rows(compact, padded):
    for pair in range(BLOCK_PAIRS):
        padded[PAIR_PAD * pair : PAIR_PAD * pair + PAIR] = compact[PAIR * pair : PAIR * pair + PAIR]


def gather_rows(padded, compact):
    for pair in range(BLOCK_PAIRS):
        compact[PAIR * pair : PAIR * pair + PAIR] = padded[PAIR_PAD * pair : PAIR_PAD * pair + PAIR]


def clear_gaps(padded):
    for pair in range(BLOCK_PAIRS):
        low = PAIR_PAD * pair + PAIR
        padded[low : low + PAIR_PAD - PAIR] = jnp.zeros((PAIR_PAD - PAIR, padded.shape[1]), F32)


def image_of(position):
    return (position >= PATCHES).astype(jnp.int32) + (position >= PAIR).astype(jnp.int32)


def same_image():
    rows = lax.broadcasted_iota(jnp.int32, (2 * PAIR_PAD, PAIR_PAD), 0)
    rows = jnp.where(rows >= PAIR_PAD, rows - PAIR_PAD, rows)
    cols = lax.broadcasted_iota(jnp.int32, (2 * PAIR_PAD, PAIR_PAD), 1)
    return image_of(rows) == image_of(cols)


def low_half():
    return lax.broadcasted_iota(jnp.int32, (PAIR_PAD, LANES), 1) < LANES // 2


def two_heads(values, low):
    zero = jnp.zeros_like(values)
    return jnp.concatenate([jnp.where(low, values, zero), jnp.where(low, zero, values)], axis=0)


def one_row(values, low):
    return jnp.where(low, values[:PAIR_PAD], values[PAIR_PAD:])


def attend_kernel(
    tok_ref, gain_one_ref, qkv_w_ref, proj_w_ref, gain_two_ref,
    hidden_ref, rows_ref, qkv_ref, probs_ref, mixed_ref,
    compact, padded,
):
    width = tok_ref.shape[1]
    factor_qk = (width // HEADS) ** (-0.5)
    clear_gaps(padded)
    inputs = tok_ref[...].astype(F32)
    compact[...] = norm_parts(inputs)[0] * gain_one_ref[...]
    spread_rows(compact, padded)
    qkv_ref[...] = dot(padded[...].astype(BF), qkv_w_ref[...]).astype(BF)
    valid = same_image()
    low = low_half()
    for pair in range(BLOCK_PAIRS):
        rows = slice(PAIR_PAD * pair, PAIR_PAD * (pair + 1))
        for two in range(width // LANES):
            cols = slice(LANES * two, LANES * (two + 1))
            query = qkv_ref[rows, cols]
            keys = qkv_ref[rows, width + LANES * two : width + LANES * (two + 1)]
            values = qkv_ref[rows, 2 * width + LANES * two : 2 * width + LANES * (two + 1)]
            scores = jnp.where(valid, dot_rt(two_heads(query, low), keys), -1e30)
            highest = jnp.max(scores, axis=-1, keepdims=True)
            expo = jnp.exp((scores - highest) * factor_qk)
            probs = (expo / jnp.sum(expo, axis=-1, keepdims=True)).astype(BF)
            step = (pair * (width // LANES) + two) * 2 * PAIR_PAD
            probs_ref[step : step + 2 * PAIR_PAD, :] = probs
            mixed_ref[rows, cols] = one_row(dot(probs, values), low).astype(BF)
    padded[...] = dot(mixed_ref[...], proj_w_ref[...])
    gather_rows(padded, compact)
    hidden = inputs + compact[...]
    hidden_ref[...] = hidden
    rows_ref[...] = (norm_parts(hidden)[0] * gain_two_ref[...]).astype(BF)


def attend(tokens, gain_one, w_qkv, w_proj, gain_two):
    count, width = tokens.shape
    blocks = count // BLOCK
    prob_rows = BLOCK_PAIRS * (width // LANES) * 2 * PAIR_PAD
    row = lambda shape: pl.BlockSpec(shape, lambda step: (step, 0))
    flops = 2 * blocks * BLOCK_PAD * width * (4 * width + 4 * PAIR_PAD)
    return pl.pallas_call(
        attend_kernel,
        grid=(blocks,),
        in_specs=[
            row((BLOCK, width)), whole((1, width)), whole(w_qkv.shape), whole(w_proj.shape),
            whole((1, width)),
        ],
        out_specs=[
            row((BLOCK, width)), row((BLOCK, width)), row((BLOCK_PAD, 3 * width)),
            row((prob_rows, PAIR_PAD)), row((BLOCK_PAD, width)),
        ],
        out_shape=[
            jax.ShapeDtypeStruct((count, width), F32),
            jax.ShapeDtypeStruct((count, width), BF),
            jax.ShapeDtypeStruct((blocks * BLOCK_PAD, 3 * width), BF),
            jax.ShapeDtypeStruct((blocks * prob_rows, PAIR_PAD), BF),
            jax.ShapeDtypeStruct((blocks * BLOCK_PAD, width), BF),
        ],
        scratch_shapes=[pltpu.VMEM((BLOCK, width), F32), pltpu.VMEM((BLOCK_PAD, width), F32)],
        compiler_params=params(),
        cost_estimate=cost(flops, 30e6, blocks * prob_rows * LANES),
        name="attend",
    )(tokens, gain_one[None, :], w_qkv, w_proj, gain_two[None, :])


def place_kernel(capacity, ids_ref, picks_ref, index_ref, starts_ref, carry):
    step = pl.program_id(0)

    @pl.when(step == 0)
    def _():
        carry[...] = jnp.zeros(carry.shape, F32)
        starts_ref[...] = jnp.zeros(starts_ref.shape, jnp.int32)

    experts, block = ids_ref.shape[0], picks_ref.shape[2]
    ids = ids_ref[...]
    names = [picks_ref[0, c : c + 1, :] == ids for c in (0, 1)]
    named = (names[0] | names[1]).astype(F32)
    earlier = lax.broadcasted_iota(jnp.int32, (block, block), 0) < lax.broadcasted_iota(
        jnp.int32, (block, block), 1
    )
    before = dot(named.astype(BF), earlier.astype(F32).astype(BF)) + carry[:, 0:1]
    spot = before + (lax.broadcasted_iota(jnp.int32, (experts, block), 0) * capacity).astype(F32)
    for c in (0, 1):
        found = jnp.sum(jnp.where(names[c], spot, 0.0), axis=0, keepdims=True).astype(jnp.int32)
        index_ref[0, c : c + 1, :] = jnp.where(picks_ref[0, 2 + c : 3 + c, :] > 0, found, -1)
    after = carry[...] + jnp.sum(named, axis=1, keepdims=True)
    carry[...] = after
    lane = lax.broadcasted_iota(jnp.int32, (experts, LANES), 1)
    starts_ref[...] = jnp.where(lane == step + 1, after.astype(jnp.int32), starts_ref[...])


def places(ids, picks, keep, capacity):
    count = picks.shape[0]
    blocks = count // BLOCK
    experts = ids.shape[0]
    turned = jnp.concatenate([picks, keep], axis=1).reshape(blocks, BLOCK, 4).transpose(0, 2, 1)
    return pl.pallas_call(
        functools.partial(place_kernel, capacity),
        grid=(blocks,),
        in_specs=[whole((experts, 1)), pl.BlockSpec((1, 4, BLOCK), lambda step: (step, 0, 0))],
        out_specs=[
            pl.BlockSpec((1, 2, BLOCK), lambda step: (step, 0, 0)), whole((experts, LANES)),
        ],
        out_shape=[
            jax.ShapeDtypeStruct((blocks, 2, BLOCK), jnp.int32),
            jax.ShapeDtypeStruct((experts, LANES), jnp.int32),
        ],
        scratch_shapes=[pltpu.VMEM((experts, LANES), F32)],
        compiler_params=params(),
        cost_estimate=cost(1e8, 1e5),
        name="places",
    )(ids[:, None], turned)


def window_rows(experts, capacity):
    return min(capacity, 16 * -(-2 * BLOCK * 8 // (5 * 16 * experts)))


def window_at(starts_ref, expert, step, turn, window, capacity):
    low = starts_ref[expert, step]
    begin = (low // 16) * 16 + turn * window
    at = pl.multiple_of(jnp.minimum(begin, capacity - window), 16)
    return begin, starts_ref[expert, step + 1], at


def turns(starts_ref, step, experts, window):
    most = 0
    for expert in experts:
        low = (starts_ref[expert, step] // 16) * 16
        most = jnp.maximum(most, (starts_ref[expert, step + 1] - low + window - 1) // window)
    return most


def dispatch_kernel(window, capacity, plan, sources, starts_ref, index_ref, *refs):
    src_refs, outs, (spots, got) = refs[:sources], refs[sources:-2], refs[-2:]
    owners = outs[0].shape[0]
    step = pl.program_id(0)
    named = [owners * part + owner for part, _ in plan for owner in range(owners)]

    @pl.when(step == 0)
    def _():
        for out in outs:
            out[...] = jnp.zeros(out.shape, out.dtype)

    place = lax.broadcasted_iota(jnp.int32, (window, index_ref.shape[2]), 0)
    first, second = index_ref[0, 0:1, :], index_ref[0, 1:2, :]

    def one_turn(turn, carry):
        for (part, used), out in zip(plan, outs):
            spans = []
            for owner in range(owners):
                expert = part * owners + owner
                begin, _, at = window_at(starts_ref, expert, step, turn, window, capacity)
                shift = expert * capacity
                near = jnp.where(first >= shift + begin, first - (shift + at), -1)
                far = jnp.where(second >= shift + begin, second - (shift + at), -1)
                hit = jnp.where((near >= 0) & (near < window), near, far)
                spots[window * owner : window * (owner + 1), :] = (
                    (place == hit).astype(F32).astype(BF)
                )
                spans.append(at)
            for order, which in enumerate(used):
                got[...] = dot(spots[...], src_refs[which][...])
                for owner, at in enumerate(spans):
                    rows = pl.ds(pl.multiple_of(at + order * capacity, 16), window)
                    held = out[owner, rows, :].astype(F32)
                    out[owner, rows, :] = (
                        held + got[window * owner : window * (owner + 1), :]
                    ).astype(BF)
        return carry

    lax.fori_loop(0, turns(starts_ref, step, named, window), one_turn, 0)


def dispatch(srcs, starts, index_rows, owners, capacity, plan):
    count, width = srcs[0].shape
    window = window_rows(starts.shape[0], capacity)
    shapes = [(owners, len(used) * capacity, width) for _, used in plan]
    return pl.pallas_call(
        functools.partial(dispatch_kernel, window, capacity, plan, len(srcs)),
        grid_spec=pltpu.PrefetchScalarGridSpec(
            num_scalar_prefetch=1,
            grid=(count // BLOCK,),
            in_specs=[pl.BlockSpec((1, 2, BLOCK), lambda step, *_: (step, 0, 0))]
            + [pl.BlockSpec((BLOCK, width), lambda step, *_: (step, 0))] * len(srcs),
            out_specs=[whole(shape) for shape in shapes],
            scratch_shapes=[
                pltpu.VMEM((owners * window, BLOCK), BF),
                pltpu.VMEM((owners * window, width), F32),
            ],
        ),
        out_shape=[jax.ShapeDtypeStruct(shape, BF) for shape in shapes],
        compiler_params=params(),
        cost_estimate=cost(6e9, 8e6),
        name="dispatch",
    )(starts, index_rows, *srcs)


def combine_block(window, step, starts_ref, index_ref, bufs, wins, acc):
    owners, capacity = bufs[0].shape[:2]
    experts = owners * len(bufs)
    lane = lax.broadcasted_iota(jnp.int32, (1, experts * window), 1)
    acc[...] = jnp.zeros(acc.shape, F32)

    def one_turn(turn, carry):
        seen = jnp.full((1, experts * window), -2, jnp.int32)
        for expert in range(experts):
            begin, high, at = window_at(starts_ref, expert, step, turn, window, capacity)
            slot = lane + (at - expert * window)
            fresh = (slot >= begin) & (slot < high)
            mine = (lane >= expert * window) & (lane < (expert + 1) * window)
            seen = jnp.where(mine & fresh, slot + expert * capacity, seen)
            wins[window * expert : window * (expert + 1), :] = (
                bufs[expert // owners][expert % owners, pl.ds(at, window), :]
            )
        hit = (index_ref[:, 0:1] == seen) | (index_ref[:, 1:2] == seen)
        acc[...] += dot(hit.astype(F32).astype(BF), wins[...])
        return carry

    lax.fori_loop(0, turns(starts_ref, step, range(experts), window), one_turn, 0)


def back_specs(parts, capacity):
    return [
        pl.BlockSpec((array.shape[0], capacity, array.shape[2]), lambda *_, at=at: (0, at, 0))
        for array, at in parts
    ]


def top_kernel(window, starts_ref, index_ref, hidden_ref, *refs):
    *bufs, out_ref, wins, acc = refs
    combine_block(window, pl.program_id(0), starts_ref, index_ref, bufs, wins, acc)
    out_ref[...] = (hidden_ref[...] + acc[...]).astype(BF)


def top(starts, index, hidden, parts, capacity):
    count, width = hidden.shape
    experts = starts.shape[0]
    window = window_rows(experts, capacity)
    row = lambda shape: pl.BlockSpec(shape, lambda step, *_: (step, 0))
    return pl.pallas_call(
        functools.partial(top_kernel, window),
        grid_spec=pltpu.PrefetchScalarGridSpec(
            num_scalar_prefetch=1,
            grid=(count // BLOCK,),
            in_specs=[row((BLOCK, 2)), row((BLOCK, width))] + back_specs(parts, capacity),
            out_specs=row((BLOCK, width)),
            scratch_shapes=[
                pltpu.VMEM((experts * window, width), BF), pltpu.VMEM((BLOCK, width), F32),
            ],
        ),
        out_shape=jax.ShapeDtypeStruct((count, width), BF),
        compiler_params=params(),
        cost_estimate=cost(6e9, 12e6),
        name="top",
    )(starts, index, hidden, *[array for array, _ in parts])


def gelu_parts(values):
    size = jnp.abs(values)
    near = 1.0 / (1.0 + (0.3275911 * 0.7071067811865476) * size)
    expo = jnp.exp(-0.5 * (values * values))
    poly = 0.5 * 1.061405429
    for term in (-1.453152027, 1.421413741, -0.284496736, 0.254829592):
        poly = poly * near + 0.5 * term
    tail = poly * near * expo
    share = jnp.where(values >= 0, 1.0 - tail, tail)
    return values * share, share + values * (0.3989422804014327 * expo)


def expert_kernel(
    experts, fcut, mine_ref, up_ref, down_ref, router_ref, back_ref, x_ref, dy_ref, *refs
):
    dx_ref, out_ref = refs[0], refs[-8]
    grad_ref, grouter_ref, acc_up, acc_down, acc_router, acc_out, acc_dx = refs[-7:]
    step = pl.program_id(0)
    hidden_units = up_ref.shape[1]
    times, capacity, width = x_ref.shape
    count = times * capacity

    @pl.when(step == 0)
    def _():
        acc_up[...] = jnp.zeros(acc_up.shape, F32)
        acc_down[...] = jnp.zeros(acc_down.shape, F32)
        acc_router[...] = jnp.zeros(acc_router.shape, F32)

    rows = x_ref[...].reshape(count, width)
    logits = dot(rows, router_ref[...])
    logits = logits[:, :LANES] + logits[:, LANES:]
    lane = lax.broadcasted_iota(jnp.int32, (count, LANES), 1)
    logits = jnp.where(lane < experts, logits, -1e30)
    expo = jnp.exp(logits - jnp.max(logits, axis=-1, keepdims=True))
    gates = expo / jnp.sum(expo, axis=-1, keepdims=True)
    own = (lane == mine_ref[0]).astype(F32)
    chosen = jnp.sum(gates * own, axis=-1, keepdims=True)
    pair = (chosen * dy_ref[...].reshape(count, width).astype(F32)).astype(BF)
    rows_t = rows.T
    pair_t = pair.T
    inner = jnp.zeros((count, LANES), F32)
    for low in range(0, hidden_units, fcut):
        cols = slice(low, low + fcut)
        pre = dot(rows, up_ref[:, cols])
        grad_act = dot_rt(pair, down_ref[cols, :])
        act, slope = gelu_parts(pre)
        both = act * grad_act
        for part in range(0, fcut, LANES):
            inner = inner + both[:, part : part + LANES]
        act = act.astype(BF)
        grad_pre = (grad_act * slope).astype(BF)
        acc_up[:, cols] += dot(rows_t, grad_pre)
        acc_down[:, cols] += dot(pair_t, act)
        if low == 0:
            acc_out[...] = dot(act, down_ref[cols, :])
            acc_dx[...] = dot_rt(grad_pre, up_ref[:, cols])
        else:
            acc_out[...] += dot(act, down_ref[cols, :])
            acc_dx[...] += dot_rt(grad_pre, up_ref[:, cols])
    grad_logits = jnp.sum(inner, axis=-1, keepdims=True) * (own - gates)
    head = grad_logits.astype(BF)
    rest = (grad_logits - head.astype(F32)).astype(BF)
    acc_router[...] += dot(rows_t, jnp.concatenate([head, rest], axis=1))
    shape = (times, capacity, width)
    out_ref[:, out_ref.shape[1] - capacity :, :] = (chosen * acc_out[...]).astype(BF).reshape(shape)
    dx_ref[:, :capacity, :] = (
        acc_dx[...] + dot(jnp.concatenate([head, head], axis=1), back_ref[...])
    ).astype(BF).reshape(shape)

    @pl.when(step == pl.num_programs(0) - 1)
    def _():
        shards, tall, _ = grad_ref.shape
        up_rows, down_rows = width // shards, hidden_units // shards
        piece = tall - up_rows
        for shard in range(shards):
            grad_ref[shard, :up_rows, :] = acc_up[up_rows * shard : up_rows * (shard + 1), :].astype(BF)
            turned = acc_down[:, down_rows * shard : down_rows * (shard + 1)].T.astype(BF)
            for part in range(down_rows // piece):
                grad_ref[shard, up_rows:, width * part : width * (part + 1)] = (
                    turned[piece * part : piece * (part + 1), :]
                )
        grouter_ref[...] = acc_router[:, :LANES] + acc_router[:, LANES:]


def expert_pass(mine, rows, grads, w_up, w_down, router, router_back, experts, capacity, shards, joined):
    (rows, rows_at), (grads, grads_at) = rows, grads
    sources, _, width = rows.shape
    units = w_up.shape[1]
    times = max(
        n for n in range(1, sources + 1) if sources % n == 0 and n * capacity <= max(TILE_ROWS, capacity)
    )
    tile = times * capacity
    block = lambda tall, at: pl.BlockSpec((times, tall, width), lambda step, *_: (step, at, 0))
    sent = [2 * capacity] if joined else [capacity, capacity]
    grad_shape = (shards, width // shards * 2, units)
    return pl.pallas_call(
        functools.partial(expert_kernel, experts, min(FCUT, units)),
        grid_spec=pltpu.PrefetchScalarGridSpec(
            num_scalar_prefetch=1,
            grid=(sources // times,),
            in_specs=[
                whole(w_up.shape), whole(w_down.shape), whole(router.shape), whole(router_back.shape),
                block(capacity, rows_at), block(capacity, grads_at),
            ],
            out_specs=[block(tall, 0) for tall in sent] + [whole(grad_shape), whole((width, LANES))],
            scratch_shapes=[
                pltpu.VMEM((width, units), F32),
                pltpu.VMEM((width, units), F32),
                pltpu.VMEM((width, 2 * LANES), F32),
                pltpu.VMEM((tile, width), F32),
                pltpu.VMEM((tile, width), F32),
            ],
        ),
        out_shape=[jax.ShapeDtypeStruct((sources, tall, width), BF) for tall in sent] + [
            jax.ShapeDtypeStruct(grad_shape, BF),
            jax.ShapeDtypeStruct((width, LANES), F32),
        ],
        compiler_params=params(),
        cost_estimate=cost(
            20 * sources * capacity * width * units, 30e6, 2 * sources * capacity * units
        ),
        name="expert_pass",
    )(mine, w_up, w_down, router, router_back, rows, grads)


def back_kernel(
    window, groups, starts_ref, here_ref, index_ref, hidden_ref, tok_ref, dy_ref, qkv_ref,
    probs_ref, mixed_ref, gain_one_ref, qkv_w_ref, proj_w_ref, gain_two_ref, *refs,
):
    *bufs, ghid_ref, dqkv_ref, sum_ref, ggain_one_ref, ggain_two_ref = refs[:-6]
    wins, acc, compact, padded, acc_qkv, acc_proj = refs[-6:]
    step = pl.program_id(0)
    width = tok_ref.shape[1]
    factor_qk = (width // HEADS) ** (-0.5)

    @pl.when(step == 0)
    def _():
        for ref in (acc_qkv, acc_proj, ggain_two_ref):
            ref[...] = jnp.zeros(ref.shape, F32)

    combine_block(window, step, starts_ref, index_ref, bufs, wins, acc)
    clear_gaps(padded)
    hat_two, scale_two = norm_parts(hidden_ref[...])
    grad_normed = acc[...]
    ggain_two_ref[...] += jnp.sum(grad_normed * hat_two, axis=0, keepdims=True)
    grad_hidden = dy_ref[...].astype(F32) + norm_back(
        grad_normed, hat_two, scale_two, gain_two_ref[...]
    )
    ghid_ref[...] = grad_hidden
    compact[...] = grad_hidden
    spread_rows(compact, padded)
    grad_attn = padded[...].astype(BF)
    acc_proj[...] += dot_lt(mixed_ref[...], grad_attn)
    grad_mixed = dot_rt(grad_attn, proj_w_ref[...]).astype(BF)
    low = low_half()
    for pair in range(BLOCK_PAIRS):
        rows = slice(PAIR_PAD * pair, PAIR_PAD * (pair + 1))
        for two in range(width // LANES):
            cols = slice(LANES * two, LANES * (two + 1))
            key_cols = slice(width + LANES * two, width + LANES * (two + 1))
            value_cols = slice(2 * width + LANES * two, 2 * width + LANES * (two + 1))
            at = (pair * (width // LANES) + two) * 2 * PAIR_PAD
            probs = probs_ref[at : at + 2 * PAIR_PAD, :]
            wide = probs.astype(F32)
            grad_out = two_heads(grad_mixed[rows, cols], low)
            grad_probs = dot_rt(grad_out, qkv_ref[rows, value_cols])
            meet = jnp.sum(wide * grad_probs, axis=-1, keepdims=True)
            grad_scores = (wide * (grad_probs - meet) * factor_qk).astype(BF)
            grad_query = one_row(dot(grad_scores, qkv_ref[rows, key_cols]), low)
            dqkv_ref[rows, cols] = grad_query.astype(BF)
            dqkv_ref[rows, key_cols] = dot_lt(
                grad_scores, two_heads(qkv_ref[rows, cols], low)
            ).astype(BF)
            dqkv_ref[rows, value_cols] = dot_lt(probs, grad_out).astype(BF)
    compact[...] = norm_parts(tok_ref[...].astype(F32))[0] * gain_one_ref[...]
    spread_rows(compact, padded)
    acc_qkv[...] += dot_lt(padded[...].astype(BF), dqkv_ref[...])

    @pl.when(step == pl.num_programs(0) - 1)
    def _():
        cores, sides, layers = groups
        tall = sum_ref.shape[2]
        for core in range(cores):
            for side in range(sides):
                for layer in range(layers):
                    low = ((core * sides + side) * layers + layer) * tall
                    part, at = low // width, low % width
                    if part < 3:
                        piece = acc_qkv[at : at + tall, width * part : width * (part + 1)]
                    else:
                        piece = acc_proj[at : at + tall, :]
                    spot = (side ^ here_ref[1]) * layers + (layer ^ here_ref[2])
                    sum_ref[core ^ here_ref[0], spot] = piece.astype(BF)
        ggain_one_ref[...] = jnp.sum(
            acc_qkv[...] * qkv_w_ref[...].astype(F32), axis=-1, keepdims=True
        )


def back(starts, here, groups, index, hidden, tokens, dy, qkv, probs, mixed, gain_one, w_qkv, w_proj, gain_two, parts, capacity):
    count, width = tokens.shape
    blocks = count // BLOCK
    experts = starts.shape[0]
    window = window_rows(experts, capacity)
    row = lambda shape: pl.BlockSpec(shape, lambda step, *_: (step, 0))
    cores, sides, layers = groups
    sum_shape = (cores, sides * layers, 4 * width // (cores * sides * layers), width)
    flops = 2 * blocks * BLOCK_PAD * width * (8 * width + 10 * PAIR_PAD)
    return pl.pallas_call(
        functools.partial(back_kernel, window, groups),
        grid_spec=pltpu.PrefetchScalarGridSpec(
            num_scalar_prefetch=2,
            grid=(blocks,),
            in_specs=[
                row((BLOCK, 2)), row((BLOCK, width)), row((BLOCK, width)), row((BLOCK, width)),
                row((BLOCK_PAD, 3 * width)), row((probs.shape[0] // blocks, PAIR_PAD)),
                row((BLOCK_PAD, width)),
                whole((1, width)), whole(w_qkv.shape), whole(w_proj.shape), whole((1, width)),
            ] + back_specs(parts, capacity),
            out_specs=[
                row((BLOCK, width)), row((BLOCK_PAD, 3 * width)), whole(sum_shape),
                whole((width, 1)), whole((1, width)),
            ],
            scratch_shapes=[
                pltpu.VMEM((experts * window, width), BF),
                pltpu.VMEM((BLOCK, width), F32),
                pltpu.VMEM((BLOCK, width), F32),
                pltpu.VMEM((BLOCK_PAD, width), F32),
                pltpu.VMEM(w_qkv.shape, F32),
                pltpu.VMEM(w_proj.shape, F32),
            ],
        ),
        out_shape=[
            jax.ShapeDtypeStruct((count, width), F32),
            jax.ShapeDtypeStruct(qkv.shape, BF),
            jax.ShapeDtypeStruct(sum_shape, BF),
            jax.ShapeDtypeStruct((width, 1), F32),
            jax.ShapeDtypeStruct((1, width), F32),
        ],
        compiler_params=params(),
        cost_estimate=cost(flops + 12e9, 40e6),
        name="back",
    )(
        starts, here, index, hidden, tokens, dy, qkv, probs, mixed, gain_one[None, :], w_qkv,
        w_proj, gain_two[None, :], *[array for array, _ in parts],
    )


def last_kernel(dqkv_ref, ghid_ref, tok_ref, gain_one_ref, qkv_w_ref, out_ref, compact, padded):
    padded[...] = dot_rt(dqkv_ref[...], qkv_w_ref[...])
    gather_rows(padded, compact)
    hat_one, scale_one = norm_parts(tok_ref[...].astype(F32))
    out_ref[...] = ghid_ref[...] + norm_back(compact[...], hat_one, scale_one, gain_one_ref[...])


def last(dqkv, ghid, tokens, gain_one, w_qkv):
    count, width = tokens.shape
    row = lambda shape: pl.BlockSpec(shape, lambda step: (step, 0))
    return pl.pallas_call(
        last_kernel,
        grid=(count // BLOCK,),
        in_specs=[
            row((BLOCK_PAD, 3 * width)), row((BLOCK, width)), row((BLOCK, width)),
            whole((1, width)), whole(w_qkv.shape),
        ],
        out_specs=row((BLOCK, width)),
        out_shape=jax.ShapeDtypeStruct((count, width), F32),
        scratch_shapes=[pltpu.VMEM((BLOCK, width), F32), pltpu.VMEM((BLOCK_PAD, width), F32)],
        compiler_params=params(),
        cost_estimate=cost(6 * dqkv.shape[0] * width * width, 20e6),
        name="last",
    )(dqkv, ghid, tokens, gain_one[None, :], w_qkv)


def lay_kernel(groups, here_ref, own_ref, other_ref, qkv_ref, proj_ref):
    cores, sides, layers = groups
    tall, width = own_ref.shape[1:]
    for core in range(cores):
        for side in range(sides):
            for layer in range(layers):
                low = ((core * sides + side) * layers + layer) * tall
                part, at = low // width, low % width
                spot = (side ^ here_ref[1]) * layers + (layer ^ here_ref[2])
                piece = jnp.where(core == here_ref[0], own_ref[spot].astype(F32), other_ref[spot].astype(F32))
                if part < 3:
                    qkv_ref[at : at + tall, width * part : width * (part + 1)] = piece
                else:
                    proj_ref[at : at + tall, :] = piece


def lay(groups, here, own, other):
    width = own.shape[2]
    return pl.pallas_call(
        functools.partial(lay_kernel, groups),
        grid_spec=pltpu.PrefetchScalarGridSpec(
            num_scalar_prefetch=1,
            grid=(1,),
            in_specs=[whole(own.shape)] * 2,
            out_specs=[whole((width, 3 * width)), whole((width, width))],
        ),
        out_shape=[
            jax.ShapeDtypeStruct((width, 3 * width), F32),
            jax.ShapeDtypeStruct((width, width), F32),
        ],
        compiler_params=params(),
        cost_estimate=cost(1e6, 8e6),
        name="lay",
    )(here, own, other)


def jump(value, axis, far):
    size = lax.axis_size(axis)
    return lax.ppermute(value, axis, [(at, at ^ far) for at in range(size)])


def add_up(parts):
    return sum(part.astype(F32) for part in parts).astype(BF)


def sum_over_all(sums, groups):
    cores, sides, layers = groups
    half = add_up([sums[0], jump(sums[1], "dp", 1)])
    tall, width = half.shape[1:]
    half = half.reshape(sides, layers, tall, width)
    flat = add_up([half[0]] + [jump(half[side], "expert", side) for side in range(1, sides)])
    spot = add_up([flat[0]] + [jump(flat[layer], "dp", cores * layer) for layer in range(1, layers)])
    flat = jnp.stack([spot] + [jump(spot, "dp", cores * layer) for layer in range(1, layers)])
    half = jnp.stack([flat] + [jump(flat, "expert", side) for side in range(1, sides)])
    half = half.reshape(sides * layers, tall, width)
    return half, jump(half, "dp", 1)


def sum_small(value):
    for axis in ("dp", "expert"):
        far = 1
        while far < lax.axis_size(axis):
            value = value + jump(value, axis, far)
            far = far * 2
    return value


def per_device(
    tokens, gain_one, w_qkv, w_proj, gain_two, w_router, w_in, w_eout, picks, keep, grad_out
):
    count, width = tokens.shape
    local = w_in.shape[0]
    owners = lax.axis_size("expert")
    shards = lax.axis_size("dp")
    experts = local * owners
    capacity = 8 * ((21 * count + 80 * experts - 1) // (80 * experts))
    me, row = lax.axis_index("expert"), lax.axis_index("dp")
    cores = 2
    groups = (cores, owners, shards // cores)
    here = jnp.stack([row % cores, me, row // cores]).astype(jnp.int32)
    ids = jnp.arange(experts, dtype=jnp.int32).reshape(owners, local).T.reshape(-1)

    def swap(sent):
        return lax.all_to_all(sent, "expert", split_axis=0, concat_axis=0, tiled=True)

    def after(value, *others):
        return lax.optimization_barrier((value, *others))[0]

    index_rows, starts = places(ids, picks, keep, capacity)
    (sent,) = dispatch([grad_out], starts, index_rows, owners, capacity, ((0, (0,)),))
    grads_first = swap(sent)
    hidden, rows, qkv, probs, mixed = attend(after(tokens, sent), gain_one, w_qkv, w_proj, gain_two)
    plan = ((0, (0,)),) + tuple((part, (0, 1)) for part in range(1, local))
    sent, *others = dispatch(
        [after(rows, grads_first), grad_out], starts, index_rows, owners, capacity, plan
    )
    got = swap(sent)
    came = [((got, 0), (grads_first, 0))]
    for sent in others:
        got = swap(after(sent, got))
        came.append(((got, 0), (got, 1)))
    index = index_rows.transpose(0, 2, 1).reshape(count, 2)
    head = w_router.astype(BF)
    rest = (w_router - head.astype(F32)).astype(BF)
    gap = ((0, 0), (0, LANES - experts))
    router = jnp.concatenate([jnp.pad(head, gap), jnp.pad(rest, gap)], axis=1)
    router_back = jnp.concatenate([jnp.pad(head, gap).T, jnp.pad(rest, gap).T], axis=0)
    outs, downs, sums, grad_router = [], [], [], 0
    for part in range(local):
        mine = (me * local + part).astype(jnp.int32)[None]
        joined = part < local - 1
        *sent, grad, router_part = expert_pass(
            mine, *came[part], w_in[part], w_eout[part], router, router_back, experts, capacity,
            shards, joined,
        )
        if part:
            sent = [after(sent[0], got), *sent[1:]]
        got = swap(sent[0])
        downs.append((got, 0))
        outs.append((got, 1))
        grad = grad.reshape(shards * grad.shape[1], grad.shape[2])
        sums.append(lax.psum_scatter(grad, "dp", scatter_dimension=0, tiled=True))
        grad_router = grad_router + router_part[:, :experts]
    outs[-1] = (swap(after(sent[1], got)), 0)
    grad_hidden, dqkv, pieces, grad_gain_one, grad_gain_two = back(
        starts, here, groups, index, hidden, tokens, grad_out, qkv, probs, mixed, gain_one,
        w_qkv, w_proj, gain_two, downs, capacity,
    )
    pieces = after(pieces, outs[-1][0])
    small = jnp.concatenate([grad_router.T, grad_gain_two, grad_gain_one.T], axis=0)
    small = sum_small(small)
    own, other = sum_over_all(pieces, groups)
    block_out = top(starts, index, hidden, outs, capacity)
    grad_tokens = last(dqkv, grad_hidden, tokens, gain_one, w_qkv)
    grad_qkv, grad_proj = lay(groups, here, own, other)
    tall = width // shards
    grad_in = jnp.stack([part[:tall] for part in sums]).astype(F32)
    grad_eout = jnp.stack(
        [part[tall:].reshape(tall, -1, width).transpose(1, 0, 2).reshape(-1, width) for part in sums]
    ).astype(F32)
    return (
        block_out,
        grad_tokens,
        small[experts + 1] / gain_one,
        grad_qkv,
        grad_proj,
        small[experts],
        small[:experts].T,
        grad_in,
        grad_eout,
    )


def solution(mesh):
    rows = P(("dp", "expert"), None)
    experts = P("expert", None, None)
    return jax.shard_map(
        per_device,
        mesh=mesh,
        in_specs=(rows, P(), P(), P(), P(), P(), experts, experts, rows, rows, rows),
        out_specs=(
            rows, rows, P(), P(), P(), P(), P(), P("expert", "dp", None), P("expert", "dp", None),
        ),
        check_vma=False,
    )
```

time: 575 us -> 429 us (0.75)
  blocking collectives: 139 us -> 0 us
  starting transfers between devices: 26.4 us -> 45.6 us
  Pallas kernels: 254 us -> 235 us
  other arithmetic: 18.8 us -> 5.78 us
  waiting for transfers between devices: 92.7 us -> 100 us
    psum x1 -> x0, blocking collectives: 70 us -> none  [per_device(): small = lax.psum((grad_gain_one[0], grad_gain_two[0], grad_router), both)]
    all_to_all x2 -> x0, blocking collectives: 68.9 us -> none  [swap(): lax.all_to_all(sent, 'expert', split_axis=0, concat_axis=0, tiled=True)]
    ppermute x0 -> x19, waiting for transfers between devices: none -> 33.6 us  [jump(): return lax.ppermute(value, axis, [(at, at ^ far) for at in range(size)])]
    psum x1 -> x0, waiting for transfers between devices: 26.7 us -> none  [per_device(): big = lax.psum((grad_qkv.astype(BF), grad_proj.astype(BF)), both)]
    pallas_call x6 -> x9, Pallas kernels: 233 us -> 214 us  [the longest x2 102 us: expert_pass(): pl.pallas_call(functools.partial(expert_kernel, experts, min(FCUT, units)...]
    ppermute x0 -> x19, starting transfers between devices: none -> 18.2 us  [jump(): return lax.ppermute(value, axis, [(at, at ^ far) for at in range(size)])]
    convert_element_type x7 -> x5, other arithmetic: 13 us -> 2.6 us  [the longest x1 1.04 us: per_device(): grad_eout = jnp.stack([part[tall:].reshape(tall, -1, width).transpose(1,...]
  transfers between devices with their start and end apart: 11 -> 27, of which waited for: 4 -> 15; matrix products, arithmetic and copies ran while one was open for 3% -> 4% of each run, Pallas kernels for 26% -> 50%
where the time goes in v2:
time: 429 us; the launch traced here: 422 us
  Pallas kernels  235 us (55%)
  waiting for transfers between devices  100 us (23%)
  starting transfers between devices  45.6 us (11%)
  local copies, waits for them, and re-layouts  20.8 us (5%)
  between operations  14.9 us (3%)
  other arithmetic  5.78 us (1%)
    pallas_call x2, Pallas kernels, expert_pass(): pl.pallas_call(functools.partial(expert_kernel, experts, min(FCUT, units)...  102 us
    all_to_all x6, waiting for transfers between devices, swap(): lax.all_to_all(sent, 'expert', split_axis=0, concat_axis=0, tiled=True)  66 us
    pallas_call x1, Pallas kernels, back(): pl.pallas_call(functools.partial(back_kernel, window, groups), grid_spec=...  57.6 us
    ppermute x19, waiting for transfers between devices, jump(): return lax.ppermute(value, axis, [(at, at ^ far) for at in range(size)])  33.6 us
    all_to_all x6, starting transfers between devices, swap(): lax.all_to_all(sent, 'expert', split_axis=0, concat_axis=0, tiled=True)  27.1 us
    pallas_call x2, Pallas kernels, dispatch(): pl.pallas_call(functools.partial(dispatch_kernel, window, capacity, plan,...  21.9 us
    pallas_call x1, Pallas kernels, attend(): pl.pallas_call(attend_kernel, grid=(blocks,), in_specs=[row((BLOCK, width...  20.8 us
    ppermute x19, starting transfers between devices, jump(): return lax.ppermute(value, axis, [(at, at ^ far) for at in range(size)])  18.2 us
  transfers between devices with their start and end apart: 27, of which 15 were waited for; matrix products, arithmetic and copies ran while one was open for 4% of the time, Pallas kernels for 50%

profile of v2, /device:TPU:0, one launch (start us, length us, event | category | flops | bytes accessed | tf_op | source)
XLA Modules:
  0.0 422.3 jit_solution(16309244090878243710)
XLA Ops:
  9.4 4.0 places.1
  13.4 7.7 %dispatch.2 = bf16[4,624,512]{2,1,0:T(8,128)(2,1)} custom-call(s32[8,128]{1,0:T(8,128)} %get-tuple-element.38.starts_ref, s32[6,2,392]{2,1,0:T(2,128)} %get-tuple-element.39.index_ref, bf16[2352,512]{1,0:T(8,128)(2,1)} %dy_ref.1), custom_call_target="tpu_custom_call" | custom-call | flops 6000000000 | bytes 8000000 | tf_op jit(solution)/shard_map/dispatch/pallas_call | solution.py:286
  21.1 5.2 %all-to-all-start = ((bf16[4,624,512]{2,1,0:T(8,128)(2,1)}), bf16[4,624,512]{2,1,0:T(8,128)(2,1)S(1)}, u32[]{:S(2)}, u32[]{:S(2)}) async-start(bf16[4,624,512]{2,1,0:T(8,128)(2,1)} %dispatch.2), calls=%async_computation | async-start | bytes 5111808 | tf_op jit(solution)/shard_map/all_to_all | solution.py:722
  26.3 20.8 %attend.1 = (f32[2352,512]{1,0:T(8,128)}, bf16[2352,512]{1,0:T(8,128)(2,1)}, bf16[2688,1536]{1,0:T(8,128)(2,1)}, bf16[21504,112]{1,0:T(8,128)(2,1)}, bf16[2688,512]{1,0:T(8,128)(2,1)}) custom-call(bf16[2352,512]{1,0:T(8,128)(2,1)} %tok_ref.4, f32[1,512]{1,0:T(1,128)} %bitcast.100, bf16[512,1536]{1,0:T(8,128)(2,1)} %qkv_w_ref.5, bf16[512,512]{1,0:T(8,128)(2,1)} %proj_w_ref.3, ...), custom_call_target="tpu_custom_call" | custom-call | flops 6870269952 | bytes 30000000 | tf_op jit(solution)/shard_map/attend/pallas_call | solution.py:148
  47.1 9.0 %all-to-all-done.dy_ref = bf16[4,624,512]{2,1,0:T(8,128)(2,1)S(1)} async-done(((bf16[4,624,512]{2,1,0:T(8,128)(2,1)}), bf16[4,624,512]{2,1,0:T(8,128)(2,1)S(1)}, u32[]{:S(2)}, u32[]{:S(2)}) %all-to-all-start) | async-done | bytes 2555936 | tf_op jit(solution)/shard_map/all_to_all | solution.py:722
  56.1 14.2 %dispatch.3 = (bf16[4,624,512]{2,1,0:T(8,128)(2,1)}, bf16[4,1248,512]{2,1,0:T(8,128)(2,1)}) custom-call(s32[8,128]{1,0:T(8,128)} %get-tuple-element.38.starts_ref, s32[6,2,392]{2,1,0:T(2,128)} %get-tuple-element.39.index_ref, bf16[2352,512]{1,0:T(8,128)(2,1)} %get-tuple-element.43.refs_0_, bf16[2352,512]{1,0:T(8,128)(2,1)} %dy_ref.1), custom_call_target="tpu_custom_call" | custom-call | flops 6000000000 | bytes 8000000 | tf_op jit(solution)/shard_map/dispatch/pallas_call | solution.py:286
  75.7 5.0 %slice_bitcast_fusion.1 = (bf16[512,2048]{1,0:T(8,128)(2,1)}, bf16[512,2048]{1,0:T(8,128)(2,1)}) fusion(bf16[2,512,2048]{2,1,0:T(8,128)(2,1)} %param.17), kind=kLoop, calls=%fused_computation.3 | loop fusion | bytes 8388608 | tf_op jit(solution)/shard_map/squeeze | solution.py:751
  82.9 20.4 %all-to-all-done.1.x_ref = bf16[4,624,512]{2,1,0:T(8,128)(2,1)S(1)} async-done(((bf16[4,624,512]{2,1,0:T(8,128)(2,1)}), bf16[4,624,512]{2,1,0:T(8,128)(2,1)S(1)}, u32[]{:S(2)}, u32[]{:S(2)}) %all-to-all-start.1) | async-done | bytes 2555936 | tf_op jit(solution)/shard_map/all_to_all | solution.py:722
  104.8 5.1 %all-to-all-start.3 = ((bf16[4,1248,512]{2,1,0:T(8,128)(2,1)}), bf16[4,1248,512]{2,1,0:T(8,128)(2,1)}, u32[]{:S(2)}, u32[]{:S(2)}) async-start(bf16[4,1248,512]{2,1,0:T(8,128)(2,1)} %get-tuple-element.47), calls=%async_computation.3 | async-start | bytes 10223616 | tf_op jit(solution)/shard_map/all_to_all | solution.py:722
  110.0 51.2 %expert_pass.2 = (bf16[4,1248,512]{2,1,0:T(8,128)(2,1)}, bf16[8,128,2048]{2,1,0:T(8,128)(2,1)}, f32[512,128]{1,0:T(8,128)}) custom-call(s32[1]{0:T(128)} %bitcast.5.mine_ref, bf16[512,2048]{1,0:T(8,128)(2,1)} %get-tuple-element.90.up_ref, bf16[2048,512]{1,0:T(8,128)(2,1)} %get-tuple-element.88.down_ref, bf16[512,256]{1,0:T(8,128)(2,1)} %copy.48.router_ref, ...), custom_call_target="tpu_custom_call" | custom-call | flops 52344913920 | bytes 30000000 | tf_op jit(solution)/shard_map/expert_pass/pallas_call | solution.py:461
  161.3 5.2 %all-to-all-done.3.x_ref.dy_ref = bf16[4,1248,512]{2,1,0:T(8,128)(2,1)} async-done(((bf16[4,1248,512]{2,1,0:T(8,128)(2,1)}), bf16[4,1248,512]{2,1,0:T(8,128)(2,1)}, u32[]{:S(2)}, u32[]{:S(2)}) %all-to-all-start.3) | async-done | bytes 5111840 | tf_op jit(solution)/shard_map/all_to_all | solution.py:722
  166.5 5.5 %all-to-all-start.2 = ((bf16[4,1248,512]{2,1,0:T(8,128)(2,1)}), bf16[4,1248,512]{2,1,0:T(8,128)(2,1)}, u32[]{:S(2)}, u32[]{:S(2)}) async-start(bf16[4,1248,512]{2,1,0:T(8,128)(2,1)} %get-tuple-element.45), calls=%async_computation.2 | async-start | bytes 10223616 | tf_op jit(solution)/shard_map/all_to_all | solution.py:722
  172.0 51.2 %expert_pass.3 = (bf16[4,624,512]{2,1,0:T(8,128)(2,1)}, bf16[4,624,512]{2,1,0:T(8,128)(2,1)}, bf16[8,128,2048]{2,1,0:T(8,128)(2,1)}, f32[512,128]{1,0:T(8,128)}) custom-call(s32[1]{0:T(128)} %bitcast.10.mine_ref, bf16[512,2048]{1,0:T(8,128)(2,1)} %get-tuple-element.89.up_ref, bf16[2048,512]{1,0:T(8,128)(2,1)} %get-tuple-element.87.down_ref, ...), custom_call_target="tpu_custom_call" | custom-call | flops 52344913920 | bytes 30000000 | tf_op jit(solution)/shard_map/expert_pass/pallas_call | solution.py:461
  223.3 5.2 %all-to-all-done.2.refs_0_ = bf16[4,1248,512]{2,1,0:T(8,128)(2,1)} async-done(((bf16[4,1248,512]{2,1,0:T(8,128)(2,1)}), bf16[4,1248,512]{2,1,0:T(8,128)(2,1)}, u32[]{:S(2)}, u32[]{:S(2)}) %all-to-all-start.2) | async-done | bytes 5111840 | tf_op jit(solution)/shard_map/all_to_all | solution.py:722
  235.1 26.3 %all-to-all-done.4.refs_1_ = bf16[4,624,512]{2,1,0:T(8,128)(2,1)S(1)} async-done(((bf16[4,624,512]{2,1,0:T(8,128)(2,1)}), bf16[4,624,512]{2,1,0:T(8,128)(2,1)S(1)}, u32[]{:S(2)}, u32[]{:S(2)}) %all-to-all-start.4) | async-done | bytes 2555936 | tf_op jit(solution)/shard_map/all_to_all | solution.py:722
  262.8 3.9 all-to-all-start.5
  266.7 57.6 %back.1 = (f32[2352,512]{1,0:T(8,128)}, bf16[2688,1536]{1,0:T(8,128)(2,1)}, bf16[2,16,64,512]{3,2,1,0:T(8,128)(2,1)}, f32[512,1]{1,0:T(8,128)}, f32[1,512]{1,0:T(1,128)}) custom-call(s32[8,128]{1,0:T(8,128)} %get-tuple-element.38.starts_ref, s32[3]{0:T(128)} %pad_add_fusion.1.here_ref, s32[2352,2]{1,0:T(8,128)} %bitcast.83, ...), custom_call_target="tpu_custom_call" | custom-call | flops 26357102592 | bytes 40000000 | tf_op jit(solution)/shard_map/back/pallas_call | solution.py:573
  333.7 5.3 %collective-permute-done.6 = bf16[4,64,512]{2,1,0:T(8,128)(2,1)S(1)} collective-permute-done((bf16[4,64,512]{2,1,0:T(8,128)(2,1)S(1)}, bf16[4,64,512]{2,1,0:T(8,128)(2,1)S(1)}, u32[]{:S(2)}, u32[]{:S(2)}) %collective-permute-start.6) | collective-permute-done | bytes 262176 | tf_op jit(solution)/shard_map/ppermute | solution.py:677
  339.0 6.4 %collective-permute-done.8 = bf16[4,64,512]{2,1,0:T(8,128)(2,1)S(1)} collective-permute-done((bf16[4,64,512]{2,1,0:T(8,128)(2,1)S(1)}, bf16[4,64,512]{2,1,0:T(8,128)(2,1)S(1)}, u32[]{:S(2)}, u32[]{:S(2)}) %collective-permute-start.8) | collective-permute-done | bytes 262176 | tf_op jit(solution)/shard_map/ppermute | solution.py:677
  362.2 4.0 collective-permute-done.1
  366.6 4.7 %collective-permute-done.2 = f32[10,512]{1,0:T(8,128)S(1)} collective-permute-done((f32[10,512]{1,0:T(8,128)S(1)}, f32[10,512]{1,0:T(8,128)S(1)}, u32[]{:S(2)}, u32[]{:S(2)}) %collective-permute-start.2) | collective-permute-done | bytes 20512 | tf_op jit(solution)/shard_map/ppermute | solution.py:677
  379.5 12.4 %last.1 = f32[2352,512]{1,0:T(8,128)} custom-call(bf16[2688,1536]{1,0:T(8,128)(2,1)} %get-tuple-element.55.dqkv_ref, f32[2352,512]{1,0:T(8,128)} %get-tuple-element.56.ghid_ref, bf16[2352,512]{1,0:T(8,128)(2,1)} %tok_ref.4, f32[1,512]{1,0:T(1,128)} %bitcast.102, bf16[512,1536]{1,0:T(8,128)(2,1)} %qkv_w_ref.5), custom_call_target="tpu_custom_call" | custom-call | flops 4227858432 | bytes 20000000 | tf_op jit(solution)/shard_map/last/pallas_call | solution.py:623
  394.0 11.3 %top.1 = bf16[2352,512]{1,0:T(8,128)(2,1)} custom-call(s32[8,128]{1,0:T(8,128)} %get-tuple-element.38.starts_ref, s32[2352,2]{1,0:T(8,128)} %bitcast.84, f32[2352,512]{1,0:T(8,128)} %get-tuple-element.41.hidden_ref, bf16[4,1248,512]{2,1,0:T(8,128)(2,1)} %all-to-all-done.2.refs_0_, bf16[4,624,512]{2,1,0:T(8,128)(2,1)} %copy-done.2), custom_call_target="tpu_custom_call" | custom-call | flops 6000000000 | bytes 12000000 | tf_op jit(solution)/shard_map/top/pallas_call | solution.py:348
  407.3 4.5 %lay.1 = (f32[512,1536]{1,0:T(8,128)}, f32[512,512]{1,0:T(8,128)}) custom-call(s32[3]{0:T(128)} %pad_add_fusion.1.here_ref, bf16[16,64,512]{2,1,0:T(8,128)(2,1)} %bitcast.80, bf16[16,64,512]{2,1,0:T(8,128)(2,1)} %copy-done.7), custom_call_target="tpu_custom_call" | custom-call | flops 1000000 | bytes 8000000 | tf_op jit(solution)/shard_map/lay/pallas_call | solution.py:657
  (112 shorter events, 61.4 us)
Async XLA Ops:
  21.1 35.0 %all-to-all-start = ((bf16[4,624,512]{2,1,0:T(8,128)(2,1)}), bf16[4,624,512]{2,1,0:T(8,128)(2,1)S(1)}, u32[]{:S(2)}, u32[]{:S(2)}) async-start(bf16[4,624,512]{2,1,0:T(8,128)(2,1)} %dispatch.2), calls=%async_computation | async-start | bytes 5111808 | tf_op jit(solution)/shard_map/all_to_all | solution.py:722
  70.3 33.0 %all-to-all-start.1 = ((bf16[4,624,512]{2,1,0:T(8,128)(2,1)}), bf16[4,624,512]{2,1,0:T(8,128)(2,1)S(1)}, u32[]{:S(2)}, u32[]{:S(2)}) async-start(bf16[4,624,512]{2,1,0:T(8,128)(2,1)} %get-tuple-element.44), calls=%async_computation.1 | async-start | bytes 5111808 | tf_op jit(solution)/shard_map/all_to_all | solution.py:722
  104.8 61.8 %all-to-all-start.3 = ((bf16[4,1248,512]{2,1,0:T(8,128)(2,1)}), bf16[4,1248,512]{2,1,0:T(8,128)(2,1)}, u32[]{:S(2)}, u32[]{:S(2)}) async-start(bf16[4,1248,512]{2,1,0:T(8,128)(2,1)} %get-tuple-element.47), calls=%async_computation.3 | async-start | bytes 10223616 | tf_op jit(solution)/shard_map/all_to_all | solution.py:722
  109.8 295.4 %reduce-scatter.3.cloned.1.call-start = ((), (), s32[]{:S(2)}) async-start(), calls=%async_computation.8 | async-start | bytes 4718592 | tf_op jit(solution)/shard_map/reduce_scatter | solution.py:760
  166.5 61.9 %all-to-all-start.2 = ((bf16[4,1248,512]{2,1,0:T(8,128)(2,1)}), bf16[4,1248,512]{2,1,0:T(8,128)(2,1)}, u32[]{:S(2)}, u32[]{:S(2)}) async-start(bf16[4,1248,512]{2,1,0:T(8,128)(2,1)} %get-tuple-element.45), calls=%async_computation.2 | async-start | bytes 10223616 | tf_op jit(solution)/shard_map/all_to_all | solution.py:722
  228.4 32.9 %all-to-all-start.4 = ((bf16[4,624,512]{2,1,0:T(8,128)(2,1)}), bf16[4,624,512]{2,1,0:T(8,128)(2,1)S(1)}, u32[]{:S(2)}, u32[]{:S(2)}) async-start(bf16[4,624,512]{2,1,0:T(8,128)(2,1)} %get-tuple-element.50), calls=%async_computation.4 | async-start | bytes 5111808 | tf_op jit(solution)/shard_map/all_to_all | solution.py:722
  232.1 179.8 %reduce-scatter.5.cloned.1.call-start = ((), (), s32[]{:S(2)}) async-start(), calls=%async_computation.9 | async-start | bytes 4718592 | tf_op jit(solution)/shard_map/reduce_scatter | solution.py:760
  262.8 61.5 %all-to-all-start.5 = ((bf16[4,624,512]{2,1,0:T(8,128)(2,1)}), bf16[4,624,512]{2,1,0:T(8,128)(2,1)S(1)}, u32[]{:S(2)}, u32[]{:S(2)}) async-start(bf16[4,624,512]{2,1,0:T(8,128)(2,1)} %get-tuple-element.51), calls=%async_computation.5 | async-start | bytes 5111808 | tf_op jit(solution)/shard_map/all_to_all | solution.py:722
  329.8 9.2 %collective-permute-start.6 = (bf16[4,64,512]{2,1,0:T(8,128)(2,1)S(1)}, bf16[4,64,512]{2,1,0:T(8,128)(2,1)S(1)}, u32[]{:S(2)}, u32[]{:S(2)}) collective-permute-start(bf16[4,64,512]{2,1,0:T(8,128)(2,1)S(1)} %get-tuple-element.91), channel_id=1, source_target_pairs={{0,1},{1,0},{2,3},{3,2},{4,5},{5,4},{6,7},{7,6},{8,9},{9,8},{10,11... | collective-permute-start | bytes 786440 | tf_op jit(solution)/shard_map/ppermute | solution.py:677
  331.9 13.5 %collective-permute-start.8 = (bf16[4,64,512]{2,1,0:T(8,128)(2,1)S(1)}, bf16[4,64,512]{2,1,0:T(8,128)(2,1)S(1)}, u32[]{:S(2)}, u32[]{:S(2)}) collective-permute-start(bf16[4,64,512]{2,1,0:T(8,128)(2,1)S(1)} %get-tuple-element.92), channel_id=1, source_target_pairs={{0,3},{1,2},{2,1},{3,0},{4,7},{5,6},{6,5},{7,4},{8,11},{9,10},{10,... | collective-permute-start | bytes 786440 | tf_op jit(solution)/shard_map/ppermute | solution.py:677
  333.4 13.4 %collective-permute-start.7 = (bf16[4,64,512]{2,1,0:T(8,128)(2,1)S(1)}, bf16[4,64,512]{2,1,0:T(8,128)(2,1)S(1)}, u32[]{:S(2)}, u32[]{:S(2)}) collective-permute-start(bf16[4,64,512]{2,1,0:T(8,128)(2,1)S(1)} %get-tuple-element.93), channel_id=1, source_target_pairs={{0,2},{1,3},{2,0},{3,1},{4,6},{5,7},{6,4},{7,5},{8,10},{9,11},{10,... | collective-permute-start | bytes 786440 | tf_op jit(solution)/shard_map/ppermute | solution.py:677
  346.9 5.0 %collective-permute-start.9 = (bf16[64,512]{1,0:T(8,128)(2,1)S(1)}, bf16[64,512]{1,0:T(8,128)(2,1)S(1)}, u32[]{:S(2)}, u32[]{:S(2)}) collective-permute-start(bf16[64,512]{1,0:T(8,128)(2,1)S(1)} %get-tuple-element.100), channel_id=1, source_target_pairs={{0,8},{4,12},{8,0},{12,4},{16,24},{20,28},{24,16},{28,20},{1,9},{5... | collective-permute-start | bytes 196616 | tf_op jit(solution)/shard_map/ppermute | solution.py:677
  348.7 6.1 %collective-permute-start.11 = (bf16[64,512]{1,0:T(8,128)(2,1)S(1)}, bf16[64,512]{1,0:T(8,128)(2,1)S(1)}, u32[]{:S(2)}, u32[]{:S(2)}) collective-permute-start(bf16[64,512]{1,0:T(8,128)(2,1)S(1)} %get-tuple-element.101), channel_id=1, source_target_pairs={{0,24},{4,28},{8,16},{12,20},{16,8},{20,12},{24,0},{28,4},{1,25},{... | collective-permute-start | bytes 196616 | tf_op jit(solution)/shard_map/ppermute | solution.py:677
  351.2 6.4 %collective-permute-start.10 = (bf16[64,512]{1,0:T(8,128)(2,1)S(1)}, bf16[64,512]{1,0:T(8,128)(2,1)S(1)}, u32[]{:S(2)}, u32[]{:S(2)}) collective-permute-start(bf16[64,512]{1,0:T(8,128)(2,1)S(1)} %get-tuple-element.102), channel_id=1, source_target_pairs={{0,16},{4,20},{8,24},{12,28},{16,0},{20,4},{24,8},{28,12},{1,17},{... | collective-permute-start | bytes 196616 | tf_op jit(solution)/shard_map/ppermute | solution.py:677
  351.4 10.8 %collective-permute-start = (f32[10,512]{1,0:T(8,128)S(1)}, f32[10,512]{1,0:T(8,128)S(1)}, u32[]{:S(2)}, u32[]{:S(2)}) collective-permute-start(f32[10,512]{1,0:T(8,128)S(1)} %pad_maximum_fusion.4), channel_id=1, source_target_pairs={{0,4},{4,0},{8,12},{12,8},{16,20},{20,16},{24,28},{28,24},{1,5},{5... | collective-permute-start | bytes 61448 | tf_op jit(solution)/shard_map/ppermute | solution.py:677
  357.7 18.1 %collective-permute-start.14 = (bf16[64,512]{1,0:T(8,128)(2,1)S(1)}, bf16[64,512]{1,0:T(8,128)(2,1)S(1)}, u32[]{:S(2)}, u32[]{:S(2)}) collective-permute-start(bf16[64,512]{1,0:T(8,128)(2,1)S(1)} %fusion.3), channel_id=1, source_target_pairs={{0,24},{4,28},{8,16},{12,20},{16,8},{20,12},{24,0},{28,4},{1,25},{... | collective-permute-start | bytes 196616 | tf_op jit(solution)/shard_map/ppermute | solution.py:677
  359.1 16.7 %collective-permute-start.13 = (bf16[64,512]{1,0:T(8,128)(2,1)S(1)}, bf16[64,512]{1,0:T(8,128)(2,1)S(1)}, u32[]{:S(2)}, u32[]{:S(2)}) collective-permute-start(bf16[64,512]{1,0:T(8,128)(2,1)S(1)} %fusion.3), channel_id=1, source_target_pairs={{0,16},{4,20},{8,24},{12,28},{16,0},{20,4},{24,8},{28,12},{1,17},{... | collective-permute-start | bytes 196616 | tf_op jit(solution)/shard_map/ppermute | solution.py:677
  359.1 16.7 %collective-permute-start.12 = (bf16[64,512]{1,0:T(8,128)(2,1)S(1)}, bf16[64,512]{1,0:T(8,128)(2,1)S(1)}, u32[]{:S(2)}, u32[]{:S(2)}) collective-permute-start(bf16[64,512]{1,0:T(8,128)(2,1)S(1)} %fusion.3), channel_id=1, source_target_pairs={{0,8},{4,12},{8,0},{12,4},{16,24},{20,28},{24,16},{28,20},{1,9},{5... | collective-permute-start | bytes 196616 | tf_op jit(solution)/shard_map/ppermute | solution.py:677
  366.3 5.1 %collective-permute-start.2 = (f32[10,512]{1,0:T(8,128)S(1)}, f32[10,512]{1,0:T(8,128)S(1)}, u32[]{:S(2)}, u32[]{:S(2)}) collective-permute-start(f32[10,512]{1,0:T(8,128)S(1)} %add.69), channel_id=1, source_target_pairs={{0,16},{4,20},{8,24},{12,28},{16,0},{20,4},{24,8},{28,12},{1,17},{... | collective-permute-start | bytes 61448 | tf_op jit(solution)/shard_map/ppermute | solution.py:677
  375.7 16.1 %collective-permute-start.4 = (f32[10,512]{1,0:T(8,128)S(1)}, f32[10,512]{1,0:T(8,128)S(1)}, u32[]{:S(2)}, u32[]{:S(2)}) collective-permute-start(f32[10,512]{1,0:T(8,128)S(1)} %add.71), channel_id=1, source_target_pairs={{0,2},{1,3},{2,0},{3,1},{4,6},{5,7},{6,4},{7,5},{8,10},{9,11},{10,... | collective-permute-start | bytes 61448 | tf_op jit(solution)/shard_map/ppermute | solution.py:677
  375.9 16.6 %collective-permute-start.16 = (bf16[4,64,512]{2,1,0:T(8,128)(2,1)S(1)}, bf16[4,64,512]{2,1,0:T(8,128)(2,1)S(1)}, u32[]{:S(2)}, u32[]{:S(2)}) collective-permute-start(bf16[4,64,512]{2,1,0:T(8,128)(2,1)S(1)} %get-tuple-element.99), channel_id=1, source_target_pairs={{0,2},{1,3},{2,0},{3,1},{4,6},{5,7},{6,4},{7,5},{8,10},{9,11},{10,... | collective-permute-start | bytes 786440 | tf_op jit(solution)/shard_map/ppermute | solution.py:677
  377.9 14.6 %collective-permute-start.15 = (bf16[4,64,512]{2,1,0:T(8,128)(2,1)S(1)}, bf16[4,64,512]{2,1,0:T(8,128)(2,1)S(1)}, u32[]{:S(2)}, u32[]{:S(2)}) collective-permute-start(bf16[4,64,512]{2,1,0:T(8,128)(2,1)S(1)} %get-tuple-element.99), channel_id=1, source_target_pairs={{0,1},{1,0},{2,3},{3,2},{4,5},{5,4},{6,7},{7,6},{8,9},{9,8},{10,11... | collective-permute-start | bytes 786440 | tf_op jit(solution)/shard_map/ppermute | solution.py:677
  379.3 13.2 %collective-permute-start.17 = (bf16[4,64,512]{2,1,0:T(8,128)(2,1)S(1)}, bf16[4,64,512]{2,1,0:T(8,128)(2,1)S(1)}, u32[]{:S(2)}, u32[]{:S(2)}) collective-permute-start(bf16[4,64,512]{2,1,0:T(8,128)(2,1)S(1)} %get-tuple-element.99), channel_id=1, source_target_pairs={{0,3},{1,2},{2,1},{3,0},{4,7},{5,6},{6,5},{7,4},{8,11},{9,10},{10,... | collective-permute-start | bytes 786440 | tf_op jit(solution)/shard_map/ppermute | solution.py:677
  392.6 13.7 %collective-permute-start.18 = (bf16[16,64,512]{2,1,0:T(8,128)(2,1)S(1)}, bf16[16,64,512]{2,1,0:T(8,128)(2,1)S(1)}, u32[]{:S(2)}, u32[]{:S(2)}) collective-permute-start(bf16[16,64,512]{2,1,0:T(8,128)(2,1)S(1)} %bitcast.79), channel_id=1, source_target_pairs={{0,4},{4,0},{8,12},{12,8},{16,20},{20,16},{24,28},{28,24},{1,5},{5... | collective-permute-start | bytes 3145736 | tf_op jit(solution)/shard_map/ppermute | solution.py:677
  (18 other events, 115.0 us)
Sparse Core Ops, SparseCore 0:
  161.4 51.8 reduce-scatter.2
  235.2 51.8 reduce-scatter.4

commit v3 on v2

--- a/solution.py
+++ b/solution.py
@@ -18,7 +18,6 @@
 BF = jnp.bfloat16
 F32 = jnp.float32
 VMEM_BYTES = 56 * 1024 * 1024
-TILE_ROWS = 640
 FCUT = 1024
 
 
@@ -303,7 +302,7 @@
     )(starts, index_rows, *srcs)
 
 
-def combine_block(window, step, starts_ref, index_ref, bufs, wins, acc):
+def combine_block(window, step, me, starts_ref, index_ref, bufs, own_bufs, wins, acc):
     owners, capacity = bufs[0].shape[:2]
     experts = owners * len(bufs)
     lane = lax.broadcasted_iota(jnp.int32, (1, experts * window), 1)
@@ -312,13 +311,15 @@
     def one_turn(turn, carry):
         seen = jnp.full((1, experts * window), -2, jnp.int32)
         for expert in range(experts):
+            part, owner = expert // owners, expert % owners
             begin, high, at = window_at(starts_ref, expert, step, turn, window, capacity)
             slot = lane + (at - expert * window)
             fresh = (slot >= begin) & (slot < high)
             mine = (lane >= expert * window) & (lane < (expert + 1) * window)
             seen = jnp.where(mine & fresh, slot + expert * capacity, seen)
-            wins[window * expert : window * (expert + 1), :] = (
-                bufs[expert // owners][expert % owners, pl.ds(at, window), :]
+            wins[window * expert : window * (expert + 1), :] = jnp.where(
+                me == owner, own_bufs[part][0, pl.ds(at, window), :],
+                bufs[part][owner, pl.ds(at, window), :],
             )
         hit = (index_ref[:, 0:1] == seen) | (index_ref[:, 1:2] == seen)
         acc[...] += dot(hit.astype(F32).astype(BF), wins[...])
@@ -327,30 +328,33 @@
     lax.fori_loop(0, turns(starts_ref, step, range(experts), window), one_turn, 0)
 
 
-def back_specs(parts, capacity):
+def back_specs(parts, own, capacity):
+    width = own[0].shape[2]
     return [
-        pl.BlockSpec((array.shape[0], capacity, array.shape[2]), lambda *_, at=at: (0, at, 0))
+        pl.BlockSpec((array.shape[0], capacity, width), lambda *_, at=at: (0, at, 0))
         for array, at in parts
-    ]
-
-
-def top_kernel(window, starts_ref, index_ref, hidden_ref, *refs):
-    *bufs, out_ref, wins, acc = refs
-    combine_block(window, pl.program_id(0), starts_ref, index_ref, bufs, wins, acc)
+    ] + [whole((1, capacity, width))] * len(own)
+
+
+def top_kernel(window, local, starts_ref, here_ref, index_ref, hidden_ref, *refs):
+    bufs, own_bufs, (out_ref, wins, acc) = refs[:local], refs[local : 2 * local], refs[2 * local :]
+    combine_block(
+        window, pl.program_id(0), here_ref[1], starts_ref, index_ref, bufs, own_bufs, wins, acc
+    )
     out_ref[...] = (hidden_ref[...] + acc[...]).astype(BF)
 
 
-def top(starts, index, hidden, parts, capacity):
+def top(starts, here, index, hidden, parts, own, capacity):
     count, width = hidden.shape
     experts = starts.shape[0]
     window = window_rows(experts, capacity)
     row = lambda shape: pl.BlockSpec(shape, lambda step, *_: (step, 0))
     return pl.pallas_call(
-        functools.partial(top_kernel, window),
+        functools.partial(top_kernel, window, len(parts)),
         grid_spec=pltpu.PrefetchScalarGridSpec(
-            num_scalar_prefetch=1,
+            num_scalar_prefetch=2,
             grid=(count // BLOCK,),
-            in_specs=[row((BLOCK, 2)), row((BLOCK, width))] + back_specs(parts, capacity),
+            in_specs=[row((BLOCK, 2)), row((BLOCK, width))] + back_specs(parts, own, capacity),
             out_specs=row((BLOCK, width)),
             scratch_shapes=[
                 pltpu.VMEM((experts * window, width), BF), pltpu.VMEM((BLOCK, width), F32),
@@ -360,7 +364,7 @@
         compiler_params=params(),
         cost_estimate=cost(6e9, 12e6),
         name="top",
-    )(starts, index, hidden, *[array for array, _ in parts])
+    )(starts, here, index, hidden, *[array for array, _ in parts], *own)
 
 
 def gelu_parts(values):
@@ -376,20 +380,29 @@
 
 
 def expert_kernel(
-    experts, fcut, mine_ref, up_ref, down_ref, router_ref, back_ref, x_ref, dy_ref, *refs
+    experts, fcut, begun, ends, mine_ref, up_ref, down_ref, router_ref, back_ref, x_ref, dy_ref, *refs
 ):
-    dx_ref, out_ref = refs[0], refs[-8]
-    grad_ref, grouter_ref, acc_up, acc_down, acc_router, acc_out, acc_dx = refs[-7:]
+    given, refs = refs[: 3 * begun], refs[3 * begun :]
+    acc_up, acc_down, acc_router, acc_out, acc_dx = refs[-5:]
+    grouter_ref = refs[-6]
+    grad_refs = refs[-7:-6] if ends else refs[-8:-6]
+    dx_ref, out_ref = refs[-9:-7] if ends else refs[-10:-8]
     step = pl.program_id(0)
     hidden_units = up_ref.shape[1]
-    times, capacity, width = x_ref.shape
-    count = times * capacity
+    _, capacity, width = x_ref.shape
+    count = capacity
 
     @pl.when(step == 0)
     def _():
-        acc_up[...] = jnp.zeros(acc_up.shape, F32)
-        acc_down[...] = jnp.zeros(acc_down.shape, F32)
-        acc_router[...] = jnp.zeros(acc_router.shape, F32)
+        if begun:
+            acc_up[...] = given[0][...].astype(F32)
+            acc_down[...] = given[1][...].astype(F32)
+            acc_router[:, :LANES] = given[2][...]
+            acc_router[:, LANES:] = jnp.zeros((width, LANES), F32)
+        else:
+            acc_up[...] = jnp.zeros(acc_up.shape, F32)
+            acc_down[...] = jnp.zeros(acc_down.shape, F32)
+            acc_router[...] = jnp.zeros(acc_router.shape, F32)
 
     rows = x_ref[...].reshape(count, width)
     logits = dot(rows, router_ref[...])
@@ -426,14 +439,19 @@
     head = grad_logits.astype(BF)
     rest = (grad_logits - head.astype(F32)).astype(BF)
     acc_router[...] += dot(rows_t, jnp.concatenate([head, rest], axis=1))
-    shape = (times, capacity, width)
-    out_ref[:, out_ref.shape[1] - capacity :, :] = (chosen * acc_out[...]).astype(BF).reshape(shape)
-    dx_ref[:, :capacity, :] = (
+    out_ref[0] = (chosen * acc_out[...]).astype(BF)
+    dx_ref[0] = (
         acc_dx[...] + dot(jnp.concatenate([head, head], axis=1), back_ref[...])
-    ).astype(BF).reshape(shape)
+    ).astype(BF)
 
     @pl.when(step == pl.num_programs(0) - 1)
     def _():
+        grouter_ref[...] = acc_router[:, :LANES] + acc_router[:, LANES:]
+        if not ends:
+            grad_refs[0][...] = acc_up[...].astype(BF)
+            grad_refs[1][...] = acc_down[...].astype(BF)
+            return
+        grad_ref = grad_refs[0]
         shards, tall, _ = grad_ref.shape
         up_rows, down_rows = width // shards, hidden_units // shards
         piece = tall - up_rows
@@ -444,70 +462,95 @@
                 grad_ref[shard, up_rows:, width * part : width * (part + 1)] = (
                     turned[piece * part : piece * (part + 1), :]
                 )
-        grouter_ref[...] = acc_router[:, :LANES] + acc_router[:, LANES:]
-
-
-def expert_pass(mine, rows, grads, w_up, w_down, router, router_back, experts, capacity, shards, joined):
+
+
+def expert_pass(part, mine, rows, grads, w_up, w_down, router, router_back, experts, capacity, shards, own, given, outs):
     (rows, rows_at), (grads, grads_at) = rows, grads
     sources, _, width = rows.shape
-    units = w_up.shape[1]
-    times = max(
-        n for n in range(1, sources + 1) if sources % n == 0 and n * capacity <= max(TILE_ROWS, capacity)
-    )
-    tile = times * capacity
-    block = lambda tall, at: pl.BlockSpec((times, tall, width), lambda step, *_: (step, at, 0))
-    sent = [2 * capacity] if joined else [capacity, capacity]
+    local, _, units = w_up.shape
+    ends = given is not None
+    source = lambda step, mine_ref: (mine_ref[1] + (0 if own else 1) + step) % sources
+    block = lambda at: pl.BlockSpec(
+        (1, capacity, width), lambda step, mine_ref: (source(step, mine_ref), at, 0)
+    )
+    only = whole((1, capacity, width))
+    weight = lambda shape: pl.BlockSpec((None,) + shape[1:], lambda *_: (part, 0, 0))
     grad_shape = (shards, width // shards * 2, units)
+    given = list(given or ())
+    taken = [] if outs is None else [outs]
+    if own:
+        sent = [jax.ShapeDtypeStruct((1, capacity, width), BF)] * 2
+        sent_specs = [only, only]
+    else:
+        sent = [
+            jax.ShapeDtypeStruct((sources, capacity, width), BF),
+            jax.ShapeDtypeStruct((sources, local * capacity, width), BF),
+        ]
+        sent_specs = [block(0), block(part)]
+    if ends:
+        sums = [jax.ShapeDtypeStruct(grad_shape, BF)]
+    else:
+        sums = [jax.ShapeDtypeStruct((width, units), BF)] * 2
+    sums.append(jax.ShapeDtypeStruct((width, LANES), F32))
+    steps = 1 if own else sources - 1
+
+    def body(*refs):
+        refs = list(refs)
+        if taken:
+            del refs[7 + len(given)]
+        expert_kernel(experts, min(FCUT, units), bool(given), ends, *refs)
+
     return pl.pallas_call(
-        functools.partial(expert_kernel, experts, min(FCUT, units)),
+        body,
         grid_spec=pltpu.PrefetchScalarGridSpec(
             num_scalar_prefetch=1,
-            grid=(sources // times,),
+            grid=(steps,),
             in_specs=[
-                whole(w_up.shape), whole(w_down.shape), whole(router.shape), whole(router_back.shape),
-                block(capacity, rows_at), block(capacity, grads_at),
-            ],
-            out_specs=[block(tall, 0) for tall in sent] + [whole(grad_shape), whole((width, LANES))],
+                weight(w_up.shape), weight(w_down.shape), whole(router.shape),
+                whole(router_back.shape), block(rows_at), block(grads_at),
+            ] + [whole(array.shape) for array in given] + [pl.BlockSpec(memory_space=pl.ANY)] * len(taken),
+            out_specs=sent_specs + [whole(array.shape) for array in sums],
             scratch_shapes=[
                 pltpu.VMEM((width, units), F32),
                 pltpu.VMEM((width, units), F32),
                 pltpu.VMEM((width, 2 * LANES), F32),
-                pltpu.VMEM((tile, width), F32),
-                pltpu.VMEM((tile, width), F32),
+                pltpu.VMEM((capacity, width), F32),
+                pltpu.VMEM((capacity, width), F32),
             ],
         ),
-        out_shape=[jax.ShapeDtypeStruct((sources, tall, width), BF) for tall in sent] + [
-            jax.ShapeDtypeStruct(grad_shape, BF),
-            jax.ShapeDtypeStruct((width, LANES), F32),
-        ],
+        out_shape=sent + sums,
+        input_output_aliases={7 + len(given): 1} if taken else {},
         compiler_params=params(),
         cost_estimate=cost(
-            20 * sources * capacity * width * units, 30e6, 2 * sources * capacity * units
+            20 * steps * capacity * width * units, 30e6, 2 * steps * capacity * units
         ),
-        name="expert_pass",
-    )(mine, w_up, w_down, router, router_back, rows, grads)
+        name="expert_own" if own else "expert_others",
+    )(mine, w_up, w_down, router, router_back, rows, grads, *given, *taken)
 
 
 def back_kernel(
-    window, groups, starts_ref, here_ref, index_ref, hidden_ref, tok_ref, dy_ref, qkv_ref,
+    window, groups, local, starts_ref, here_ref, index_ref, hidden_ref, tok_ref, dy_ref, qkv_ref,
     probs_ref, mixed_ref, gain_one_ref, qkv_w_ref, proj_w_ref, gain_two_ref, *refs,
 ):
-    *bufs, ghid_ref, dqkv_ref, sum_ref, ggain_one_ref, ggain_two_ref = refs[:-6]
-    wins, acc, compact, padded, acc_qkv, acc_proj = refs[-6:]
+    bufs, own_bufs = refs[:local], refs[local : 2 * local]
+    router_refs = refs[2 * local : 3 * local]
+    ghid_ref, dqkv_ref, own_ref, sent_ref = refs[3 * local : -7]
+    wins, acc, compact, padded, acc_qkv, acc_proj, acc_gain = refs[-7:]
+    experts = starts_ref.shape[0]
     step = pl.program_id(0)
     width = tok_ref.shape[1]
     factor_qk = (width // HEADS) ** (-0.5)
 
     @pl.when(step == 0)
     def _():
-        for ref in (acc_qkv, acc_proj, ggain_two_ref):
+        for ref in (acc_qkv, acc_proj, acc_gain):
             ref[...] = jnp.zeros(ref.shape, F32)
 
-    combine_block(window, step, starts_ref, index_ref, bufs, wins, acc)
+    combine_block(window, step, here_ref[1], starts_ref, index_ref, bufs, own_bufs, wins, acc)
     clear_gaps(padded)
     hat_two, scale_two = norm_parts(hidden_ref[...])
     grad_normed = acc[...]
-    ggain_two_ref[...] += jnp.sum(grad_normed * hat_two, axis=0, keepdims=True)
+    acc_gain[...] += jnp.sum(grad_normed * hat_two, axis=0, keepdims=True)
     grad_hidden = dy_ref[...].astype(F32) + norm_back(
         grad_normed, hat_two, scale_two, gain_two_ref[...]
     )
@@ -544,34 +587,49 @@
     @pl.when(step == pl.num_programs(0) - 1)
     def _():
         cores, sides, layers = groups
-        tall = sum_ref.shape[2]
-        for core in range(cores):
-            for side in range(sides):
-                for layer in range(layers):
-                    low = ((core * sides + side) * layers + layer) * tall
-                    part, at = low // width, low % width
-                    if part < 3:
-                        piece = acc_qkv[at : at + tall, width * part : width * (part + 1)]
-                    else:
-                        piece = acc_proj[at : at + tall, :]
-                    spot = (side ^ here_ref[1]) * layers + (layer ^ here_ref[2])
-                    sum_ref[core ^ here_ref[0], spot] = piece.astype(BF)
-        ggain_one_ref[...] = jnp.sum(
-            acc_qkv[...] * qkv_w_ref[...].astype(F32), axis=-1, keepdims=True
-        )
-
-
-def back(starts, here, groups, index, hidden, tokens, dy, qkv, probs, mixed, gain_one, w_qkv, w_proj, gain_two, parts, capacity):
+        half = acc_qkv.shape[0] * 4 // cores
+        tall = half // (sides * layers)
+
+        def piece(row):
+            part, at = row // width, row % width
+            if part < 3:
+                return acc_qkv[at : at + tall, width * part : width * (part + 1)]
+            return acc_proj[at : at + tall, :]
+
+        for side in range(sides):
+            for layer in range(layers):
+                low = (side * layers + layer) * tall
+                spot = (side ^ here_ref[1]) * layers + (layer ^ here_ref[2])
+                to = pl.ds(pl.multiple_of(spot * tall, tall), tall)
+                even, odd = piece(low), piece(half + low)
+                own_ref[to, :] = jnp.where(here_ref[0] == 0, even, odd).astype(BF)
+                sent_ref[to, :] = jnp.where(here_ref[0] == 0, odd, even).astype(BF)
+        gain_one_sum = jnp.sum(acc_qkv[...] * qkv_w_ref[...].astype(F32), axis=-1, keepdims=True)
+        lane = lax.broadcasted_iota(jnp.int32, (width, LANES), 1)
+        router = sum(ref[...] for ref in router_refs)
+        small = jnp.where(lane == experts, gain_one_sum, router).T[: own_ref.shape[0] - half, :]
+        row = lax.broadcasted_iota(jnp.int32, small.shape, 0)
+        small = jnp.where(row == experts + 1, acc_gain[...], small).astype(BF)
+        own_ref[half:, :] = small
+        sent_ref[half:, :] = small
+
+
+def small_rows(experts):
+    return 16 * -(-(experts + 2) // 16)
+
+
+def back(starts, here, groups, index, hidden, tokens, dy, qkv, probs, mixed, gain_one, w_qkv, w_proj, gain_two, parts, own, routers, capacity):
     count, width = tokens.shape
     blocks = count // BLOCK
     experts = starts.shape[0]
     window = window_rows(experts, capacity)
     row = lambda shape: pl.BlockSpec(shape, lambda step, *_: (step, 0))
     cores, sides, layers = groups
-    sum_shape = (cores, sides * layers, 4 * width // (cores * sides * layers), width)
+    assert cores == 2
+    sum_shape = (2 * width + small_rows(experts), width)
     flops = 2 * blocks * BLOCK_PAD * width * (8 * width + 10 * PAIR_PAD)
     return pl.pallas_call(
-        functools.partial(back_kernel, window, groups),
+        functools.partial(back_kernel, window, groups, len(parts)),
         grid_spec=pltpu.PrefetchScalarGridSpec(
             num_scalar_prefetch=2,
             grid=(blocks,),
@@ -580,10 +638,9 @@
                 row((BLOCK_PAD, 3 * width)), row((probs.shape[0] // blocks, PAIR_PAD)),
                 row((BLOCK_PAD, width)),
                 whole((1, width)), whole(w_qkv.shape), whole(w_proj.shape), whole((1, width)),
-            ] + back_specs(parts, capacity),
+            ] + back_specs(parts, own, capacity) + [whole((width, LANES))] * len(routers),
             out_specs=[
-                row((BLOCK, width)), row((BLOCK_PAD, 3 * width)), whole(sum_shape),
-                whole((width, 1)), whole((1, width)),
+                row((BLOCK, width)), row((BLOCK_PAD, 3 * width)), whole(sum_shape), whole(sum_shape),
             ],
             scratch_shapes=[
                 pltpu.VMEM((experts * window, width), BF),
@@ -592,48 +649,51 @@
                 pltpu.VMEM((BLOCK_PAD, width), F32),
                 pltpu.VMEM(w_qkv.shape, F32),
                 pltpu.VMEM(w_proj.shape, F32),
+                pltpu.VMEM((1, width), F32),
             ],
         ),
         out_shape=[
             jax.ShapeDtypeStruct((count, width), F32),
             jax.ShapeDtypeStruct(qkv.shape, BF),
             jax.ShapeDtypeStruct(sum_shape, BF),
-            jax.ShapeDtypeStruct((width, 1), F32),
-            jax.ShapeDtypeStruct((1, width), F32),
+            jax.ShapeDtypeStruct(sum_shape, BF),
         ],
         compiler_params=params(),
         cost_estimate=cost(flops + 12e9, 40e6),
         name="back",
     )(
         starts, here, index, hidden, tokens, dy, qkv, probs, mixed, gain_one[None, :], w_qkv,
-        w_proj, gain_two[None, :], *[array for array, _ in parts],
-    )
-
-
-def last_kernel(dqkv_ref, ghid_ref, tok_ref, gain_one_ref, qkv_w_ref, out_ref, compact, padded):
+        w_proj, gain_two[None, :], *[array for array, _ in parts], *own, *routers,
+    )
+
+
+def last_kernel(dqkv_ref, ghid_ref, tok_ref, gain_one_ref, qkv_w_ref, *refs):
+    out_ref, compact, padded = refs[-3:]
     padded[...] = dot_rt(dqkv_ref[...], qkv_w_ref[...])
     gather_rows(padded, compact)
     hat_one, scale_one = norm_parts(tok_ref[...].astype(F32))
     out_ref[...] = ghid_ref[...] + norm_back(compact[...], hat_one, scale_one, gain_one_ref[...])
 
 
-def last(dqkv, ghid, tokens, gain_one, w_qkv):
+def last(low, high, so_far, dqkv, ghid, tokens, gain_one, w_qkv):
     count, width = tokens.shape
-    row = lambda shape: pl.BlockSpec(shape, lambda step: (step, 0))
+    row = lambda shape: pl.BlockSpec(shape, lambda step: (step + low, 0))
+    taken = [] if so_far is None else [so_far]
     return pl.pallas_call(
         last_kernel,
-        grid=(count // BLOCK,),
+        grid=(high - low,),
         in_specs=[
             row((BLOCK_PAD, 3 * width)), row((BLOCK, width)), row((BLOCK, width)),
             whole((1, width)), whole(w_qkv.shape),
-        ],
+        ] + [pl.BlockSpec(memory_space=pl.ANY)] * len(taken),
         out_specs=row((BLOCK, width)),
         out_shape=jax.ShapeDtypeStruct((count, width), F32),
         scratch_shapes=[pltpu.VMEM((BLOCK, width), F32), pltpu.VMEM((BLOCK_PAD, width), F32)],
+        input_output_aliases={5: 0} if taken else {},
         compiler_params=params(),
-        cost_estimate=cost(6 * dqkv.shape[0] * width * width, 20e6),
+        cost_estimate=cost(6 * BLOCK_PAD * (high - low) * width * width, 20e6),
         name="last",
-    )(dqkv, ghid, tokens, gain_one[None, :], w_qkv)
+    )(dqkv, ghid, tokens, gain_one[None, :], w_qkv, *taken)
 
 
 def lay_kernel(groups, here_ref, own_ref, other_ref, qkv_ref, proj_ref):
@@ -677,30 +737,66 @@
     return lax.ppermute(value, axis, [(at, at ^ far) for at in range(size)])
 
 
-def add_up(parts):
-    return sum(part.astype(F32) for part in parts).astype(BF)
-
-
-def sum_over_all(sums, groups):
+def merge_kernel(cuts, extra, count, *refs):
+    parts, outs = refs[:count], refs[count:]
+    tall = (parts[0].shape[0] - extra) // cuts
+
+    def total(rows):
+        value = parts[0][rows, :].astype(F32)
+        for part in parts[1:]:
+            value = value + part[rows, :].astype(F32)
+        return value
+
+    small = total(slice(cuts * tall, None))
+    for cut, out in enumerate(outs):
+        if cut == cuts:
+            out[...] = small
+            continue
+        out[:tall, :] = total(slice(cut * tall, (cut + 1) * tall)).astype(BF)
+        if out.shape[0] > tall:
+            out[tall:, :] = small.astype(BF)
+
+
+def merge(parts, cuts, extra, ends):
+    rows, width = parts[0].shape
+    tall = (rows - extra) // cuts
+    if ends:
+        outs = [jax.ShapeDtypeStruct((tall, width), BF), jax.ShapeDtypeStruct((extra, width), F32)]
+    else:
+        outs = [jax.ShapeDtypeStruct((tall + extra, width), BF)] * cuts
+    return pl.pallas_call(
+        functools.partial(merge_kernel, cuts, extra, len(parts)),
+        grid=(1,),
+        in_specs=[whole((rows, width))] * len(parts),
+        out_specs=[whole(out.shape) for out in outs],
+        out_shape=outs,
+        compiler_params=params(),
+        cost_estimate=cost(1e6, 4e6),
+        name="merge",
+    )(*parts)
+
+
+def after(value, *others):
+    return lax.optimization_barrier((value, *others))[0]
+
+
+def sum_over_all(own, sent, groups, extra, beside):
     cores, sides, layers = groups
-    half = add_up([sums[0], jump(sums[1], "dp", 1)])
-    tall, width = half.shape[1:]
-    half = half.reshape(sides, layers, tall, width)
-    flat = add_up([half[0]] + [jump(half[side], "expert", side) for side in range(1, sides)])
-    spot = add_up([flat[0]] + [jump(flat[layer], "dp", cores * layer) for layer in range(1, layers)])
-    flat = jnp.stack([spot] + [jump(spot, "dp", cores * layer) for layer in range(1, layers)])
-    half = jnp.stack([flat] + [jump(flat, "expert", side) for side in range(1, sides)])
-    half = half.reshape(sides * layers, tall, width)
-    return half, jump(half, "dp", 1)
-
-
-def sum_small(value):
-    for axis in ("dp", "expert"):
-        far = 1
-        while far < lax.axis_size(axis):
-            value = value + jump(value, axis, far)
-            far = far * 2
-    return value
+    done = []
+
+    def spread(own, sent, axis, scale):
+        came = [jump(part, axis, scale * far) for far, part in enumerate(sent, 1)]
+        work = beside[len(done)](own)
+        done.append(work)
+        return [own] + list(after(tuple(came), work))
+
+    half = merge([own, jump(sent, "dp", 1)], sides, extra, False)
+    flat = merge(spread(half[0], half[1:], "expert", 1), layers, extra, False)
+    spot, small = merge(spread(flat[0], flat[1:], "dp", cores), 1, extra, True)
+    flat = jnp.stack(spread(spot, [spot] * (layers - 1), "dp", cores))
+    half = jnp.stack(spread(flat, [flat] * (sides - 1), "expert", 1))
+    half = half.reshape(sides * layers, *spot.shape)
+    return half, jump(half, "dp", 1), small, done
 
 
 def per_device(
@@ -721,55 +817,76 @@
     def swap(sent):
         return lax.all_to_all(sent, "expert", split_axis=0, concat_axis=0, tiled=True)
 
-    def after(value, *others):
-        return lax.optimization_barrier((value, *others))[0]
-
     index_rows, starts = places(ids, picks, keep, capacity)
-    (sent,) = dispatch([grad_out], starts, index_rows, owners, capacity, ((0, (0,)),))
-    grads_first = swap(sent)
-    hidden, rows, qkv, probs, mixed = attend(after(tokens, sent), gain_one, w_qkv, w_proj, gain_two)
-    plan = ((0, (0,)),) + tuple((part, (0, 1)) for part in range(1, local))
-    sent, *others = dispatch(
-        [after(rows, grads_first), grad_out], starts, index_rows, owners, capacity, plan
-    )
-    got = swap(sent)
-    came = [((got, 0), (grads_first, 0))]
+    send = lambda srcs, *plan: dispatch(srcs, starts, index_rows, owners, capacity, plan)
+    (dy_first,) = send([grad_out], (0, (0,)))
+    got = swap(dy_first)
+    hidden, rows, qkv, probs, mixed = attend(
+        after(tokens, dy_first), gain_one, w_qkv, w_proj, gain_two
+    )
+    (x_first,) = send([rows], (0, (0,)))
+    arrived = [[(swap(after(x_first, got)), 0), (got, 0)]]
+    kept = [[(x_first, 0), (dy_first, 0)]]
+    others = send([after(rows, x_first), grad_out], *[(part, (0, 1)) for part in range(1, local)])
     for sent in others:
-        got = swap(after(sent, got))
-        came.append(((got, 0), (got, 1)))
+        got = swap(after(sent, arrived[-1][0][0]))
+        arrived.append([(got, 0), (got, 1)])
+        kept.append([(sent, 0), (sent, 1)])
     index = index_rows.transpose(0, 2, 1).reshape(count, 2)
     head = w_router.astype(BF)
     rest = (w_router - head.astype(F32)).astype(BF)
     gap = ((0, 0), (0, LANES - experts))
     router = jnp.concatenate([jnp.pad(head, gap), jnp.pad(rest, gap)], axis=1)
     router_back = jnp.concatenate([jnp.pad(head, gap).T, jnp.pad(rest, gap).T], axis=0)
-    outs, downs, sums, grad_router = [], [], [], 0
+    downs, own_dx, own_out, sums, outs, routers = [], [], [], [], None, []
     for part in range(local):
-        mine = (me * local + part).astype(jnp.int32)[None]
-        joined = part < local - 1
-        *sent, grad, router_part = expert_pass(
-            mine, *came[part], w_in[part], w_eout[part], router, router_back, experts, capacity,
-            shards, joined,
+        mine = jnp.stack([me * local + part, me]).astype(jnp.int32)
+        final = part == local - 1
+        one = lambda own, given, outs: expert_pass(
+            part, mine, *(kept if own else arrived)[part], w_in, w_eout, router, router_back,
+            experts, capacity, shards, own, given, outs,
         )
-        if part:
-            sent = [after(sent[0], got), *sent[1:]]
-        got = swap(sent[0])
+        if final:
+            dx, outs, *given = one(False, None, outs)
+            own_parts = list(one(True, given, None))
+        else:
+            own_parts = list(one(True, None, None))
+            dx, outs, *own_parts[2:] = one(False, own_parts[2:], outs)
+        got = swap(after(dx, got))
         downs.append((got, 0))
-        outs.append((got, 1))
+        own_dx.append(own_parts[0])
+        own_out.append(own_parts[1])
+        grad, router_part = own_parts[2:]
         grad = grad.reshape(shards * grad.shape[1], grad.shape[2])
         sums.append(lax.psum_scatter(grad, "dp", scatter_dimension=0, tiled=True))
-        grad_router = grad_router + router_part[:, :experts]
-    outs[-1] = (swap(after(sent[1], got)), 0)
-    grad_hidden, dqkv, pieces, grad_gain_one, grad_gain_two = back(
+        routers.append(router_part)
+    outs = swap(after(outs, got))
+    grad_hidden, dqkv, own, sent = back(
         starts, here, groups, index, hidden, tokens, grad_out, qkv, probs, mixed, gain_one,
-        w_qkv, w_proj, gain_two, downs, capacity,
-    )
-    pieces = after(pieces, outs[-1][0])
-    small = jnp.concatenate([grad_router.T, grad_gain_two, grad_gain_one.T], axis=0)
-    small = sum_small(small)
-    own, other = sum_over_all(pieces, groups)
-    block_out = top(starts, index, hidden, outs, capacity)
-    grad_tokens = last(dqkv, grad_hidden, tokens, gain_one, w_qkv)
+        w_qkv, w_proj, gain_two, downs, own_dx, routers, capacity,
+    )
+    sent = after(sent, outs)
+    blocks = count // BLOCK
+    cuts = [0, blocks // 3, 2 * blocks // 3, blocks]
+    grad_tokens = [None]
+
+    def make_top(tie):
+        parts = [(outs, part) for part in range(local)]
+        return top(starts, here, index, after(hidden, tie), parts, own_out, capacity)
+
+    def make_last(turn, tie):
+        grad_tokens.append(
+            last(
+                cuts[turn], cuts[turn + 1], grad_tokens[-1], after(dqkv, tie), grad_hidden,
+                tokens, gain_one, w_qkv,
+            )
+        )
+        return grad_tokens[-1]
+
+    own, other, small, done = sum_over_all(
+        own, sent, groups, small_rows(experts), [make_top] + [functools.partial(make_last, turn) for turn in range(3)]
+    )
+    block_out, grad_tokens = done[0], done[3]
     grad_qkv, grad_proj = lay(groups, here, own, other)
     tall = width // shards
     grad_in = jnp.stack([part[:tall] for part in sums]).astype(F32)
@@ -779,10 +896,10 @@
     return (
         block_out,
         grad_tokens,
-        small[experts + 1] / gain_one,
+        small[experts] / gain_one,
         grad_qkv,
         grad_proj,
-        small[experts],
+        small[experts + 1],
         small[:experts].T,
         grad_in,
         grad_eout,

time: 429 us -> 386 us (0.90)
  waiting for transfers between devices: 100 us -> 33.6 us
  Pallas kernels: 235 us -> 266 us
  local copies, waits for them, and re-layouts: 20.8 us -> 14.3 us
    all_to_all x6, waiting for transfers between devices: 66 us -> 26.6 us  [swap(): lax.all_to_all(sent, 'expert', split_axis=0, concat_axis=0, tiled=True)]
    ppermute x19 -> x14, waiting for transfers between devices: 33.6 us -> 6.99 us  [jump(): return lax.ppermute(value, axis, [(at, at ^ far) for at in range(size)])]
    pallas_call x5 -> x12, Pallas kernels: 184 us -> 210 us  [the longest x4 116 us: expert_pass(): pl.pallas_call(body, grid_spec=pltpu.PrefetchScalarGridSpec(num_scalar_pr...]
    squeeze x4 -> x0, local copies, waits for them, and re-layouts: 9.43 us -> none  [the longest x1 4.97 us: per_device(): w_in[part]]
    pallas_call x2 -> x3, Pallas kernels: 21.9 us -> 26.1 us  [dispatch(): pl.pallas_call(functools.partial(dispatch_kernel, window, capacity, plan,...]
    ppermute x19 -> x14, starting transfers between devices: 18.2 us -> 16 us  [jump(): return lax.ppermute(value, axis, [(at, at ^ far) for at in range(size)])]
  transfers between devices with their start and end apart: 27 -> 22, of which waited for: 15 -> 8; matrix products, arithmetic and copies ran while one was open for 4% -> 3% of each run, Pallas kernels for 50% -> 66%
where the time goes in v3:
time: 386 us; the launch traced here: 380 us
  Pallas kernels  266 us (69%)
  starting transfers between devices  45.5 us (12%)
  waiting for transfers between devices  33.6 us (9%)
  between operations  14.8 us (4%)
  local copies, waits for them, and re-layouts  14.3 us (4%)
  other arithmetic  6.13 us (2%)
    pallas_call x4, Pallas kernels, expert_pass(): pl.pallas_call(body, grid_spec=pltpu.PrefetchScalarGridSpec(num_scalar_pr...  116 us
    pallas_call x1, Pallas kernels, back(): pl.pallas_call(functools.partial(back_kernel, window, groups, len(parts))...  59 us
    all_to_all x6, starting transfers between devices, swap(): lax.all_to_all(sent, 'expert', split_axis=0, concat_axis=0, tiled=True)  28.8 us
    all_to_all x6, waiting for transfers between devices, swap(): lax.all_to_all(sent, 'expert', split_axis=0, concat_axis=0, tiled=True)  26.6 us
    pallas_call x3, Pallas kernels, dispatch(): pl.pallas_call(functools.partial(dispatch_kernel, window, capacity, plan,...  26.1 us
    pallas_call x1, Pallas kernels, attend(): pl.pallas_call(attend_kernel, grid=(blocks,), in_specs=[row((BLOCK, width...  20.9 us
    pallas_call x3, Pallas kernels, last(): pl.pallas_call(last_kernel, grid=(high - low,), in_specs=[row((BLOCK_PAD,...  16.9 us
    ppermute x14, starting transfers between devices, jump(): return lax.ppermute(value, axis, [(at, at ^ far) for at in range(size)])  16 us
  transfers between devices with their start and end apart: 22, of which 8 were waited for; matrix products, arithmetic and copies ran while one was open for 3% of the time, Pallas kernels for 66%

profile of v3, /device:TPU:0, one launch (start us, length us, event | category | flops | bytes accessed | tf_op | source)
XLA Modules:
  0.0 380.2 jit_solution(7436961047788178638)
XLA Ops:
  9.4 4.0 %places.1 = (s32[6,2,392]{2,1,0:T(2,128)}, s32[8,128]{1,0:T(8,128)}) custom-call(s32[8,1]{1,0:T(8,128)} %reshape.86.ids_ref, s32[6,4,392]{2,1,0:T(4,128)} %bitcast.69), custom_call_target="tpu_custom_call" | custom-call | flops 100000000 | bytes 100000 | tf_op jit(solution)/shard_map/places/pallas_call | solution.py:203
  13.4 7.8 %dispatch.3.refs_6_ = bf16[4,624,512]{2,1,0:T(8,128)(2,1)} custom-call(s32[8,128]{1,0:T(8,128)} %get-tuple-element.74.starts_ref, s32[6,2,392]{2,1,0:T(2,128)} %get-tuple-element.75.index_ref, bf16[2352,512]{1,0:T(8,128)(2,1)} %dy_ref.1), custom_call_target="tpu_custom_call" | custom-call | flops 6000000000 | bytes 8000000 | tf_op jit(solution)/shard_map/dispatch/pallas_call | solution.py:285
  21.2 5.3 %all-to-all-start = ((bf16[4,624,512]{2,1,0:T(8,128)(2,1)}), bf16[4,624,512]{2,1,0:T(8,128)(2,1)S(1)}, u32[]{:S(2)}, u32[]{:S(2)}) async-start(bf16[4,624,512]{2,1,0:T(8,128)(2,1)} %dispatch.3.refs_6_), calls=%async_computation | async-start | bytes 5111808 | tf_op jit(solution)/shard_map/all_to_all | solution.py:818
  26.6 20.9 %attend.1 = (f32[2352,512]{1,0:T(8,128)}, bf16[2352,512]{1,0:T(8,128)(2,1)}, bf16[2688,1536]{1,0:T(8,128)(2,1)}, bf16[21504,112]{1,0:T(8,128)(2,1)}, bf16[2688,512]{1,0:T(8,128)(2,1)}) custom-call(bf16[2352,512]{1,0:T(8,128)(2,1)} %tok_ref.8, f32[1,512]{1,0:T(1,128)} %bitcast.70, bf16[512,1536]{1,0:T(8,128)(2,1)} %qkv_w_ref.9, bf16[512,512]{1,0:T(8,128)(2,1)} %proj_w_ref.3, ...), custom_call_target="tpu_custom_call" | custom-call | flops 6870269952 | bytes 30000000 | tf_op jit(solution)/shard_map/attend/pallas_call | solution.py:147
  47.4 7.8 %dispatch.4.refs_5_ = bf16[4,624,512]{2,1,0:T(8,128)(2,1)} custom-call(s32[8,128]{1,0:T(8,128)} %get-tuple-element.74.starts_ref, s32[6,2,392]{2,1,0:T(2,128)} %get-tuple-element.75.index_ref, bf16[2352,512]{1,0:T(8,128)(2,1)} %get-tuple-element.87.refs_0_), custom_call_target="tpu_custom_call" | custom-call | flops 6000000000 | bytes 8000000 | tf_op jit(solution)/shard_map/dispatch/pallas_call | solution.py:285
  57.7 4.8 %all-to-all-start.1 = ((bf16[4,624,512]{2,1,0:T(8,128)(2,1)}), bf16[4,624,512]{2,1,0:T(8,128)(2,1)}, u32[]{:S(2)}, u32[]{:S(2)}) async-start(bf16[4,624,512]{2,1,0:T(8,128)(2,1)} %dispatch.4.refs_5_), calls=%async_computation.1 | async-start | bytes 5111808 | tf_op jit(solution)/shard_map/all_to_all | solution.py:818
  64.6 10.5 %dispatch.5.refs_5_.refs_6_ = bf16[4,1248,512]{2,1,0:T(8,128)(2,1)} custom-call(s32[8,128]{1,0:T(8,128)} %get-tuple-element.74.starts_ref, s32[6,2,392]{2,1,0:T(2,128)} %get-tuple-element.75.index_ref, bf16[2352,512]{1,0:T(8,128)(2,1)} %get-tuple-element.87.refs_0_, bf16[2352,512]{1,0:T(8,128)(2,1)} %dy_ref.1), custom_call_target="tpu_custom_call" | custom-call | flops 6000000000 | bytes 8000000 | tf_op jit(solution)/shard_map/dispatch/pallas_call | solution.py:285
  75.2 15.4 %expert_own.2 = (bf16[1,624,512]{2,1,0:T(8,128)(2,1)}, bf16[1,624,512]{2,1,0:T(8,128)(2,1)}, bf16[512,2048]{1,0:T(8,128)(2,1)}, bf16[512,2048]{1,0:T(8,128)(2,1)}, f32[512,128]{1,0:T(8,128)}) custom-call(s32[2]{0:T(128)} %pad_add_fusion.2.refs_0_, bf16[2,512,2048]{2,1,0:T(8,128)(2,1)} %refs_1_.9, bf16[2,2048,512]{2,1,0:T(8,128)(2,1)} %refs_2_.7, ...), custom_call_target="tpu_custom_call" | custom-call | flops 13086228480 | bytes 30000000 | tf_op jit(solution)/shard_map/expert_own/pallas_call | solution.py:503
  91.8 5.0 %all-to-all-start.2 = ((bf16[4,1248,512]{2,1,0:T(8,128)(2,1)}), bf16[4,1248,512]{2,1,0:T(8,128)(2,1)}, u32[]{:S(2)}, u32[]{:S(2)}) async-start(bf16[4,1248,512]{2,1,0:T(8,128)(2,1)} %dispatch.5.refs_5_.refs_6_), calls=%async_computation.2 | async-start | bytes 10223616 | tf_op jit(solution)/shard_map/all_to_all | solution.py:818
  97.3 42.1 %expert_others.2 = (bf16[4,624,512]{2,1,0:T(8,128)(2,1)}, bf16[4,1248,512]{2,1,0:T(8,128)(2,1)}, bf16[8,128,2048]{2,1,0:T(8,128)(2,1)}, f32[512,128]{1,0:T(8,128)}) custom-call(s32[2]{0:T(128)} %pad_add_fusion.2.refs_0_, bf16[2,512,2048]{2,1,0:T(8,128)(2,1)} %refs_1_.9, bf16[2,2048,512]{2,1,0:T(8,128)(2,1)} %refs_2_.7, bf16[512,256]{1,0:T(8,128)(2,1)} %copy.35.refs_3_, ...), custom_call_target="tpu_custom_call" | custom-call | flops 39258685440 | bytes 30000000 | tf_op jit(solution)/shard_map/expert_others/pallas_call | solution.py:503
  140.0 13.5 %all-to-all-done.2.refs_5_.refs_6_ = bf16[4,1248,512]{2,1,0:T(8,128)(2,1)} async-done(((bf16[4,1248,512]{2,1,0:T(8,128)(2,1)}), bf16[4,1248,512]{2,1,0:T(8,128)(2,1)}, u32[]{:S(2)}, u32[]{:S(2)}) %all-to-all-start.2) | async-done | bytes 5111840 | tf_op jit(solution)/shard_map/all_to_all | solution.py:818
  153.5 3.8 %all-to-all-start.3 = ((bf16[4,624,512]{2,1,0:T(8,128)(2,1)}), bf16[4,624,512]{2,1,0:T(8,128)(2,1)S(1)}, u32[]{:S(2)}, u32[]{:S(2)}) async-start(bf16[4,624,512]{2,1,0:T(8,128)(2,1)} %get-tuple-element.89), calls=%async_computation.3 | async-start | bytes 5111808 | tf_op jit(solution)/shard_map/all_to_all | solution.py:818
  157.4 40.5 %expert_others.3 = (bf16[4,624,512]{2,1,0:T(8,128)(2,1)}, bf16[4,1248,512]{2,1,0:T(8,128)(2,1)}, bf16[512,2048]{1,0:T(8,128)(2,1)}, bf16[512,2048]{1,0:T(8,128)(2,1)}, f32[512,128]{1,0:T(8,128)}) custom-call(s32[2]{0:T(128)} %pad_add_fusion.3.refs_0_, bf16[2,512,2048]{2,1,0:T(8,128)(2,1)} %refs_1_.9, ...), custom_call_target="tpu_custom_call", output_to_operand_aliasing={{1}: (7, {})} | custom-call | flops 39258685440 | bytes 30000000 | tf_op jit(solution)/shard_map/expert_others/pallas_call | solution.py:503
  199.3 4.5 %all-to-all-start.4 = ((bf16[4,624,512]{2,1,0:T(8,128)(2,1)}), bf16[4,624,512]{2,1,0:T(8,128)(2,1)}, u32[]{:S(2)}, u32[]{:S(2)}) async-start(bf16[4,624,512]{2,1,0:T(8,128)(2,1)} %get-tuple-element.92), calls=%async_computation.4 | async-start | bytes 5111808 | tf_op jit(solution)/shard_map/all_to_all | solution.py:818
  204.1 18.2 %expert_own.3 = (bf16[1,624,512]{2,1,0:T(8,128)(2,1)}, bf16[1,624,512]{2,1,0:T(8,128)(2,1)}, bf16[8,128,2048]{2,1,0:T(8,128)(2,1)}, f32[512,128]{1,0:T(8,128)}) custom-call(s32[2]{0:T(128)} %pad_add_fusion.3.refs_0_, bf16[2,512,2048]{2,1,0:T(8,128)(2,1)} %refs_1_.9, bf16[2,2048,512]{2,1,0:T(8,128)(2,1)} %refs_2_.7, bf16[512,256]{1,0:T(8,128)(2,1)} %copy.35.refs_3_, ...), custom_call_target="tpu_custom_call" | custom-call | flops 13086228480 | bytes 30000000 | tf_op jit(solution)/shard_map/expert_own/pallas_call | solution.py:503
  222.4 10.8 %all-to-all-done.4.refs_1_ = bf16[4,624,512]{2,1,0:T(8,128)(2,1)} async-done(((bf16[4,624,512]{2,1,0:T(8,128)(2,1)}), bf16[4,624,512]{2,1,0:T(8,128)(2,1)}, u32[]{:S(2)}, u32[]{:S(2)}) %all-to-all-start.4) | async-done | bytes 2555936 | tf_op jit(solution)/shard_map/all_to_all | solution.py:818
  233.2 5.4 %all-to-all-start.5 = ((bf16[4,1248,512]{2,1,0:T(8,128)(2,1)}), bf16[4,1248,512]{2,1,0:T(8,128)(2,1)}, u32[]{:S(2)}, u32[]{:S(2)}) async-start(bf16[4,1248,512]{2,1,0:T(8,128)(2,1)} %get-tuple-element.103), calls=%async_computation.5 | async-start | bytes 10223616 | tf_op jit(solution)/shard_map/all_to_all | solution.py:818
  240.7 59.0 %back.1 = (f32[2352,512]{1,0:T(8,128)}, bf16[2688,1536]{1,0:T(8,128)(2,1)}, bf16[1040,512]{1,0:T(8,128)(2,1)}, bf16[1040,512]{1,0:T(8,128)(2,1)}) custom-call(s32[8,128]{1,0:T(8,128)} %get-tuple-element.74.starts_ref, s32[3]{0:T(128)} %pad_add_fusion.1.here_ref, s32[2352,2]{1,0:T(8,128)} %bitcast.56, f32[2352,512]{1,0:T(8,128)} %get-tuple-element.106.hidden_ref, ...), custom_call_target="tpu_custom_call" | custom-call | flops 26357102592 | bytes 40000000 | tf_op jit(solution)/shard_map/back/pallas_call | solution.py:631
  309.7 11.9 %top.1 = bf16[2352,512]{1,0:T(8,128)(2,1)} custom-call(s32[8,128]{1,0:T(8,128)} %get-tuple-element.74.starts_ref, s32[3]{0:T(128)} %pad_add_fusion.1.here_ref, s32[2352,2]{1,0:T(8,128)} %bitcast.57, f32[2352,512]{1,0:T(8,128)} %get-tuple-element.106.hidden_ref, bf16[4,1248,512]{2,1,0:T(8,128)(2,1)} %all-to-all-done.5.refs_0_.refs_1_, ...), custom_call_target="tpu_custom_call" | custom-call | flops 6000000000 | bytes 12000000 | tf_op jit(solution)/shard_map/top/pallas_call | solution.py:352
  330.6 5.6 %last.3.refs_0_ = f32[2352,512]{1,0:T(8,128)} custom-call(bf16[2688,1536]{1,0:T(8,128)(2,1)} %get-tuple-element.130.dqkv_ref, f32[2352,512]{1,0:T(8,128)} %get-tuple-element.121.ghid_ref, bf16[2352,512]{1,0:T(8,128)(2,1)} %tok_ref.8, f32[1,512]{1,0:T(1,128)} %bitcast.72, bf16[512,1536]{1,0:T(8,128)(2,1)} %qkv_w_ref.9), custom_call_target="tpu_custom_call" | custom-call | flops 1409286144 | bytes 20000000 | tf_op jit(solution)/shard_map/last/pallas_call | solution.py:682
  339.4 3.6 collective-permute-start.9
  343.8 5.6 %last.4.refs_0_ = f32[2352,512]{1,0:T(8,128)} custom-call(bf16[2688,1536]{1,0:T(8,128)(2,1)} %get-tuple-element.130.dqkv_ref, f32[2352,512]{1,0:T(8,128)} %get-tuple-element.121.ghid_ref, bf16[2352,512]{1,0:T(8,128)(2,1)} %tok_ref.8, f32[1,512]{1,0:T(1,128)} %bitcast.73, bf16[512,1536]{1,0:T(8,128)(2,1)} %qkv_w_ref.9, ...), custom_call_target="tpu_custom_call", output_to_operand_aliasing={{}: (5, {})} | custom-call | flops 1409286144 | bytes 20000000 | tf_op jit(solution)/shard_map/last/pallas_call | solution.py:682
  354.2 5.7 %last.5 = f32[2352,512]{1,0:T(8,128)} custom-call(bf16[2688,1536]{1,0:T(8,128)(2,1)} %get-tuple-element.130.dqkv_ref, f32[2352,512]{1,0:T(8,128)} %get-tuple-element.121.ghid_ref, bf16[2352,512]{1,0:T(8,128)(2,1)} %tok_ref.8, f32[1,512]{1,0:T(1,128)} %bitcast.74, bf16[512,1536]{1,0:T(8,128)(2,1)} %qkv_w_ref.9, ...), custom_call_target="tpu_custom_call", output_to_operand_aliasing={{}: (5, {})} | custom-call | flops 1409286144 | bytes 20000000 | tf_op jit(solution)/shard_map/last/pallas_call | solution.py:682
  368.4 4.5 %lay.1 = (f32[512,1536]{1,0:T(8,128)}, f32[512,512]{1,0:T(8,128)}) custom-call(s32[3]{0:T(128)} %pad_add_fusion.1.here_ref, bf16[16,64,512]{2,1,0:T(8,128)(2,1)} %bitcast.53, bf16[16,64,512]{2,1,0:T(8,128)(2,1)} %copy-done.4), custom_call_target="tpu_custom_call" | custom-call | flops 1000000 | bytes 8000000 | tf_op jit(solution)/shard_map/lay/pallas_call | solution.py:717
  (97 shorter events, 49.1 us)
Async XLA Ops:
  21.2 35.1 %all-to-all-start = ((bf16[4,624,512]{2,1,0:T(8,128)(2,1)}), bf16[4,624,512]{2,1,0:T(8,128)(2,1)S(1)}, u32[]{:S(2)}, u32[]{:S(2)}) async-start(bf16[4,624,512]{2,1,0:T(8,128)(2,1)} %dispatch.3.refs_6_), calls=%async_computation | async-start | bytes 5111808 | tf_op jit(solution)/shard_map/all_to_all | solution.py:818
  57.7 34.1 %all-to-all-start.1 = ((bf16[4,624,512]{2,1,0:T(8,128)(2,1)}), bf16[4,624,512]{2,1,0:T(8,128)(2,1)}, u32[]{:S(2)}, u32[]{:S(2)}) async-start(bf16[4,624,512]{2,1,0:T(8,128)(2,1)} %dispatch.4.refs_5_), calls=%async_computation.1 | async-start | bytes 5111808 | tf_op jit(solution)/shard_map/all_to_all | solution.py:818
  91.8 61.7 %all-to-all-start.2 = ((bf16[4,1248,512]{2,1,0:T(8,128)(2,1)}), bf16[4,1248,512]{2,1,0:T(8,128)(2,1)}, u32[]{:S(2)}, u32[]{:S(2)}) async-start(bf16[4,1248,512]{2,1,0:T(8,128)(2,1)} %dispatch.5.refs_5_.refs_6_), calls=%async_computation.2 | async-start | bytes 10223616 | tf_op jit(solution)/shard_map/all_to_all | solution.py:818
  96.8 256.3 %reduce-scatter.3.cloned.1.call-start = ((), (), s32[]{:S(2)}) async-start(), calls=%async_computation.8 | async-start | bytes 4718592 | tf_op jit(solution)/shard_map/reduce_scatter | solution.py:861
  153.5 44.3 %all-to-all-start.3 = ((bf16[4,624,512]{2,1,0:T(8,128)(2,1)}), bf16[4,624,512]{2,1,0:T(8,128)(2,1)S(1)}, u32[]{:S(2)}, u32[]{:S(2)}) async-start(bf16[4,624,512]{2,1,0:T(8,128)(2,1)} %get-tuple-element.89), calls=%async_computation.3 | async-start | bytes 5111808 | tf_op jit(solution)/shard_map/all_to_all | solution.py:818
  199.3 33.8 %all-to-all-start.4 = ((bf16[4,624,512]{2,1,0:T(8,128)(2,1)}), bf16[4,624,512]{2,1,0:T(8,128)(2,1)}, u32[]{:S(2)}, u32[]{:S(2)}) async-start(bf16[4,624,512]{2,1,0:T(8,128)(2,1)} %get-tuple-element.92), calls=%async_computation.4 | async-start | bytes 5111808 | tf_op jit(solution)/shard_map/all_to_all | solution.py:818
  203.9 158.3 %reduce-scatter.5.cloned.1.call-start = ((), (), s32[]{:S(2)}) async-start(), calls=%async_computation.9 | async-start | bytes 4718592 | tf_op jit(solution)/shard_map/reduce_scatter | solution.py:861
  233.2 5.4 %copy-start.13 = (s32[6,2,392]{2,1,0:T(2,128)S(1)}, s32[6,2,392]{2,1,0:T(2,128)}, u32[]{:S(2)}) copy-start(s32[6,2,392]{2,1,0:T(2,128)} %get-tuple-element.75.index_ref) | copy-start | bytes 56452
  233.2 66.5 %all-to-all-start.5 = ((bf16[4,1248,512]{2,1,0:T(8,128)(2,1)}), bf16[4,1248,512]{2,1,0:T(8,128)(2,1)}, u32[]{:S(2)}, u32[]{:S(2)}) async-start(bf16[4,1248,512]{2,1,0:T(8,128)(2,1)} %get-tuple-element.103), calls=%async_computation.5 | async-start | bytes 10223616 | tf_op jit(solution)/shard_map/all_to_all | solution.py:818
  299.7 3.0 collective-permute-start
  306.2 15.4 %collective-permute-start.1 = (bf16[272,512]{1,0:T(8,128)(2,1)}, bf16[272,512]{1,0:T(8,128)(2,1)S(1)}, u32[]{:S(2)}, u32[]{:S(2)}) collective-permute-start(bf16[272,512]{1,0:T(8,128)(2,1)} %get-tuple-element.110), channel_id=1, source_target_pairs={{0,1},{1,0},{2,3},{3,2},{4,5},{5,4},{6,7},{7,6},{8,9},{9,8},{10,11... | collective-permute-start | bytes 835592 | tf_op jit(solution)/shard_map/ppermute | solution.py:737
  308.2 14.6 %collective-permute-start.2 = (bf16[272,512]{1,0:T(8,128)(2,1)}, bf16[272,512]{1,0:T(8,128)(2,1)S(1)}, u32[]{:S(2)}, u32[]{:S(2)}) collective-permute-start(bf16[272,512]{1,0:T(8,128)(2,1)} %get-tuple-element.111), channel_id=1, source_target_pairs={{0,2},{1,3},{2,0},{3,1},{4,6},{5,7},{6,4},{7,5},{8,10},{9,11},{10,... | collective-permute-start | bytes 835592 | tf_op jit(solution)/shard_map/ppermute | solution.py:737
  309.7 13.1 %collective-permute-start.3 = (bf16[272,512]{1,0:T(8,128)(2,1)}, bf16[272,512]{1,0:T(8,128)(2,1)S(1)}, u32[]{:S(2)}, u32[]{:S(2)}) collective-permute-start(bf16[272,512]{1,0:T(8,128)(2,1)} %get-tuple-element.112), channel_id=1, source_target_pairs={{0,3},{1,2},{2,1},{3,0},{4,7},{5,6},{6,5},{7,4},{8,11},{9,10},{10,... | collective-permute-start | bytes 835592 | tf_op jit(solution)/shard_map/ppermute | solution.py:737
  326.2 10.1 %collective-permute-start.4 = (bf16[80,512]{1,0:T(8,128)(2,1)}, bf16[80,512]{1,0:T(8,128)(2,1)S(1)}, u32[]{:S(2)}, u32[]{:S(2)}) collective-permute-start(bf16[80,512]{1,0:T(8,128)(2,1)} %get-tuple-element.117), channel_id=1, source_target_pairs={{0,8},{4,12},{8,0},{12,4},{16,24},{20,28},{24,16},{28,20},{1,9},{5... | collective-permute-start | bytes 245768 | tf_op jit(solution)/shard_map/ppermute | solution.py:737
  328.1 8.2 %collective-permute-start.5 = (bf16[80,512]{1,0:T(8,128)(2,1)}, bf16[80,512]{1,0:T(8,128)(2,1)S(1)}, u32[]{:S(2)}, u32[]{:S(2)}) collective-permute-start(bf16[80,512]{1,0:T(8,128)(2,1)} %get-tuple-element.118), channel_id=1, source_target_pairs={{0,16},{4,20},{8,24},{12,28},{16,0},{20,4},{24,8},{28,12},{1,17},{... | collective-permute-start | bytes 245768 | tf_op jit(solution)/shard_map/ppermute | solution.py:737
  330.6 6.5 %collective-permute-start.6 = (bf16[80,512]{1,0:T(8,128)(2,1)}, bf16[80,512]{1,0:T(8,128)(2,1)S(1)}, u32[]{:S(2)}, u32[]{:S(2)}) collective-permute-start(bf16[80,512]{1,0:T(8,128)(2,1)} %get-tuple-element.119), channel_id=1, source_target_pairs={{0,24},{4,28},{8,16},{12,20},{16,8},{20,12},{24,0},{28,4},{1,25},{... | collective-permute-start | bytes 245768 | tf_op jit(solution)/shard_map/ppermute | solution.py:737
  339.4 10.0 %copy-start.11 = (bf16[64,512]{1,0:T(8,128)(2,1)S(1)}, bf16[64,512]{1,0:T(8,128)(2,1)}, u32[]{:S(2)}) copy-start(bf16[64,512]{1,0:T(8,128)(2,1)} %get-tuple-element.125) | copy-start | bytes 196612
  339.4 10.0 %collective-permute-start.9 = (bf16[64,512]{1,0:T(8,128)(2,1)}, bf16[64,512]{1,0:T(8,128)(2,1)S(1)}, u32[]{:S(2)}, u32[]{:S(2)}) collective-permute-start(bf16[64,512]{1,0:T(8,128)(2,1)} %get-tuple-element.125), channel_id=1, source_target_pairs={{0,24},{4,28},{8,16},{12,20},{16,8},{20,12},{24,0},{28,4},{1,25},{... | collective-permute-start | bytes 196616 | tf_op jit(solution)/shard_map/ppermute | solution.py:737
  343.1 6.4 %collective-permute-start.8 = (bf16[64,512]{1,0:T(8,128)(2,1)}, bf16[64,512]{1,0:T(8,128)(2,1)S(1)}, u32[]{:S(2)}, u32[]{:S(2)}) collective-permute-start(bf16[64,512]{1,0:T(8,128)(2,1)} %get-tuple-element.125), channel_id=1, source_target_pairs={{0,16},{4,20},{8,24},{12,28},{16,0},{20,4},{24,8},{28,12},{1,17},{... | collective-permute-start | bytes 196616 | tf_op jit(solution)/shard_map/ppermute | solution.py:737
  343.1 6.4 %collective-permute-start.7 = (bf16[64,512]{1,0:T(8,128)(2,1)}, bf16[64,512]{1,0:T(8,128)(2,1)S(1)}, u32[]{:S(2)}, u32[]{:S(2)}) collective-permute-start(bf16[64,512]{1,0:T(8,128)(2,1)} %get-tuple-element.125), channel_id=1, source_target_pairs={{0,8},{4,12},{8,0},{12,4},{16,24},{20,28},{24,16},{28,20},{1,9},{5... | collective-permute-start | bytes 196616 | tf_op jit(solution)/shard_map/ppermute | solution.py:737
  349.5 10.3 %collective-permute-start.11 = (bf16[4,64,512]{2,1,0:T(8,128)(2,1)S(1)}, bf16[4,64,512]{2,1,0:T(8,128)(2,1)S(1)}, u32[]{:S(2)}, u32[]{:S(2)}) collective-permute-start(bf16[4,64,512]{2,1,0:T(8,128)(2,1)S(1)} %get-tuple-element.146), channel_id=1, source_target_pairs={{0,2},{1,3},{2,0},{3,1},{4,6},{5,7},{6,4},{7,5},{8,10},{9,11},{10,... | collective-permute-start | bytes 786440 | tf_op jit(solution)/shard_map/ppermute | solution.py:737
  351.2 8.7 %collective-permute-start.10 = (bf16[4,64,512]{2,1,0:T(8,128)(2,1)S(1)}, bf16[4,64,512]{2,1,0:T(8,128)(2,1)S(1)}, u32[]{:S(2)}, u32[]{:S(2)}) collective-permute-start(bf16[4,64,512]{2,1,0:T(8,128)(2,1)S(1)} %get-tuple-element.146), channel_id=1, source_target_pairs={{0,1},{1,0},{2,3},{3,2},{4,5},{5,4},{6,7},{7,6},{8,9},{9,8},{10,11... | collective-permute-start | bytes 786440 | tf_op jit(solution)/shard_map/ppermute | solution.py:737
  352.0 9.9 %collective-permute-start.12 = (bf16[4,64,512]{2,1,0:T(8,128)(2,1)S(1)}, bf16[4,64,512]{2,1,0:T(8,128)(2,1)S(1)}, u32[]{:S(2)}, u32[]{:S(2)}) collective-permute-start(bf16[4,64,512]{2,1,0:T(8,128)(2,1)S(1)} %get-tuple-element.146), channel_id=1, source_target_pairs={{0,3},{1,2},{2,1},{3,0},{4,7},{5,6},{6,5},{7,4},{8,11},{9,10},{10,... | collective-permute-start | bytes 786440 | tf_op jit(solution)/shard_map/ppermute | solution.py:737
  362.1 5.3 %collective-permute-start.13 = (bf16[16,64,512]{2,1,0:T(8,128)(2,1)S(1)}, bf16[16,64,512]{2,1,0:T(8,128)(2,1)S(1)}, u32[]{:S(2)}, u32[]{:S(2)}) collective-permute-start(bf16[16,64,512]{2,1,0:T(8,128)(2,1)S(1)} %bitcast.52), channel_id=1, source_target_pairs={{0,4},{4,0},{8,12},{12,8},{16,20},{20,16},{24,28},{28,24},{1,5},{5... | collective-permute-start | bytes 3145736 | tf_op jit(solution)/shard_map/ppermute | solution.py:737
  (14 other events, 28.3 us)
Sparse Core Ops, SparseCore 0:
  139.6 51.8 reduce-scatter.2
  222.5 51.9 reduce-scatter.4

commit v4 on v3

--- a/solution.py
+++ b/solution.py
@@ -17,8 +17,8 @@
 BLOCK_PAD = BLOCK_PAIRS * PAIR_PAD
 BF = jnp.bfloat16
 F32 = jnp.float32
-VMEM_BYTES = 56 * 1024 * 1024
-FCUT = 1024
+VMEM_BYTES = 62 * 1024 * 1024
+FCUT = 256
 
 
 def params():
@@ -106,7 +106,7 @@
 def attend_kernel(
     tok_ref, gain_one_ref, qkv_w_ref, proj_w_ref, gain_two_ref,
     hidden_ref, rows_ref, qkv_ref, probs_ref, mixed_ref,
-    compact, padded,
+    compact, padded, scores,
 ):
     width = tok_ref.shape[1]
     factor_qk = (width // HEADS) ** (-0.5)
@@ -123,13 +123,24 @@
             cols = slice(LANES * two, LANES * (two + 1))
             query = qkv_ref[rows, cols]
             keys = qkv_ref[rows, width + LANES * two : width + LANES * (two + 1)]
+            step = (pair * (width // LANES) + two) * 2 * PAIR_PAD
+            scores[step : step + 2 * PAIR_PAD, :] = jnp.where(
+                valid, dot_rt(two_heads(query, low), keys), -1e30
+            )
+    for pair in range(BLOCK_PAIRS):
+        each = 2 * PAIR_PAD * (width // LANES)
+        part = slice(each * pair, each * (pair + 1))
+        logits = scores[part, :]
+        highest = jnp.max(logits, axis=-1, keepdims=True)
+        expo = jnp.exp((logits - highest) * factor_qk)
+        probs_ref[part, :] = (expo / jnp.sum(expo, axis=-1, keepdims=True)).astype(BF)
+    for pair in range(BLOCK_PAIRS):
+        rows = slice(PAIR_PAD * pair, PAIR_PAD * (pair + 1))
+        for two in range(width // LANES):
+            cols = slice(LANES * two, LANES * (two + 1))
             values = qkv_ref[rows, 2 * width + LANES * two : 2 * width + LANES * (two + 1)]
-            scores = jnp.where(valid, dot_rt(two_heads(query, low), keys), -1e30)
-            highest = jnp.max(scores, axis=-1, keepdims=True)
-            expo = jnp.exp((scores - highest) * factor_qk)
-            probs = (expo / jnp.sum(expo, axis=-1, keepdims=True)).astype(BF)
             step = (pair * (width // LANES) + two) * 2 * PAIR_PAD
-            probs_ref[step : step + 2 * PAIR_PAD, :] = probs
+            probs = probs_ref[step : step + 2 * PAIR_PAD, :]
             mixed_ref[rows, cols] = one_row(dot(probs, values), low).astype(BF)
     padded[...] = dot(mixed_ref[...], proj_w_ref[...])
     gather_rows(padded, compact)
@@ -162,7 +173,10 @@
             jax.ShapeDtypeStruct((blocks * prob_rows, PAIR_PAD), BF),
             jax.ShapeDtypeStruct((blocks * BLOCK_PAD, width), BF),
         ],
-        scratch_shapes=[pltpu.VMEM((BLOCK, width), F32), pltpu.VMEM((BLOCK_PAD, width), F32)],
+        scratch_shapes=[
+            pltpu.VMEM((BLOCK, width), F32), pltpu.VMEM((BLOCK_PAD, width), F32),
+            pltpu.VMEM((prob_rows, PAIR_PAD), F32),
+        ],
         compiler_params=params(),
         cost_estimate=cost(flops, 30e6, blocks * prob_rows * LANES),
         name="attend",
@@ -219,7 +233,7 @@
 
 
 def window_rows(experts, capacity):
-    return min(capacity, 16 * -(-2 * BLOCK * 8 // (5 * 16 * experts)))
+    return min(capacity, 1024 // experts)
 
 
 def window_at(starts_ref, expert, step, turn, window, capacity):
@@ -317,10 +331,14 @@
             fresh = (slot >= begin) & (slot < high)
             mine = (lane >= expert * window) & (lane < (expert + 1) * window)
             seen = jnp.where(mine & fresh, slot + expert * capacity, seen)
-            wins[window * expert : window * (expert + 1), :] = jnp.where(
-                me == owner, own_bufs[part][0, pl.ds(at, window), :],
-                bufs[part][owner, pl.ds(at, window), :],
-            )
+            to = slice(window * expert, window * (expert + 1))
+            if own_bufs[part] is None:
+                wins[to, :] = bufs[part][owner, pl.ds(at, window), :]
+            else:
+                wins[to, :] = jnp.where(
+                    me == owner, own_bufs[part][0, pl.ds(at, window), :],
+                    bufs[part][owner, pl.ds(at, window), :],
+                )
         hit = (index_ref[:, 0:1] == seen) | (index_ref[:, 1:2] == seen)
         acc[...] += dot(hit.astype(F32).astype(BF), wins[...])
         return carry
@@ -328,49 +346,67 @@
     lax.fori_loop(0, turns(starts_ref, step, range(experts), window), one_turn, 0)
 
 
-def back_specs(parts, own, capacity):
-    width = own[0].shape[2]
-    return [
-        pl.BlockSpec((array.shape[0], capacity, width), lambda *_, at=at: (0, at, 0))
-        for array, at in parts
-    ] + [whole((1, capacity, width))] * len(own)
-
-
-def top_kernel(window, local, starts_ref, here_ref, index_ref, hidden_ref, *refs):
-    bufs, own_bufs, (out_ref, wins, acc) = refs[:local], refs[local : 2 * local], refs[2 * local :]
-    combine_block(
-        window, pl.program_id(0), here_ref[1], starts_ref, index_ref, bufs, own_bufs, wins, acc
-    )
+def top_kernel(early, starts_ref, here_ref, index_ref, hidden_ref, head_ref, tail_ref, own_first_ref, own_second_ref, out_ref, first, second, wins, acc, sems):
+    step = pl.program_id(0)
+    experts = starts_ref.shape[0]
+    window, capacity = wins.shape[0] // experts, first.shape[1]
+    late = capacity - early
+
+    @pl.when(step == 0)
+    def _():
+        copies = [
+            pltpu.make_async_copy(head_ref.at[:, pl.ds(capacity, early), :], first.at[:, pl.ds(0, early), :], sems.at[0]),
+            pltpu.make_async_copy(tail_ref.at[:, pl.ds(0, late), :], first.at[:, pl.ds(early, late), :], sems.at[1]),
+            pltpu.make_async_copy(tail_ref.at[:, pl.ds(late, capacity), :], second, sems.at[2]),
+        ]
+        for copy in copies:
+            copy.start()
+        for copy in copies:
+            copy.wait()
+        me = pl.ds(here_ref[1], 1)
+        copies = [
+            pltpu.make_async_copy(own_first_ref.at[me], first.at[me, pl.ds(early, late), :], sems.at[3]),
+            pltpu.make_async_copy(own_second_ref, second.at[me], sems.at[4]),
+        ]
+        for copy in copies:
+            copy.start()
+        for copy in copies:
+            copy.wait()
+
+    combine_block(window, step, 0, starts_ref, index_ref, [first, second], [None, None], wins, acc)
     out_ref[...] = (hidden_ref[...] + acc[...]).astype(BF)
 
 
-def top(starts, here, index, hidden, parts, own, capacity):
+def top(starts, here, index, hidden, head, tail, own_first, own_second, early, capacity):
     count, width = hidden.shape
     experts = starts.shape[0]
     window = window_rows(experts, capacity)
     row = lambda shape: pl.BlockSpec(shape, lambda step, *_: (step, 0))
+    held = pltpu.VMEM((head.shape[0], capacity, width), BF)
     return pl.pallas_call(
-        functools.partial(top_kernel, window, len(parts)),
+        functools.partial(top_kernel, early),
         grid_spec=pltpu.PrefetchScalarGridSpec(
             num_scalar_prefetch=2,
             grid=(count // BLOCK,),
-            in_specs=[row((BLOCK, 2)), row((BLOCK, width))] + back_specs(parts, own, capacity),
+            in_specs=[row((BLOCK, 2)), row((BLOCK, width))] + [pl.BlockSpec(memory_space=pl.ANY)] * 4,
             out_specs=row((BLOCK, width)),
             scratch_shapes=[
-                pltpu.VMEM((experts * window, width), BF), pltpu.VMEM((BLOCK, width), F32),
+                held, held, pltpu.VMEM((experts * window, width), BF),
+                pltpu.VMEM((BLOCK, width), F32), pltpu.SemaphoreType.DMA((5,)),
             ],
         ),
         out_shape=jax.ShapeDtypeStruct((count, width), BF),
         compiler_params=params(),
         cost_estimate=cost(6e9, 12e6),
         name="top",
-    )(starts, here, index, hidden, *[array for array, _ in parts], *own)
+    )(starts, here, index, hidden, head, tail, own_first, own_second)
 
 
 def gelu_parts(values):
-    size = jnp.abs(values)
-    near = 1.0 / (1.0 + (0.3275911 * 0.7071067811865476) * size)
-    expo = jnp.exp(-0.5 * (values * values))
+    size = 1.0 + (0.3275911 * 0.7071067811865476) * jnp.abs(values)
+    near = pl.reciprocal(size, approx=True)
+    near = near * (2.0 - size * near)
+    expo = jnp.exp2((-0.5 * 1.4426950408889634) * (values * values))
     poly = 0.5 * 1.061405429
     for term in (-1.453152027, 1.421413741, -0.284496736, 0.254829592):
         poly = poly * near + 0.5 * term
@@ -380,13 +416,13 @@
 
 
 def expert_kernel(
-    experts, fcut, begun, ends, mine_ref, up_ref, down_ref, router_ref, back_ref, x_ref, dy_ref, *refs
+    experts, fcut, begun, part, joins, mine_ref, up_ref, down_ref, router_ref, back_ref, x_ref, dy_ref, *refs
 ):
     given, refs = refs[: 3 * begun], refs[3 * begun :]
+    if joins:
+        before_ref, refs = refs[0], refs[1:]
+    *grad_refs, grouter_ref = refs[2:-5]
     acc_up, acc_down, acc_router, acc_out, acc_dx = refs[-5:]
-    grouter_ref = refs[-6]
-    grad_refs = refs[-7:-6] if ends else refs[-8:-6]
-    dx_ref, out_ref = refs[-9:-7] if ends else refs[-10:-8]
     step = pl.program_id(0)
     hidden_units = up_ref.shape[1]
     _, capacity, width = x_ref.shape
@@ -416,38 +452,47 @@
     pair = (chosen * dy_ref[...].reshape(count, width).astype(F32)).astype(BF)
     rows_t = rows.T
     pair_t = pair.T
-    inner = jnp.zeros((count, LANES), F32)
-    for low in range(0, hidden_units, fcut):
-        cols = slice(low, low + fcut)
-        pre = dot(rows, up_ref[:, cols])
-        grad_act = dot_rt(pair, down_ref[cols, :])
+    chunks = [slice(low, low + fcut) for low in range(0, hidden_units, fcut)]
+    ahead = lambda cols: (dot(rows, up_ref[:, cols]), dot_rt(pair, down_ref[cols, :]))
+    ready = ahead(chunks[0])
+    for turn, cols in enumerate(chunks):
+        pre, grad_act = ready
+        if turn + 1 < len(chunks):
+            ready = ahead(chunks[turn + 1])
         act, slope = gelu_parts(pre)
-        both = act * grad_act
-        for part in range(0, fcut, LANES):
-            inner = inner + both[:, part : part + LANES]
         act = act.astype(BF)
         grad_pre = (grad_act * slope).astype(BF)
         acc_up[:, cols] += dot(rows_t, grad_pre)
         acc_down[:, cols] += dot(pair_t, act)
-        if low == 0:
+        if turn == 0:
             acc_out[...] = dot(act, down_ref[cols, :])
             acc_dx[...] = dot_rt(grad_pre, up_ref[:, cols])
         else:
             acc_out[...] += dot(act, down_ref[cols, :])
             acc_dx[...] += dot_rt(grad_pre, up_ref[:, cols])
-    grad_logits = jnp.sum(inner, axis=-1, keepdims=True) * (own - gates)
+    inner = jnp.sum(acc_out[...] * pair.astype(F32), axis=-1, keepdims=True)
+    grad_logits = inner * (own - gates)
     head = grad_logits.astype(BF)
     rest = (grad_logits - head.astype(F32)).astype(BF)
     acc_router[...] += dot(rows_t, jnp.concatenate([head, rest], axis=1))
-    out_ref[0] = (chosen * acc_out[...]).astype(BF)
-    dx_ref[0] = (
-        acc_dx[...] + dot(jnp.concatenate([head, head], axis=1), back_ref[...])
-    ).astype(BF)
+    out = (chosen * acc_out[...]).astype(BF)
+    grad_rows = (acc_dx[...] + dot(jnp.concatenate([head, head], axis=1), back_ref[...])).astype(BF)
+    if part:
+        refs[0][0] = grad_rows
+        late = refs[1].shape[1] - capacity
+        if late:
+            refs[1][0, :late, :] = before_ref[0]
+        refs[1][0, late:, :] = out
+    else:
+        early = refs[0].shape[1] - capacity
+        refs[0][0, :capacity, :] = grad_rows
+        refs[0][0, capacity:, :] = out[:early]
+        refs[1][0] = out[early:]
 
     @pl.when(step == pl.num_programs(0) - 1)
     def _():
         grouter_ref[...] = acc_router[:, :LANES] + acc_router[:, LANES:]
-        if not ends:
+        if not begun:
             grad_refs[0][...] = acc_up[...].astype(BF)
             grad_refs[1][...] = acc_down[...].astype(BF)
             return
@@ -464,41 +509,38 @@
                 )
 
 
-def expert_pass(part, mine, rows, grads, w_up, w_down, router, router_back, experts, capacity, shards, own, given, outs):
+def expert_pass(part, mine, rows, grads, weights, early, experts, capacity, shards, own, given, before, taken):
     (rows, rows_at), (grads, grads_at) = rows, grads
+    w_up, w_down, router, router_back = weights
     sources, _, width = rows.shape
-    local, _, units = w_up.shape
-    ends = given is not None
+    units = w_up.shape[2]
     source = lambda step, mine_ref: (mine_ref[1] + (0 if own else 1) + step) % sources
-    block = lambda at: pl.BlockSpec(
-        (1, capacity, width), lambda step, mine_ref: (source(step, mine_ref), at, 0)
-    )
-    only = whole((1, capacity, width))
+    block = lambda tall, at: pl.BlockSpec(
+        (1, tall, width), lambda step, mine_ref: (source(step, mine_ref), at, 0)
+    )
     weight = lambda shape: pl.BlockSpec((None,) + shape[1:], lambda *_: (part, 0, 0))
-    grad_shape = (shards, width // shards * 2, units)
-    given = list(given or ())
-    taken = [] if outs is None else [outs]
-    if own:
+    late = capacity - early
+    talls = [capacity, late + capacity] if part else [capacity + early, late]
+    sent = [jax.ShapeDtypeStruct((sources, tall, width), BF) for tall in talls]
+    sent_specs = [block(tall, 0) for tall in talls]
+    if part and own:
         sent = [jax.ShapeDtypeStruct((1, capacity, width), BF)] * 2
-        sent_specs = [only, only]
-    else:
-        sent = [
-            jax.ShapeDtypeStruct((sources, capacity, width), BF),
-            jax.ShapeDtypeStruct((sources, local * capacity, width), BF),
-        ]
-        sent_specs = [block(0), block(part)]
-    if ends:
-        sums = [jax.ShapeDtypeStruct(grad_shape, BF)]
+        sent_specs = [whole((1, capacity, width))] * 2
+    if given:
+        sums = [jax.ShapeDtypeStruct((shards, width // shards * 2, units), BF)]
     else:
         sums = [jax.ShapeDtypeStruct((width, units), BF)] * 2
     sums.append(jax.ShapeDtypeStruct((width, LANES), F32))
     steps = 1 if own else sources - 1
+    joins = bool(part) and not own
+    more = list(given) + ([before] if joins else [])
+    more_specs = [whole(array.shape) for array in given] + ([block(late, 0)] if joins else [])
+    skip = 7 + len(more)
 
     def body(*refs):
-        refs = list(refs)
-        if taken:
-            del refs[7 + len(given)]
-        expert_kernel(experts, min(FCUT, units), bool(given), ends, *refs)
+        expert_kernel(
+            experts, min(FCUT, units), bool(given), part, joins, *refs[:skip], *refs[skip + len(taken) :]
+        )
 
     return pl.pallas_call(
         body,
@@ -507,8 +549,8 @@
             grid=(steps,),
             in_specs=[
                 weight(w_up.shape), weight(w_down.shape), whole(router.shape),
-                whole(router_back.shape), block(rows_at), block(grads_at),
-            ] + [whole(array.shape) for array in given] + [pl.BlockSpec(memory_space=pl.ANY)] * len(taken),
+                whole(router_back.shape), block(capacity, rows_at), block(capacity, grads_at),
+            ] + more_specs + [pl.BlockSpec(memory_space=pl.ANY)] * len(taken),
             out_specs=sent_specs + [whole(array.shape) for array in sums],
             scratch_shapes=[
                 pltpu.VMEM((width, units), F32),
@@ -519,23 +561,22 @@
             ],
         ),
         out_shape=sent + sums,
-        input_output_aliases={7 + len(given): 1} if taken else {},
+        input_output_aliases={skip + at: to for at, to in enumerate(taken)},
         compiler_params=params(),
         cost_estimate=cost(
             20 * steps * capacity * width * units, 30e6, 2 * steps * capacity * units
         ),
         name="expert_own" if own else "expert_others",
-    )(mine, w_up, w_down, router, router_back, rows, grads, *given, *taken)
+    )(mine, *weights, rows, grads, *more, *taken.values())
 
 
 def back_kernel(
-    window, groups, local, starts_ref, here_ref, index_ref, hidden_ref, tok_ref, dy_ref, qkv_ref,
+    window, groups, starts_ref, here_ref, index_ref, hidden_ref, tok_ref, dy_ref, qkv_ref,
     probs_ref, mixed_ref, gain_one_ref, qkv_w_ref, proj_w_ref, gain_two_ref, *refs,
 ):
-    bufs, own_bufs = refs[:local], refs[local : 2 * local]
-    router_refs = refs[2 * local : 3 * local]
-    ghid_ref, dqkv_ref, own_ref, sent_ref = refs[3 * local : -7]
-    wins, acc, compact, padded, acc_qkv, acc_proj, acc_gain = refs[-7:]
+    bufs, own_bufs, router_refs = refs[:2], [None, refs[2]], refs[3:5]
+    ghid_ref, dqkv_ref, own_ref, sent_ref = refs[5:-9]
+    wins, acc, compact, padded, acc_qkv, acc_proj, acc_gain, dscores, dscores_low = refs[-9:]
     experts = starts_ref.shape[0]
     step = pl.program_id(0)
     width = tok_ref.shape[1]
@@ -568,12 +609,25 @@
             key_cols = slice(width + LANES * two, width + LANES * (two + 1))
             value_cols = slice(2 * width + LANES * two, 2 * width + LANES * (two + 1))
             at = (pair * (width // LANES) + two) * 2 * PAIR_PAD
+            dscores[at : at + 2 * PAIR_PAD, :] = dot_rt(
+                two_heads(grad_mixed[rows, cols], low), qkv_ref[rows, value_cols]
+            )
+    for pair in range(BLOCK_PAIRS):
+        each = 2 * PAIR_PAD * (width // LANES)
+        part = slice(each * pair, each * (pair + 1))
+        wide, grad_probs = probs_ref[part, :].astype(F32), dscores[part, :]
+        meet = jnp.sum(wide * grad_probs, axis=-1, keepdims=True)
+        dscores_low[part, :] = (wide * (grad_probs - meet) * factor_qk).astype(BF)
+    for pair in range(BLOCK_PAIRS):
+        rows = slice(PAIR_PAD * pair, PAIR_PAD * (pair + 1))
+        for two in range(width // LANES):
+            cols = slice(LANES * two, LANES * (two + 1))
+            key_cols = slice(width + LANES * two, width + LANES * (two + 1))
+            value_cols = slice(2 * width + LANES * two, 2 * width + LANES * (two + 1))
+            at = (pair * (width // LANES) + two) * 2 * PAIR_PAD
             probs = probs_ref[at : at + 2 * PAIR_PAD, :]
-            wide = probs.astype(F32)
             grad_out = two_heads(grad_mixed[rows, cols], low)
-            grad_probs = dot_rt(grad_out, qkv_ref[rows, value_cols])
-            meet = jnp.sum(wide * grad_probs, axis=-1, keepdims=True)
-            grad_scores = (wide * (grad_probs - meet) * factor_qk).astype(BF)
+            grad_scores = dscores_low[at : at + 2 * PAIR_PAD, :]
             grad_query = one_row(dot(grad_scores, qkv_ref[rows, key_cols]), low)
             dqkv_ref[rows, cols] = grad_query.astype(BF)
             dqkv_ref[rows, key_cols] = dot_lt(
@@ -618,7 +672,7 @@
     return 16 * -(-(experts + 2) // 16)
 
 
-def back(starts, here, groups, index, hidden, tokens, dy, qkv, probs, mixed, gain_one, w_qkv, w_proj, gain_two, parts, own, routers, capacity):
+def back(starts, here, groups, index, hidden, tokens, dy, qkv, probs, mixed, gain_one, w_qkv, w_proj, gain_two, downs, own, routers, capacity):
     count, width = tokens.shape
     blocks = count // BLOCK
     experts = starts.shape[0]
@@ -629,7 +683,7 @@
     sum_shape = (2 * width + small_rows(experts), width)
     flops = 2 * blocks * BLOCK_PAD * width * (8 * width + 10 * PAIR_PAD)
     return pl.pallas_call(
-        functools.partial(back_kernel, window, groups, len(parts)),
+        functools.partial(back_kernel, window, groups),
         grid_spec=pltpu.PrefetchScalarGridSpec(
             num_scalar_prefetch=2,
             grid=(blocks,),
@@ -638,7 +692,8 @@
                 row((BLOCK_PAD, 3 * width)), row((probs.shape[0] // blocks, PAIR_PAD)),
                 row((BLOCK_PAD, width)),
                 whole((1, width)), whole(w_qkv.shape), whole(w_proj.shape), whole((1, width)),
-            ] + back_specs(parts, own, capacity) + [whole((width, LANES))] * len(routers),
+            ] + [whole((downs[0].shape[0], capacity, width))] * 2 + [whole(own.shape)]
+            + [whole((width, LANES))] * 2,
             out_specs=[
                 row((BLOCK, width)), row((BLOCK_PAD, 3 * width)), whole(sum_shape), whole(sum_shape),
             ],
@@ -650,6 +705,8 @@
                 pltpu.VMEM(w_qkv.shape, F32),
                 pltpu.VMEM(w_proj.shape, F32),
                 pltpu.VMEM((1, width), F32),
+                pltpu.VMEM((probs.shape[0] // blocks, PAIR_PAD), F32),
+                pltpu.VMEM((probs.shape[0] // blocks, PAIR_PAD), BF),
             ],
         ),
         out_shape=[
@@ -659,11 +716,11 @@
             jax.ShapeDtypeStruct(sum_shape, BF),
         ],
         compiler_params=params(),
-        cost_estimate=cost(flops + 12e9, 40e6),
+        cost_estimate=cost(1e12, 4000e6),
         name="back",
     )(
         starts, here, index, hidden, tokens, dy, qkv, probs, mixed, gain_one[None, :], w_qkv,
-        w_proj, gain_two[None, :], *[array for array, _ in parts], *own, *routers,
+        w_proj, gain_two[None, :], *downs, own, *routers,
     )
 
 
@@ -788,7 +845,7 @@
         came = [jump(part, axis, scale * far) for far, part in enumerate(sent, 1)]
         work = beside[len(done)](own)
         done.append(work)
-        return [own] + list(after(tuple(came), work))
+        return [own] + list(after(tuple(came), jax.tree.leaves(work)[0]))
 
     half = merge([own, jump(sent, "dp", 1)], sides, extra, False)
     flat = merge(spread(half[0], half[1:], "expert", 1), layers, extra, False)
@@ -804,6 +861,7 @@
 ):
     count, width = tokens.shape
     local = w_in.shape[0]
+    assert local == 2
     owners = lax.axis_size("expert")
     shards = lax.axis_size("dp")
     experts = local * owners
@@ -838,41 +896,43 @@
     gap = ((0, 0), (0, LANES - experts))
     router = jnp.concatenate([jnp.pad(head, gap), jnp.pad(rest, gap)], axis=1)
     router_back = jnp.concatenate([jnp.pad(head, gap).T, jnp.pad(rest, gap).T], axis=0)
-    downs, own_dx, own_out, sums, outs, routers = [], [], [], [], None, []
-    for part in range(local):
+    early = 16 * (capacity // 32)
+    weights = (w_in, w_eout, router, router_back)
+
+    def one(part, own, given, before, *taken):
         mine = jnp.stack([me * local + part, me]).astype(jnp.int32)
-        final = part == local - 1
-        one = lambda own, given, outs: expert_pass(
-            part, mine, *(kept if own else arrived)[part], w_in, w_eout, router, router_back,
-            experts, capacity, shards, own, given, outs,
+        came = (kept if own else arrived)[part]
+        taken = dict(zip(range(2 - len(taken), 2), taken))
+        return expert_pass(
+            part, mine, *came, weights, early, experts, capacity, shards, own, given, before, taken
         )
-        if final:
-            dx, outs, *given = one(False, None, outs)
-            own_parts = list(one(True, given, None))
-        else:
-            own_parts = list(one(True, None, None))
-            dx, outs, *own_parts[2:] = one(False, own_parts[2:], outs)
-        got = swap(after(dx, got))
-        downs.append((got, 0))
-        own_dx.append(own_parts[0])
-        own_out.append(own_parts[1])
-        grad, router_part = own_parts[2:]
+
+    def reduce(grad):
         grad = grad.reshape(shards * grad.shape[1], grad.shape[2])
-        sums.append(lax.psum_scatter(grad, "dp", scatter_dimension=0, tiled=True))
-        routers.append(router_part)
-    outs = swap(after(outs, got))
+        return lax.psum_scatter(grad, "dp", scatter_dimension=0, tiled=True)
+
+    head, tail, *given = one(0, True, [], None)
+    head, tail, grad, router_first = one(0, False, given, None, head, tail)
+    sums, tail_first = [reduce(grad)], tail
+    head = swap(after(head, got))
+    down, tail, *given = one(1, False, [], tail_first)
+    down = swap(after(down, head))
+    own_down, own_out, grad, router_second = one(1, True, given, None)
+    sums.append(reduce(grad))
+    tail = swap(after(tail, down))
     grad_hidden, dqkv, own, sent = back(
         starts, here, groups, index, hidden, tokens, grad_out, qkv, probs, mixed, gain_one,
-        w_qkv, w_proj, gain_two, downs, own_dx, routers, capacity,
-    )
-    sent = after(sent, outs)
+        w_qkv, w_proj, gain_two, [head, down], own_down, [router_first, router_second], capacity,
+    )
+    sent = after(sent, tail)
     blocks = count // BLOCK
     cuts = [0, blocks // 3, 2 * blocks // 3, blocks]
     grad_tokens = [None]
 
+    tall = width // shards
+
     def make_top(tie):
-        parts = [(outs, part) for part in range(local)]
-        return top(starts, here, index, after(hidden, tie), parts, own_out, capacity)
+        return top(starts, here, index, after(hidden, tie), head, tail, tail_first, own_out, early, capacity)
 
     def make_last(turn, tie):
         grad_tokens.append(
@@ -881,18 +941,20 @@
                 tokens, gain_one, w_qkv,
             )
         )
-        return grad_tokens[-1]
+        if turn < 2:
+            return grad_tokens[-1]
+        parts = sums
+        grad_in = jnp.stack([part[:tall] for part in parts]).astype(F32)
+        grad_eout = jnp.stack(
+            [part[tall:].reshape(tall, -1, width).transpose(1, 0, 2).reshape(-1, width) for part in parts]
+        ).astype(F32)
+        return grad_tokens[-1], grad_in, grad_eout
 
     own, other, small, done = sum_over_all(
         own, sent, groups, small_rows(experts), [make_top] + [functools.partial(make_last, turn) for turn in range(3)]
     )
-    block_out, grad_tokens = done[0], done[3]
+    block_out, (grad_tokens, grad_in, grad_eout) = done[0], done[3]
     grad_qkv, grad_proj = lay(groups, here, own, other)
-    tall = width // shards
-    grad_in = jnp.stack([part[:tall] for part in sums]).astype(F32)
-    grad_eout = jnp.stack(
-        [part[tall:].reshape(tall, -1, width).transpose(1, 0, 2).reshape(-1, width) for part in sums]
-    ).astype(F32)
     return (
         block_out,
         grad_tokens,

time: 386 us -> 372 us (0.964)
  Pallas kernels: 266 us -> 243 us
  waiting for transfers between devices: 33.6 us -> 43.4 us
    pallas_call x2, Pallas kernels: 70.9 us -> 50.7 us  [the longest x1 37.6 us: back(): pl.pallas_call(functools.partial(back_kernel, window, groups), grid_spec=...]
    all_to_all x6, waiting for transfers between devices: 26.6 us -> 37.6 us  [swap(): lax.all_to_all(sent, 'expert', split_axis=0, concat_axis=0, tiled=True)]
  transfers between devices with their start and end apart: 22 -> 22, of which waited for: 8 -> 9; matrix products, arithmetic and copies ran while one was open for 3% -> 3% of each run, Pallas kernels for 66% -> 62%
where the time goes in v4:
time: 372 us; the launch traced here: 366 us
  Pallas kernels  243 us (65%)
  starting transfers between devices  46.2 us (12%)
  waiting for transfers between devices  43.4 us (12%)
  between operations  14.8 us (4%)
  local copies, waits for them, and re-layouts  11.8 us (3%)
  other arithmetic  7.32 us (2%)
    pallas_call x4, Pallas kernels, expert_pass(): pl.pallas_call(body, grid_spec=pltpu.PrefetchScalarGridSpec(num_scalar_pr...  115 us
    all_to_all x6, waiting for transfers between devices, swap(): lax.all_to_all(sent, 'expert', split_axis=0, concat_axis=0, tiled=True)  37.6 us
    pallas_call x1, Pallas kernels, back(): pl.pallas_call(functools.partial(back_kernel, window, groups), grid_spec=...  37.6 us
    all_to_all x6, starting transfers between devices, swap(): lax.all_to_all(sent, 'expert', split_axis=0, concat_axis=0, tiled=True)  29.7 us
    pallas_call x3, Pallas kernels, dispatch(): pl.pallas_call(functools.partial(dispatch_kernel, window, capacity, plan,...  24.8 us
    pallas_call x1, Pallas kernels, attend(): pl.pallas_call(attend_kernel, grid=(blocks,), in_specs=[row((BLOCK, width...  20.7 us
    pallas_call x3, Pallas kernels, last(): pl.pallas_call(last_kernel, grid=(high - low,), in_specs=[row((BLOCK_PAD,...  16.9 us
    ppermute x14, starting transfers between devices, jump(): return lax.ppermute(value, axis, [(at, at ^ far) for at in range(size)])  15.9 us
  transfers between devices with their start and end apart: 22, of which 9 were waited for; matrix products, arithmetic and copies ran while one was open for 3% of the time, Pallas kernels for 62%

profile of v4, /device:TPU:0, one launch (start us, length us, event | category | flops | bytes accessed | tf_op | source)
XLA Modules:
  0.0 366.2 jit_solution(1474944817609767780)
XLA Ops:
  9.4 4.0 %places.1 = (s32[6,2,392]{2,1,0:T(2,128)}, s32[8,128]{1,0:T(8,128)}) custom-call(s32[8,1]{1,0:T(8,128)} %reshape.86.ids_ref, s32[6,4,392]{2,1,0:T(4,128)} %bitcast.69), custom_call_target="tpu_custom_call" | custom-call | flops 100000000 | bytes 100000 | tf_op jit(solution)/shard_map/places/pallas_call | solution.py:217
  13.4 7.4 %dispatch.3.refs_6_ = bf16[4,624,512]{2,1,0:T(8,128)(2,1)} custom-call(s32[8,128]{1,0:T(8,128)} %get-tuple-element.74.starts_ref, s32[6,2,392]{2,1,0:T(2,128)} %get-tuple-element.75.index_ref, bf16[2352,512]{1,0:T(8,128)(2,1)} %dy_ref.1), custom_call_target="tpu_custom_call" | custom-call | flops 6000000000 | bytes 8000000 | tf_op jit(solution)/shard_map/dispatch/pallas_call | solution.py:299
  20.8 5.3 %all-to-all-start = ((bf16[4,624,512]{2,1,0:T(8,128)(2,1)}), bf16[4,624,512]{2,1,0:T(8,128)(2,1)}, u32[]{:S(2)}, u32[]{:S(2)}) async-start(bf16[4,624,512]{2,1,0:T(8,128)(2,1)} %dispatch.3.refs_6_), calls=%async_computation | async-start | bytes 5111808 | tf_op jit(solution)/shard_map/all_to_all | solution.py:876
  26.2 20.7 %attend.1 = (f32[2352,512]{1,0:T(8,128)}, bf16[2352,512]{1,0:T(8,128)(2,1)}, bf16[2688,1536]{1,0:T(8,128)(2,1)}, bf16[21504,112]{1,0:T(8,128)(2,1)}, bf16[2688,512]{1,0:T(8,128)(2,1)}) custom-call(bf16[2352,512]{1,0:T(8,128)(2,1)} %tok_ref.8, f32[1,512]{1,0:T(1,128)} %bitcast.70, bf16[512,1536]{1,0:T(8,128)(2,1)} %qkv_w_ref.9, bf16[512,512]{1,0:T(8,128)(2,1)} %proj_w_ref.3, ...), custom_call_target="tpu_custom_call" | custom-call | flops 6870269952 | bytes 30000000 | tf_op jit(solution)/shard_map/attend/pallas_call | solution.py:158
  46.9 7.5 %dispatch.4.refs_5_ = bf16[4,624,512]{2,1,0:T(8,128)(2,1)} custom-call(s32[8,128]{1,0:T(8,128)} %get-tuple-element.74.starts_ref, s32[6,2,392]{2,1,0:T(2,128)} %get-tuple-element.75.index_ref, bf16[2352,512]{1,0:T(8,128)(2,1)} %get-tuple-element.89.refs_0_), custom_call_target="tpu_custom_call" | custom-call | flops 6000000000 | bytes 8000000 | tf_op jit(solution)/shard_map/dispatch/pallas_call | solution.py:299
  56.9 4.8 %all-to-all-start.1 = ((bf16[4,624,512]{2,1,0:T(8,128)(2,1)}), bf16[4,624,512]{2,1,0:T(8,128)(2,1)}, u32[]{:S(2)}, u32[]{:S(2)}) async-start(bf16[4,624,512]{2,1,0:T(8,128)(2,1)} %dispatch.4.refs_5_), calls=%async_computation.1 | async-start | bytes 5111808 | tf_op jit(solution)/shard_map/all_to_all | solution.py:876
  63.8 9.9 %dispatch.5.refs_5_.refs_6_ = bf16[4,1248,512]{2,1,0:T(8,128)(2,1)} custom-call(s32[8,128]{1,0:T(8,128)} %get-tuple-element.74.starts_ref, s32[6,2,392]{2,1,0:T(2,128)} %get-tuple-element.75.index_ref, bf16[2352,512]{1,0:T(8,128)(2,1)} %get-tuple-element.89.refs_0_, bf16[2352,512]{1,0:T(8,128)(2,1)} %dy_ref.1), custom_call_target="tpu_custom_call" | custom-call | flops 6000000000 | bytes 8000000 | tf_op jit(solution)/shard_map/dispatch/pallas_call | solution.py:299
  73.8 15.5 %expert_own.2 = (bf16[4,928,512]{2,1,0:T(8,128)(2,1)}, bf16[4,320,512]{2,1,0:T(8,128)(2,1)}, bf16[512,2048]{1,0:T(8,128)(2,1)}, bf16[512,2048]{1,0:T(8,128)(2,1)}, f32[512,128]{1,0:T(8,128)}) custom-call(s32[2]{0:T(128)} %pad_add_fusion.2.refs_0_, bf16[2,512,2048]{2,1,0:T(8,128)(2,1)} %refs_1_.9, bf16[2,2048,512]{2,1,0:T(8,128)(2,1)} %refs_2_.7, ...), custom_call_target="tpu_custom_call" | custom-call | flops 13086228480 | bytes 30000000 | tf_op jit(solution)/shard_map/expert_own/pallas_call | solution.py:545
  91.8 5.0 %all-to-all-start.2 = ((bf16[4,1248,512]{2,1,0:T(8,128)(2,1)}), bf16[4,1248,512]{2,1,0:T(8,128)(2,1)}, u32[]{:S(2)}, u32[]{:S(2)}) async-start(bf16[4,1248,512]{2,1,0:T(8,128)(2,1)} %dispatch.5.refs_5_.refs_6_), calls=%async_computation.2 | async-start | bytes 10223616 | tf_op jit(solution)/shard_map/all_to_all | solution.py:876
  97.3 41.3 %expert_others.2 = (bf16[4,928,512]{2,1,0:T(8,128)(2,1)}, bf16[4,320,512]{2,1,0:T(8,128)(2,1)}, bf16[8,128,2048]{2,1,0:T(8,128)(2,1)}, f32[512,128]{1,0:T(8,128)}) custom-call(s32[2]{0:T(128)} %pad_add_fusion.2.refs_0_, bf16[2,512,2048]{2,1,0:T(8,128)(2,1)} %refs_1_.9, ...), custom_call_target="tpu_custom_call", output_to_operand_aliasing={{0}: (10, {}), {1}: (11, {})} | custom-call | flops 39258685440 | bytes 30000000 | tf_op jit(solution)/shard_map/expert_others/pallas_call | solution.py:545
  139.3 15.0 %all-to-all-done.2.refs_5_.refs_6_ = bf16[4,1248,512]{2,1,0:T(8,128)(2,1)} async-done(((bf16[4,1248,512]{2,1,0:T(8,128)(2,1)}), bf16[4,1248,512]{2,1,0:T(8,128)(2,1)}, u32[]{:S(2)}, u32[]{:S(2)}) %all-to-all-start.2) | async-done | bytes 5111840 | tf_op jit(solution)/shard_map/all_to_all | solution.py:876
  154.3 5.0 %all-to-all-start.3 = ((bf16[4,928,512]{2,1,0:T(8,128)(2,1)}), bf16[4,928,512]{2,1,0:T(8,128)(2,1)}, u32[]{:S(2)}, u32[]{:S(2)}) async-start(bf16[4,928,512]{2,1,0:T(8,128)(2,1)} %get-tuple-element.91), calls=%async_computation.3 | async-start | bytes 7602176 | tf_op jit(solution)/shard_map/all_to_all | solution.py:876
  159.3 40.1 %expert_others.3 = (bf16[4,624,512]{2,1,0:T(8,128)(2,1)}, bf16[4,944,512]{2,1,0:T(8,128)(2,1)}, bf16[512,2048]{1,0:T(8,128)(2,1)}, bf16[512,2048]{1,0:T(8,128)(2,1)}, f32[512,128]{1,0:T(8,128)}) custom-call(s32[2]{0:T(128)} %pad_add_fusion.3.refs_0_, bf16[2,512,2048]{2,1,0:T(8,128)(2,1)} %refs_1_.9, bf16[2,2048,512]{2,1,0:T(8,128)(2,1)} %refs_2_.7, ...), custom_call_target="tpu_custom_call" | custom-call | flops 39258685440 | bytes 30000000 | tf_op jit(solution)/shard_map/expert_others/pallas_call | solution.py:545
  202.0 4.6 %all-to-all-start.4 = ((bf16[4,624,512]{2,1,0:T(8,128)(2,1)}), bf16[4,624,512]{2,1,0:T(8,128)(2,1)}, u32[]{:S(2)}, u32[]{:S(2)}) async-start(bf16[4,624,512]{2,1,0:T(8,128)(2,1)} %get-tuple-element.94), calls=%async_computation.4 | async-start | bytes 5111808 | tf_op jit(solution)/shard_map/all_to_all | solution.py:876
  208.9 17.6 %expert_own.3 = (bf16[1,624,512]{2,1,0:T(8,128)(2,1)}, bf16[1,624,512]{2,1,0:T(8,128)(2,1)}, bf16[8,128,2048]{2,1,0:T(8,128)(2,1)}, f32[512,128]{1,0:T(8,128)}) custom-call(s32[2]{0:T(128)} %pad_add_fusion.3.refs_0_, bf16[2,512,2048]{2,1,0:T(8,128)(2,1)} %refs_1_.9, bf16[2,2048,512]{2,1,0:T(8,128)(2,1)} %refs_2_.7, bf16[512,256]{1,0:T(8,128)(2,1)} %copy.36.refs_3_, ...), custom_call_target="tpu_custom_call" | custom-call | flops 13086228480 | bytes 30000000 | tf_op jit(solution)/shard_map/expert_own/pallas_call | solution.py:545
  226.6 9.3 %all-to-all-done.4.refs_1_ = bf16[4,624,512]{2,1,0:T(8,128)(2,1)} async-done(((bf16[4,624,512]{2,1,0:T(8,128)(2,1)}), bf16[4,624,512]{2,1,0:T(8,128)(2,1)}, u32[]{:S(2)}, u32[]{:S(2)}) %all-to-all-start.4) | async-done | bytes 2555936 | tf_op jit(solution)/shard_map/all_to_all | solution.py:876
  235.8 5.0 %all-to-all-start.5 = ((bf16[4,944,512]{2,1,0:T(8,128)(2,1)}), bf16[4,944,512]{2,1,0:T(8,128)(2,1)}, u32[]{:S(2)}, u32[]{:S(2)}) async-start(bf16[4,944,512]{2,1,0:T(8,128)(2,1)} %get-tuple-element.104), calls=%async_computation.5 | async-start | bytes 7733248 | tf_op jit(solution)/shard_map/all_to_all | solution.py:876
  240.9 37.6 %back.1 = (f32[2352,512]{1,0:T(8,128)}, bf16[2688,1536]{1,0:T(8,128)(2,1)}, bf16[1040,512]{1,0:T(8,128)(2,1)}, bf16[1040,512]{1,0:T(8,128)(2,1)}) custom-call(s32[8,128]{1,0:T(8,128)} %get-tuple-element.74.starts_ref, s32[3]{0:T(128)} %pad_add_fusion.1.here_ref, s32[2352,2]{1,0:T(8,128)} %bitcast.56, f32[2352,512]{1,0:T(8,128)} %get-tuple-element.107.hidden_ref, ...), custom_call_target="tpu_custom_call" | custom-call | flops 999999995904 | bytes 4000000000 | tf_op jit(solution)/shard_map/back/pallas_call | solution.py:685
  278.5 5.8 %all-to-all-done.5.tail_ref = bf16[4,944,512]{2,1,0:T(8,128)(2,1)} async-done(((bf16[4,944,512]{2,1,0:T(8,128)(2,1)}), bf16[4,944,512]{2,1,0:T(8,128)(2,1)}, u32[]{:S(2)}, u32[]{:S(2)}) %all-to-all-start.5) | async-done | bytes 3866656 | tf_op jit(solution)/shard_map/all_to_all | solution.py:876
  294.2 13.1 %top.1 = bf16[2352,512]{1,0:T(8,128)(2,1)} custom-call(s32[8,128]{1,0:T(8,128)} %get-tuple-element.74.starts_ref, s32[3]{0:T(128)} %pad_add_fusion.1.here_ref, s32[2352,2]{1,0:T(8,128)} %bitcast.57, f32[2352,512]{1,0:T(8,128)} %get-tuple-element.107.hidden_ref, bf16[4,928,512]{2,1,0:T(8,128)(2,1)} %all-to-all-done.3.refs_0_.head_ref, ...), custom_call_target="tpu_custom_call" | custom-call | flops 6000000000 | bytes 12000000 | tf_op jit(solution)/shard_map/top/pallas_call | solution.py:386
  315.2 5.6 %last.3.refs_0_ = f32[2352,512]{1,0:T(8,128)} custom-call(bf16[2688,1536]{1,0:T(8,128)(2,1)} %get-tuple-element.130.dqkv_ref, f32[2352,512]{1,0:T(8,128)} %get-tuple-element.121.ghid_ref, bf16[2352,512]{1,0:T(8,128)(2,1)} %tok_ref.8, f32[1,512]{1,0:T(1,128)} %bitcast.72, bf16[512,1536]{1,0:T(8,128)(2,1)} %qkv_w_ref.9), custom_call_target="tpu_custom_call" | custom-call | flops 1409286144 | bytes 20000000 | tf_op jit(solution)/shard_map/last/pallas_call | solution.py:739
  328.2 5.6 %last.4.refs_0_ = f32[2352,512]{1,0:T(8,128)} custom-call(bf16[2688,1536]{1,0:T(8,128)(2,1)} %get-tuple-element.130.dqkv_ref, f32[2352,512]{1,0:T(8,128)} %get-tuple-element.121.ghid_ref, bf16[2352,512]{1,0:T(8,128)(2,1)} %tok_ref.8, f32[1,512]{1,0:T(1,128)} %bitcast.73, bf16[512,1536]{1,0:T(8,128)(2,1)} %qkv_w_ref.9, ...), custom_call_target="tpu_custom_call", output_to_operand_aliasing={{}: (5, {})} | custom-call | flops 1409286144 | bytes 20000000 | tf_op jit(solution)/shard_map/last/pallas_call | solution.py:739
  338.5 5.7 %last.5 = f32[2352,512]{1,0:T(8,128)} custom-call(bf16[2688,1536]{1,0:T(8,128)(2,1)} %get-tuple-element.130.dqkv_ref, f32[2352,512]{1,0:T(8,128)} %get-tuple-element.121.ghid_ref, bf16[2352,512]{1,0:T(8,128)(2,1)} %tok_ref.8, f32[1,512]{1,0:T(1,128)} %bitcast.74, bf16[512,1536]{1,0:T(8,128)(2,1)} %qkv_w_ref.9, ...), custom_call_target="tpu_custom_call", output_to_operand_aliasing={{}: (5, {})} | custom-call | flops 1409286144 | bytes 20000000 | tf_op jit(solution)/shard_map/last/pallas_call | solution.py:739
  354.3 4.5 %lay.1 = (f32[512,1536]{1,0:T(8,128)}, f32[512,512]{1,0:T(8,128)}) custom-call(s32[3]{0:T(128)} %pad_add_fusion.1.here_ref, bf16[16,64,512]{2,1,0:T(8,128)(2,1)} %bitcast.53, bf16[16,64,512]{2,1,0:T(8,128)(2,1)} %collective-permute-done.13.other_ref), custom_call_target="tpu_custom_call" | custom-call | flops 1000000 | bytes 8000000 | tf_op jit(solution)/shard_map/lay/pallas_call | solution.py:774
  (97 shorter events, 55.4 us)
Async XLA Ops:
  20.8 36.0 %all-to-all-start = ((bf16[4,624,512]{2,1,0:T(8,128)(2,1)}), bf16[4,624,512]{2,1,0:T(8,128)(2,1)}, u32[]{:S(2)}, u32[]{:S(2)}) async-start(bf16[4,624,512]{2,1,0:T(8,128)(2,1)} %dispatch.3.refs_6_), calls=%async_computation | async-start | bytes 5111808 | tf_op jit(solution)/shard_map/all_to_all | solution.py:876
  56.9 35.0 %all-to-all-start.1 = ((bf16[4,624,512]{2,1,0:T(8,128)(2,1)}), bf16[4,624,512]{2,1,0:T(8,128)(2,1)}, u32[]{:S(2)}, u32[]{:S(2)}) async-start(bf16[4,624,512]{2,1,0:T(8,128)(2,1)} %dispatch.4.refs_5_), calls=%async_computation.1 | async-start | bytes 5111808 | tf_op jit(solution)/shard_map/all_to_all | solution.py:876
  91.8 62.5 %all-to-all-start.2 = ((bf16[4,1248,512]{2,1,0:T(8,128)(2,1)}), bf16[4,1248,512]{2,1,0:T(8,128)(2,1)}, u32[]{:S(2)}, u32[]{:S(2)}) async-start(bf16[4,1248,512]{2,1,0:T(8,128)(2,1)} %dispatch.5.refs_5_.refs_6_), calls=%async_computation.2 | async-start | bytes 10223616 | tf_op jit(solution)/shard_map/all_to_all | solution.py:876
  96.9 240.6 %reduce-scatter.3.cloned.1.call-start = ((), (), s32[]{:S(2)}) async-start(), calls=%async_computation.8 | async-start | bytes 4718592 | tf_op jit(solution)/shard_map/reduce_scatter | solution.py:912
  154.3 47.7 %all-to-all-start.3 = ((bf16[4,928,512]{2,1,0:T(8,128)(2,1)}), bf16[4,928,512]{2,1,0:T(8,128)(2,1)}, u32[]{:S(2)}, u32[]{:S(2)}) async-start(bf16[4,928,512]{2,1,0:T(8,128)(2,1)} %get-tuple-element.91), calls=%async_computation.3 | async-start | bytes 7602176 | tf_op jit(solution)/shard_map/all_to_all | solution.py:876
  199.4 7.5 %copy-start.13 = (s32[6,2,392]{2,1,0:T(2,128)S(1)}, s32[6,2,392]{2,1,0:T(2,128)}, u32[]{:S(2)}) copy-start(s32[6,2,392]{2,1,0:T(2,128)} %get-tuple-element.75.index_ref) | copy-start | bytes 56452
  202.0 33.9 %all-to-all-start.4 = ((bf16[4,624,512]{2,1,0:T(8,128)(2,1)}), bf16[4,624,512]{2,1,0:T(8,128)(2,1)}, u32[]{:S(2)}, u32[]{:S(2)}) async-start(bf16[4,624,512]{2,1,0:T(8,128)(2,1)} %get-tuple-element.94), calls=%async_computation.4 | async-start | bytes 5111808 | tf_op jit(solution)/shard_map/all_to_all | solution.py:876
  206.5 142.6 %reduce-scatter.5.cloned.1.call-start = ((), (), s32[]{:S(2)}) async-start(), calls=%async_computation.9 | async-start | bytes 4718592 | tf_op jit(solution)/shard_map/reduce_scatter | solution.py:912
  235.8 48.4 %all-to-all-start.5 = ((bf16[4,944,512]{2,1,0:T(8,128)(2,1)}), bf16[4,944,512]{2,1,0:T(8,128)(2,1)}, u32[]{:S(2)}, u32[]{:S(2)}) async-start(bf16[4,944,512]{2,1,0:T(8,128)(2,1)} %get-tuple-element.104), calls=%async_computation.5 | async-start | bytes 7733248 | tf_op jit(solution)/shard_map/all_to_all | solution.py:876
  284.2 2.9 collective-permute-start
  290.7 16.6 %collective-permute-start.1 = (bf16[272,512]{1,0:T(8,128)(2,1)}, bf16[272,512]{1,0:T(8,128)(2,1)S(1)}, u32[]{:S(2)}, u32[]{:S(2)}) collective-permute-start(bf16[272,512]{1,0:T(8,128)(2,1)} %get-tuple-element.110), channel_id=1, source_target_pairs={{0,1},{1,0},{2,3},{3,2},{4,5},{5,4},{6,7},{7,6},{8,9},{9,8},{10,11... | collective-permute-start | bytes 835592 | tf_op jit(solution)/shard_map/ppermute | solution.py:794
  292.1 15.1 %collective-permute-start.2 = (bf16[272,512]{1,0:T(8,128)(2,1)}, bf16[272,512]{1,0:T(8,128)(2,1)S(1)}, u32[]{:S(2)}, u32[]{:S(2)}) collective-permute-start(bf16[272,512]{1,0:T(8,128)(2,1)} %get-tuple-element.111), channel_id=1, source_target_pairs={{0,2},{1,3},{2,0},{3,1},{4,6},{5,7},{6,4},{7,5},{8,10},{9,11},{10,... | collective-permute-start | bytes 835592 | tf_op jit(solution)/shard_map/ppermute | solution.py:794
  292.7 14.6 %collective-permute-start.3 = (bf16[272,512]{1,0:T(8,128)(2,1)}, bf16[272,512]{1,0:T(8,128)(2,1)S(1)}, u32[]{:S(2)}, u32[]{:S(2)}) collective-permute-start(bf16[272,512]{1,0:T(8,128)(2,1)} %get-tuple-element.112), channel_id=1, source_target_pairs={{0,3},{1,2},{2,1},{3,0},{4,7},{5,6},{6,5},{7,4},{8,11},{9,10},{10,... | collective-permute-start | bytes 835592 | tf_op jit(solution)/shard_map/ppermute | solution.py:794
  310.8 10.0 %collective-permute-start.4 = (bf16[80,512]{1,0:T(8,128)(2,1)}, bf16[80,512]{1,0:T(8,128)(2,1)S(1)}, u32[]{:S(2)}, u32[]{:S(2)}) collective-permute-start(bf16[80,512]{1,0:T(8,128)(2,1)} %get-tuple-element.117), channel_id=1, source_target_pairs={{0,8},{4,12},{8,0},{12,4},{16,24},{20,28},{24,16},{28,20},{1,9},{5... | collective-permute-start | bytes 245768 | tf_op jit(solution)/shard_map/ppermute | solution.py:794
  311.6 9.2 %collective-permute-start.5 = (bf16[80,512]{1,0:T(8,128)(2,1)}, bf16[80,512]{1,0:T(8,128)(2,1)S(1)}, u32[]{:S(2)}, u32[]{:S(2)}) collective-permute-start(bf16[80,512]{1,0:T(8,128)(2,1)} %get-tuple-element.118), channel_id=1, source_target_pairs={{0,16},{4,20},{8,24},{12,28},{16,0},{20,4},{24,8},{28,12},{1,17},{... | collective-permute-start | bytes 245768 | tf_op jit(solution)/shard_map/ppermute | solution.py:794
  313.6 7.3 %collective-permute-start.6 = (bf16[80,512]{1,0:T(8,128)(2,1)}, bf16[80,512]{1,0:T(8,128)(2,1)S(1)}, u32[]{:S(2)}, u32[]{:S(2)}) collective-permute-start(bf16[80,512]{1,0:T(8,128)(2,1)} %get-tuple-element.119), channel_id=1, source_target_pairs={{0,24},{4,28},{8,16},{12,20},{16,8},{20,12},{24,0},{28,4},{1,25},{... | collective-permute-start | bytes 245768 | tf_op jit(solution)/shard_map/ppermute | solution.py:794
  323.8 10.0 %copy-start.11 = (bf16[64,512]{1,0:T(8,128)(2,1)S(1)}, bf16[64,512]{1,0:T(8,128)(2,1)}, u32[]{:S(2)}) copy-start(bf16[64,512]{1,0:T(8,128)(2,1)} %get-tuple-element.125) | copy-start | bytes 196612
  323.8 10.0 %collective-permute-start.9 = (bf16[64,512]{1,0:T(8,128)(2,1)}, bf16[64,512]{1,0:T(8,128)(2,1)S(1)}, u32[]{:S(2)}, u32[]{:S(2)}) collective-permute-start(bf16[64,512]{1,0:T(8,128)(2,1)} %get-tuple-element.125), channel_id=1, source_target_pairs={{0,24},{4,28},{8,16},{12,20},{16,8},{20,12},{24,0},{28,4},{1,25},{... | collective-permute-start | bytes 196616 | tf_op jit(solution)/shard_map/ppermute | solution.py:794
  326.0 7.8 %collective-permute-start.8 = (bf16[64,512]{1,0:T(8,128)(2,1)}, bf16[64,512]{1,0:T(8,128)(2,1)S(1)}, u32[]{:S(2)}, u32[]{:S(2)}) collective-permute-start(bf16[64,512]{1,0:T(8,128)(2,1)} %get-tuple-element.125), channel_id=1, source_target_pairs={{0,16},{4,20},{8,24},{12,28},{16,0},{20,4},{24,8},{28,12},{1,17},{... | collective-permute-start | bytes 196616 | tf_op jit(solution)/shard_map/ppermute | solution.py:794
  326.0 7.8 %collective-permute-start.7 = (bf16[64,512]{1,0:T(8,128)(2,1)}, bf16[64,512]{1,0:T(8,128)(2,1)S(1)}, u32[]{:S(2)}, u32[]{:S(2)}) collective-permute-start(bf16[64,512]{1,0:T(8,128)(2,1)} %get-tuple-element.125), channel_id=1, source_target_pairs={{0,8},{4,12},{8,0},{12,4},{16,24},{20,28},{24,16},{28,20},{1,9},{5... | collective-permute-start | bytes 196616 | tf_op jit(solution)/shard_map/ppermute | solution.py:794
  333.9 10.3 %collective-permute-start.11 = (bf16[4,64,512]{2,1,0:T(8,128)(2,1)S(1)}, bf16[4,64,512]{2,1,0:T(8,128)(2,1)S(1)}, u32[]{:S(2)}, u32[]{:S(2)}) collective-permute-start(bf16[4,64,512]{2,1,0:T(8,128)(2,1)S(1)} %get-tuple-element.146), channel_id=1, source_target_pairs={{0,2},{1,3},{2,0},{3,1},{4,6},{5,7},{6,4},{7,5},{8,10},{9,11},{10,... | collective-permute-start | bytes 786440 | tf_op jit(solution)/shard_map/ppermute | solution.py:794
  335.5 9.0 %collective-permute-start.10 = (bf16[4,64,512]{2,1,0:T(8,128)(2,1)S(1)}, bf16[4,64,512]{2,1,0:T(8,128)(2,1)S(1)}, u32[]{:S(2)}, u32[]{:S(2)}) collective-permute-start(bf16[4,64,512]{2,1,0:T(8,128)(2,1)S(1)} %get-tuple-element.146), channel_id=1, source_target_pairs={{0,1},{1,0},{2,3},{3,2},{4,5},{5,4},{6,7},{7,6},{8,9},{9,8},{10,11... | collective-permute-start | bytes 786440 | tf_op jit(solution)/shard_map/ppermute | solution.py:794
  336.0 11.1 %collective-permute-start.12 = (bf16[4,64,512]{2,1,0:T(8,128)(2,1)S(1)}, bf16[4,64,512]{2,1,0:T(8,128)(2,1)S(1)}, u32[]{:S(2)}, u32[]{:S(2)}) collective-permute-start(bf16[4,64,512]{2,1,0:T(8,128)(2,1)S(1)} %get-tuple-element.146), channel_id=1, source_target_pairs={{0,3},{1,2},{2,1},{3,0},{4,7},{5,6},{6,5},{7,4},{8,11},{9,10},{10,... | collective-permute-start | bytes 786440 | tf_op jit(solution)/shard_map/ppermute | solution.py:794
  349.0 5.3 %collective-permute-start.13 = (bf16[16,64,512]{2,1,0:T(8,128)(2,1)S(1)}, bf16[16,64,512]{2,1,0:T(8,128)(2,1)}, u32[]{:S(2)}, u32[]{:S(2)}) collective-permute-start(bf16[16,64,512]{2,1,0:T(8,128)(2,1)S(1)} %bitcast.52), channel_id=1, source_target_pairs={{0,4},{4,0},{8,12},{12,8},{16,20},{20,16},{24,28},{28,24},{1,5},{5... | collective-permute-start | bytes 3145736 | tf_op jit(solution)/shard_map/ppermute | solution.py:794
  (14 other events, 29.6 us)
Sparse Core Ops, SparseCore 0:
  138.8 51.0 reduce-scatter.2
  226.7 50.2 reduce-scatter.4

commit v5 on v4

--- a/solution.py
+++ b/solution.py
@@ -19,6 +19,7 @@
 F32 = jnp.float32
 VMEM_BYTES = 62 * 1024 * 1024
 FCUT = 256
+CHUNK = 256
 
 
 def params():
@@ -339,8 +340,12 @@
                     me == owner, own_bufs[part][0, pl.ds(at, window), :],
                     bufs[part][owner, pl.ds(at, window), :],
                 )
-        hit = (index_ref[:, 0:1] == seen) | (index_ref[:, 1:2] == seen)
-        acc[...] += dot(hit.astype(F32).astype(BF), wins[...])
+        total = acc[...]
+        for low in range(0, experts * window, CHUNK):
+            part = slice(low, min(low + CHUNK, experts * window))
+            hit = (index_ref[:, 0:1] == seen[:, part]) | (index_ref[:, 1:2] == seen[:, part])
+            total = total + dot(hit.astype(F32).astype(BF), wins[part, :])
+        acc[...] = total
         return carry
 
     lax.fori_loop(0, turns(starts_ref, step, range(experts), window), one_turn, 0)
@@ -756,17 +761,19 @@
 def lay_kernel(groups, here_ref, own_ref, other_ref, qkv_ref, proj_ref):
     cores, sides, layers = groups
     tall, width = own_ref.shape[1:]
-    for core in range(cores):
-        for side in range(sides):
-            for layer in range(layers):
-                low = ((core * sides + side) * layers + layer) * tall
-                part, at = low // width, low % width
+    each = width // tall
+    for part in range(4):
+
+        @pl.when(pl.program_id(0) == part)
+        def _():
+            for turn in range(each):
+                core, spot = divmod(part * each + turn, sides * layers)
+                side, layer = divmod(spot, layers)
                 spot = (side ^ here_ref[1]) * layers + (layer ^ here_ref[2])
-                piece = jnp.where(core == here_ref[0], own_ref[spot].astype(F32), other_ref[spot].astype(F32))
-                if part < 3:
-                    qkv_ref[at : at + tall, width * part : width * (part + 1)] = piece
-                else:
-                    proj_ref[at : at + tall, :] = piece
+                piece = jnp.where(
+                    core == here_ref[0], own_ref[spot].astype(F32), other_ref[spot].astype(F32)
+                )
+                (qkv_ref if part < 3 else proj_ref)[tall * turn : tall * (turn + 1), :] = piece
 
 
 def lay(groups, here, own, other):
@@ -775,9 +782,12 @@
         functools.partial(lay_kernel, groups),
         grid_spec=pltpu.PrefetchScalarGridSpec(
             num_scalar_prefetch=1,
-            grid=(1,),
+            grid=(4,),
             in_specs=[whole(own.shape)] * 2,
-            out_specs=[whole((width, 3 * width)), whole((width, width))],
+            out_specs=[
+                pl.BlockSpec((width, width), lambda step, *_: (0, jnp.minimum(step, 2))),
+                whole((width, width)),
+            ],
         ),
         out_shape=[
             jax.ShapeDtypeStruct((width, 3 * width), F32),
@@ -787,6 +797,35 @@
         cost_estimate=cost(1e6, 8e6),
         name="lay",
     )(here, own, other)
+
+
+def unpack_kernel(*refs):
+    parts, (up_ref, down_ref) = refs[:-2], refs[-2:]
+    tall, width = up_ref.shape[1], down_ref.shape[2]
+    for which, part in enumerate(parts):
+        up_ref[which] = part[:tall, :].astype(F32)
+        for turn in range(down_ref.shape[1] // tall):
+            down_ref[which, tall * turn : tall * (turn + 1), :] = (
+                part[tall:, width * turn : width * (turn + 1)].astype(F32)
+            )
+
+
+def unpack(parts, width):
+    tall, units = parts[0].shape[0] // 2, parts[0].shape[1]
+    outs = [
+        jax.ShapeDtypeStruct((len(parts), tall, units), F32),
+        jax.ShapeDtypeStruct((len(parts), tall * units // width, width), F32),
+    ]
+    return pl.pallas_call(
+        unpack_kernel,
+        grid=(1,),
+        in_specs=[whole(part.shape) for part in parts],
+        out_specs=[whole(out.shape) for out in outs],
+        out_shape=outs,
+        compiler_params=params(),
+        cost_estimate=cost(1e6, 4e6),
+        name="unpack",
+    )(*parts)
 
 
 def jump(value, axis, far):
@@ -837,23 +876,22 @@
     return lax.optimization_barrier((value, *others))[0]
 
 
-def sum_over_all(own, sent, groups, extra, beside):
+def sum_over_all(own, sent, groups, extra, arrived, beside):
     cores, sides, layers = groups
-    done = []
+    beside = iter(beside)
 
     def spread(own, sent, axis, scale):
         came = [jump(part, axis, scale * far) for far, part in enumerate(sent, 1)]
-        work = beside[len(done)](own)
-        done.append(work)
-        return [own] + list(after(tuple(came), jax.tree.leaves(work)[0]))
+        return [own] + list(after(tuple(came), next(beside)(own)))
 
     half = merge([own, jump(sent, "dp", 1)], sides, extra, False)
+    half = list(after(tuple(half), arrived))
     flat = merge(spread(half[0], half[1:], "expert", 1), layers, extra, False)
     spot, small = merge(spread(flat[0], flat[1:], "dp", cores), 1, extra, True)
     flat = jnp.stack(spread(spot, [spot] * (layers - 1), "dp", cores))
     half = jnp.stack(spread(flat, [flat] * (sides - 1), "expert", 1))
     half = half.reshape(sides * layers, *spot.shape)
-    return half, jump(half, "dp", 1), small, done
+    return half, jump(half, "dp", 1), small
 
 
 def per_device(
@@ -924,36 +962,41 @@
         starts, here, groups, index, hidden, tokens, grad_out, qkv, probs, mixed, gain_one,
         w_qkv, w_proj, gain_two, [head, down], own_down, [router_first, router_second], capacity,
     )
-    sent = after(sent, tail)
     blocks = count // BLOCK
-    cuts = [0, blocks // 3, 2 * blocks // 3, blocks]
-    grad_tokens = [None]
-
-    tall = width // shards
+    some = blocks // 3
 
     def make_top(tie):
-        return top(starts, here, index, after(hidden, tie), head, tail, tail_first, own_out, early, capacity)
-
-    def make_last(turn, tie):
-        grad_tokens.append(
-            last(
-                cuts[turn], cuts[turn + 1], grad_tokens[-1], after(dqkv, tie), grad_hidden,
-                tokens, gain_one, w_qkv,
-            )
+        return top(
+            starts, here, index, after(hidden, tie), head, tail, tail_first, own_out, early, capacity
         )
-        if turn < 2:
-            return grad_tokens[-1]
-        parts = sums
-        grad_in = jnp.stack([part[:tall] for part in parts]).astype(F32)
-        grad_eout = jnp.stack(
-            [part[tall:].reshape(tall, -1, width).transpose(1, 0, 2).reshape(-1, width) for part in parts]
-        ).astype(F32)
-        return grad_tokens[-1], grad_in, grad_eout
-
-    own, other, small, done = sum_over_all(
-        own, sent, groups, small_rows(experts), [make_top] + [functools.partial(make_last, turn) for turn in range(3)]
+
+    def make_unpack(tie):
+        return unpack(after(tuple(sums), tie), width)
+
+    def make_last(low, high, tie, so_far=None):
+        return last(
+            low, high, so_far, after(dqkv, tie), grad_hidden, tokens, gain_one, w_qkv
+        )
+
+    made = {}
+
+    def beside(name, work):
+        def go(tie):
+            made[name] = work(tie)
+            return jax.tree.leaves(made[name])[0]
+
+        return go
+
+    own, other, small = sum_over_all(
+        own, sent, groups, small_rows(experts), tail,
+        [
+            beside("top", make_top),
+            beside("unpack", make_unpack),
+            beside("some", lambda tie: make_last(0, some, tie)),
+            beside("last", lambda tie: make_last(some, blocks, tie, made["some"])),
+        ],
     )
-    block_out, (grad_tokens, grad_in, grad_eout) = done[0], done[3]
+    block_out, grad_tokens, (grad_in, grad_eout) = made["top"], made["last"], made["unpack"]
     grad_qkv, grad_proj = lay(groups, here, own, other)
     return (
         block_out,

time: 372 us -> 364 us (0.978)
  waiting for transfers between devices: 43.4 us -> 38.3 us
    all_to_all x6, waiting for transfers between devices: 37.6 us -> 31.4 us  [swap(): lax.all_to_all(sent, 'expert', split_axis=0, concat_axis=0, tiled=True)]
    pallas_call x3 -> x2, Pallas kernels: 16.9 us -> 14.6 us  [last(): pl.pallas_call(last_kernel, grid=(high - low,), in_specs=[row((BLOCK_PAD,...]
  transfers between devices with their start and end apart: 22 -> 22, of which waited for: 9 -> 8; matrix products, arithmetic and copies ran while one was open for 3% -> 2% of each run, Pallas kernels for 62% -> 63%
where the time goes in v5:
time: 364 us; the launch traced here: 359 us
  Pallas kernels  246 us (68%)
  starting transfers between devices  46 us (13%)
  waiting for transfers between devices  38.3 us (11%)
  between operations  14.8 us (4%)
  local copies, waits for them, and re-layouts  8.89 us (2%)
  other arithmetic  5.02 us (1%)
    pallas_call x4, Pallas kernels, expert_pass(): pl.pallas_call(body, grid_spec=pltpu.PrefetchScalarGridSpec(num_scalar_pr...  115 us
    pallas_call x1, Pallas kernels, back(): pl.pallas_call(functools.partial(back_kernel, window, groups), grid_spec=...  38.3 us
    all_to_all x6, waiting for transfers between devices, swap(): lax.all_to_all(sent, 'expert', split_axis=0, concat_axis=0, tiled=True)  31.4 us
    all_to_all x6, starting transfers between devices, swap(): lax.all_to_all(sent, 'expert', split_axis=0, concat_axis=0, tiled=True)  29.4 us
    pallas_call x3, Pallas kernels, dispatch(): pl.pallas_call(functools.partial(dispatch_kernel, window, capacity, plan,...  25.8 us
    pallas_call x1, Pallas kernels, attend(): pl.pallas_call(attend_kernel, grid=(blocks,), in_specs=[row((BLOCK, width...  20.8 us
    ppermute x14, starting transfers between devices, jump(): return lax.ppermute(value, axis, [(at, at ^ far) for at in range(size)])  16 us
    pallas_call x2, Pallas kernels, last(): pl.pallas_call(last_kernel, grid=(high - low,), in_specs=[row((BLOCK_PAD,...  14.6 us
  transfers between devices with their start and end apart: 22, of which 8 were waited for; matrix products, arithmetic and copies ran while one was open for 2% of the time, Pallas kernels for 63%

profile of v5, /device:TPU:0, one launch (start us, length us, event | category | flops | bytes accessed | tf_op | source)
XLA Modules:
  0.0 358.7 jit_solution(9106394275210876338)
XLA Ops:
  9.4 4.0 %places.1 = (s32[6,2,392]{2,1,0:T(2,128)}, s32[8,128]{1,0:T(8,128)}) custom-call(s32[8,1]{1,0:T(8,128)} %reshape.78.ids_ref, s32[6,4,392]{2,1,0:T(4,128)} %bitcast.47), custom_call_target="tpu_custom_call" | custom-call | flops 100000000 | bytes 100000 | tf_op jit(solution)/shard_map/places/pallas_call | solution.py:218
  13.4 7.9 %dispatch.3.refs_6_ = bf16[4,624,512]{2,1,0:T(8,128)(2,1)} custom-call(s32[8,128]{1,0:T(8,128)} %get-tuple-element.80.starts_ref, s32[6,2,392]{2,1,0:T(2,128)} %get-tuple-element.81.index_ref, bf16[2352,512]{1,0:T(8,128)(2,1)} %dy_ref.1), custom_call_target="tpu_custom_call" | custom-call | flops 6000000000 | bytes 8000000 | tf_op jit(solution)/shard_map/dispatch/pallas_call | solution.py:300
  21.3 4.9 %all-to-all-start = ((bf16[4,624,512]{2,1,0:T(8,128)(2,1)}), bf16[4,624,512]{2,1,0:T(8,128)(2,1)}, u32[]{:S(2)}, u32[]{:S(2)}) async-start(bf16[4,624,512]{2,1,0:T(8,128)(2,1)} %dispatch.3.refs_6_), calls=%async_computation | async-start | bytes 5111808 | tf_op jit(solution)/shard_map/all_to_all | solution.py:914
  26.2 20.8 %attend.1 = (f32[2352,512]{1,0:T(8,128)}, bf16[2352,512]{1,0:T(8,128)(2,1)}, bf16[2688,1536]{1,0:T(8,128)(2,1)}, bf16[21504,112]{1,0:T(8,128)(2,1)}, bf16[2688,512]{1,0:T(8,128)(2,1)}) custom-call(bf16[2352,512]{1,0:T(8,128)(2,1)} %tok_ref.6, f32[1,512]{1,0:T(1,128)} %bitcast.49, bf16[512,1536]{1,0:T(8,128)(2,1)} %qkv_w_ref.7, bf16[512,512]{1,0:T(8,128)(2,1)} %proj_w_ref.3, ...), custom_call_target="tpu_custom_call" | custom-call | flops 6870269952 | bytes 30000000 | tf_op jit(solution)/shard_map/attend/pallas_call | solution.py:159
  47.1 7.8 %dispatch.4.refs_5_ = bf16[4,624,512]{2,1,0:T(8,128)(2,1)} custom-call(s32[8,128]{1,0:T(8,128)} %get-tuple-element.80.starts_ref, s32[6,2,392]{2,1,0:T(2,128)} %get-tuple-element.81.index_ref, bf16[2352,512]{1,0:T(8,128)(2,1)} %get-tuple-element.95.refs_0_), custom_call_target="tpu_custom_call" | custom-call | flops 6000000000 | bytes 8000000 | tf_op jit(solution)/shard_map/dispatch/pallas_call | solution.py:300
  56.9 4.8 %all-to-all-start.1 = ((bf16[4,624,512]{2,1,0:T(8,128)(2,1)}), bf16[4,624,512]{2,1,0:T(8,128)(2,1)}, u32[]{:S(2)}, u32[]{:S(2)}) async-start(bf16[4,624,512]{2,1,0:T(8,128)(2,1)} %dispatch.4.refs_5_), calls=%async_computation.1 | async-start | bytes 5111808 | tf_op jit(solution)/shard_map/all_to_all | solution.py:914
  63.8 10.0 %dispatch.5.refs_5_.refs_6_ = bf16[4,1248,512]{2,1,0:T(8,128)(2,1)} custom-call(s32[8,128]{1,0:T(8,128)} %get-tuple-element.80.starts_ref, s32[6,2,392]{2,1,0:T(2,128)} %get-tuple-element.81.index_ref, bf16[2352,512]{1,0:T(8,128)(2,1)} %get-tuple-element.95.refs_0_, bf16[2352,512]{1,0:T(8,128)(2,1)} %dy_ref.1), custom_call_target="tpu_custom_call" | custom-call | flops 6000000000 | bytes 8000000 | tf_op jit(solution)/shard_map/dispatch/pallas_call | solution.py:300
  73.8 15.5 %expert_own.2 = (bf16[4,928,512]{2,1,0:T(8,128)(2,1)}, bf16[4,320,512]{2,1,0:T(8,128)(2,1)}, bf16[512,2048]{1,0:T(8,128)(2,1)}, bf16[512,2048]{1,0:T(8,128)(2,1)}, f32[512,128]{1,0:T(8,128)}) custom-call(s32[2]{0:T(128)} %pad_add_fusion.2.refs_0_, bf16[2,512,2048]{2,1,0:T(8,128)(2,1)} %refs_1_.9, bf16[2,2048,512]{2,1,0:T(8,128)(2,1)} %refs_2_.7, ...), custom_call_target="tpu_custom_call" | custom-call | flops 13086228480 | bytes 30000000 | tf_op jit(solution)/shard_map/expert_own/pallas_call | solution.py:550
  91.9 5.0 %all-to-all-start.2 = ((bf16[4,1248,512]{2,1,0:T(8,128)(2,1)}), bf16[4,1248,512]{2,1,0:T(8,128)(2,1)}, u32[]{:S(2)}, u32[]{:S(2)}) async-start(bf16[4,1248,512]{2,1,0:T(8,128)(2,1)} %dispatch.5.refs_5_.refs_6_), calls=%async_computation.2 | async-start | bytes 10223616 | tf_op jit(solution)/shard_map/all_to_all | solution.py:914
  97.4 41.3 %expert_others.2 = (bf16[4,928,512]{2,1,0:T(8,128)(2,1)}, bf16[4,320,512]{2,1,0:T(8,128)(2,1)}, bf16[8,128,2048]{2,1,0:T(8,128)(2,1)}, f32[512,128]{1,0:T(8,128)}) custom-call(s32[2]{0:T(128)} %pad_add_fusion.2.refs_0_, bf16[2,512,2048]{2,1,0:T(8,128)(2,1)} %refs_1_.9, ...), custom_call_target="tpu_custom_call", output_to_operand_aliasing={{0}: (10, {}), {1}: (11, {})} | custom-call | flops 39258685440 | bytes 30000000 | tf_op jit(solution)/shard_map/expert_others/pallas_call | solution.py:550
  139.3 15.1 %all-to-all-done.2.refs_5_.refs_6_ = bf16[4,1248,512]{2,1,0:T(8,128)(2,1)} async-done(((bf16[4,1248,512]{2,1,0:T(8,128)(2,1)}), bf16[4,1248,512]{2,1,0:T(8,128)(2,1)}, u32[]{:S(2)}, u32[]{:S(2)}) %all-to-all-start.2) | async-done | bytes 5111840 | tf_op jit(solution)/shard_map/all_to_all | solution.py:914
  154.4 5.0 %all-to-all-start.3 = ((bf16[4,928,512]{2,1,0:T(8,128)(2,1)}), bf16[4,928,512]{2,1,0:T(8,128)(2,1)}, u32[]{:S(2)}, u32[]{:S(2)}) async-start(bf16[4,928,512]{2,1,0:T(8,128)(2,1)} %get-tuple-element.97), calls=%async_computation.3 | async-start | bytes 7602176 | tf_op jit(solution)/shard_map/all_to_all | solution.py:914
  159.4 40.1 %expert_others.3 = (bf16[4,624,512]{2,1,0:T(8,128)(2,1)}, bf16[4,944,512]{2,1,0:T(8,128)(2,1)}, bf16[512,2048]{1,0:T(8,128)(2,1)}, bf16[512,2048]{1,0:T(8,128)(2,1)}, f32[512,128]{1,0:T(8,128)}) custom-call(s32[2]{0:T(128)} %pad_add_fusion.3.refs_0_, bf16[2,512,2048]{2,1,0:T(8,128)(2,1)} %refs_1_.9, bf16[2,2048,512]{2,1,0:T(8,128)(2,1)} %refs_2_.7, ...), custom_call_target="tpu_custom_call" | custom-call | flops 39258685440 | bytes 30000000 | tf_op jit(solution)/shard_map/expert_others/pallas_call | solution.py:550
  202.1 4.7 %all-to-all-start.4 = ((bf16[4,624,512]{2,1,0:T(8,128)(2,1)}), bf16[4,624,512]{2,1,0:T(8,128)(2,1)}, u32[]{:S(2)}, u32[]{:S(2)}) async-start(bf16[4,624,512]{2,1,0:T(8,128)(2,1)} %get-tuple-element.100), calls=%async_computation.4 | async-start | bytes 5111808 | tf_op jit(solution)/shard_map/all_to_all | solution.py:914
  209.2 17.7 %expert_own.3 = (bf16[1,624,512]{2,1,0:T(8,128)(2,1)}, bf16[1,624,512]{2,1,0:T(8,128)(2,1)}, bf16[8,128,2048]{2,1,0:T(8,128)(2,1)}, f32[512,128]{1,0:T(8,128)}) custom-call(s32[2]{0:T(128)} %pad_add_fusion.3.refs_0_, bf16[2,512,2048]{2,1,0:T(8,128)(2,1)} %refs_1_.9, bf16[2,2048,512]{2,1,0:T(8,128)(2,1)} %refs_2_.7, bf16[512,256]{1,0:T(8,128)(2,1)} %copy.33.refs_3_, ...), custom_call_target="tpu_custom_call" | custom-call | flops 13086228480 | bytes 30000000 | tf_op jit(solution)/shard_map/expert_own/pallas_call | solution.py:550
  226.9 9.2 %all-to-all-done.4.refs_1_ = bf16[4,624,512]{2,1,0:T(8,128)(2,1)} async-done(((bf16[4,624,512]{2,1,0:T(8,128)(2,1)}), bf16[4,624,512]{2,1,0:T(8,128)(2,1)}, u32[]{:S(2)}, u32[]{:S(2)}) %all-to-all-start.4) | async-done | bytes 2555936 | tf_op jit(solution)/shard_map/all_to_all | solution.py:914
  236.1 5.0 %all-to-all-start.5 = ((bf16[4,944,512]{2,1,0:T(8,128)(2,1)}), bf16[4,944,512]{2,1,0:T(8,128)(2,1)}, u32[]{:S(2)}, u32[]{:S(2)}) async-start(bf16[4,944,512]{2,1,0:T(8,128)(2,1)} %get-tuple-element.114), calls=%async_computation.5 | async-start | bytes 7733248 | tf_op jit(solution)/shard_map/all_to_all | solution.py:914
  241.1 38.3 %back.1 = (f32[2352,512]{1,0:T(8,128)}, bf16[2688,1536]{1,0:T(8,128)(2,1)}, bf16[1040,512]{1,0:T(8,128)(2,1)}, bf16[1040,512]{1,0:T(8,128)(2,1)}) custom-call(s32[8,128]{1,0:T(8,128)} %get-tuple-element.80.starts_ref, s32[3]{0:T(128)} %pad_add_fusion.1.here_ref, s32[2352,2]{1,0:T(8,128)} %bitcast.38, f32[2352,512]{1,0:T(8,128)} %get-tuple-element.116.hidden_ref, ...), custom_call_target="tpu_custom_call" | custom-call | flops 999999995904 | bytes 4000000000 | tf_op jit(solution)/shard_map/back/pallas_call | solution.py:690
  279.5 2.9 collective-permute-done.refs_1_
  289.4 13.6 %top.1 = bf16[2352,512]{1,0:T(8,128)(2,1)} custom-call(s32[8,128]{1,0:T(8,128)} %get-tuple-element.80.starts_ref, s32[3]{0:T(128)} %pad_add_fusion.1.here_ref, s32[2352,2]{1,0:T(8,128)} %bitcast.39, f32[2352,512]{1,0:T(8,128)} %get-tuple-element.116.hidden_ref, bf16[4,928,512]{2,1,0:T(8,128)(2,1)} %all-to-all-done.3.refs_0_.head_ref, ...), custom_call_target="tpu_custom_call" | custom-call | flops 6000000000 | bytes 12000000 | tf_op jit(solution)/shard_map/top/pallas_call | solution.py:391
  313.6 3.1 collective-permute-done.5.refs_2_
  323.4 5.7 %last.2.refs_0_ = f32[2352,512]{1,0:T(8,128)} custom-call(bf16[2688,1536]{1,0:T(8,128)(2,1)} %get-tuple-element.143.dqkv_ref, f32[2352,512]{1,0:T(8,128)} %get-tuple-element.139.ghid_ref, bf16[2352,512]{1,0:T(8,128)(2,1)} %tok_ref.6, f32[1,512]{1,0:T(1,128)} %bitcast.51, bf16[512,1536]{1,0:T(8,128)(2,1)} %qkv_w_ref.7), custom_call_target="tpu_custom_call" | custom-call | flops 1409286144 | bytes 20000000 | tf_op jit(solution)/shard_map/last/pallas_call | solution.py:744
  332.7 8.9 %last.3 = f32[2352,512]{1,0:T(8,128)} custom-call(bf16[2688,1536]{1,0:T(8,128)(2,1)} %get-tuple-element.143.dqkv_ref, f32[2352,512]{1,0:T(8,128)} %get-tuple-element.139.ghid_ref, bf16[2352,512]{1,0:T(8,128)(2,1)} %tok_ref.6, f32[1,512]{1,0:T(1,128)} %bitcast.52, bf16[512,1536]{1,0:T(8,128)(2,1)} %qkv_w_ref.7, ...), custom_call_target="tpu_custom_call", output_to_operand_aliasing={{}: (5, {})} | custom-call | flops 2818572288 | bytes 20000000 | tf_op jit(solution)/shard_map/last/pallas_call | solution.py:744
  346.3 5.1 %lay.1 = (f32[512,1536]{1,0:T(8,128)}, f32[512,512]{1,0:T(8,128)}) custom-call(s32[3]{0:T(128)} %pad_add_fusion.1.here_ref, bf16[16,64,512]{2,1,0:T(8,128)(2,1)} %bitcast.35, bf16[16,64,512]{2,1,0:T(8,128)(2,1)} %collective-permute-done.13.other_ref), custom_call_target="tpu_custom_call" | custom-call | flops 1000000 | bytes 8000000 | tf_op jit(solution)/shard_map/lay/pallas_call | solution.py:781
  (87 shorter events, 47.4 us)
Async XLA Ops:
  21.3 35.6 %all-to-all-start = ((bf16[4,624,512]{2,1,0:T(8,128)(2,1)}), bf16[4,624,512]{2,1,0:T(8,128)(2,1)}, u32[]{:S(2)}, u32[]{:S(2)}) async-start(bf16[4,624,512]{2,1,0:T(8,128)(2,1)} %dispatch.3.refs_6_), calls=%async_computation | async-start | bytes 5111808 | tf_op jit(solution)/shard_map/all_to_all | solution.py:914
  56.9 35.0 %all-to-all-start.1 = ((bf16[4,624,512]{2,1,0:T(8,128)(2,1)}), bf16[4,624,512]{2,1,0:T(8,128)(2,1)}, u32[]{:S(2)}, u32[]{:S(2)}) async-start(bf16[4,624,512]{2,1,0:T(8,128)(2,1)} %dispatch.4.refs_5_), calls=%async_computation.1 | async-start | bytes 5111808 | tf_op jit(solution)/shard_map/all_to_all | solution.py:914
  91.9 62.5 %all-to-all-start.2 = ((bf16[4,1248,512]{2,1,0:T(8,128)(2,1)}), bf16[4,1248,512]{2,1,0:T(8,128)(2,1)}, u32[]{:S(2)}, u32[]{:S(2)}) async-start(bf16[4,1248,512]{2,1,0:T(8,128)(2,1)} %dispatch.5.refs_5_.refs_6_), calls=%async_computation.2 | async-start | bytes 10223616 | tf_op jit(solution)/shard_map/all_to_all | solution.py:914
  96.9 214.1 %reduce-scatter.3.cloned.1.call-start = ((), (), s32[]{:S(2)}) async-start(), calls=%async_computation.8 | async-start | bytes 4718592 | tf_op jit(solution)/shard_map/reduce_scatter | solution.py:950
  154.4 47.7 %all-to-all-start.3 = ((bf16[4,928,512]{2,1,0:T(8,128)(2,1)}), bf16[4,928,512]{2,1,0:T(8,128)(2,1)}, u32[]{:S(2)}, u32[]{:S(2)}) async-start(bf16[4,928,512]{2,1,0:T(8,128)(2,1)} %get-tuple-element.97), calls=%async_computation.3 | async-start | bytes 7602176 | tf_op jit(solution)/shard_map/all_to_all | solution.py:914
  202.1 34.0 %all-to-all-start.4 = ((bf16[4,624,512]{2,1,0:T(8,128)(2,1)}), bf16[4,624,512]{2,1,0:T(8,128)(2,1)}, u32[]{:S(2)}, u32[]{:S(2)}) async-start(bf16[4,624,512]{2,1,0:T(8,128)(2,1)} %get-tuple-element.100), calls=%async_computation.4 | async-start | bytes 5111808 | tf_op jit(solution)/shard_map/all_to_all | solution.py:914
  206.8 104.2 %reduce-scatter.5.cloned.1.call-start = ((), (), s32[]{:S(2)}) async-start(), calls=%async_computation.9 | async-start | bytes 4718592 | tf_op jit(solution)/shard_map/reduce_scatter | solution.py:950
  236.1 49.9 %all-to-all-start.5 = ((bf16[4,944,512]{2,1,0:T(8,128)(2,1)}), bf16[4,944,512]{2,1,0:T(8,128)(2,1)}, u32[]{:S(2)}, u32[]{:S(2)}) async-start(bf16[4,944,512]{2,1,0:T(8,128)(2,1)} %get-tuple-element.114), calls=%async_computation.5 | async-start | bytes 7733248 | tf_op jit(solution)/shard_map/all_to_all | solution.py:914
  279.4 3.0 collective-permute-start
  285.9 17.1 %collective-permute-start.1 = (bf16[272,512]{1,0:T(8,128)(2,1)}, bf16[272,512]{1,0:T(8,128)(2,1)S(1)}, u32[]{:S(2)}, u32[]{:S(2)}) collective-permute-start(bf16[272,512]{1,0:T(8,128)(2,1)} %get-tuple-element.119), channel_id=1, source_target_pairs={{0,1},{1,0},{2,3},{3,2},{4,5},{5,4},{6,7},{7,6},{8,9},{9,8},{10,11... | collective-permute-start | bytes 835592 | tf_op jit(solution)/shard_map/ppermute | solution.py:833
  287.2 15.9 %collective-permute-start.2 = (bf16[272,512]{1,0:T(8,128)(2,1)}, bf16[272,512]{1,0:T(8,128)(2,1)S(1)}, u32[]{:S(2)}, u32[]{:S(2)}) collective-permute-start(bf16[272,512]{1,0:T(8,128)(2,1)} %get-tuple-element.120), channel_id=1, source_target_pairs={{0,2},{1,3},{2,0},{3,1},{4,6},{5,7},{6,4},{7,5},{8,10},{9,11},{10,... | collective-permute-start | bytes 835592 | tf_op jit(solution)/shard_map/ppermute | solution.py:833
  289.4 13.7 %collective-permute-start.3 = (bf16[272,512]{1,0:T(8,128)(2,1)}, bf16[272,512]{1,0:T(8,128)(2,1)S(1)}, u32[]{:S(2)}, u32[]{:S(2)}) collective-permute-start(bf16[272,512]{1,0:T(8,128)(2,1)} %get-tuple-element.121), channel_id=1, source_target_pairs={{0,3},{1,2},{2,1},{3,0},{4,7},{5,6},{6,5},{7,4},{8,11},{9,10},{10,... | collective-permute-start | bytes 835592 | tf_op jit(solution)/shard_map/ppermute | solution.py:833
  306.6 7.0 %collective-permute-start.4 = (bf16[80,512]{1,0:T(8,128)(2,1)}, bf16[80,512]{1,0:T(8,128)(2,1)S(1)}, u32[]{:S(2)}, u32[]{:S(2)}) collective-permute-start(bf16[80,512]{1,0:T(8,128)(2,1)} %get-tuple-element.126), channel_id=1, source_target_pairs={{0,8},{4,12},{8,0},{12,4},{16,24},{20,28},{24,16},{28,20},{1,9},{5... | collective-permute-start | bytes 245768 | tf_op jit(solution)/shard_map/ppermute | solution.py:833
  307.1 9.6 %collective-permute-start.5 = (bf16[80,512]{1,0:T(8,128)(2,1)}, bf16[80,512]{1,0:T(8,128)(2,1)S(1)}, u32[]{:S(2)}, u32[]{:S(2)}) collective-permute-start(bf16[80,512]{1,0:T(8,128)(2,1)} %get-tuple-element.127), channel_id=1, source_target_pairs={{0,16},{4,20},{8,24},{12,28},{16,0},{20,4},{24,8},{28,12},{1,17},{... | collective-permute-start | bytes 245768 | tf_op jit(solution)/shard_map/ppermute | solution.py:833
  309.2 7.5 %collective-permute-start.6 = (bf16[80,512]{1,0:T(8,128)(2,1)}, bf16[80,512]{1,0:T(8,128)(2,1)S(1)}, u32[]{:S(2)}, u32[]{:S(2)}) collective-permute-start(bf16[80,512]{1,0:T(8,128)(2,1)} %get-tuple-element.128), channel_id=1, source_target_pairs={{0,24},{4,28},{8,16},{12,20},{16,8},{20,12},{24,0},{28,4},{1,25},{... | collective-permute-start | bytes 245768 | tf_op jit(solution)/shard_map/ppermute | solution.py:833
  319.0 10.1 %collective-permute-start.9 = (bf16[64,512]{1,0:T(8,128)(2,1)}, bf16[64,512]{1,0:T(8,128)(2,1)S(1)}, u32[]{:S(2)}, u32[]{:S(2)}) collective-permute-start(bf16[64,512]{1,0:T(8,128)(2,1)} %get-tuple-element.137), channel_id=1, source_target_pairs={{0,24},{4,28},{8,16},{12,20},{16,8},{20,12},{24,0},{28,4},{1,25},{... | collective-permute-start | bytes 196616 | tf_op jit(solution)/shard_map/ppermute | solution.py:833
  321.0 8.0 %collective-permute-start.8 = (bf16[64,512]{1,0:T(8,128)(2,1)}, bf16[64,512]{1,0:T(8,128)(2,1)S(1)}, u32[]{:S(2)}, u32[]{:S(2)}) collective-permute-start(bf16[64,512]{1,0:T(8,128)(2,1)} %get-tuple-element.137), channel_id=1, source_target_pairs={{0,16},{4,20},{8,24},{12,28},{16,0},{20,4},{24,8},{28,12},{1,17},{... | collective-permute-start | bytes 196616 | tf_op jit(solution)/shard_map/ppermute | solution.py:833
  321.9 7.2 %collective-permute-start.7 = (bf16[64,512]{1,0:T(8,128)(2,1)}, bf16[64,512]{1,0:T(8,128)(2,1)S(1)}, u32[]{:S(2)}, u32[]{:S(2)}) collective-permute-start(bf16[64,512]{1,0:T(8,128)(2,1)} %get-tuple-element.137), channel_id=1, source_target_pairs={{0,8},{4,12},{8,0},{12,4},{16,24},{20,28},{24,16},{28,20},{1,9},{5... | collective-permute-start | bytes 196616 | tf_op jit(solution)/shard_map/ppermute | solution.py:833
  329.1 14.4 %copy-start.13 = (f32[16,512]{1,0:T(8,128)S(1)}, f32[16,512]{1,0:T(8,128)}, u32[]{:S(2)}) copy-start(f32[16,512]{1,0:T(8,128)} %get-tuple-element.144) | copy-start | bytes 98308
  329.1 15.1 %copy-start.11 = (f32[512]{0:T(512)S(1)}, f32[512]{0:T(512)}, u32[]{:S(2)}) copy-start(f32[512]{0:T(512)} %param.12) | copy-start | bytes 6148
  329.1 12.5 %collective-permute-start.11 = (bf16[4,64,512]{2,1,0:T(8,128)(2,1)S(1)}, bf16[4,64,512]{2,1,0:T(8,128)(2,1)S(1)}, u32[]{:S(2)}, u32[]{:S(2)}) collective-permute-start(bf16[4,64,512]{2,1,0:T(8,128)(2,1)S(1)} %get-tuple-element.154), channel_id=1, source_target_pairs={{0,2},{1,3},{2,0},{3,1},{4,6},{5,7},{6,4},{7,5},{8,10},{9,11},{10,... | collective-permute-start | bytes 786440 | tf_op jit(solution)/shard_map/ppermute | solution.py:833
  330.0 11.7 %collective-permute-start.10 = (bf16[4,64,512]{2,1,0:T(8,128)(2,1)S(1)}, bf16[4,64,512]{2,1,0:T(8,128)(2,1)S(1)}, u32[]{:S(2)}, u32[]{:S(2)}) collective-permute-start(bf16[4,64,512]{2,1,0:T(8,128)(2,1)S(1)} %get-tuple-element.154), channel_id=1, source_target_pairs={{0,1},{1,0},{2,3},{3,2},{4,5},{5,4},{6,7},{7,6},{8,9},{9,8},{10,11... | collective-permute-start | bytes 786440 | tf_op jit(solution)/shard_map/ppermute | solution.py:833
  331.9 9.8 %collective-permute-start.12 = (bf16[4,64,512]{2,1,0:T(8,128)(2,1)S(1)}, bf16[4,64,512]{2,1,0:T(8,128)(2,1)S(1)}, u32[]{:S(2)}, u32[]{:S(2)}) collective-permute-start(bf16[4,64,512]{2,1,0:T(8,128)(2,1)S(1)} %get-tuple-element.154), channel_id=1, source_target_pairs={{0,3},{1,2},{2,1},{3,0},{4,7},{5,6},{6,5},{7,4},{8,11},{9,10},{10,... | collective-permute-start | bytes 786440 | tf_op jit(solution)/shard_map/ppermute | solution.py:833
  343.5 2.9 collective-permute-start.13
  (12 other events, 26.6 us)
Sparse Core Ops, SparseCore 0:
  138.8 51.4 reduce-scatter.2
  227.0 50.6 reduce-scatter.4

commit v6 on v5

--- a/solution.py
+++ b/solution.py
@@ -20,6 +20,7 @@
 VMEM_BYTES = 62 * 1024 * 1024
 FCUT = 256
 CHUNK = 256
+TOP_SUBS, SEND_SUBS, LAST_SUBS = 2, 2, 2
 
 
 def params():
@@ -32,6 +33,10 @@
     return pl.CostEstimate(
         flops=int(flops), bytes_accessed=int(moved), transcendentals=int(special)
     )
+
+
+def step_blocks(blocks, most):
+    return max(n for n in range(1, most + 1) if blocks % n == 0)
 
 
 def whole(shape):
@@ -184,53 +189,53 @@
     )(tokens, gain_one[None, :], w_qkv, w_proj, gain_two[None, :])
 
 
-def place_kernel(capacity, ids_ref, picks_ref, index_ref, starts_ref, carry):
-    step = pl.program_id(0)
-
-    @pl.when(step == 0)
-    def _():
-        carry[...] = jnp.zeros(carry.shape, F32)
-        starts_ref[...] = jnp.zeros(starts_ref.shape, jnp.int32)
-
-    experts, block = ids_ref.shape[0], picks_ref.shape[2]
-    ids = ids_ref[...]
-    names = [picks_ref[0, c : c + 1, :] == ids for c in (0, 1)]
-    named = (names[0] | names[1]).astype(F32)
+def place_kernel(local, capacity, picks_ref, keep_ref, index_ref, starts_ref):
+    blocks, _, block = index_ref.shape
+    experts = starts_ref.shape[0]
+    owners = experts // local
+    row = lax.broadcasted_iota(jnp.int32, (experts, block), 0)
+    ids = row * local
+    for part in range(1, local):
+        ids = jnp.where(row >= owners * part, (row - owners * part) * local + part, ids)
     earlier = lax.broadcasted_iota(jnp.int32, (block, block), 0) < lax.broadcasted_iota(
         jnp.int32, (block, block), 1
     )
-    before = dot(named.astype(BF), earlier.astype(F32).astype(BF)) + carry[:, 0:1]
-    spot = before + (lax.broadcasted_iota(jnp.int32, (experts, block), 0) * capacity).astype(F32)
-    for c in (0, 1):
-        found = jnp.sum(jnp.where(names[c], spot, 0.0), axis=0, keepdims=True).astype(jnp.int32)
-        index_ref[0, c : c + 1, :] = jnp.where(picks_ref[0, 2 + c : 3 + c, :] > 0, found, -1)
-    after = carry[...] + jnp.sum(named, axis=1, keepdims=True)
-    carry[...] = after
+    earlier = earlier.astype(F32).astype(BF)
+    base = (row * capacity).astype(F32)
     lane = lax.broadcasted_iota(jnp.int32, (experts, LANES), 1)
-    starts_ref[...] = jnp.where(lane == step + 1, after.astype(jnp.int32), starts_ref[...])
-
-
-def places(ids, picks, keep, capacity):
+    starts = jnp.zeros((experts, LANES), jnp.int32)
+    carry = jnp.zeros((experts, 1), F32)
+    for step in range(blocks):
+        cols = slice(block * step, block * (step + 1))
+        names = [picks_ref[c : c + 1, cols] == ids for c in (0, 1)]
+        named = (names[0] | names[1]).astype(F32)
+        spot = base + (dot(named.astype(BF), earlier) + carry)
+        for c in (0, 1):
+            found = jnp.sum(jnp.where(names[c], spot, 0.0), axis=0, keepdims=True)
+            index_ref[step, c : c + 1, :] = jnp.where(
+                keep_ref[c : c + 1, cols] > 0, found.astype(jnp.int32), -1
+            )
+        carry = carry + jnp.sum(named, axis=1, keepdims=True)
+        starts = jnp.where(lane == step + 1, carry.astype(jnp.int32), starts)
+    starts_ref[...] = starts
+
+
+def places(picks, keep, experts, local, capacity):
     count = picks.shape[0]
-    blocks = count // BLOCK
-    experts = ids.shape[0]
-    turned = jnp.concatenate([picks, keep], axis=1).reshape(blocks, BLOCK, 4).transpose(0, 2, 1)
+    outs = [
+        jax.ShapeDtypeStruct((count // BLOCK, 2, BLOCK), jnp.int32),
+        jax.ShapeDtypeStruct((experts, LANES), jnp.int32),
+    ]
     return pl.pallas_call(
-        functools.partial(place_kernel, capacity),
-        grid=(blocks,),
-        in_specs=[whole((experts, 1)), pl.BlockSpec((1, 4, BLOCK), lambda step: (step, 0, 0))],
-        out_specs=[
-            pl.BlockSpec((1, 2, BLOCK), lambda step: (step, 0, 0)), whole((experts, LANES)),
-        ],
-        out_shape=[
-            jax.ShapeDtypeStruct((blocks, 2, BLOCK), jnp.int32),
-            jax.ShapeDtypeStruct((experts, LANES), jnp.int32),
-        ],
-        scratch_shapes=[pltpu.VMEM((experts, LANES), F32)],
+        functools.partial(place_kernel, local, capacity),
+        grid=(1,),
+        in_specs=[whole((2, count))] * 2,
+        out_specs=[whole(out.shape) for out in outs],
+        out_shape=outs,
         compiler_params=params(),
         cost_estimate=cost(1e8, 1e5),
         name="places",
-    )(ids[:, None], turned)
+    )(picks.T, keep.T)
 
 
 def window_rows(experts, capacity):
@@ -255,55 +260,59 @@
 def dispatch_kernel(window, capacity, plan, sources, starts_ref, index_ref, *refs):
     src_refs, outs, (spots, got) = refs[:sources], refs[sources:-2], refs[-2:]
     owners = outs[0].shape[0]
-    step = pl.program_id(0)
     named = [owners * part + owner for part, _ in plan for owner in range(owners)]
-
-    @pl.when(step == 0)
+    subs = index_ref.shape[0]
+
+    @pl.when(pl.program_id(0) == 0)
     def _():
         for out in outs:
             out[...] = jnp.zeros(out.shape, out.dtype)
 
     place = lax.broadcasted_iota(jnp.int32, (window, index_ref.shape[2]), 0)
-    first, second = index_ref[0, 0:1, :], index_ref[0, 1:2, :]
-
-    def one_turn(turn, carry):
-        for (part, used), out in zip(plan, outs):
-            spans = []
-            for owner in range(owners):
-                expert = part * owners + owner
-                begin, _, at = window_at(starts_ref, expert, step, turn, window, capacity)
-                shift = expert * capacity
-                near = jnp.where(first >= shift + begin, first - (shift + at), -1)
-                far = jnp.where(second >= shift + begin, second - (shift + at), -1)
-                hit = jnp.where((near >= 0) & (near < window), near, far)
-                spots[window * owner : window * (owner + 1), :] = (
-                    (place == hit).astype(F32).astype(BF)
-                )
-                spans.append(at)
-            for order, which in enumerate(used):
-                got[...] = dot(spots[...], src_refs[which][...])
-                for owner, at in enumerate(spans):
-                    rows = pl.ds(pl.multiple_of(at + order * capacity, 16), window)
-                    held = out[owner, rows, :].astype(F32)
-                    out[owner, rows, :] = (
-                        held + got[window * owner : window * (owner + 1), :]
-                    ).astype(BF)
-        return carry
-
-    lax.fori_loop(0, turns(starts_ref, step, named, window), one_turn, 0)
+    for sub in range(subs):
+        step = pl.program_id(0) * subs + sub
+        block = slice(BLOCK * sub, BLOCK * (sub + 1))
+        first, second = index_ref[sub, 0:1, :], index_ref[sub, 1:2, :]
+
+        def one_turn(turn, carry):
+            for (part, used), out in zip(plan, outs):
+                spans = []
+                for owner in range(owners):
+                    expert = part * owners + owner
+                    begin, _, at = window_at(starts_ref, expert, step, turn, window, capacity)
+                    shift = expert * capacity
+                    near = jnp.where(first >= shift + begin, first - (shift + at), -1)
+                    far = jnp.where(second >= shift + begin, second - (shift + at), -1)
+                    hit = jnp.where((near >= 0) & (near < window), near, far)
+                    spots[window * owner : window * (owner + 1), :] = (
+                        (place == hit).astype(F32).astype(BF)
+                    )
+                    spans.append(at)
+                for order, which in enumerate(used):
+                    got[...] = dot(spots[...], src_refs[which][block, :])
+                    for owner, at in enumerate(spans):
+                        rows = pl.ds(pl.multiple_of(at + order * capacity, 16), window)
+                        held = out[owner, rows, :].astype(F32)
+                        out[owner, rows, :] = (
+                            held + got[window * owner : window * (owner + 1), :]
+                        ).astype(BF)
+            return carry
+
+        lax.fori_loop(0, turns(starts_ref, step, named, window), one_turn, 0)
 
 
 def dispatch(srcs, starts, index_rows, owners, capacity, plan):
     count, width = srcs[0].shape
+    subs = step_blocks(count // BLOCK, SEND_SUBS)
     window = window_rows(starts.shape[0], capacity)
     shapes = [(owners, len(used) * capacity, width) for _, used in plan]
     return pl.pallas_call(
         functools.partial(dispatch_kernel, window, capacity, plan, len(srcs)),
         grid_spec=pltpu.PrefetchScalarGridSpec(
             num_scalar_prefetch=1,
-            grid=(count // BLOCK,),
-            in_specs=[pl.BlockSpec((1, 2, BLOCK), lambda step, *_: (step, 0, 0))]
-            + [pl.BlockSpec((BLOCK, width), lambda step, *_: (step, 0))] * len(srcs),
+            grid=(count // BLOCK // subs,),
+            in_specs=[pl.BlockSpec((subs, 2, BLOCK), lambda step, *_: (step, 0, 0))]
+            + [pl.BlockSpec((BLOCK * subs, width), lambda step, *_: (step, 0))] * len(srcs),
             out_specs=[whole(shape) for shape in shapes],
             scratch_shapes=[
                 pltpu.VMEM((owners * window, BLOCK), BF),
@@ -317,7 +326,7 @@
     )(starts, index_rows, *srcs)
 
 
-def combine_block(window, step, me, starts_ref, index_ref, bufs, own_bufs, wins, acc):
+def combine_block(window, step, me, starts_ref, index, bufs, own_bufs, wins, acc):
     owners, capacity = bufs[0].shape[:2]
     experts = owners * len(bufs)
     lane = lax.broadcasted_iota(jnp.int32, (1, experts * window), 1)
@@ -343,7 +352,7 @@
         total = acc[...]
         for low in range(0, experts * window, CHUNK):
             part = slice(low, min(low + CHUNK, experts * window))
-            hit = (index_ref[:, 0:1] == seen[:, part]) | (index_ref[:, 1:2] == seen[:, part])
+            hit = (index[:, 0:1] == seen[:, part]) | (index[:, 1:2] == seen[:, part])
             total = total + dot(hit.astype(F32).astype(BF), wins[part, :])
         acc[...] = total
         return carry
@@ -359,27 +368,39 @@
 
     @pl.when(step == 0)
     def _():
-        copies = [
-            pltpu.make_async_copy(head_ref.at[:, pl.ds(capacity, early), :], first.at[:, pl.ds(0, early), :], sems.at[0]),
-            pltpu.make_async_copy(tail_ref.at[:, pl.ds(0, late), :], first.at[:, pl.ds(early, late), :], sems.at[1]),
-            pltpu.make_async_copy(tail_ref.at[:, pl.ds(late, capacity), :], second, sems.at[2]),
-        ]
-        for copy in copies:
-            copy.start()
-        for copy in copies:
-            copy.wait()
-        me = pl.ds(here_ref[1], 1)
-        copies = [
-            pltpu.make_async_copy(own_first_ref.at[me], first.at[me, pl.ds(early, late), :], sems.at[3]),
-            pltpu.make_async_copy(own_second_ref, second.at[me], sems.at[4]),
-        ]
-        for copy in copies:
-            copy.start()
-        for copy in copies:
-            copy.wait()
-
-    combine_block(window, step, 0, starts_ref, index_ref, [first, second], [None, None], wins, acc)
-    out_ref[...] = (hidden_ref[...] + acc[...]).astype(BF)
+        me, owners = here_ref[1], first.shape[0]
+
+        def move(go):
+            go(pltpu.make_async_copy(
+                head_ref.at[:, pl.ds(capacity, early), :], first.at[:, pl.ds(0, early), :], sems.at[0]
+            ))
+            for owner in range(owners):
+                to_first = first.at[owner, pl.ds(early, late), :]
+                one, two = sems.at[1 + owner], sems.at[1 + owners + owner]
+
+                @pl.when(me == owner)
+                def _():
+                    go(pltpu.make_async_copy(own_first_ref.at[owner], to_first, one))
+                    go(pltpu.make_async_copy(own_second_ref.at[0], second.at[owner], two))
+
+                @pl.when(me != owner)
+                def _():
+                    go(pltpu.make_async_copy(tail_ref.at[owner, pl.ds(0, late), :], to_first, one))
+                    go(pltpu.make_async_copy(
+                        tail_ref.at[owner, pl.ds(late, capacity), :], second.at[owner], two
+                    ))
+
+        move(lambda copy: copy.start())
+        move(lambda copy: copy.wait())
+
+    subs = hidden_ref.shape[0] // BLOCK
+    for sub in range(subs):
+        rows = slice(BLOCK * sub, BLOCK * (sub + 1))
+        combine_block(
+            window, step * subs + sub, 0, starts_ref, index_ref[rows, :], [first, second],
+            [None, None], wins, acc,
+        )
+        out_ref[rows, :] = (hidden_ref[rows, :] + acc[...]).astype(BF)
 
 
 def top(starts, here, index, hidden, head, tail, own_first, own_second, early, capacity):
@@ -387,17 +408,18 @@
     experts = starts.shape[0]
     window = window_rows(experts, capacity)
     row = lambda shape: pl.BlockSpec(shape, lambda step, *_: (step, 0))
+    tall = BLOCK * step_blocks(count // BLOCK, TOP_SUBS)
     held = pltpu.VMEM((head.shape[0], capacity, width), BF)
     return pl.pallas_call(
         functools.partial(top_kernel, early),
         grid_spec=pltpu.PrefetchScalarGridSpec(
             num_scalar_prefetch=2,
-            grid=(count // BLOCK,),
-            in_specs=[row((BLOCK, 2)), row((BLOCK, width))] + [pl.BlockSpec(memory_space=pl.ANY)] * 4,
-            out_specs=row((BLOCK, width)),
+            grid=(count // tall,),
+            in_specs=[row((tall, 2)), row((tall, width))] + [pl.BlockSpec(memory_space=pl.ANY)] * 4,
+            out_specs=pl.BlockSpec((tall, width), lambda step, *_: (step, 0)),
             scratch_shapes=[
                 held, held, pltpu.VMEM((experts * window, width), BF),
-                pltpu.VMEM((BLOCK, width), F32), pltpu.SemaphoreType.DMA((5,)),
+                pltpu.VMEM((BLOCK, width), F32), pltpu.SemaphoreType.DMA((1 + 2 * head.shape[0],)),
             ],
         ),
         out_shape=jax.ShapeDtypeStruct((count, width), BF),
@@ -592,7 +614,9 @@
         for ref in (acc_qkv, acc_proj, acc_gain):
             ref[...] = jnp.zeros(ref.shape, F32)
 
-    combine_block(window, step, here_ref[1], starts_ref, index_ref, bufs, own_bufs, wins, acc)
+    combine_block(
+        window, step, here_ref[1], starts_ref, index_ref[...], bufs, own_bufs, wins, acc
+    )
     clear_gaps(padded)
     hat_two, scale_two = norm_parts(hidden_ref[...])
     grad_normed = acc[...]
@@ -731,24 +755,29 @@
 
 def last_kernel(dqkv_ref, ghid_ref, tok_ref, gain_one_ref, qkv_w_ref, *refs):
     out_ref, compact, padded = refs[-3:]
-    padded[...] = dot_rt(dqkv_ref[...], qkv_w_ref[...])
-    gather_rows(padded, compact)
-    hat_one, scale_one = norm_parts(tok_ref[...].astype(F32))
-    out_ref[...] = ghid_ref[...] + norm_back(compact[...], hat_one, scale_one, gain_one_ref[...])
+    for sub in range(tok_ref.shape[0] // BLOCK):
+        rows = slice(BLOCK * sub, BLOCK * (sub + 1))
+        spread = slice(BLOCK_PAD * sub, BLOCK_PAD * (sub + 1))
+        padded[...] = dot_rt(dqkv_ref[spread, :], qkv_w_ref[...])
+        gather_rows(padded, compact)
+        hat_one, scale_one = norm_parts(tok_ref[rows, :].astype(F32))
+        out_ref[rows, :] = ghid_ref[rows, :] + norm_back(
+            compact[...], hat_one, scale_one, gain_one_ref[...]
+        )
 
 
 def last(low, high, so_far, dqkv, ghid, tokens, gain_one, w_qkv):
     count, width = tokens.shape
-    row = lambda shape: pl.BlockSpec(shape, lambda step: (step + low, 0))
+    subs = max(n for n in range(1, LAST_SUBS + 1) if low % n == 0 and high % n == 0)
+    row = lambda tall: pl.BlockSpec((tall * subs, width), lambda step: (step + low // subs, 0))
+    wide = pl.BlockSpec((BLOCK_PAD * subs, 3 * width), lambda step: (step + low // subs, 0))
     taken = [] if so_far is None else [so_far]
     return pl.pallas_call(
         last_kernel,
-        grid=(high - low,),
-        in_specs=[
-            row((BLOCK_PAD, 3 * width)), row((BLOCK, width)), row((BLOCK, width)),
-            whole((1, width)), whole(w_qkv.shape),
-        ] + [pl.BlockSpec(memory_space=pl.ANY)] * len(taken),
-        out_specs=row((BLOCK, width)),
+        grid=((high - low) // subs,),
+        in_specs=[wide, row(BLOCK), row(BLOCK), whole((1, width)), whole(w_qkv.shape)]
+        + [pl.BlockSpec(memory_space=pl.ANY)] * len(taken),
+        out_specs=row(BLOCK),
         out_shape=jax.ShapeDtypeStruct((count, width), F32),
         scratch_shapes=[pltpu.VMEM((BLOCK, width), F32), pltpu.VMEM((BLOCK_PAD, width), F32)],
         input_output_aliases={5: 0} if taken else {},
@@ -908,12 +937,11 @@
     cores = 2
     groups = (cores, owners, shards // cores)
     here = jnp.stack([row % cores, me, row // cores]).astype(jnp.int32)
-    ids = jnp.arange(experts, dtype=jnp.int32).reshape(owners, local).T.reshape(-1)
 
     def swap(sent):
         return lax.all_to_all(sent, "expert", split_axis=0, concat_axis=0, tiled=True)
 
-    index_rows, starts = places(ids, picks, keep, capacity)
+    index_rows, starts = places(picks, keep, experts, local, capacity)
     send = lambda srcs, *plan: dispatch(srcs, starts, index_rows, owners, capacity, plan)
     (dy_first,) = send([grad_out], (0, (0,)))
     got = swap(dy_first)

time: 364 us -> 359 us (0.986)
  Pallas kernels: 246 us -> 238 us
  transfers between devices with their start and end apart: 22 -> 22, of which waited for: 8 -> 11; matrix products, arithmetic and copies ran while one was open for 2% -> 2% of each run, Pallas kernels for 63% -> 63%
where the time goes in v6:
time: 359 us; the launch traced here: 352 us
  Pallas kernels  238 us (66%)
  starting transfers between devices  47.1 us (13%)
  waiting for transfers between devices  40.8 us (11%)
  between operations  14.8 us (4%)
  local copies, waits for them, and re-layouts  6.72 us (2%)
  other arithmetic  4.32 us (1%)
    pallas_call x4, Pallas kernels, expert_pass(): pl.pallas_call(body, grid_spec=pltpu.PrefetchScalarGridSpec(num_scalar_pr...  115 us
    pallas_call x1, Pallas kernels, back(): pl.pallas_call(functools.partial(back_kernel, window, groups), grid_spec=...  37.6 us
    all_to_all x6, waiting for transfers between devices, swap(): lax.all_to_all(sent, 'expert', split_axis=0, concat_axis=0, tiled=True)  31.3 us
    all_to_all x6, starting transfers between devices, swap(): lax.all_to_all(sent, 'expert', split_axis=0, concat_axis=0, tiled=True)  29.5 us
    pallas_call x3, Pallas kernels, dispatch(): pl.pallas_call(functools.partial(dispatch_kernel, window, capacity, plan,...  23.3 us
    pallas_call x1, Pallas kernels, attend(): pl.pallas_call(attend_kernel, grid=(blocks,), in_specs=[row((BLOCK, width...  20.7 us
    ppermute x14, starting transfers between devices, jump(): return lax.ppermute(value, axis, [(at, at ^ far) for at in range(size)])  17.4 us
    pallas_call x2, Pallas kernels, last(): pl.pallas_call(last_kernel, grid=((high - low) // subs,), in_specs=[wide,...  15.1 us
  transfers between devices with their start and end apart: 22, of which 11 were waited for; matrix products, arithmetic and copies ran while one was open for 2% of the time, Pallas kernels for 63%

profile of v6, /device:TPU:0, one launch (start us, length us, event | category | flops | bytes accessed | tf_op | source)
XLA Modules:
  0.0 352.2 jit_solution(11252264415810933270)
XLA Ops:
  9.1 6.7 %dispatch.3.refs_6_ = bf16[4,624,512]{2,1,0:T(8,128)(2,1)} custom-call(s32[8,128]{1,0:T(8,128)} %get-tuple-element.80.starts_ref, s32[6,2,392]{2,1,0:T(2,128)} %get-tuple-element.81.index_ref, bf16[2352,512]{1,0:T(8,128)(2,1)} %dy_ref.1), custom_call_target="tpu_custom_call" | custom-call | flops 6000000000 | bytes 8000000 | tf_op jit(solution)/shard_map/dispatch/pallas_call | solution.py:309
  15.8 5.3 %all-to-all-start = ((bf16[4,624,512]{2,1,0:T(8,128)(2,1)}), bf16[4,624,512]{2,1,0:T(8,128)(2,1)}, u32[]{:S(2)}, u32[]{:S(2)}) async-start(bf16[4,624,512]{2,1,0:T(8,128)(2,1)} %dispatch.3.refs_6_), calls=%async_computation | async-start | bytes 5111808 | tf_op jit(solution)/shard_map/all_to_all | solution.py:942
  21.2 20.7 %attend.1 = (f32[2352,512]{1,0:T(8,128)}, bf16[2352,512]{1,0:T(8,128)(2,1)}, bf16[2688,1536]{1,0:T(8,128)(2,1)}, bf16[21504,112]{1,0:T(8,128)(2,1)}, bf16[2688,512]{1,0:T(8,128)(2,1)}) custom-call(bf16[2352,512]{1,0:T(8,128)(2,1)} %tok_ref.6, f32[1,512]{1,0:T(1,128)} %bitcast.45, bf16[512,1536]{1,0:T(8,128)(2,1)} %qkv_w_ref.7, bf16[512,512]{1,0:T(8,128)(2,1)} %proj_w_ref.3, ...), custom_call_target="tpu_custom_call" | custom-call | flops 6870269952 | bytes 30000000 | tf_op jit(solution)/shard_map/attend/pallas_call | solution.py:164
  41.9 6.7 %dispatch.4.refs_5_ = bf16[4,624,512]{2,1,0:T(8,128)(2,1)} custom-call(s32[8,128]{1,0:T(8,128)} %get-tuple-element.80.starts_ref, s32[6,2,392]{2,1,0:T(2,128)} %get-tuple-element.81.index_ref, bf16[2352,512]{1,0:T(8,128)(2,1)} %get-tuple-element.95.refs_0_), custom_call_target="tpu_custom_call" | custom-call | flops 6000000000 | bytes 8000000 | tf_op jit(solution)/shard_map/dispatch/pallas_call | solution.py:309
  48.5 3.3 all-to-all-done.refs_6_
  51.8 4.5 %all-to-all-start.1 = ((bf16[4,624,512]{2,1,0:T(8,128)(2,1)}), bf16[4,624,512]{2,1,0:T(8,128)(2,1)}, u32[]{:S(2)}, u32[]{:S(2)}) async-start(bf16[4,624,512]{2,1,0:T(8,128)(2,1)} %dispatch.4.refs_5_), calls=%async_computation.1 | async-start | bytes 5111808 | tf_op jit(solution)/shard_map/all_to_all | solution.py:942
  58.5 10.0 %dispatch.5.refs_5_.refs_6_ = bf16[4,1248,512]{2,1,0:T(8,128)(2,1)} custom-call(s32[8,128]{1,0:T(8,128)} %get-tuple-element.80.starts_ref, s32[6,2,392]{2,1,0:T(2,128)} %get-tuple-element.81.index_ref, bf16[2352,512]{1,0:T(8,128)(2,1)} %get-tuple-element.95.refs_0_, bf16[2352,512]{1,0:T(8,128)(2,1)} %dy_ref.1), custom_call_target="tpu_custom_call" | custom-call | flops 6000000000 | bytes 8000000 | tf_op jit(solution)/shard_map/dispatch/pallas_call | solution.py:309
  68.5 15.5 %expert_own.2 = (bf16[4,928,512]{2,1,0:T(8,128)(2,1)}, bf16[4,320,512]{2,1,0:T(8,128)(2,1)}, bf16[512,2048]{1,0:T(8,128)(2,1)}, bf16[512,2048]{1,0:T(8,128)(2,1)}, f32[512,128]{1,0:T(8,128)}) custom-call(s32[2]{0:T(128)} %pad_add_fusion.1.refs_0_, bf16[2,512,2048]{2,1,0:T(8,128)(2,1)} %refs_1_.9, bf16[2,2048,512]{2,1,0:T(8,128)(2,1)} %refs_2_.7, ...), custom_call_target="tpu_custom_call" | custom-call | flops 13086228480 | bytes 30000000 | tf_op jit(solution)/shard_map/expert_own/pallas_call | solution.py:572
  85.9 5.0 %all-to-all-start.2 = ((bf16[4,1248,512]{2,1,0:T(8,128)(2,1)}), bf16[4,1248,512]{2,1,0:T(8,128)(2,1)}, u32[]{:S(2)}, u32[]{:S(2)}) async-start(bf16[4,1248,512]{2,1,0:T(8,128)(2,1)} %dispatch.5.refs_5_.refs_6_), calls=%async_computation.2 | async-start | bytes 10223616 | tf_op jit(solution)/shard_map/all_to_all | solution.py:942
  91.0 41.7 %expert_others.2 = (bf16[4,928,512]{2,1,0:T(8,128)(2,1)}, bf16[4,320,512]{2,1,0:T(8,128)(2,1)}, bf16[8,128,2048]{2,1,0:T(8,128)(2,1)}, f32[512,128]{1,0:T(8,128)}) custom-call(s32[2]{0:T(128)} %pad_add_fusion.1.refs_0_, bf16[2,512,2048]{2,1,0:T(8,128)(2,1)} %refs_1_.9, ...), custom_call_target="tpu_custom_call", output_to_operand_aliasing={{0}: (10, {}), {1}: (11, {})} | custom-call | flops 39258685440 | bytes 30000000 | tf_op jit(solution)/shard_map/expert_others/pallas_call | solution.py:572
  133.4 14.2 %all-to-all-done.2.refs_5_.refs_6_ = bf16[4,1248,512]{2,1,0:T(8,128)(2,1)} async-done(((bf16[4,1248,512]{2,1,0:T(8,128)(2,1)}), bf16[4,1248,512]{2,1,0:T(8,128)(2,1)}, u32[]{:S(2)}, u32[]{:S(2)}) %all-to-all-start.2) | async-done | bytes 5111840 | tf_op jit(solution)/shard_map/all_to_all | solution.py:942
  147.6 4.9 %all-to-all-start.3 = ((bf16[4,928,512]{2,1,0:T(8,128)(2,1)}), bf16[4,928,512]{2,1,0:T(8,128)(2,1)}, u32[]{:S(2)}, u32[]{:S(2)}) async-start(bf16[4,928,512]{2,1,0:T(8,128)(2,1)} %get-tuple-element.97), calls=%async_computation.3 | async-start | bytes 7602176 | tf_op jit(solution)/shard_map/all_to_all | solution.py:942
  152.6 40.0 %expert_others.3 = (bf16[4,624,512]{2,1,0:T(8,128)(2,1)}, bf16[4,944,512]{2,1,0:T(8,128)(2,1)}, bf16[512,2048]{1,0:T(8,128)(2,1)}, bf16[512,2048]{1,0:T(8,128)(2,1)}, f32[512,128]{1,0:T(8,128)}) custom-call(s32[2]{0:T(128)} %pad_add_fusion.2.refs_0_, bf16[2,512,2048]{2,1,0:T(8,128)(2,1)} %refs_1_.9, bf16[2,2048,512]{2,1,0:T(8,128)(2,1)} %refs_2_.7, ...), custom_call_target="tpu_custom_call" | custom-call | flops 39258685440 | bytes 30000000 | tf_op jit(solution)/shard_map/expert_others/pallas_call | solution.py:572
  195.2 4.7 %all-to-all-start.4 = ((bf16[4,624,512]{2,1,0:T(8,128)(2,1)}), bf16[4,624,512]{2,1,0:T(8,128)(2,1)}, u32[]{:S(2)}, u32[]{:S(2)}) async-start(bf16[4,624,512]{2,1,0:T(8,128)(2,1)} %get-tuple-element.100), calls=%async_computation.4 | async-start | bytes 5111808 | tf_op jit(solution)/shard_map/all_to_all | solution.py:942
  202.2 17.6 %expert_own.3 = (bf16[1,624,512]{2,1,0:T(8,128)(2,1)}, bf16[1,624,512]{2,1,0:T(8,128)(2,1)}, bf16[8,128,2048]{2,1,0:T(8,128)(2,1)}, f32[512,128]{1,0:T(8,128)}) custom-call(s32[2]{0:T(128)} %pad_add_fusion.2.refs_0_, bf16[2,512,2048]{2,1,0:T(8,128)(2,1)} %refs_1_.9, bf16[2,2048,512]{2,1,0:T(8,128)(2,1)} %refs_2_.7, bf16[512,256]{1,0:T(8,128)(2,1)} %copy.25.refs_3_, ...), custom_call_target="tpu_custom_call" | custom-call | flops 13086228480 | bytes 30000000 | tf_op jit(solution)/shard_map/expert_own/pallas_call | solution.py:572
  219.9 9.3 %all-to-all-done.4.refs_1_ = bf16[4,624,512]{2,1,0:T(8,128)(2,1)} async-done(((bf16[4,624,512]{2,1,0:T(8,128)(2,1)}), bf16[4,624,512]{2,1,0:T(8,128)(2,1)}, u32[]{:S(2)}, u32[]{:S(2)}) %all-to-all-start.4) | async-done | bytes 2555936 | tf_op jit(solution)/shard_map/all_to_all | solution.py:942
  229.2 5.0 %all-to-all-start.5 = ((bf16[4,944,512]{2,1,0:T(8,128)(2,1)}), bf16[4,944,512]{2,1,0:T(8,128)(2,1)}, u32[]{:S(2)}, u32[]{:S(2)}) async-start(bf16[4,944,512]{2,1,0:T(8,128)(2,1)} %get-tuple-element.114), calls=%async_computation.5 | async-start | bytes 7733248 | tf_op jit(solution)/shard_map/all_to_all | solution.py:942
  234.2 37.6 %back.1 = (f32[2352,512]{1,0:T(8,128)}, bf16[2688,1536]{1,0:T(8,128)(2,1)}, bf16[1040,512]{1,0:T(8,128)(2,1)}, bf16[1040,512]{1,0:T(8,128)(2,1)}) custom-call(s32[8,128]{1,0:T(8,128)} %get-tuple-element.80.starts_ref, s32[3]{0:T(128)} %pad_add_fusion.here_ref, s32[2352,2]{1,0:T(8,128)} %bitcast.35, f32[2352,512]{1,0:T(8,128)} %get-tuple-element.116.hidden_ref, ...), custom_call_target="tpu_custom_call" | custom-call | flops 999999995904 | bytes 4000000000 | tf_op jit(solution)/shard_map/back/pallas_call | solution.py:714
  271.9 2.9 collective-permute-done.refs_1_
  282.6 11.0 %top.1 = bf16[2352,512]{1,0:T(8,128)(2,1)} custom-call(s32[8,128]{1,0:T(8,128)} %get-tuple-element.80.starts_ref, s32[3]{0:T(128)} %pad_add_fusion.here_ref, s32[2352,2]{1,0:T(8,128)} %bitcast.36, f32[2352,512]{1,0:T(8,128)} %get-tuple-element.116.hidden_ref, bf16[4,928,512]{2,1,0:T(8,128)(2,1)} %all-to-all-done.3.refs_0_.head_ref, ...), custom_call_target="tpu_custom_call" | custom-call | flops 6000000000 | bytes 12000000 | tf_op jit(solution)/shard_map/top/pallas_call | solution.py:413
  300.0 3.2 collective-permute-start.5
  316.4 6.2 %last.2.refs_0_ = f32[2352,512]{1,0:T(8,128)} custom-call(bf16[2688,1536]{1,0:T(8,128)(2,1)} %get-tuple-element.143.dqkv_ref, f32[2352,512]{1,0:T(8,128)} %get-tuple-element.139.ghid_ref, bf16[2352,512]{1,0:T(8,128)(2,1)} %tok_ref.6, f32[1,512]{1,0:T(1,128)} %bitcast.47, bf16[512,1536]{1,0:T(8,128)(2,1)} %qkv_w_ref.7), custom_call_target="tpu_custom_call" | custom-call | flops 1409286144 | bytes 20000000 | tf_op jit(solution)/shard_map/last/pallas_call | solution.py:775
  326.2 8.9 %last.3 = f32[2352,512]{1,0:T(8,128)} custom-call(bf16[2688,1536]{1,0:T(8,128)(2,1)} %get-tuple-element.143.dqkv_ref, f32[2352,512]{1,0:T(8,128)} %get-tuple-element.139.ghid_ref, bf16[2352,512]{1,0:T(8,128)(2,1)} %tok_ref.6, f32[1,512]{1,0:T(1,128)} %bitcast.48, bf16[512,1536]{1,0:T(8,128)(2,1)} %qkv_w_ref.7, ...), custom_call_target="tpu_custom_call", output_to_operand_aliasing={{}: (5, {})} | custom-call | flops 2818572288 | bytes 20000000 | tf_op jit(solution)/shard_map/last/pallas_call | solution.py:775
  339.8 5.1 %lay.1 = (f32[512,1536]{1,0:T(8,128)}, f32[512,512]{1,0:T(8,128)}) custom-call(s32[3]{0:T(128)} %pad_add_fusion.here_ref, bf16[16,64,512]{2,1,0:T(8,128)(2,1)} %bitcast.32, bf16[16,64,512]{2,1,0:T(8,128)(2,1)} %collective-permute-done.13.other_ref), custom_call_target="tpu_custom_call" | custom-call | flops 1000000 | bytes 8000000 | tf_op jit(solution)/shard_map/lay/pallas_call | solution.py:810
  (82 shorter events, 47.3 us)
Async XLA Ops:
  15.8 36.0 %all-to-all-start = ((bf16[4,624,512]{2,1,0:T(8,128)(2,1)}), bf16[4,624,512]{2,1,0:T(8,128)(2,1)}, u32[]{:S(2)}, u32[]{:S(2)}) async-start(bf16[4,624,512]{2,1,0:T(8,128)(2,1)} %dispatch.3.refs_6_), calls=%async_computation | async-start | bytes 5111808 | tf_op jit(solution)/shard_map/all_to_all | solution.py:942
  51.8 34.1 %all-to-all-start.1 = ((bf16[4,624,512]{2,1,0:T(8,128)(2,1)}), bf16[4,624,512]{2,1,0:T(8,128)(2,1)}, u32[]{:S(2)}, u32[]{:S(2)}) async-start(bf16[4,624,512]{2,1,0:T(8,128)(2,1)} %dispatch.4.refs_5_), calls=%async_computation.1 | async-start | bytes 5111808 | tf_op jit(solution)/shard_map/all_to_all | solution.py:942
  85.9 61.7 %all-to-all-start.2 = ((bf16[4,1248,512]{2,1,0:T(8,128)(2,1)}), bf16[4,1248,512]{2,1,0:T(8,128)(2,1)}, u32[]{:S(2)}, u32[]{:S(2)}) async-start(bf16[4,1248,512]{2,1,0:T(8,128)(2,1)} %dispatch.5.refs_5_.refs_6_), calls=%async_computation.2 | async-start | bytes 10223616 | tf_op jit(solution)/shard_map/all_to_all | solution.py:942
  90.9 212.3 %reduce-scatter.3.cloned.1.call-start = ((), (), s32[]{:S(2)}) async-start(), calls=%async_computation.8 | async-start | bytes 4718592 | tf_op jit(solution)/shard_map/reduce_scatter | solution.py:978
  147.6 47.6 %all-to-all-start.3 = ((bf16[4,928,512]{2,1,0:T(8,128)(2,1)}), bf16[4,928,512]{2,1,0:T(8,128)(2,1)}, u32[]{:S(2)}, u32[]{:S(2)}) async-start(bf16[4,928,512]{2,1,0:T(8,128)(2,1)} %get-tuple-element.97), calls=%async_computation.3 | async-start | bytes 7602176 | tf_op jit(solution)/shard_map/all_to_all | solution.py:942
  195.2 34.0 %all-to-all-start.4 = ((bf16[4,624,512]{2,1,0:T(8,128)(2,1)}), bf16[4,624,512]{2,1,0:T(8,128)(2,1)}, u32[]{:S(2)}, u32[]{:S(2)}) async-start(bf16[4,624,512]{2,1,0:T(8,128)(2,1)} %get-tuple-element.100), calls=%async_computation.4 | async-start | bytes 5111808 | tf_op jit(solution)/shard_map/all_to_all | solution.py:942
  199.9 103.3 %reduce-scatter.5.cloned.1.call-start = ((), (), s32[]{:S(2)}) async-start(), calls=%async_computation.9 | async-start | bytes 4718592 | tf_op jit(solution)/shard_map/reduce_scatter | solution.py:978
  229.2 49.2 %all-to-all-start.5 = ((bf16[4,944,512]{2,1,0:T(8,128)(2,1)}), bf16[4,944,512]{2,1,0:T(8,128)(2,1)}, u32[]{:S(2)}, u32[]{:S(2)}) async-start(bf16[4,944,512]{2,1,0:T(8,128)(2,1)} %get-tuple-element.114), calls=%async_computation.5 | async-start | bytes 7733248 | tf_op jit(solution)/shard_map/all_to_all | solution.py:942
  271.8 3.0 collective-permute-start
  278.4 15.2 %collective-permute-start.1 = (bf16[272,512]{1,0:T(8,128)(2,1)}, bf16[272,512]{1,0:T(8,128)(2,1)S(1)}, u32[]{:S(2)}, u32[]{:S(2)}) collective-permute-start(bf16[272,512]{1,0:T(8,128)(2,1)} %get-tuple-element.119), channel_id=1, source_target_pairs={{0,1},{1,0},{2,3},{3,2},{4,5},{5,4},{6,7},{7,6},{8,9},{9,8},{10,11... | collective-permute-start | bytes 835592 | tf_op jit(solution)/shard_map/ppermute | solution.py:862
  280.4 13.7 %collective-permute-start.2 = (bf16[272,512]{1,0:T(8,128)(2,1)}, bf16[272,512]{1,0:T(8,128)(2,1)S(1)}, u32[]{:S(2)}, u32[]{:S(2)}) collective-permute-start(bf16[272,512]{1,0:T(8,128)(2,1)} %get-tuple-element.120), channel_id=1, source_target_pairs={{0,2},{1,3},{2,0},{3,1},{4,6},{5,7},{6,4},{7,5},{8,10},{9,11},{10,... | collective-permute-start | bytes 835592 | tf_op jit(solution)/shard_map/ppermute | solution.py:862
  281.9 13.6 %collective-permute-start.3 = (bf16[272,512]{1,0:T(8,128)(2,1)}, bf16[272,512]{1,0:T(8,128)(2,1)S(1)}, u32[]{:S(2)}, u32[]{:S(2)}) collective-permute-start(bf16[272,512]{1,0:T(8,128)(2,1)} %get-tuple-element.121), channel_id=1, source_target_pairs={{0,3},{1,2},{2,1},{3,0},{4,7},{5,6},{6,5},{7,4},{8,11},{9,10},{10,... | collective-permute-start | bytes 835592 | tf_op jit(solution)/shard_map/ppermute | solution.py:862
  298.1 7.7 %collective-permute-start.4 = (bf16[80,512]{1,0:T(8,128)(2,1)}, bf16[80,512]{1,0:T(8,128)(2,1)S(1)}, u32[]{:S(2)}, u32[]{:S(2)}) collective-permute-start(bf16[80,512]{1,0:T(8,128)(2,1)} %get-tuple-element.126), channel_id=1, source_target_pairs={{0,8},{4,12},{8,0},{12,4},{16,24},{20,28},{24,16},{28,20},{1,9},{5... | collective-permute-start | bytes 245768 | tf_op jit(solution)/shard_map/ppermute | solution.py:862
  300.0 7.9 %collective-permute-start.5 = (bf16[80,512]{1,0:T(8,128)(2,1)}, bf16[80,512]{1,0:T(8,128)(2,1)S(1)}, u32[]{:S(2)}, u32[]{:S(2)}) collective-permute-start(bf16[80,512]{1,0:T(8,128)(2,1)} %get-tuple-element.127), channel_id=1, source_target_pairs={{0,16},{4,20},{8,24},{12,28},{16,0},{20,4},{24,8},{28,12},{1,17},{... | collective-permute-start | bytes 245768 | tf_op jit(solution)/shard_map/ppermute | solution.py:862
  303.2 6.5 %collective-permute-start.6 = (bf16[80,512]{1,0:T(8,128)(2,1)}, bf16[80,512]{1,0:T(8,128)(2,1)S(1)}, u32[]{:S(2)}, u32[]{:S(2)}) collective-permute-start(bf16[80,512]{1,0:T(8,128)(2,1)} %get-tuple-element.128), channel_id=1, source_target_pairs={{0,24},{4,28},{8,16},{12,20},{16,8},{20,12},{24,0},{28,4},{1,25},{... | collective-permute-start | bytes 245768 | tf_op jit(solution)/shard_map/ppermute | solution.py:862
  312.0 10.5 %collective-permute-start.9 = (bf16[64,512]{1,0:T(8,128)(2,1)}, bf16[64,512]{1,0:T(8,128)(2,1)S(1)}, u32[]{:S(2)}, u32[]{:S(2)}) collective-permute-start(bf16[64,512]{1,0:T(8,128)(2,1)} %get-tuple-element.137), channel_id=1, source_target_pairs={{0,24},{4,28},{8,16},{12,20},{16,8},{20,12},{24,0},{28,4},{1,25},{... | collective-permute-start | bytes 196616 | tf_op jit(solution)/shard_map/ppermute | solution.py:862
  313.8 8.8 %collective-permute-start.8 = (bf16[64,512]{1,0:T(8,128)(2,1)}, bf16[64,512]{1,0:T(8,128)(2,1)S(1)}, u32[]{:S(2)}, u32[]{:S(2)}) collective-permute-start(bf16[64,512]{1,0:T(8,128)(2,1)} %get-tuple-element.137), channel_id=1, source_target_pairs={{0,16},{4,20},{8,24},{12,28},{16,0},{20,4},{24,8},{28,12},{1,17},{... | collective-permute-start | bytes 196616 | tf_op jit(solution)/shard_map/ppermute | solution.py:862
  313.8 8.8 %collective-permute-start.7 = (bf16[64,512]{1,0:T(8,128)(2,1)}, bf16[64,512]{1,0:T(8,128)(2,1)S(1)}, u32[]{:S(2)}, u32[]{:S(2)}) collective-permute-start(bf16[64,512]{1,0:T(8,128)(2,1)} %get-tuple-element.137), channel_id=1, source_target_pairs={{0,8},{4,12},{8,0},{12,4},{16,24},{20,28},{24,16},{28,20},{1,9},{5... | collective-permute-start | bytes 196616 | tf_op jit(solution)/shard_map/ppermute | solution.py:862
  322.6 14.4 %copy-start.13 = (f32[16,512]{1,0:T(8,128)S(1)}, f32[16,512]{1,0:T(8,128)}, u32[]{:S(2)}) copy-start(f32[16,512]{1,0:T(8,128)} %get-tuple-element.144) | copy-start | bytes 98308
  322.6 15.1 %copy-start.11 = (f32[512]{0:T(512)S(1)}, f32[512]{0:T(512)}, u32[]{:S(2)}) copy-start(f32[512]{0:T(512)} %param.12) | copy-start | bytes 6148
  322.6 12.5 %collective-permute-start.11 = (bf16[4,64,512]{2,1,0:T(8,128)(2,1)S(1)}, bf16[4,64,512]{2,1,0:T(8,128)(2,1)S(1)}, u32[]{:S(2)}, u32[]{:S(2)}) collective-permute-start(bf16[4,64,512]{2,1,0:T(8,128)(2,1)S(1)} %get-tuple-element.154), channel_id=1, source_target_pairs={{0,2},{1,3},{2,0},{3,1},{4,6},{5,7},{6,4},{7,5},{8,10},{9,11},{10,... | collective-permute-start | bytes 786440 | tf_op jit(solution)/shard_map/ppermute | solution.py:862
  323.9 11.2 %collective-permute-start.10 = (bf16[4,64,512]{2,1,0:T(8,128)(2,1)S(1)}, bf16[4,64,512]{2,1,0:T(8,128)(2,1)S(1)}, u32[]{:S(2)}, u32[]{:S(2)}) collective-permute-start(bf16[4,64,512]{2,1,0:T(8,128)(2,1)S(1)} %get-tuple-element.154), channel_id=1, source_target_pairs={{0,1},{1,0},{2,3},{3,2},{4,5},{5,4},{6,7},{7,6},{8,9},{9,8},{10,11... | collective-permute-start | bytes 786440 | tf_op jit(solution)/shard_map/ppermute | solution.py:862
  324.6 10.5 %collective-permute-start.12 = (bf16[4,64,512]{2,1,0:T(8,128)(2,1)S(1)}, bf16[4,64,512]{2,1,0:T(8,128)(2,1)S(1)}, u32[]{:S(2)}, u32[]{:S(2)}) collective-permute-start(bf16[4,64,512]{2,1,0:T(8,128)(2,1)S(1)} %get-tuple-element.154), channel_id=1, source_target_pairs={{0,3},{1,2},{2,1},{3,0},{4,7},{5,6},{6,5},{7,4},{8,11},{9,10},{10,... | collective-permute-start | bytes 786440 | tf_op jit(solution)/shard_map/ppermute | solution.py:862
  336.9 2.9 collective-permute-start.13
  (12 other events, 31.2 us)
Sparse Core Ops, SparseCore 0:
  132.9 51.5 reduce-scatter.2
  220.0 51.5 reduce-scatter.4

commit v7 on v6

--- a/solution.py
+++ b/solution.py
@@ -791,18 +791,27 @@
     cores, sides, layers = groups
     tall, width = own_ref.shape[1:]
     each = width // tall
-    for part in range(4):
-
-        @pl.when(pl.program_id(0) == part)
-        def _():
-            for turn in range(each):
-                core, spot = divmod(part * each + turn, sides * layers)
-                side, layer = divmod(spot, layers)
-                spot = (side ^ here_ref[1]) * layers + (layer ^ here_ref[2])
-                piece = jnp.where(
-                    core == here_ref[0], own_ref[spot].astype(F32), other_ref[spot].astype(F32)
-                )
-                (qkv_ref if part < 3 else proj_ref)[tall * turn : tall * (turn + 1), :] = piece
+
+    def fill(core, source):
+        for place in range(core * 2 * each, (core + 1) * 2 * each):
+            part, turn = divmod(place, each)
+            side, layer = divmod(place % (sides * layers), layers)
+            spot = (side ^ here_ref[1]) * layers + (layer ^ here_ref[2])
+            rows = slice(tall * turn, tall * (turn + 1))
+            if part < 3:
+                qkv_ref[rows, width * part : width * (part + 1)] = source[spot].astype(F32)
+            else:
+                proj_ref[rows, :] = source[spot].astype(F32)
+
+    @pl.when(here_ref[0] == 0)
+    def _():
+        fill(0, own_ref)
+        fill(1, other_ref)
+
+    @pl.when(here_ref[0] == 1)
+    def _():
+        fill(0, other_ref)
+        fill(1, own_ref)
 
 
 def lay(groups, here, own, other):
@@ -811,12 +820,9 @@
         functools.partial(lay_kernel, groups),
         grid_spec=pltpu.PrefetchScalarGridSpec(
             num_scalar_prefetch=1,
-            grid=(4,),
+            grid=(1,),
             in_specs=[whole(own.shape)] * 2,
-            out_specs=[
-                pl.BlockSpec((width, width), lambda step, *_: (0, jnp.minimum(step, 2))),
-                whole((width, width)),
-            ],
+            out_specs=[whole((width, 3 * width)), whole((width, width))],
         ),
         out_shape=[
             jax.ShapeDtypeStruct((width, 3 * width), F32),
@@ -962,7 +968,7 @@
     gap = ((0, 0), (0, LANES - experts))
     router = jnp.concatenate([jnp.pad(head, gap), jnp.pad(rest, gap)], axis=1)
     router_back = jnp.concatenate([jnp.pad(head, gap).T, jnp.pad(rest, gap).T], axis=0)
-    early = 16 * (capacity // 32)
+    early = 16 * (capacity // 39)
     weights = (w_in, w_eout, router, router_back)
 
     def one(part, own, given, before, *taken):

time: 359 us -> 356 us (level)
  waiting for transfers between devices: 40.8 us -> 36.1 us
  transfers between devices with their start and end apart: 22 -> 22, of which waited for: 11 -> 11; matrix products, arithmetic and copies ran while one was open for 2% -> 2% of each run, Pallas kernels for 63% -> 65%
where the time goes in v7:
time: 356 us; the launch traced here: 349 us
  Pallas kernels  240 us (67%)
  starting transfers between devices  46.4 us (13%)
  waiting for transfers between devices  36.1 us (10%)
  between operations  14.8 us (4%)
  local copies, waits for them, and re-layouts  7.43 us (2%)
  other arithmetic  4.36 us (1%)
    pallas_call x4, Pallas kernels, expert_pass(): pl.pallas_call(body, grid_spec=pltpu.PrefetchScalarGridSpec(num_scalar_pr...  115 us
    pallas_call x1, Pallas kernels, back(): pl.pallas_call(functools.partial(back_kernel, window, groups), grid_spec=...  38.3 us
    all_to_all x6, starting transfers between devices, swap(): lax.all_to_all(sent, 'expert', split_axis=0, concat_axis=0, tiled=True)  29.9 us
    all_to_all x6, waiting for transfers between devices, swap(): lax.all_to_all(sent, 'expert', split_axis=0, concat_axis=0, tiled=True)  29.2 us
    pallas_call x3, Pallas kernels, dispatch(): pl.pallas_call(functools.partial(dispatch_kernel, window, capacity, plan,...  24.1 us
    pallas_call x1, Pallas kernels, attend(): pl.pallas_call(attend_kernel, grid=(blocks,), in_specs=[row((BLOCK, width...  20.7 us
    ppermute x14, starting transfers between devices, jump(): return lax.ppermute(value, axis, [(at, at ^ far) for at in range(size)])  16.1 us
    pallas_call x2, Pallas kernels, last(): pl.pallas_call(last_kernel, grid=((high - low) // subs,), in_specs=[wide,...  15.1 us
  transfers between devices with their start and end apart: 22, of which 11 were waited for; matrix products, arithmetic and copies ran while one was open for 2% of the time, Pallas kernels for 65%

profile of v7, /device:TPU:0, one launch (start us, length us, event | category | flops | bytes accessed | tf_op | source)
XLA Modules:
  0.0 349.1 jit_solution(18203300634674762800)
XLA Ops:
  9.1 6.7 %dispatch.3.refs_6_ = bf16[4,624,512]{2,1,0:T(8,128)(2,1)} custom-call(s32[8,128]{1,0:T(8,128)} %get-tuple-element.80.starts_ref, s32[6,2,392]{2,1,0:T(2,128)} %get-tuple-element.81.index_ref, bf16[2352,512]{1,0:T(8,128)(2,1)} %dy_ref.1), custom_call_target="tpu_custom_call" | custom-call | flops 6000000000 | bytes 8000000 | tf_op jit(solution)/shard_map/dispatch/pallas_call | solution.py:309
  15.8 5.7 %all-to-all-start = ((bf16[4,624,512]{2,1,0:T(8,128)(2,1)}), bf16[4,624,512]{2,1,0:T(8,128)(2,1)}, u32[]{:S(2)}, u32[]{:S(2)}) async-start(bf16[4,624,512]{2,1,0:T(8,128)(2,1)} %dispatch.3.refs_6_), calls=%async_computation | async-start | bytes 5111808 | tf_op jit(solution)/shard_map/all_to_all | solution.py:948
  21.6 20.7 %attend.1 = (f32[2352,512]{1,0:T(8,128)}, bf16[2352,512]{1,0:T(8,128)(2,1)}, bf16[2688,1536]{1,0:T(8,128)(2,1)}, bf16[21504,112]{1,0:T(8,128)(2,1)}, bf16[2688,512]{1,0:T(8,128)(2,1)}) custom-call(bf16[2352,512]{1,0:T(8,128)(2,1)} %tok_ref.6, f32[1,512]{1,0:T(1,128)} %bitcast.45, bf16[512,1536]{1,0:T(8,128)(2,1)} %qkv_w_ref.7, bf16[512,512]{1,0:T(8,128)(2,1)} %proj_w_ref.3, ...), custom_call_target="tpu_custom_call" | custom-call | flops 6870269952 | bytes 30000000 | tf_op jit(solution)/shard_map/attend/pallas_call | solution.py:164
  42.3 6.7 %dispatch.4.refs_5_ = bf16[4,624,512]{2,1,0:T(8,128)(2,1)} custom-call(s32[8,128]{1,0:T(8,128)} %get-tuple-element.80.starts_ref, s32[6,2,392]{2,1,0:T(2,128)} %get-tuple-element.81.index_ref, bf16[2352,512]{1,0:T(8,128)(2,1)} %get-tuple-element.95.refs_0_), custom_call_target="tpu_custom_call" | custom-call | flops 6000000000 | bytes 8000000 | tf_op jit(solution)/shard_map/dispatch/pallas_call | solution.py:309
  48.9 3.3 all-to-all-done.refs_6_
  52.2 4.5 %all-to-all-start.1 = ((bf16[4,624,512]{2,1,0:T(8,128)(2,1)}), bf16[4,624,512]{2,1,0:T(8,128)(2,1)}, u32[]{:S(2)}, u32[]{:S(2)}) async-start(bf16[4,624,512]{2,1,0:T(8,128)(2,1)} %dispatch.4.refs_5_), calls=%async_computation.1 | async-start | bytes 5111808 | tf_op jit(solution)/shard_map/all_to_all | solution.py:948
  59.0 10.8 %dispatch.5.refs_5_.refs_6_ = bf16[4,1248,512]{2,1,0:T(8,128)(2,1)} custom-call(s32[8,128]{1,0:T(8,128)} %get-tuple-element.80.starts_ref, s32[6,2,392]{2,1,0:T(2,128)} %get-tuple-element.81.index_ref, bf16[2352,512]{1,0:T(8,128)(2,1)} %get-tuple-element.95.refs_0_, bf16[2352,512]{1,0:T(8,128)(2,1)} %dy_ref.1), custom_call_target="tpu_custom_call" | custom-call | flops 6000000000 | bytes 8000000 | tf_op jit(solution)/shard_map/dispatch/pallas_call | solution.py:309
  69.7 15.5 %expert_own.2 = (bf16[4,880,512]{2,1,0:T(8,128)(2,1)}, bf16[4,368,512]{2,1,0:T(8,128)(2,1)}, bf16[512,2048]{1,0:T(8,128)(2,1)}, bf16[512,2048]{1,0:T(8,128)(2,1)}, f32[512,128]{1,0:T(8,128)}) custom-call(s32[2]{0:T(128)} %pad_add_fusion.1.refs_0_, bf16[2,512,2048]{2,1,0:T(8,128)(2,1)} %refs_1_.9, bf16[2,2048,512]{2,1,0:T(8,128)(2,1)} %refs_2_.7, ...), custom_call_target="tpu_custom_call" | custom-call | flops 13086228480 | bytes 30000000 | tf_op jit(solution)/shard_map/expert_own/pallas_call | solution.py:572
  86.6 5.0 %all-to-all-start.2 = ((bf16[4,1248,512]{2,1,0:T(8,128)(2,1)}), bf16[4,1248,512]{2,1,0:T(8,128)(2,1)}, u32[]{:S(2)}, u32[]{:S(2)}) async-start(bf16[4,1248,512]{2,1,0:T(8,128)(2,1)} %dispatch.5.refs_5_.refs_6_), calls=%async_computation.2 | async-start | bytes 10223616 | tf_op jit(solution)/shard_map/all_to_all | solution.py:948
  91.7 41.7 %expert_others.2 = (bf16[4,880,512]{2,1,0:T(8,128)(2,1)}, bf16[4,368,512]{2,1,0:T(8,128)(2,1)}, bf16[8,128,2048]{2,1,0:T(8,128)(2,1)}, f32[512,128]{1,0:T(8,128)}) custom-call(s32[2]{0:T(128)} %pad_add_fusion.1.refs_0_, bf16[2,512,2048]{2,1,0:T(8,128)(2,1)} %refs_1_.9, ...), custom_call_target="tpu_custom_call", output_to_operand_aliasing={{0}: (10, {}), {1}: (11, {})} | custom-call | flops 39258685440 | bytes 30000000 | tf_op jit(solution)/shard_map/expert_others/pallas_call | solution.py:572
  134.1 14.3 %all-to-all-done.2.refs_5_.refs_6_ = bf16[4,1248,512]{2,1,0:T(8,128)(2,1)} async-done(((bf16[4,1248,512]{2,1,0:T(8,128)(2,1)}), bf16[4,1248,512]{2,1,0:T(8,128)(2,1)}, u32[]{:S(2)}, u32[]{:S(2)}) %all-to-all-start.2) | async-done | bytes 5111840 | tf_op jit(solution)/shard_map/all_to_all | solution.py:948
  148.4 4.9 %all-to-all-start.3 = ((bf16[4,880,512]{2,1,0:T(8,128)(2,1)}), bf16[4,880,512]{2,1,0:T(8,128)(2,1)}, u32[]{:S(2)}, u32[]{:S(2)}) async-start(bf16[4,880,512]{2,1,0:T(8,128)(2,1)} %get-tuple-element.97), calls=%async_computation.3 | async-start | bytes 7208960 | tf_op jit(solution)/shard_map/all_to_all | solution.py:948
  153.3 40.1 %expert_others.3 = (bf16[4,624,512]{2,1,0:T(8,128)(2,1)}, bf16[4,992,512]{2,1,0:T(8,128)(2,1)}, bf16[512,2048]{1,0:T(8,128)(2,1)}, bf16[512,2048]{1,0:T(8,128)(2,1)}, f32[512,128]{1,0:T(8,128)}) custom-call(s32[2]{0:T(128)} %pad_add_fusion.2.refs_0_, bf16[2,512,2048]{2,1,0:T(8,128)(2,1)} %refs_1_.9, bf16[2,2048,512]{2,1,0:T(8,128)(2,1)} %refs_2_.7, ...), custom_call_target="tpu_custom_call" | custom-call | flops 39258685440 | bytes 30000000 | tf_op jit(solution)/shard_map/expert_others/pallas_call | solution.py:572
  193.8 4.7 %all-to-all-start.4 = ((bf16[4,624,512]{2,1,0:T(8,128)(2,1)}), bf16[4,624,512]{2,1,0:T(8,128)(2,1)}, u32[]{:S(2)}, u32[]{:S(2)}) async-start(bf16[4,624,512]{2,1,0:T(8,128)(2,1)} %get-tuple-element.100), calls=%async_computation.4 | async-start | bytes 5111808 | tf_op jit(solution)/shard_map/all_to_all | solution.py:948
  200.9 17.6 %expert_own.3 = (bf16[1,624,512]{2,1,0:T(8,128)(2,1)}, bf16[1,624,512]{2,1,0:T(8,128)(2,1)}, bf16[8,128,2048]{2,1,0:T(8,128)(2,1)}, f32[512,128]{1,0:T(8,128)}) custom-call(s32[2]{0:T(128)} %pad_add_fusion.2.refs_0_, bf16[2,512,2048]{2,1,0:T(8,128)(2,1)} %refs_1_.9, bf16[2,2048,512]{2,1,0:T(8,128)(2,1)} %refs_2_.7, bf16[512,256]{1,0:T(8,128)(2,1)} %copy.25.refs_3_, ...), custom_call_target="tpu_custom_call" | custom-call | flops 13086228480 | bytes 30000000 | tf_op jit(solution)/shard_map/expert_own/pallas_call | solution.py:572
  218.6 9.3 %all-to-all-done.4.refs_1_ = bf16[4,624,512]{2,1,0:T(8,128)(2,1)} async-done(((bf16[4,624,512]{2,1,0:T(8,128)(2,1)}), bf16[4,624,512]{2,1,0:T(8,128)(2,1)}, u32[]{:S(2)}, u32[]{:S(2)}) %all-to-all-start.4) | async-done | bytes 2555936 | tf_op jit(solution)/shard_map/all_to_all | solution.py:948
  227.8 5.1 %all-to-all-start.5 = ((bf16[4,992,512]{2,1,0:T(8,128)(2,1)}), bf16[4,992,512]{2,1,0:T(8,128)(2,1)}, u32[]{:S(2)}, u32[]{:S(2)}) async-start(bf16[4,992,512]{2,1,0:T(8,128)(2,1)} %get-tuple-element.114), calls=%async_computation.5 | async-start | bytes 8126464 | tf_op jit(solution)/shard_map/all_to_all | solution.py:948
  232.9 38.3 %back.1 = (f32[2352,512]{1,0:T(8,128)}, bf16[2688,1536]{1,0:T(8,128)(2,1)}, bf16[1040,512]{1,0:T(8,128)(2,1)}, bf16[1040,512]{1,0:T(8,128)(2,1)}) custom-call(s32[8,128]{1,0:T(8,128)} %get-tuple-element.80.starts_ref, s32[3]{0:T(128)} %pad_add_fusion.here_ref, s32[2352,2]{1,0:T(8,128)} %bitcast.35, f32[2352,512]{1,0:T(8,128)} %get-tuple-element.116.hidden_ref, ...), custom_call_target="tpu_custom_call" | custom-call | flops 999999995904 | bytes 4000000000 | tf_op jit(solution)/shard_map/back/pallas_call | solution.py:714
  271.3 2.9 collective-permute-done.refs_1_
  281.9 11.6 %top.1 = bf16[2352,512]{1,0:T(8,128)(2,1)} custom-call(s32[8,128]{1,0:T(8,128)} %get-tuple-element.80.starts_ref, s32[3]{0:T(128)} %pad_add_fusion.here_ref, s32[2352,2]{1,0:T(8,128)} %bitcast.36, f32[2352,512]{1,0:T(8,128)} %get-tuple-element.116.hidden_ref, bf16[4,880,512]{2,1,0:T(8,128)(2,1)} %all-to-all-done.3.refs_0_.head_ref, ...), custom_call_target="tpu_custom_call" | custom-call | flops 6000000000 | bytes 12000000 | tf_op jit(solution)/shard_map/top/pallas_call | solution.py:413
  302.1 2.6 unpack.1
  313.7 6.2 %last.2.refs_0_ = f32[2352,512]{1,0:T(8,128)} custom-call(bf16[2688,1536]{1,0:T(8,128)(2,1)} %get-tuple-element.143.dqkv_ref, f32[2352,512]{1,0:T(8,128)} %get-tuple-element.139.ghid_ref, bf16[2352,512]{1,0:T(8,128)(2,1)} %tok_ref.6, f32[1,512]{1,0:T(1,128)} %bitcast.47, bf16[512,1536]{1,0:T(8,128)(2,1)} %qkv_w_ref.7), custom_call_target="tpu_custom_call" | custom-call | flops 1409286144 | bytes 20000000 | tf_op jit(solution)/shard_map/last/pallas_call | solution.py:775
  323.7 8.9 %last.3 = f32[2352,512]{1,0:T(8,128)} custom-call(bf16[2688,1536]{1,0:T(8,128)(2,1)} %get-tuple-element.143.dqkv_ref, f32[2352,512]{1,0:T(8,128)} %get-tuple-element.139.ghid_ref, bf16[2352,512]{1,0:T(8,128)(2,1)} %tok_ref.6, f32[1,512]{1,0:T(1,128)} %bitcast.48, bf16[512,1536]{1,0:T(8,128)(2,1)} %qkv_w_ref.7, ...), custom_call_target="tpu_custom_call", output_to_operand_aliasing={{}: (5, {})} | custom-call | flops 2818572288 | bytes 20000000 | tf_op jit(solution)/shard_map/last/pallas_call | solution.py:775
  337.3 4.5 %lay.1 = (f32[512,1536]{1,0:T(8,128)}, f32[512,512]{1,0:T(8,128)}) custom-call(s32[3]{0:T(128)} %pad_add_fusion.here_ref, bf16[16,64,512]{2,1,0:T(8,128)(2,1)} %bitcast.32, bf16[16,64,512]{2,1,0:T(8,128)(2,1)} %collective-permute-done.13.other_ref), custom_call_target="tpu_custom_call" | custom-call | flops 1000000 | bytes 8000000 | tf_op jit(solution)/shard_map/lay/pallas_call | solution.py:819
  (82 shorter events, 42.8 us)
Async XLA Ops:
  15.8 36.4 %all-to-all-start = ((bf16[4,624,512]{2,1,0:T(8,128)(2,1)}), bf16[4,624,512]{2,1,0:T(8,128)(2,1)}, u32[]{:S(2)}, u32[]{:S(2)}) async-start(bf16[4,624,512]{2,1,0:T(8,128)(2,1)} %dispatch.3.refs_6_), calls=%async_computation | async-start | bytes 5111808 | tf_op jit(solution)/shard_map/all_to_all | solution.py:948
  52.2 34.4 %all-to-all-start.1 = ((bf16[4,624,512]{2,1,0:T(8,128)(2,1)}), bf16[4,624,512]{2,1,0:T(8,128)(2,1)}, u32[]{:S(2)}, u32[]{:S(2)}) async-start(bf16[4,624,512]{2,1,0:T(8,128)(2,1)} %dispatch.4.refs_5_), calls=%async_computation.1 | async-start | bytes 5111808 | tf_op jit(solution)/shard_map/all_to_all | solution.py:948
  86.6 61.7 %all-to-all-start.2 = ((bf16[4,1248,512]{2,1,0:T(8,128)(2,1)}), bf16[4,1248,512]{2,1,0:T(8,128)(2,1)}, u32[]{:S(2)}, u32[]{:S(2)}) async-start(bf16[4,1248,512]{2,1,0:T(8,128)(2,1)} %dispatch.5.refs_5_.refs_6_), calls=%async_computation.2 | async-start | bytes 10223616 | tf_op jit(solution)/shard_map/all_to_all | solution.py:948
  91.7 210.4 %reduce-scatter.3.cloned.1.call-start = ((), (), s32[]{:S(2)}) async-start(), calls=%async_computation.8 | async-start | bytes 4718592 | tf_op jit(solution)/shard_map/reduce_scatter | solution.py:984
  148.4 45.4 %all-to-all-start.3 = ((bf16[4,880,512]{2,1,0:T(8,128)(2,1)}), bf16[4,880,512]{2,1,0:T(8,128)(2,1)}, u32[]{:S(2)}, u32[]{:S(2)}) async-start(bf16[4,880,512]{2,1,0:T(8,128)(2,1)} %get-tuple-element.97), calls=%async_computation.3 | async-start | bytes 7208960 | tf_op jit(solution)/shard_map/all_to_all | solution.py:948
  193.8 34.0 %all-to-all-start.4 = ((bf16[4,624,512]{2,1,0:T(8,128)(2,1)}), bf16[4,624,512]{2,1,0:T(8,128)(2,1)}, u32[]{:S(2)}, u32[]{:S(2)}) async-start(bf16[4,624,512]{2,1,0:T(8,128)(2,1)} %get-tuple-element.100), calls=%async_computation.4 | async-start | bytes 5111808 | tf_op jit(solution)/shard_map/all_to_all | solution.py:948
  198.5 103.6 %reduce-scatter.5.cloned.1.call-start = ((), (), s32[]{:S(2)}) async-start(), calls=%async_computation.9 | async-start | bytes 4718592 | tf_op jit(solution)/shard_map/reduce_scatter | solution.py:984
  227.8 50.5 %all-to-all-start.5 = ((bf16[4,992,512]{2,1,0:T(8,128)(2,1)}), bf16[4,992,512]{2,1,0:T(8,128)(2,1)}, u32[]{:S(2)}, u32[]{:S(2)}) async-start(bf16[4,992,512]{2,1,0:T(8,128)(2,1)} %get-tuple-element.114), calls=%async_computation.5 | async-start | bytes 8126464 | tf_op jit(solution)/shard_map/all_to_all | solution.py:948
  271.2 3.0 collective-permute-start
  278.4 15.1 %collective-permute-start.1 = (bf16[272,512]{1,0:T(8,128)(2,1)}, bf16[272,512]{1,0:T(8,128)(2,1)S(1)}, u32[]{:S(2)}, u32[]{:S(2)}) collective-permute-start(bf16[272,512]{1,0:T(8,128)(2,1)} %get-tuple-element.119), channel_id=1, source_target_pairs={{0,1},{1,0},{2,3},{3,2},{4,5},{5,4},{6,7},{7,6},{8,9},{9,8},{10,11... | collective-permute-start | bytes 835592 | tf_op jit(solution)/shard_map/ppermute | solution.py:868
  279.8 14.5 %collective-permute-start.2 = (bf16[272,512]{1,0:T(8,128)(2,1)}, bf16[272,512]{1,0:T(8,128)(2,1)S(1)}, u32[]{:S(2)}, u32[]{:S(2)}) collective-permute-start(bf16[272,512]{1,0:T(8,128)(2,1)} %get-tuple-element.120), channel_id=1, source_target_pairs={{0,2},{1,3},{2,0},{3,1},{4,6},{5,7},{6,4},{7,5},{8,10},{9,11},{10,... | collective-permute-start | bytes 835592 | tf_op jit(solution)/shard_map/ppermute | solution.py:868
  281.2 13.1 %collective-permute-start.3 = (bf16[272,512]{1,0:T(8,128)(2,1)}, bf16[272,512]{1,0:T(8,128)(2,1)S(1)}, u32[]{:S(2)}, u32[]{:S(2)}) collective-permute-start(bf16[272,512]{1,0:T(8,128)(2,1)} %get-tuple-element.121), channel_id=1, source_target_pairs={{0,3},{1,2},{2,1},{3,0},{4,7},{5,6},{6,5},{7,4},{8,11},{9,10},{10,... | collective-permute-start | bytes 835592 | tf_op jit(solution)/shard_map/ppermute | solution.py:868
  297.7 7.0 %collective-permute-start.4 = (bf16[80,512]{1,0:T(8,128)(2,1)}, bf16[80,512]{1,0:T(8,128)(2,1)S(1)}, u32[]{:S(2)}, u32[]{:S(2)}) collective-permute-start(bf16[80,512]{1,0:T(8,128)(2,1)} %get-tuple-element.126), channel_id=1, source_target_pairs={{0,8},{4,12},{8,0},{12,4},{16,24},{20,28},{24,16},{28,20},{1,9},{5... | collective-permute-start | bytes 245768 | tf_op jit(solution)/shard_map/ppermute | solution.py:868
  299.1 6.4 %collective-permute-start.5 = (bf16[80,512]{1,0:T(8,128)(2,1)}, bf16[80,512]{1,0:T(8,128)(2,1)S(1)}, u32[]{:S(2)}, u32[]{:S(2)}) collective-permute-start(bf16[80,512]{1,0:T(8,128)(2,1)} %get-tuple-element.127), channel_id=1, source_target_pairs={{0,16},{4,20},{8,24},{12,28},{16,0},{20,4},{24,8},{28,12},{1,17},{... | collective-permute-start | bytes 245768 | tf_op jit(solution)/shard_map/ppermute | solution.py:868
  300.4 6.6 %collective-permute-start.6 = (bf16[80,512]{1,0:T(8,128)(2,1)}, bf16[80,512]{1,0:T(8,128)(2,1)S(1)}, u32[]{:S(2)}, u32[]{:S(2)}) collective-permute-start(bf16[80,512]{1,0:T(8,128)(2,1)} %get-tuple-element.128), channel_id=1, source_target_pairs={{0,24},{4,28},{8,16},{12,20},{16,8},{20,12},{24,0},{28,4},{1,25},{... | collective-permute-start | bytes 245768 | tf_op jit(solution)/shard_map/ppermute | solution.py:868
  309.3 10.5 %collective-permute-start.9 = (bf16[64,512]{1,0:T(8,128)(2,1)}, bf16[64,512]{1,0:T(8,128)(2,1)S(1)}, u32[]{:S(2)}, u32[]{:S(2)}) collective-permute-start(bf16[64,512]{1,0:T(8,128)(2,1)} %get-tuple-element.137), channel_id=1, source_target_pairs={{0,24},{4,28},{8,16},{12,20},{16,8},{20,12},{24,0},{28,4},{1,25},{... | collective-permute-start | bytes 196616 | tf_op jit(solution)/shard_map/ppermute | solution.py:868
  311.0 8.9 %collective-permute-start.8 = (bf16[64,512]{1,0:T(8,128)(2,1)}, bf16[64,512]{1,0:T(8,128)(2,1)S(1)}, u32[]{:S(2)}, u32[]{:S(2)}) collective-permute-start(bf16[64,512]{1,0:T(8,128)(2,1)} %get-tuple-element.137), channel_id=1, source_target_pairs={{0,16},{4,20},{8,24},{12,28},{16,0},{20,4},{24,8},{28,12},{1,17},{... | collective-permute-start | bytes 196616 | tf_op jit(solution)/shard_map/ppermute | solution.py:868
  311.6 8.2 %collective-permute-start.7 = (bf16[64,512]{1,0:T(8,128)(2,1)}, bf16[64,512]{1,0:T(8,128)(2,1)S(1)}, u32[]{:S(2)}, u32[]{:S(2)}) collective-permute-start(bf16[64,512]{1,0:T(8,128)(2,1)} %get-tuple-element.137), channel_id=1, source_target_pairs={{0,8},{4,12},{8,0},{12,4},{16,24},{20,28},{24,16},{28,20},{1,9},{5... | collective-permute-start | bytes 196616 | tf_op jit(solution)/shard_map/ppermute | solution.py:868
  319.9 14.6 %copy-start.13 = (f32[16,512]{1,0:T(8,128)S(1)}, f32[16,512]{1,0:T(8,128)}, u32[]{:S(2)}) copy-start(f32[16,512]{1,0:T(8,128)} %get-tuple-element.144) | copy-start | bytes 98308
  319.9 15.3 %copy-start.11 = (f32[512]{0:T(512)S(1)}, f32[512]{0:T(512)}, u32[]{:S(2)}) copy-start(f32[512]{0:T(512)} %param.12) | copy-start | bytes 6148
  319.9 12.7 %collective-permute-start.11 = (bf16[4,64,512]{2,1,0:T(8,128)(2,1)S(1)}, bf16[4,64,512]{2,1,0:T(8,128)(2,1)S(1)}, u32[]{:S(2)}, u32[]{:S(2)}) collective-permute-start(bf16[4,64,512]{2,1,0:T(8,128)(2,1)S(1)} %get-tuple-element.154), channel_id=1, source_target_pairs={{0,2},{1,3},{2,0},{3,1},{4,6},{5,7},{6,4},{7,5},{8,10},{9,11},{10,... | collective-permute-start | bytes 786440 | tf_op jit(solution)/shard_map/ppermute | solution.py:868
  322.1 10.5 %collective-permute-start.10 = (bf16[4,64,512]{2,1,0:T(8,128)(2,1)S(1)}, bf16[4,64,512]{2,1,0:T(8,128)(2,1)S(1)}, u32[]{:S(2)}, u32[]{:S(2)}) collective-permute-start(bf16[4,64,512]{2,1,0:T(8,128)(2,1)S(1)} %get-tuple-element.154), channel_id=1, source_target_pairs={{0,1},{1,0},{2,3},{3,2},{4,5},{5,4},{6,7},{7,6},{8,9},{9,8},{10,11... | collective-permute-start | bytes 786440 | tf_op jit(solution)/shard_map/ppermute | solution.py:868
  322.4 10.2 %collective-permute-start.12 = (bf16[4,64,512]{2,1,0:T(8,128)(2,1)S(1)}, bf16[4,64,512]{2,1,0:T(8,128)(2,1)S(1)}, u32[]{:S(2)}, u32[]{:S(2)}) collective-permute-start(bf16[4,64,512]{2,1,0:T(8,128)(2,1)S(1)} %get-tuple-element.154), channel_id=1, source_target_pairs={{0,3},{1,2},{2,1},{3,0},{4,7},{5,6},{6,5},{7,4},{8,11},{9,10},{10,... | collective-permute-start | bytes 786440 | tf_op jit(solution)/shard_map/ppermute | solution.py:868
  334.4 2.9 collective-permute-start.13
  (12 other events, 28.1 us)
Sparse Core Ops, SparseCore 0:
  133.6 50.8 reduce-scatter.2
  218.7 50.8 reduce-scatter.4

commit v8 on v7

--- a/solution.py
+++ b/solution.py
@@ -18,14 +18,15 @@
 BF = jnp.bfloat16
 F32 = jnp.float32
 VMEM_BYTES = 62 * 1024 * 1024
+VMEM_ALL = 64 * 1024 * 1024 - 32 * 1024
 FCUT = 256
 CHUNK = 256
 TOP_SUBS, SEND_SUBS, LAST_SUBS = 2, 2, 2
 
 
-def params():
+def params(grant=VMEM_BYTES):
     return pltpu.CompilerParams(
-        dimension_semantics=("arbitrary",), vmem_limit_bytes=VMEM_BYTES
+        dimension_semantics=("arbitrary",), vmem_limit_bytes=grant
     )
 
 
@@ -828,7 +829,7 @@
             jax.ShapeDtypeStruct((width, 3 * width), F32),
             jax.ShapeDtypeStruct((width, width), F32),
         ],
-        compiler_params=params(),
+        compiler_params=params(VMEM_ALL),
         cost_estimate=cost(1e6, 8e6),
         name="lay",
     )(here, own, other)
@@ -901,7 +902,7 @@
         in_specs=[whole((rows, width))] * len(parts),
         out_specs=[whole(out.shape) for out in outs],
         out_shape=outs,
-        compiler_params=params(),
+        compiler_params=params(VMEM_ALL),
         cost_estimate=cost(1e6, 4e6),
         name="merge",
     )(*parts)

time: 356 us -> 353 us (level)
  waiting for transfers between devices: 36.1 us -> 40.4 us
  transfers between devices with their start and end apart: 22 -> 22, of which waited for: 11 -> 11; matrix products, arithmetic and copies ran while one was open for 2% -> 2% of each run, Pallas kernels for 65% -> 64%
where the time goes in v8:
time: 353 us; the launch traced here: 347 us
  Pallas kernels  238 us (67%)
  starting transfers between devices  45.8 us (13%)
  waiting for transfers between devices  40.4 us (11%)
  between operations  14.8 us (4%)
  local copies, waits for them, and re-layouts  4.55 us (1%)
    pallas_call x4, Pallas kernels, expert_pass(): pl.pallas_call(body, grid_spec=pltpu.PrefetchScalarGridSpec(num_scalar_pr...  115 us
    pallas_call x1, Pallas kernels, back(): pl.pallas_call(functools.partial(back_kernel, window, groups), grid_spec=...  37.6 us
    all_to_all x6, waiting for transfers between devices, swap(): lax.all_to_all(sent, 'expert', split_axis=0, concat_axis=0, tiled=True)  32.2 us
    all_to_all x6, starting transfers between devices, swap(): lax.all_to_all(sent, 'expert', split_axis=0, concat_axis=0, tiled=True)  29.6 us
    pallas_call x3, Pallas kernels, dispatch(): pl.pallas_call(functools.partial(dispatch_kernel, window, capacity, plan,...  23.3 us
    pallas_call x1, Pallas kernels, attend(): pl.pallas_call(attend_kernel, grid=(blocks,), in_specs=[row((BLOCK, width...  20.7 us
    ppermute x14, starting transfers between devices, jump(): return lax.ppermute(value, axis, [(at, at ^ far) for at in range(size)])  15.9 us
    pallas_call x2, Pallas kernels, last(): pl.pallas_call(last_kernel, grid=((high - low) // subs,), in_specs=[wide,...  15.1 us
  transfers between devices with their start and end apart: 22, of which 11 were waited for; matrix products, arithmetic and copies ran while one was open for 2% of the time, Pallas kernels for 64%

profile of v8, /device:TPU:0, one launch (start us, length us, event | category | flops | bytes accessed | tf_op | source)
XLA Modules:
  0.0 346.6 jit_solution(321572406985910443)
XLA Ops:
  9.1 6.6 %dispatch.3.refs_6_ = bf16[4,624,512]{2,1,0:T(8,128)(2,1)} custom-call(s32[8,128]{1,0:T(8,128)} %get-tuple-element.80.starts_ref, s32[6,2,392]{2,1,0:T(2,128)} %get-tuple-element.81.index_ref, bf16[2352,512]{1,0:T(8,128)(2,1)} %dy_ref.1), custom_call_target="tpu_custom_call" | custom-call | flops 6000000000 | bytes 8000000 | tf_op jit(solution)/shard_map/dispatch/pallas_call | solution.py:310
  15.7 5.3 %all-to-all-start = ((bf16[4,624,512]{2,1,0:T(8,128)(2,1)}), bf16[4,624,512]{2,1,0:T(8,128)(2,1)}, u32[]{:S(2)}, u32[]{:S(2)}) async-start(bf16[4,624,512]{2,1,0:T(8,128)(2,1)} %dispatch.3.refs_6_), calls=%async_computation | async-start | bytes 5111808 | tf_op jit(solution)/shard_map/all_to_all | solution.py:949
  21.1 20.7 %attend.1 = (f32[2352,512]{1,0:T(8,128)}, bf16[2352,512]{1,0:T(8,128)(2,1)}, bf16[2688,1536]{1,0:T(8,128)(2,1)}, bf16[21504,112]{1,0:T(8,128)(2,1)}, bf16[2688,512]{1,0:T(8,128)(2,1)}) custom-call(bf16[2352,512]{1,0:T(8,128)(2,1)} %tok_ref.6, f32[1,512]{1,0:T(1,128)} %bitcast.45, bf16[512,1536]{1,0:T(8,128)(2,1)} %qkv_w_ref.7, bf16[512,512]{1,0:T(8,128)(2,1)} %proj_w_ref.3, ...), custom_call_target="tpu_custom_call" | custom-call | flops 6870269952 | bytes 30000000 | tf_op jit(solution)/shard_map/attend/pallas_call | solution.py:165
  41.9 6.7 %dispatch.4.refs_5_ = bf16[4,624,512]{2,1,0:T(8,128)(2,1)} custom-call(s32[8,128]{1,0:T(8,128)} %get-tuple-element.80.starts_ref, s32[6,2,392]{2,1,0:T(2,128)} %get-tuple-element.81.index_ref, bf16[2352,512]{1,0:T(8,128)(2,1)} %get-tuple-element.95.refs_0_), custom_call_target="tpu_custom_call" | custom-call | flops 6000000000 | bytes 8000000 | tf_op jit(solution)/shard_map/dispatch/pallas_call | solution.py:310
  48.5 3.7 %all-to-all-done.refs_6_ = bf16[4,624,512]{2,1,0:T(8,128)(2,1)} async-done(((bf16[4,624,512]{2,1,0:T(8,128)(2,1)}), bf16[4,624,512]{2,1,0:T(8,128)(2,1)}, u32[]{:S(2)}, u32[]{:S(2)}) %all-to-all-start) | async-done | bytes 2555936 | tf_op jit(solution)/shard_map/all_to_all | solution.py:949
  52.2 4.5 %all-to-all-start.1 = ((bf16[4,624,512]{2,1,0:T(8,128)(2,1)}), bf16[4,624,512]{2,1,0:T(8,128)(2,1)}, u32[]{:S(2)}, u32[]{:S(2)}) async-start(bf16[4,624,512]{2,1,0:T(8,128)(2,1)} %dispatch.4.refs_5_), calls=%async_computation.1 | async-start | bytes 5111808 | tf_op jit(solution)/shard_map/all_to_all | solution.py:949
  58.9 10.0 %dispatch.5.refs_5_.refs_6_ = bf16[4,1248,512]{2,1,0:T(8,128)(2,1)} custom-call(s32[8,128]{1,0:T(8,128)} %get-tuple-element.80.starts_ref, s32[6,2,392]{2,1,0:T(2,128)} %get-tuple-element.81.index_ref, bf16[2352,512]{1,0:T(8,128)(2,1)} %get-tuple-element.95.refs_0_, bf16[2352,512]{1,0:T(8,128)(2,1)} %dy_ref.1), custom_call_target="tpu_custom_call" | custom-call | flops 6000000000 | bytes 8000000 | tf_op jit(solution)/shard_map/dispatch/pallas_call | solution.py:310
  68.8 15.5 %expert_own.2 = (bf16[4,880,512]{2,1,0:T(8,128)(2,1)}, bf16[4,368,512]{2,1,0:T(8,128)(2,1)}, bf16[512,2048]{1,0:T(8,128)(2,1)}, bf16[512,2048]{1,0:T(8,128)(2,1)}, f32[512,128]{1,0:T(8,128)}) custom-call(s32[2]{0:T(128)} %pad_add_fusion.1.refs_0_, bf16[2,512,2048]{2,1,0:T(8,128)(2,1)} %refs_1_.9, bf16[2,2048,512]{2,1,0:T(8,128)(2,1)} %refs_2_.7, ...), custom_call_target="tpu_custom_call" | custom-call | flops 13086228480 | bytes 30000000 | tf_op jit(solution)/shard_map/expert_own/pallas_call | solution.py:573
  86.7 5.0 %all-to-all-start.2 = ((bf16[4,1248,512]{2,1,0:T(8,128)(2,1)}), bf16[4,1248,512]{2,1,0:T(8,128)(2,1)}, u32[]{:S(2)}, u32[]{:S(2)}) async-start(bf16[4,1248,512]{2,1,0:T(8,128)(2,1)} %dispatch.5.refs_5_.refs_6_), calls=%async_computation.2 | async-start | bytes 10223616 | tf_op jit(solution)/shard_map/all_to_all | solution.py:949
  91.8 41.6 %expert_others.2 = (bf16[4,880,512]{2,1,0:T(8,128)(2,1)}, bf16[4,368,512]{2,1,0:T(8,128)(2,1)}, bf16[8,128,2048]{2,1,0:T(8,128)(2,1)}, f32[512,128]{1,0:T(8,128)}) custom-call(s32[2]{0:T(128)} %pad_add_fusion.1.refs_0_, bf16[2,512,2048]{2,1,0:T(8,128)(2,1)} %refs_1_.9, ...), custom_call_target="tpu_custom_call", output_to_operand_aliasing={{0}: (10, {}), {1}: (11, {})} | custom-call | flops 39258685440 | bytes 30000000 | tf_op jit(solution)/shard_map/expert_others/pallas_call | solution.py:573
  134.1 14.4 %all-to-all-done.2.refs_5_.refs_6_ = bf16[4,1248,512]{2,1,0:T(8,128)(2,1)} async-done(((bf16[4,1248,512]{2,1,0:T(8,128)(2,1)}), bf16[4,1248,512]{2,1,0:T(8,128)(2,1)}, u32[]{:S(2)}, u32[]{:S(2)}) %all-to-all-start.2) | async-done | bytes 5111840 | tf_op jit(solution)/shard_map/all_to_all | solution.py:949
  148.5 5.0 %all-to-all-start.3 = ((bf16[4,880,512]{2,1,0:T(8,128)(2,1)}), bf16[4,880,512]{2,1,0:T(8,128)(2,1)}, u32[]{:S(2)}, u32[]{:S(2)}) async-start(bf16[4,880,512]{2,1,0:T(8,128)(2,1)} %get-tuple-element.97), calls=%async_computation.3 | async-start | bytes 7208960 | tf_op jit(solution)/shard_map/all_to_all | solution.py:949
  153.5 40.1 %expert_others.3 = (bf16[4,624,512]{2,1,0:T(8,128)(2,1)}, bf16[4,992,512]{2,1,0:T(8,128)(2,1)}, bf16[512,2048]{1,0:T(8,128)(2,1)}, bf16[512,2048]{1,0:T(8,128)(2,1)}, f32[512,128]{1,0:T(8,128)}) custom-call(s32[2]{0:T(128)} %pad_add_fusion.2.refs_0_, bf16[2,512,2048]{2,1,0:T(8,128)(2,1)} %refs_1_.9, bf16[2,2048,512]{2,1,0:T(8,128)(2,1)} %refs_2_.7, ...), custom_call_target="tpu_custom_call" | custom-call | flops 39258685440 | bytes 30000000 | tf_op jit(solution)/shard_map/expert_others/pallas_call | solution.py:573
  194.0 4.7 %all-to-all-start.4 = ((bf16[4,624,512]{2,1,0:T(8,128)(2,1)}), bf16[4,624,512]{2,1,0:T(8,128)(2,1)}, u32[]{:S(2)}, u32[]{:S(2)}) async-start(bf16[4,624,512]{2,1,0:T(8,128)(2,1)} %get-tuple-element.100), calls=%async_computation.4 | async-start | bytes 5111808 | tf_op jit(solution)/shard_map/all_to_all | solution.py:949
  201.1 17.6 %expert_own.3 = (bf16[1,624,512]{2,1,0:T(8,128)(2,1)}, bf16[1,624,512]{2,1,0:T(8,128)(2,1)}, bf16[8,128,2048]{2,1,0:T(8,128)(2,1)}, f32[512,128]{1,0:T(8,128)}) custom-call(s32[2]{0:T(128)} %pad_add_fusion.2.refs_0_, bf16[2,512,2048]{2,1,0:T(8,128)(2,1)} %refs_1_.9, bf16[2,2048,512]{2,1,0:T(8,128)(2,1)} %refs_2_.7, bf16[512,256]{1,0:T(8,128)(2,1)} %copy.25.refs_3_, ...), custom_call_target="tpu_custom_call" | custom-call | flops 13086228480 | bytes 30000000 | tf_op jit(solution)/shard_map/expert_own/pallas_call | solution.py:573
  218.7 9.3 %all-to-all-done.4.refs_1_ = bf16[4,624,512]{2,1,0:T(8,128)(2,1)} async-done(((bf16[4,624,512]{2,1,0:T(8,128)(2,1)}), bf16[4,624,512]{2,1,0:T(8,128)(2,1)}, u32[]{:S(2)}, u32[]{:S(2)}) %all-to-all-start.4) | async-done | bytes 2555936 | tf_op jit(solution)/shard_map/all_to_all | solution.py:949
  228.0 5.1 %all-to-all-start.5 = ((bf16[4,992,512]{2,1,0:T(8,128)(2,1)}), bf16[4,992,512]{2,1,0:T(8,128)(2,1)}, u32[]{:S(2)}, u32[]{:S(2)}) async-start(bf16[4,992,512]{2,1,0:T(8,128)(2,1)} %get-tuple-element.114), calls=%async_computation.5 | async-start | bytes 8126464 | tf_op jit(solution)/shard_map/all_to_all | solution.py:949
  233.1 37.6 %back.1 = (f32[2352,512]{1,0:T(8,128)}, bf16[2688,1536]{1,0:T(8,128)(2,1)}, bf16[1040,512]{1,0:T(8,128)(2,1)}, bf16[1040,512]{1,0:T(8,128)(2,1)}) custom-call(s32[8,128]{1,0:T(8,128)} %get-tuple-element.80.starts_ref, s32[3]{0:T(128)} %pad_add_fusion.here_ref, s32[2352,2]{1,0:T(8,128)} %bitcast.35, f32[2352,512]{1,0:T(8,128)} %get-tuple-element.116.hidden_ref, ...), custom_call_target="tpu_custom_call" | custom-call | flops 999999995904 | bytes 4000000000 | tf_op jit(solution)/shard_map/back/pallas_call | solution.py:715
  270.8 3.0 collective-permute-done.refs_1_
  273.8 2.6 merge.3
  282.0 11.0 %top.1 = bf16[2352,512]{1,0:T(8,128)(2,1)} custom-call(s32[8,128]{1,0:T(8,128)} %get-tuple-element.80.starts_ref, s32[3]{0:T(128)} %pad_add_fusion.here_ref, s32[2352,2]{1,0:T(8,128)} %bitcast.36, f32[2352,512]{1,0:T(8,128)} %get-tuple-element.116.hidden_ref, bf16[4,880,512]{2,1,0:T(8,128)(2,1)} %all-to-all-done.3.refs_0_.head_ref, ...), custom_call_target="tpu_custom_call" | custom-call | flops 6000000000 | bytes 12000000 | tf_op jit(solution)/shard_map/top/pallas_call | solution.py:414
  312.1 6.2 %last.2.refs_0_ = f32[2352,512]{1,0:T(8,128)} custom-call(bf16[2688,1536]{1,0:T(8,128)(2,1)} %get-tuple-element.143.dqkv_ref, f32[2352,512]{1,0:T(8,128)} %get-tuple-element.139.ghid_ref, bf16[2352,512]{1,0:T(8,128)(2,1)} %tok_ref.6, f32[1,512]{1,0:T(1,128)} %bitcast.47, bf16[512,1536]{1,0:T(8,128)(2,1)} %qkv_w_ref.7), custom_call_target="tpu_custom_call" | custom-call | flops 1409286144 | bytes 20000000 | tf_op jit(solution)/shard_map/last/pallas_call | solution.py:776
  321.9 8.9 %last.3 = f32[2352,512]{1,0:T(8,128)} custom-call(bf16[2688,1536]{1,0:T(8,128)(2,1)} %get-tuple-element.143.dqkv_ref, f32[2352,512]{1,0:T(8,128)} %get-tuple-element.139.ghid_ref, bf16[2352,512]{1,0:T(8,128)(2,1)} %tok_ref.6, f32[1,512]{1,0:T(1,128)} %bitcast.48, bf16[512,1536]{1,0:T(8,128)(2,1)} %qkv_w_ref.7, ...), custom_call_target="tpu_custom_call", output_to_operand_aliasing={{}: (5, {})} | custom-call | flops 2818572288 | bytes 20000000 | tf_op jit(solution)/shard_map/last/pallas_call | solution.py:776
  334.8 4.5 %lay.1 = (f32[512,1536]{1,0:T(8,128)}, f32[512,512]{1,0:T(8,128)}) custom-call(s32[3]{0:T(128)} %pad_add_fusion.here_ref, bf16[16,64,512]{2,1,0:T(8,128)(2,1)} %bitcast.32, bf16[16,64,512]{2,1,0:T(8,128)(2,1)} %collective-permute-done.13.other_ref), custom_call_target="tpu_custom_call" | custom-call | flops 1000000 | bytes 8000000 | tf_op jit(solution)/shard_map/lay/pallas_call | solution.py:820
  (66 shorter events, 42.3 us)
Async XLA Ops:
  15.7 36.4 %all-to-all-start = ((bf16[4,624,512]{2,1,0:T(8,128)(2,1)}), bf16[4,624,512]{2,1,0:T(8,128)(2,1)}, u32[]{:S(2)}, u32[]{:S(2)}) async-start(bf16[4,624,512]{2,1,0:T(8,128)(2,1)} %dispatch.3.refs_6_), calls=%async_computation | async-start | bytes 5111808 | tf_op jit(solution)/shard_map/all_to_all | solution.py:949
  52.2 34.6 %all-to-all-start.1 = ((bf16[4,624,512]{2,1,0:T(8,128)(2,1)}), bf16[4,624,512]{2,1,0:T(8,128)(2,1)}, u32[]{:S(2)}, u32[]{:S(2)}) async-start(bf16[4,624,512]{2,1,0:T(8,128)(2,1)} %dispatch.4.refs_5_), calls=%async_computation.1 | async-start | bytes 5111808 | tf_op jit(solution)/shard_map/all_to_all | solution.py:949
  86.7 61.7 %all-to-all-start.2 = ((bf16[4,1248,512]{2,1,0:T(8,128)(2,1)}), bf16[4,1248,512]{2,1,0:T(8,128)(2,1)}, u32[]{:S(2)}, u32[]{:S(2)}) async-start(bf16[4,1248,512]{2,1,0:T(8,128)(2,1)} %dispatch.5.refs_5_.refs_6_), calls=%async_computation.2 | async-start | bytes 10223616 | tf_op jit(solution)/shard_map/all_to_all | solution.py:949
  91.8 208.1 %reduce-scatter.3.cloned.1.call-start = ((), (), s32[]{:S(2)}) async-start(), calls=%async_computation.8 | async-start | bytes 4718592 | tf_op jit(solution)/shard_map/reduce_scatter | solution.py:985
  148.5 45.5 %all-to-all-start.3 = ((bf16[4,880,512]{2,1,0:T(8,128)(2,1)}), bf16[4,880,512]{2,1,0:T(8,128)(2,1)}, u32[]{:S(2)}, u32[]{:S(2)}) async-start(bf16[4,880,512]{2,1,0:T(8,128)(2,1)} %get-tuple-element.97), calls=%async_computation.3 | async-start | bytes 7208960 | tf_op jit(solution)/shard_map/all_to_all | solution.py:949
  194.0 34.0 %all-to-all-start.4 = ((bf16[4,624,512]{2,1,0:T(8,128)(2,1)}), bf16[4,624,512]{2,1,0:T(8,128)(2,1)}, u32[]{:S(2)}, u32[]{:S(2)}) async-start(bf16[4,624,512]{2,1,0:T(8,128)(2,1)} %get-tuple-element.100), calls=%async_computation.4 | async-start | bytes 5111808 | tf_op jit(solution)/shard_map/all_to_all | solution.py:949
  198.7 101.2 %reduce-scatter.5.cloned.1.call-start = ((), (), s32[]{:S(2)}) async-start(), calls=%async_computation.9 | async-start | bytes 4718592 | tf_op jit(solution)/shard_map/reduce_scatter | solution.py:985
  228.0 50.5 %all-to-all-start.5 = ((bf16[4,992,512]{2,1,0:T(8,128)(2,1)}), bf16[4,992,512]{2,1,0:T(8,128)(2,1)}, u32[]{:S(2)}, u32[]{:S(2)}) async-start(bf16[4,992,512]{2,1,0:T(8,128)(2,1)} %get-tuple-element.114), calls=%async_computation.5 | async-start | bytes 8126464 | tf_op jit(solution)/shard_map/all_to_all | solution.py:949
  270.7 3.1 collective-permute-start
  278.5 14.5 %collective-permute-start.1 = (bf16[272,512]{1,0:T(8,128)(2,1)}, bf16[272,512]{1,0:T(8,128)(2,1)}, u32[]{:S(2)}, u32[]{:S(2)}) collective-permute-start(bf16[272,512]{1,0:T(8,128)(2,1)} %get-tuple-element.119), channel_id=1, source_target_pairs={{0,1},{1,0},{2,3},{3,2},{4,5},{5,4},{6,7},{7,6},{8,9},{9,8},{10,11... | collective-permute-start | bytes 835592 | tf_op jit(solution)/shard_map/ppermute | solution.py:869
  280.0 13.0 %collective-permute-start.2 = (bf16[272,512]{1,0:T(8,128)(2,1)}, bf16[272,512]{1,0:T(8,128)(2,1)}, u32[]{:S(2)}, u32[]{:S(2)}) collective-permute-start(bf16[272,512]{1,0:T(8,128)(2,1)} %get-tuple-element.120), channel_id=1, source_target_pairs={{0,2},{1,3},{2,0},{3,1},{4,6},{5,7},{6,4},{7,5},{8,10},{9,11},{10,... | collective-permute-start | bytes 835592 | tf_op jit(solution)/shard_map/ppermute | solution.py:869
  280.5 13.0 %collective-permute-start.3 = (bf16[272,512]{1,0:T(8,128)(2,1)}, bf16[272,512]{1,0:T(8,128)(2,1)}, u32[]{:S(2)}, u32[]{:S(2)}) collective-permute-start(bf16[272,512]{1,0:T(8,128)(2,1)} %get-tuple-element.121), channel_id=1, source_target_pairs={{0,3},{1,2},{2,1},{3,0},{4,7},{5,6},{6,5},{7,4},{8,11},{9,10},{10,... | collective-permute-start | bytes 835592 | tf_op jit(solution)/shard_map/ppermute | solution.py:869
  295.5 7.0 %collective-permute-start.4 = (bf16[80,512]{1,0:T(8,128)(2,1)}, bf16[80,512]{1,0:T(8,128)(2,1)}, u32[]{:S(2)}, u32[]{:S(2)}) collective-permute-start(bf16[80,512]{1,0:T(8,128)(2,1)} %get-tuple-element.126), channel_id=1, source_target_pairs={{0,8},{4,12},{8,0},{12,4},{16,24},{20,28},{24,16},{28,20},{1,9},{5... | collective-permute-start | bytes 245768 | tf_op jit(solution)/shard_map/ppermute | solution.py:869
  296.9 7.9 %collective-permute-start.5 = (bf16[80,512]{1,0:T(8,128)(2,1)}, bf16[80,512]{1,0:T(8,128)(2,1)}, u32[]{:S(2)}, u32[]{:S(2)}) collective-permute-start(bf16[80,512]{1,0:T(8,128)(2,1)} %get-tuple-element.127), channel_id=1, source_target_pairs={{0,16},{4,20},{8,24},{12,28},{16,0},{20,4},{24,8},{28,12},{1,17},{... | collective-permute-start | bytes 245768 | tf_op jit(solution)/shard_map/ppermute | solution.py:869
  299.4 6.7 %collective-permute-start.6 = (bf16[80,512]{1,0:T(8,128)(2,1)}, bf16[80,512]{1,0:T(8,128)(2,1)}, u32[]{:S(2)}, u32[]{:S(2)}) collective-permute-start(bf16[80,512]{1,0:T(8,128)(2,1)} %get-tuple-element.128), channel_id=1, source_target_pairs={{0,24},{4,28},{8,16},{12,20},{16,8},{20,12},{24,0},{28,4},{1,25},{... | collective-permute-start | bytes 245768 | tf_op jit(solution)/shard_map/ppermute | solution.py:869
  307.7 10.5 %collective-permute-start.9 = (bf16[64,512]{1,0:T(8,128)(2,1)}, bf16[64,512]{1,0:T(8,128)(2,1)S(1)}, u32[]{:S(2)}, u32[]{:S(2)}) collective-permute-start(bf16[64,512]{1,0:T(8,128)(2,1)} %get-tuple-element.137), channel_id=1, source_target_pairs={{0,24},{4,28},{8,16},{12,20},{16,8},{20,12},{24,0},{28,4},{1,25},{... | collective-permute-start | bytes 196616 | tf_op jit(solution)/shard_map/ppermute | solution.py:869
  309.5 8.8 %collective-permute-start.8 = (bf16[64,512]{1,0:T(8,128)(2,1)}, bf16[64,512]{1,0:T(8,128)(2,1)S(1)}, u32[]{:S(2)}, u32[]{:S(2)}) collective-permute-start(bf16[64,512]{1,0:T(8,128)(2,1)} %get-tuple-element.137), channel_id=1, source_target_pairs={{0,16},{4,20},{8,24},{12,28},{16,0},{20,4},{24,8},{28,12},{1,17},{... | collective-permute-start | bytes 196616 | tf_op jit(solution)/shard_map/ppermute | solution.py:869
  310.2 8.1 %collective-permute-start.7 = (bf16[64,512]{1,0:T(8,128)(2,1)}, bf16[64,512]{1,0:T(8,128)(2,1)S(1)}, u32[]{:S(2)}, u32[]{:S(2)}) collective-permute-start(bf16[64,512]{1,0:T(8,128)(2,1)} %get-tuple-element.137), channel_id=1, source_target_pairs={{0,8},{4,12},{8,0},{12,4},{16,24},{20,28},{24,16},{28,20},{1,9},{5... | collective-permute-start | bytes 196616 | tf_op jit(solution)/shard_map/ppermute | solution.py:869
  318.4 13.7 %copy-start.5 = (f32[16,512]{1,0:T(8,128)S(1)}, f32[16,512]{1,0:T(8,128)}, u32[]{:S(2)}) copy-start(f32[16,512]{1,0:T(8,128)} %get-tuple-element.144) | copy-start | bytes 98308
  318.4 14.3 %copy-start.3 = (f32[512]{0:T(512)S(1)}, f32[512]{0:T(512)}, u32[]{:S(2)}) copy-start(f32[512]{0:T(512)} %param.12) | copy-start | bytes 6148
  318.4 12.5 %collective-permute-start.11 = (bf16[4,64,512]{2,1,0:T(8,128)(2,1)S(1)}, bf16[4,64,512]{2,1,0:T(8,128)(2,1)S(1)}, u32[]{:S(2)}, u32[]{:S(2)}) collective-permute-start(bf16[4,64,512]{2,1,0:T(8,128)(2,1)S(1)} %get-tuple-element.154), channel_id=1, source_target_pairs={{0,2},{1,3},{2,0},{3,1},{4,6},{5,7},{6,4},{7,5},{8,10},{9,11},{10,... | collective-permute-start | bytes 786440 | tf_op jit(solution)/shard_map/ppermute | solution.py:869
  319.3 11.6 %collective-permute-start.10 = (bf16[4,64,512]{2,1,0:T(8,128)(2,1)S(1)}, bf16[4,64,512]{2,1,0:T(8,128)(2,1)S(1)}, u32[]{:S(2)}, u32[]{:S(2)}) collective-permute-start(bf16[4,64,512]{2,1,0:T(8,128)(2,1)S(1)} %get-tuple-element.154), channel_id=1, source_target_pairs={{0,1},{1,0},{2,3},{3,2},{4,5},{5,4},{6,7},{7,6},{8,9},{9,8},{10,11... | collective-permute-start | bytes 786440 | tf_op jit(solution)/shard_map/ppermute | solution.py:869
  319.9 11.0 %collective-permute-start.12 = (bf16[4,64,512]{2,1,0:T(8,128)(2,1)S(1)}, bf16[4,64,512]{2,1,0:T(8,128)(2,1)S(1)}, u32[]{:S(2)}, u32[]{:S(2)}) collective-permute-start(bf16[4,64,512]{2,1,0:T(8,128)(2,1)S(1)} %get-tuple-element.154), channel_id=1, source_target_pairs={{0,3},{1,2},{2,1},{3,0},{4,7},{5,6},{6,5},{7,4},{8,11},{9,10},{10,... | collective-permute-start | bytes 786440 | tf_op jit(solution)/shard_map/ppermute | solution.py:869
  332.0 2.8 collective-permute-start.13
  (4 other events, 17.4 us)
Sparse Core Ops, SparseCore 0:
  133.6 51.2 reduce-scatter.2
  218.9 51.1 reduce-scatter.4
